TPU v7x, 32 devices: a whole 2x2x4 slice. The times are simulated.
32 devices in a mesh: clip: 4 (over z), tok: 4 (over x, core), head: 2 (over y).
Axes of the slice: x: 2, y: 2, z: 4, core: 2. Of those that a mesh axis runs over, the one named last changes fastest.
Arguments:
- clips_in: bfloat16 [4, 4, 16, 196, 384], P('clip', None, 'tok'), may hold values from -6 to 6
- resets: int32 [4, 4], P('clip'), may hold values from 0 to 1, as said below
- assign: int32 [4, 4], P('clip'), may hold values from 0 to 3, as said below
- w_qkv_a: bfloat16 [384, 3, 384], P('tok', None, 'head'), may hold values from -0.625 to 0.625
- w_out_a: bfloat16 [384, 384], P('tok', 'head'), may hold values from -0.15625 to 0.15625
- w_up_a: bfloat16 [384, 1536], P('tok', 'head'), may hold values from -0.3125 to 0.3125
- w_down_a: bfloat16 [384, 1536], P('tok', 'head'), may hold values from -0.15625 to 0.15625
- w_qkv_b: bfloat16 [384, 3, 768], P('tok', None, 'head'), may hold values from -0.625 to 0.625
- w_out_b: bfloat16 [768, 768], P('tok', 'head'), may hold values from -0.109375 to 0.109375
- w_skip_b: bfloat16 [768, 384], P('tok', 'head'), may hold values from -0.3125 to 0.3125
- w_up_b: bfloat16 [768, 3072], P('tok', 'head'), may hold values from -0.21875 to 0.21875
- w_down_b: bfloat16 [768, 3072], P('tok', 'head'), may hold values from -0.109375 to 0.109375
- gains_a: float32 [3, 384], replicated, may hold values from 0.25 to 1.75
- gains_b: float32 [768], replicated, may hold values from 0.25 to 1.75
- shifts_a: float32 [5, 384], replicated, may hold values from -1.2 to 1.2
- shifts_b: float32 [3, 768], replicated, may hold values from -1.2 to 1.2
- qv_bias_a: float32 [2, 384], P(None, 'head'), may hold values from -1.2 to 1.2
- qv_bias_b: float32 [2, 768], P(None, 'head'), may hold values from -1.2 to 1.2
- up_bias_a: float32 [1536], P('head'), may hold values from -1.2 to 1.2
- up_bias_b: float32 [3072], P('head'), may hold values from -1.2 to 1.2
- cotangent: bfloat16 [4, 4, 16, 49, 768], P('clip', None, 'tok'), may hold values from -6 to 6
Outputs:
- mixed: bfloat16 [4, 4, 16, 49, 768], P('clip', None, 'tok')
- grad_clips_in: float32 [4, 4, 16, 196, 384], P('clip', None, 'tok')
- grad_w_qkv_a: float32 [384, 3, 384], P('tok', None, 'head')
- grad_w_out_a: float32 [384, 384], P('tok', 'head')
- grad_w_up_a: float32 [384, 1536], P('tok', 'head')
- grad_w_down_a: float32 [384, 1536], P('tok', 'head')
- grad_w_qkv_b: float32 [384, 3, 768], P('tok', None, 'head')
- grad_w_out_b: float32 [768, 768], P('tok', 'head')
- grad_w_skip_b: float32 [768, 384], P('tok', 'head')
- grad_w_up_b: float32 [768, 3072], P('tok', 'head')
- grad_w_down_b: float32 [768, 3072], P('tok', 'head')
- grad_gains_a: float32 [3, 384], replicated
- grad_gains_b: float32 [768], replicated
- grad_shifts_a: float32 [5, 384], replicated
- grad_shifts_b: float32 [3, 768], replicated
- grad_qv_bias_a: float32 [2, 384], P(None, 'head')
- grad_qv_bias_b: float32 [2, 768], P(None, 'head')
- grad_up_bias_a: float32 [1536], P('head')
- grad_up_bias_b: float32 [3072], P('head')
Inputs may be any that keep to these rules, and one draw needn't show every extreme that they name: `resets`: 1 marks a clip that starts a new video; every micro-batch is marked at clip 0; following assign back from some micro-batch of the last clip reaches clip 0 through unmarked clips. `assign`: each row is a permutation of the 4 micro-batches.
All inputs are finite; a program needn't handle non-finite values.
Results may differ from a plain program's by a relative error of at most 0.023.
Values may be sent and summed in bfloat16 or wider, within the bound.
A program may use at most 448 MiB of HBM per device.

v0:
```python
import jax
import jax.numpy as jnp
from jax import lax
from jax.sharding import PartitionSpec as P

D1 = 384
HEADS_A = 4
D2 = 768
HEADS_B = 8
GRID = 14
POOLED = 49


eps = 1e-06
precise = lax.Precision.HIGHEST


def passed_along(shard, axis, by):
    peers = lax.axis_size(axis)
    pairs = [(i, i + by) for i in range(peers) if 0 <= i + by < peers]
    return lax.ppermute(shard, axis, pairs)


def layer_norm(tensor, gain_row, shift_row):
    average = jnp.mean(tensor, axis=-1, keepdims=True)
    centred = tensor - average
    variance = jnp.mean(centred * centred, axis=-1, keepdims=True)
    return centred * lax.rsqrt(variance + eps) * gain_row + shift_row


def norm_back(tensor, gain_row, shift_row, gradient):
    primal, pullback = jax.vjp(layer_norm, tensor, gain_row, shift_row)
    return pullback(gradient)


def gelu_back(pre_act, gradient):
    primal, pullback = jax.vjp(lambda argument: jax.nn.gelu(argument, approximate=True), pre_act)
    return pullback(gradient)[0]


def pool_grid(tensor):
    extent = tensor.shape
    half_grid = GRID // 2
    grid_view = tensor.reshape(extent[:-2] + (half_grid, 2, half_grid, 2, extent[-1]))
    return jnp.mean(grid_view, axis=(-4, -2)).reshape(
        extent[:-2] + (half_grid * half_grid, extent[-1])
    )


def unpool_grid(tensor):
    extent = tensor.shape
    half_grid = GRID // 2
    grid_view = tensor.reshape(extent[:-2] + (half_grid, 1, half_grid, 1, extent[-1])) * 0.25
    grid_view = jnp.broadcast_to(grid_view, extent[:-2] + (half_grid, 2, half_grid, 2, extent[-1]))
    return grid_view.reshape(extent[:-2] + (GRID * GRID, extent[-1]))


def to_heads(tensor, head_dim):
    return tensor.reshape(tensor.shape[:-1] + (tensor.shape[-1] // head_dim, head_dim))


def head_total(partial_sum):
    return lax.psum(partial_sum.astype(jnp.bfloat16), "head").astype(jnp.float32)


def head_grad(partial_sum):
    return lax.psum(partial_sum.astype(jnp.bfloat16), "head").astype(jnp.float32)


def compress(tensor):
    batches, frames = (tensor.shape[0], tensor.shape[1])
    frame_pairs = tensor.reshape((batches, frames // 2, 2) + tensor.shape[2:]).astype(jnp.float32)
    merged = jnp.mean(frame_pairs, axis=2).astype(jnp.bfloat16)
    return merged.reshape((batches, frames // 2 * tensor.shape[2]) + tensor.shape[3:])


def expand(tensor, frames):
    batches = tensor.shape[0]
    paired = tensor.reshape((batches, frames // 2, 1, -1) + tensor.shape[2:]) * 0.5
    paired = jnp.broadcast_to(paired, (batches, frames // 2, 2) + paired.shape[3:])
    return paired.reshape((batches, frames) + paired.shape[3:])


def share_keys(pooled_keys, pooled_values, chooser):
    clip_keys, clip_values = (
        lax.all_gather(pooled_keys, "tok", axis=1, tiled=True),
        lax.all_gather(pooled_values, "tok", axis=1, tiled=True),
    )
    sent_keys, sent_values = passed_along((compress(clip_keys), compress(clip_values)), "clip", 1)
    chooser_low = chooser.astype(jnp.bfloat16)
    mem_keys = jnp.einsum(
        "ms,sjhe->mjhe", chooser_low, sent_keys, preferred_element_type=jnp.float32
    ).astype(jnp.bfloat16)
    mem_values = jnp.einsum(
        "ms,sjhe->mjhe", chooser_low, sent_values, preferred_element_type=jnp.float32
    ).astype(jnp.bfloat16)
    flat_keys = clip_keys.reshape((clip_keys.shape[0], -1) + clip_keys.shape[3:])
    flat_values = clip_values.reshape((clip_values.shape[0], -1) + clip_values.shape[3:])
    return (flat_keys, flat_values, mem_keys, mem_values)


def return_keys(key_grad, value_grad, local_count, chooser):
    frames = local_count // POOLED
    mem_key_grad = jnp.einsum(
        "ms,mjhe->sjhe", chooser, key_grad[:, local_count:], precision=precise
    )
    mem_value_grad = jnp.einsum(
        "ms,mjhe->sjhe", chooser, value_grad[:, local_count:], precision=precise
    )
    back_keys, back_values = (
        passed_along(mem_key_grad.astype(jnp.bfloat16), "clip", -1).astype(mem_key_grad.dtype),
        passed_along(mem_value_grad.astype(jnp.bfloat16), "clip", -1).astype(mem_value_grad.dtype),
    )
    batches = key_grad.shape[0]
    total_keys = key_grad[:, :local_count].reshape(
        (batches, frames, POOLED) + key_grad.shape[2:]
    ) + expand(back_keys, frames)
    total_values = value_grad[:, :local_count].reshape(
        (batches, frames, POOLED) + value_grad.shape[2:]
    ) + expand(back_values, frames)
    return (
        lax.psum_scatter(
            total_keys.astype(jnp.bfloat16), "tok", scatter_dimension=1, tiled=True
        ).astype(jnp.float32),
        lax.psum_scatter(
            total_values.astype(jnp.bfloat16), "tok", scatter_dimension=1, tiled=True
        ).astype(jnp.float32),
    )


def keep_columns(local_count, mem_count, has_memory):
    column = jnp.arange(local_count + mem_count)
    return ((column[None, :] < local_count) | (has_memory[:, None] > 0.5))[:, None, None, :]


def attention(queries, all_keys, all_values, keep_mask):
    scaling = queries.shape[-1] ** (-0.5)
    scores = (
        jnp.einsum("mqhe,mkhe->mhqk", queries, all_keys, preferred_element_type=jnp.float32)
        * scaling
    )
    scores = jnp.where(keep_mask, scores, -1e30)
    highest = jnp.max(scores, axis=-1, keepdims=True)
    exponent = jnp.exp(scores - highest)
    denominator = jnp.sum(exponent, axis=-1, keepdims=True)
    weights_low = (exponent / denominator).astype(jnp.bfloat16)
    attended = jnp.einsum(
        "mhqk,mkhe->mqhe", weights_low, all_values, preferred_element_type=jnp.float32
    )
    return (attended, highest + jnp.log(denominator))


def attention_back(queries, all_keys, all_values, keep_mask, log_total, grad_low):
    scaling = queries.shape[-1] ** (-0.5)
    scores = (
        jnp.einsum("mqhe,mkhe->mhqk", queries, all_keys, preferred_element_type=jnp.float32)
        * scaling
    )
    scores = jnp.where(keep_mask, scores, -1e30)
    probs = jnp.exp(scores - log_total)
    value_grad = jnp.einsum(
        "mhqk,mqhe->mkhe", probs.astype(jnp.bfloat16), grad_low, preferred_element_type=jnp.float32
    )
    prob_grad = jnp.einsum(
        "mqhe,mkhe->mhqk", grad_low, all_values, preferred_element_type=jnp.float32
    )
    inner_sum = jnp.sum(prob_grad * probs, axis=-1, keepdims=True)
    score_grad = (probs * (prob_grad - inner_sum)).astype(jnp.bfloat16)
    query_grad = (
        jnp.einsum("mhqk,mkhe->mqhe", score_grad, all_keys, preferred_element_type=jnp.float32)
        * scaling
    )
    key_grad = (
        jnp.einsum("mhqk,mqhe->mkhe", score_grad, queries, preferred_element_type=jnp.float32)
        * scaling
    )
    return (query_grad, key_grad, value_grad)


def mlp_part(
    attn_partial, base, shift_attn, gain_mlp, shift_norm, shift_out, w_up, up_bias, w_down
):
    residual = head_total(attn_partial) + shift_attn
    if base is not None:
        residual = residual + base
    normed_mlp = layer_norm(residual, gain_mlp, shift_norm).astype(jnp.bfloat16)
    pre_act = (
        jnp.einsum("mfpd,dh->mfph", normed_mlp, w_up, preferred_element_type=jnp.float32) + up_bias
    )
    hidden = jax.nn.gelu(pre_act, approximate=True).astype(jnp.bfloat16)
    result = (
        residual
        + head_total(
            jnp.einsum("mfph,oh->mfpo", hidden, w_down, preferred_element_type=jnp.float32)
        )
        + shift_out
    )
    return (result, residual, normed_mlp, pre_act, hidden)


def forward_first(stream, matrices, vectors, chooser, has_memory):
    w_qkv, w_out, w_up, w_down = matrices
    gain_rows, shifts, qv_bias, up_bias = vectors
    batches, frames, patches, width = stream.shape
    head_dim = D1 // HEADS_A
    normed = layer_norm(stream, gain_rows[0], shifts[0]).astype(jnp.bfloat16)
    projected = jnp.einsum("mfpd,dke->mfpke", normed, w_qkv, preferred_element_type=jnp.float32)
    queries = (projected[..., 0, :] + qv_bias[0]).astype(jnp.bfloat16)
    pooled_keys = pool_grid(projected[..., 1, :]).astype(jnp.bfloat16)
    pooled_values = pool_grid(projected[..., 2, :] + qv_bias[1]).astype(jnp.bfloat16)
    clip_keys, clip_values, mem_keys, mem_values = share_keys(
        to_heads(pooled_keys, head_dim), to_heads(pooled_values, head_dim), chooser
    )
    keep_mask = keep_columns(clip_keys.shape[1], mem_keys.shape[1], has_memory)
    all_keys = jnp.concatenate([clip_keys, mem_keys], axis=1)
    all_values = jnp.concatenate([clip_values, mem_values], axis=1)
    query_heads = to_heads(queries, head_dim).reshape(batches, frames * patches, -1, head_dim)
    attended, log_total = attention(query_heads, all_keys, all_values, keep_mask)
    combined = (
        (attended + query_heads.astype(jnp.float32))
        .astype(jnp.bfloat16)
        .reshape(batches, frames, patches, -1)
    )
    attn_partial = jnp.einsum("mfpi,oi->mfpo", combined, w_out, preferred_element_type=jnp.float32)
    result, residual, normed_mlp, pre_act, hidden = mlp_part(
        attn_partial, stream, shifts[1], gain_rows[1], shifts[2], shifts[3], w_up, up_bias, w_down
    )
    kept_values = (
        normed,
        query_heads,
        all_keys,
        all_values,
        keep_mask,
        log_total,
        combined,
        residual,
        normed_mlp,
        pre_act,
        hidden,
        clip_keys.shape[1],
    )
    return (result, kept_values)


def backward_first(gradient, stream, matrices, vectors, chooser, kept_values):
    w_qkv, w_out, w_up, w_down = matrices
    gain_rows, shifts, qv_bias, up_bias = vectors
    (
        normed,
        query_heads,
        all_keys,
        all_values,
        keep_mask,
        log_total,
        combined,
        residual,
        normed_mlp,
        pre_act,
        hidden,
        local_count,
    ) = kept_values
    batches, frames, patches, width = stream.shape
    grad_low = gradient.astype(jnp.bfloat16)
    down_grad = jnp.einsum("mfpo,mfph->oh", grad_low, hidden, preferred_element_type=jnp.float32)
    hidden_grad = jnp.einsum("mfpo,oh->mfph", grad_low, w_down, preferred_element_type=jnp.float32)
    pre_grad = gelu_back(pre_act, hidden_grad)
    up_bias_grad = jnp.sum(pre_grad, axis=(0, 1, 2))
    pre_low = pre_grad.astype(jnp.bfloat16)
    up_grad = jnp.einsum("mfpd,mfph->dh", normed_mlp, pre_low, preferred_element_type=jnp.float32)
    mlp_in_grad = head_grad(
        jnp.einsum("mfph,dh->mfpd", pre_low, w_up, preferred_element_type=jnp.float32)
    )
    residual_grad, gain_mlp_grad, shift_mlp_grad = norm_back(
        residual, gain_rows[1], shifts[2], mlp_in_grad
    )
    residual_grad = residual_grad + gradient
    residual_low = residual_grad.astype(jnp.bfloat16)
    out_grad = jnp.einsum(
        "mfpo,mfpi->oi", residual_low, combined, preferred_element_type=jnp.float32
    )
    combined_grad = jnp.einsum(
        "mfpo,oi->mfpi", residual_low, w_out, preferred_element_type=jnp.float32
    ).astype(jnp.bfloat16)
    combined_grad = combined_grad.reshape(query_heads.shape)
    query_grad, key_grad, value_grad = attention_back(
        query_heads, all_keys, all_values, keep_mask, log_total, combined_grad
    )
    query_grad = (query_grad + combined_grad.astype(jnp.float32)).reshape(
        batches, frames, patches, -1
    )
    key_own, value_own = return_keys(key_grad, value_grad, local_count, chooser)
    key_flat = unpool_grid(key_own.reshape(key_own.shape[:3] + (-1,)))
    value_flat = unpool_grid(value_own.reshape(value_own.shape[:3] + (-1,)))
    qv_grad = jnp.stack([jnp.sum(query_grad, axis=(0, 1, 2)), jnp.sum(value_flat, axis=(0, 1, 2))])
    projected_grad = jnp.stack([query_grad, key_flat, value_flat], axis=3).astype(jnp.bfloat16)
    qkv_grad = jnp.einsum(
        "mfpd,mfpke->dke", normed, projected_grad, preferred_element_type=jnp.float32
    )
    normed_grad = head_grad(
        jnp.einsum("mfpke,dke->mfpd", projected_grad, w_qkv, preferred_element_type=jnp.float32)
    )
    stream_grad, gain_in_grad, shift_in_grad = norm_back(
        stream, gain_rows[0], shifts[0], normed_grad
    )
    small_grads = (
        gain_in_grad,
        gain_mlp_grad,
        shift_in_grad,
        jnp.sum(residual_grad, axis=(0, 1, 2)),
        shift_mlp_grad,
        jnp.sum(gradient, axis=(0, 1, 2)),
        qv_grad,
        up_bias_grad,
    )
    return (stream_grad + residual_grad, (qkv_grad, out_grad, up_grad, down_grad), small_grads)


def forward_second(stream, matrices, vectors, chooser, has_memory):
    w_qkv, w_out, w_skip, w_up, w_down = matrices
    gain_in, shift_in, gain_mlp, shifts, qv_bias, up_bias = vectors
    batches, frames, patches, width = stream.shape
    head_dim = D2 // HEADS_B
    normed_full = layer_norm(stream, gain_in, shift_in)
    normed = normed_full.astype(jnp.bfloat16)
    projected = jnp.einsum("mfpd,dke->mfpke", normed, w_qkv, preferred_element_type=jnp.float32)
    queries = pool_grid(projected[..., 0, :] + qv_bias[0]).astype(jnp.bfloat16)
    pooled_keys = pool_grid(projected[..., 1, :]).astype(jnp.bfloat16)
    pooled_values = pool_grid(projected[..., 2, :] + qv_bias[1]).astype(jnp.bfloat16)
    clip_keys, clip_values, mem_keys, mem_values = share_keys(
        to_heads(pooled_keys, head_dim), to_heads(pooled_values, head_dim), chooser
    )
    keep_mask = keep_columns(clip_keys.shape[1], mem_keys.shape[1], has_memory)
    all_keys = jnp.concatenate([clip_keys, mem_keys], axis=1)
    all_values = jnp.concatenate([clip_values, mem_values], axis=1)
    query_heads = to_heads(queries, head_dim).reshape(batches, frames * POOLED, -1, head_dim)
    attended, log_total = attention(query_heads, all_keys, all_values, keep_mask)
    combined = (
        (attended + query_heads.astype(jnp.float32))
        .astype(jnp.bfloat16)
        .reshape(batches, frames, POOLED, -1)
    )
    slice_width = w_skip.shape[1]
    own_slice = lax.dynamic_slice_in_dim(
        normed_full, lax.axis_index("head") * slice_width, slice_width, 3
    )
    skip_in = pool_grid(own_slice).astype(jnp.bfloat16)
    partial_sum = jnp.einsum("mfpi,oi->mfpo", combined, w_out, preferred_element_type=jnp.float32)
    partial_sum = partial_sum + jnp.einsum(
        "mfpi,oi->mfpo", skip_in, w_skip, preferred_element_type=jnp.float32
    )
    result, residual, normed_mlp, pre_act, hidden = mlp_part(
        partial_sum, None, shifts[0], gain_mlp, shifts[1], shifts[2], w_up, up_bias, w_down
    )
    kept_values = (
        normed,
        query_heads,
        all_keys,
        all_values,
        keep_mask,
        log_total,
        combined,
        skip_in,
        residual,
        normed_mlp,
        pre_act,
        hidden,
        clip_keys.shape[1],
    )
    return (result, kept_values)


def backward_second(gradient, stream, matrices, vectors, chooser, kept_values):
    w_qkv, w_out, w_skip, w_up, w_down = matrices
    gain_in, shift_in, gain_mlp, shifts, qv_bias, up_bias = vectors
    (
        normed,
        query_heads,
        all_keys,
        all_values,
        keep_mask,
        log_total,
        combined,
        skip_in,
        residual,
        normed_mlp,
        pre_act,
        hidden,
        local_count,
    ) = kept_values
    batches, frames, patches, width = stream.shape
    grad_low = gradient.astype(jnp.bfloat16)
    down_grad = jnp.einsum("mfpo,mfph->oh", grad_low, hidden, preferred_element_type=jnp.float32)
    hidden_grad = jnp.einsum("mfpo,oh->mfph", grad_low, w_down, preferred_element_type=jnp.float32)
    pre_grad = gelu_back(pre_act, hidden_grad)
    up_bias_grad = jnp.sum(pre_grad, axis=(0, 1, 2))
    pre_low = pre_grad.astype(jnp.bfloat16)
    up_grad = jnp.einsum("mfpd,mfph->dh", normed_mlp, pre_low, preferred_element_type=jnp.float32)
    mlp_in_grad = head_grad(
        jnp.einsum("mfph,dh->mfpd", pre_low, w_up, preferred_element_type=jnp.float32)
    )
    residual_grad, gain_mlp_grad, shift_mlp_grad = norm_back(
        residual, gain_mlp, shifts[1], mlp_in_grad
    )
    residual_grad = residual_grad + gradient
    residual_low = residual_grad.astype(jnp.bfloat16)
    out_grad = jnp.einsum(
        "mfpo,mfpi->oi", residual_low, combined, preferred_element_type=jnp.float32
    )
    skip_grad = jnp.einsum(
        "mfpo,mfpi->oi", residual_low, skip_in, preferred_element_type=jnp.float32
    )
    combined_grad = jnp.einsum(
        "mfpo,oi->mfpi", residual_low, w_out, preferred_element_type=jnp.float32
    ).astype(jnp.bfloat16)
    combined_grad = combined_grad.reshape(query_heads.shape)
    skip_in_grad = jnp.einsum(
        "mfpo,oi->mfpi", residual_low, w_skip, preferred_element_type=jnp.float32
    )
    query_grad, key_grad, value_grad = attention_back(
        query_heads, all_keys, all_values, keep_mask, log_total, combined_grad
    )
    query_grad = (query_grad + combined_grad.astype(jnp.float32)).reshape(
        batches, frames, POOLED, -1
    )
    query_flat = unpool_grid(query_grad)
    key_own, value_own = return_keys(key_grad, value_grad, local_count, chooser)
    key_flat = unpool_grid(key_own.reshape(key_own.shape[:3] + (-1,)))
    value_flat = unpool_grid(value_own.reshape(value_own.shape[:3] + (-1,)))
    qv_grad = jnp.stack([jnp.sum(query_flat, axis=(0, 1, 2)), jnp.sum(value_flat, axis=(0, 1, 2))])
    projected_grad = jnp.stack([query_flat, key_flat, value_flat], axis=3).astype(jnp.bfloat16)
    qkv_grad = jnp.einsum(
        "mfpd,mfpke->dke", normed, projected_grad, preferred_element_type=jnp.float32
    )
    partial_sum = jnp.einsum(
        "mfpke,dke->mfpd", projected_grad, w_qkv, preferred_element_type=jnp.float32
    )
    slice_width = w_skip.shape[1]
    slice_start = lax.axis_index("head") * slice_width
    current = lax.dynamic_slice_in_dim(partial_sum, slice_start, slice_width, 3)
    partial_sum = lax.dynamic_update_slice_in_dim(
        partial_sum, current + unpool_grid(skip_in_grad), slice_start, 3
    )
    normed_grad = head_grad(partial_sum)
    stream_grad, gain_in_grad, shift_in_grad = norm_back(stream, gain_in, shift_in, normed_grad)
    small_grads = (
        gain_in_grad,
        shift_in_grad,
        gain_mlp_grad,
        jnp.sum(residual_grad, axis=(0, 1, 2)),
        shift_mlp_grad,
        jnp.sum(gradient, axis=(0, 1, 2)),
        qv_grad,
        up_bias_grad,
    )
    return (stream_grad, (qkv_grad, out_grad, skip_grad, up_grad, down_grad), small_grads)


def fetch_first(w_qkv_a, w_out_a, w_up_a, w_down_a):
    return (
        lax.all_gather(w_qkv_a, "tok", axis=0, tiled=True),
        lax.all_gather(w_out_a, "tok", axis=0, tiled=True),
        lax.all_gather(w_up_a, "tok", axis=0, tiled=True),
        lax.all_gather(w_down_a, "tok", axis=0, tiled=True),
    )


def fetch_second(w_qkv_b, w_out_b, w_skip_b, w_up_b, w_down_b):
    return (
        lax.all_gather(w_qkv_b, "tok", axis=0, tiled=True),
        lax.all_gather(w_out_b, "tok", axis=0, tiled=True),
        lax.all_gather(w_skip_b, "tok", axis=0, tiled=True),
        lax.all_gather(w_up_b, "tok", axis=0, tiled=True),
        lax.all_gather(w_down_b, "tok", axis=0, tiled=True),
    )


def local(
    clips_in,
    resets,
    assign,
    w_qkv_a,
    w_out_a,
    w_up_a,
    w_down_a,
    w_qkv_b,
    w_out_b,
    w_skip_b,
    w_up_b,
    w_down_b,
    gains_a,
    gains_b,
    shifts_a,
    shifts_b,
    qv_bias_a,
    qv_bias_b,
    up_bias_a,
    up_bias_b,
    cotangent,
):
    batches = clips_in.shape[1]
    chooser = (assign[0][:, None] == jnp.arange(batches)[None, :]).astype(jnp.float32)
    has_memory = ((resets[0] == 0) & (lax.axis_index("clip") > 0)).astype(jnp.float32)
    stream = clips_in[0].astype(jnp.float32)
    vectors_first = (gains_a, shifts_a, qv_bias_a, up_bias_a)
    vectors_second = (gains_a[2], shifts_a[4], gains_b, shifts_b, qv_bias_b, up_bias_b)
    first_weights = fetch_first(w_qkv_a, w_out_a, w_up_a, w_down_a)
    second_weights = fetch_second(w_qkv_b, w_out_b, w_skip_b, w_up_b, w_down_b)
    middle, unused = forward_first(stream, first_weights, vectors_first, chooser, has_memory)
    result, unused = forward_second(middle, second_weights, vectors_second, chooser, has_memory)
    second_back = fetch_second(w_qkv_b, w_out_b, w_skip_b, w_up_b, w_down_b)
    first_back = fetch_first(w_qkv_a, w_out_a, w_up_a, w_down_a)
    unused, kept_second = forward_second(middle, second_back, vectors_second, chooser, has_memory)
    middle_grad, grads_second, small_second = backward_second(
        cotangent[0].astype(jnp.float32), middle, second_back, vectors_second, chooser, kept_second
    )
    unused, kept_first = forward_first(stream, first_back, vectors_first, chooser, has_memory)
    stream_grad, grads_first, small_first = backward_first(
        middle_grad, stream, first_back, vectors_first, chooser, kept_first
    )
    local_qkv_a, local_out_a, local_up_a, local_down_a = grads_first
    local_qkv_b, local_out_b, local_skip_b, local_up_b, local_down_b = grads_second
    (
        shard_qkv_a,
        shard_out_a,
        shard_up_a,
        shard_down_a,
        shard_qkv_b,
        shard_out_b,
        shard_skip_b,
        shard_up_b,
        shard_down_b,
    ) = (
        lax.psum_scatter(
            local_qkv_a.astype(jnp.bfloat16), "tok", scatter_dimension=0, tiled=True
        ).astype(jnp.float32),
        lax.psum_scatter(
            local_out_a.astype(jnp.bfloat16), "tok", scatter_dimension=0, tiled=True
        ).astype(jnp.float32),
        lax.psum_scatter(
            local_up_a.astype(jnp.bfloat16), "tok", scatter_dimension=0, tiled=True
        ).astype(jnp.float32),
        lax.psum_scatter(
            local_down_a.astype(jnp.bfloat16), "tok", scatter_dimension=0, tiled=True
        ).astype(jnp.float32),
        lax.psum_scatter(
            local_qkv_b.astype(jnp.bfloat16), "tok", scatter_dimension=0, tiled=True
        ).astype(jnp.float32),
        lax.psum_scatter(
            local_out_b.astype(jnp.bfloat16), "tok", scatter_dimension=0, tiled=True
        ).astype(jnp.float32),
        lax.psum_scatter(
            local_skip_b.astype(jnp.bfloat16), "tok", scatter_dimension=0, tiled=True
        ).astype(jnp.float32),
        lax.psum_scatter(
            local_up_b.astype(jnp.bfloat16), "tok", scatter_dimension=0, tiled=True
        ).astype(jnp.float32),
        lax.psum_scatter(
            local_down_b.astype(jnp.bfloat16), "tok", scatter_dimension=0, tiled=True
        ).astype(jnp.float32),
    )
    summed_weights = (
        lax.psum(shard_qkv_a.astype(jnp.bfloat16), "clip").astype(jnp.float32),
        lax.psum(shard_out_a.astype(jnp.bfloat16), "clip").astype(jnp.float32),
        lax.psum(shard_up_a.astype(jnp.bfloat16), "clip").astype(jnp.float32),
        lax.psum(shard_down_a.astype(jnp.bfloat16), "clip").astype(jnp.float32),
        lax.psum(shard_qkv_b.astype(jnp.bfloat16), "clip").astype(jnp.float32),
        lax.psum(shard_out_b.astype(jnp.bfloat16), "clip").astype(jnp.float32),
        lax.psum(shard_skip_b.astype(jnp.bfloat16), "clip").astype(jnp.float32),
        lax.psum(shard_up_b.astype(jnp.bfloat16), "clip").astype(jnp.float32),
        lax.psum(shard_down_b.astype(jnp.bfloat16), "clip").astype(jnp.float32),
    )
    (
        gain_in_a,
        gain_mlp_a,
        shift_in_a,
        proj_bias_a,
        shift_mlp_a,
        down_bias_a,
        qv_grad_a,
        up_grad_a,
    ) = small_first
    (
        gain_in_b,
        shift_in_b,
        gain_mlp_b,
        proj_bias_b,
        shift_mlp_b,
        down_bias_b,
        qv_grad_b,
        up_grad_b,
    ) = small_second
    gains_a_grad = jnp.stack([gain_in_a, gain_mlp_a, gain_in_b])
    shifts_a_grad = jnp.stack([shift_in_a, proj_bias_a, shift_mlp_a, down_bias_a, shift_in_b])
    shifts_b_grad = jnp.stack([proj_bias_b, shift_mlp_b, down_bias_b])
    summed_small = lax.psum(
        (
            gains_a_grad,
            gain_mlp_b,
            shifts_a_grad,
            shifts_b_grad,
            qv_grad_a,
            qv_grad_b,
            up_grad_a,
            up_grad_b,
        ),
        ("clip", "tok"),
    )
    return (
        result[None].astype(jnp.bfloat16),
        stream_grad[None],
        summed_weights[0],
        summed_weights[1],
        summed_weights[2],
        summed_weights[3],
        summed_weights[4],
        summed_weights[5],
        summed_weights[6],
        summed_weights[7],
        summed_weights[8],
        summed_small[0],
        summed_small[1],
        summed_small[2],
        summed_small[3],
        summed_small[4],
        summed_small[5],
        summed_small[6],
        summed_small[7],
    )


def solution(mesh):
    in_specs = (
        P("clip", None, "tok", None, None),
        P("clip", None),
        P("clip", None),
        P("tok", None, "head"),
        P("tok", "head"),
        P("tok", "head"),
        P("tok", "head"),
        P("tok", None, "head"),
        P("tok", "head"),
        P("tok", "head"),
        P("tok", "head"),
        P("tok", "head"),
        P(),
        P(),
        P(),
        P(),
        P(None, "head"),
        P(None, "head"),
        P("head"),
        P("head"),
        P("clip", None, "tok", None, None),
    )
    out_specs = (
        P("clip", None, "tok", None, None),
        P("clip", None, "tok", None, None),
        P("tok", None, "head"),
        P("tok", "head"),
        P("tok", "head"),
        P("tok", "head"),
        P("tok", None, "head"),
        P("tok", "head"),
        P("tok", "head"),
        P("tok", "head"),
        P("tok", "head"),
        P(),
        P(),
        P(),
        P(),
        P(None, "head"),
        P(None, "head"),
        P("head"),
        P("head"),
    )
    return jax.shard_map(local, mesh=mesh, in_specs=in_specs, out_specs=out_specs, check_vma=False)
```

profile of v0, /device:TPU:0, one launch (start us, length us, event | category | flops | bytes accessed | tf_op | source)
XLA Modules:
  0.0 1919.6 jit_solution(10603079539719749252)
XLA Ops:
  203.7 53.4 %all-reduce.20.cloned.1.call-done = bf16[4,4,196,384]{3,2,1,0:T(8,128)(2,1)} async-done(((bf16[4,4,196,384]{3,2,1,0:T(8,128)(2,1)}), bf16[4,4,196,384]{3,2,1,0:T(8,128)(2,1)}) %all-reduce.20.cloned.1.call-update) | async-done | bytes 2408464 | tf_op jit(solution)/shard_map/psum | solution.py:63
  285.9 61.8 %all-reduce.22.cloned.1.call-done = bf16[4,4,196,384]{3,2,1,0:T(8,128)(2,1)} async-done(((bf16[4,4,196,384]{3,2,1,0:T(8,128)(2,1)}), bf16[4,4,196,384]{3,2,1,0:T(8,128)(2,1)}) %all-reduce.22.cloned.1.call-update) | async-done | bytes 2408464 | tf_op jit(solution)/shard_map/psum | solution.py:63
  432.7 17.0 all-gather.11.cloned.1.call-done
  539.4 42.9 %all-reduce.24.cloned.1.call-done = bf16[4,4,49,768]{3,2,1,0:T(8,128)(2,1)} async-done(((bf16[4,4,49,768]{3,2,1,0:T(8,128)(2,1)}), bf16[4,4,49,768]{3,2,1,0:T(8,128)(2,1)}) %all-reduce.24.cloned.1.call-update) | async-done | bytes 1204240 | tf_op jit(solution)/shard_map/psum | solution.py:63
  586.0 22.1 %all-gather.15.cloned.1.call-done = bf16[768,1536]{1,0:T(8,128)(2,1)} async-done(((bf16[192,1536]{1,0:T(8,128)(2,1)}), bf16[768,1536]{1,0:T(8,128)(2,1)}) %all-gather.15.cloned.1.call-update) | async-done | bytes 2359312 | tf_op jit(solution)/shard_map/all_gather | solution.py:472
  617.3 16.5 all-gather.17.cloned.1.call-done
  648.0 46.9 %all-reduce.26.cloned.1.call-done = bf16[4,4,49,768]{3,2,1,0:T(8,128)(2,1)} async-done(((bf16[4,4,49,768]{3,2,1,0:T(8,128)(2,1)}), bf16[4,4,49,768]{3,2,1,0:T(8,128)(2,1)}) %all-reduce.26.cloned.1.call-update) | async-done | bytes 1204240 | tf_op jit(solution)/shard_map/psum | solution.py:67
  781.2 19.7 %collective-permute-done.4 = bf16[4,392,4,96]{1,3,2,0:T(8,128)(2,1)} collective-permute-done((bf16[4,392,4,96]{1,3,2,0:T(8,128)(2,1)}, bf16[4,392,4,96]{1,3,2,0:T(8,128)(2,1)}, u32[]{:S(2)}, u32[]{:S(2)}) %collective-permute-start.4) | collective-permute-done | bytes 1204256 | tf_op jit(solution)/shard_map/ppermute | solution.py:21
  849.7 101.9 %all-reduce.34.cloned.1.call-done = (bf16[4,16,49,4,96]{4,3,2,1,0:T(4,128)(2,1)}, bf16[4,16,49,4,96]{4,3,2,1,0:T(4,128)(2,1)}) async-done(((bf16[4,16,49,4,96]{4,3,2,1,0:T(4,128)(2,1)}, bf16[4,16,49,4,96]{4,3,2,1,0:T(4,128)(2,1)}), (bf16[4,16,49,4,96]{4,3,2,1,0:T(4,128)(2,1)}, bf16[4,16,49,4,96]{4,3,2,1,0:T(4,128)(2,1)})) %all-reduce.34.cloned.1.call-update) | async-done | bytes 4816912
  989.5 72.8 %all-reduce.28.cloned.1.call-done = bf16[4,4,196,384]{3,2,1,0:T(8,128)(2,1)} async-done(((bf16[4,4,196,384]{3,2,1,0:T(8,128)(2,1)}), bf16[4,4,196,384]{3,2,1,0:T(8,128)(2,1)}) %all-reduce.28.cloned.1.call-update) | async-done | bytes 2408464 | tf_op jit(solution)/shard_map/psum | solution.py:67
  1090.4 70.8 %all-reduce.30.cloned.1.call-done = bf16[4,4,196,384]{3,2,1,0:T(8,128)(2,1)} async-done(((bf16[4,4,196,384]{3,2,1,0:T(8,128)(2,1)}), bf16[4,4,196,384]{3,2,1,0:T(8,128)(2,1)}) %all-reduce.30.cloned.1.call-update) | async-done | bytes 2408464 | tf_op jit(solution)/shard_map/psum | solution.py:67
  1200.9 23.9 %multiply_reduce_fusion = (f32[4,2,784]{2,1,0:T(2,128)S(1)}, f32[4,2,784,1176]{3,2,1,0:T(8,128)}) fusion(f32[4,2,784,1176]{3,2,1,0:T(8,128)} %get-tuple-element.188, f32[4,2,784]{2,1,0:T(2,128)S(1)} %bitcast.441, bf16[4,784,2,96]{1,3,2,0:T(8,128)(2,1)S(1)} %copy-done.14, bf16[4,392,2,96]{1,3,2,0:T(8,128)(2,1)S(1)} %copy-done.45, ...), kind=kOutput, calls=%fused_computation.1 | convolution fusion | flops 1441901440 | bytes 62067712 | tf_op jit(solution)/shard_map/mqhe,mkhe->mhqk/dot_general | solution.py:164
  1229.3 26.8 %multiply_convert_fusion = bf16[4,2,784,1176]{3,2,1,0:T(8,128)(2,1)} fusion(f32[4,2,784,1176]{3,2,1,0:T(8,128)} %get-tuple-element.200, f32[4,2,784,1176]{3,2,1,0:T(8,128)} %get-tuple-element.188, f32[4,2,784]{2,1,0:T(2,128)S(1)} %get-tuple-element.199, f32[4,2,784]{2,1,0:T(2,128)S(1)} %bitcast.442), kind=kLoop, calls=%fused_computation | loop fusion | flops 29503488 | bytes 73808896 | tf_op jit(solution)/shard_map/convert_element_type | solution.py:168
  1428.2 21.0 %reduce-scatter.26.cloned.1.call-done = bf16[192,192]{1,0:T(8,128)(2,1)} async-done(((bf16[768,192]{1,0:T(8,128)(2,1)}), bf16[192,192]{1,0:T(8,128)(2,1)}) %reduce-scatter.26.cloned.1.call-update) | async-done | bytes 73744 | tf_op jit(solution)/shard_map/reduce_scatter | solution.py:551
  1449.2 24.5 %reduce-scatter.24.cloned.1.call-done = bf16[192,384]{1,0:T(8,128)(2,1)} async-done(((bf16[768,384]{1,0:T(8,128)(2,1)}), bf16[192,384]{1,0:T(8,128)(2,1)}) %reduce-scatter.24.cloned.1.call-update) | async-done | bytes 147472 | tf_op jit(solution)/shard_map/reduce_scatter | solution.py:548
  1473.7 36.1 %reduce-scatter.28.cloned.1.call-done = bf16[192,1536]{1,0:T(8,128)(2,1)} async-done(((bf16[768,1536]{1,0:T(8,128)(2,1)}), bf16[192,1536]{1,0:T(8,128)(2,1)}) %reduce-scatter.28.cloned.1.call-update) | async-done | bytes 589840 | tf_op jit(solution)/shard_map/reduce_scatter | solution.py:554
  1509.7 27.2 %reduce-scatter.22.cloned.1.call-done = bf16[96,3,384]{2,0,1:T(8,128)(2,1)} async-done(((bf16[384,3,384]{2,0,1:T(8,128)(2,1)}), bf16[96,3,384]{2,0,1:T(8,128)(2,1)}) %reduce-scatter.22.cloned.1.call-update) | async-done | bytes 221200 | tf_op jit(solution)/shard_map/reduce_scatter | solution.py:545
  1536.9 24.4 %reduce-scatter.18.cloned.1.call-done = bf16[96,768]{1,0:T(8,128)(2,1)} async-done(((bf16[384,768]{1,0:T(8,128)(2,1)}), bf16[96,768]{1,0:T(8,128)(2,1)}) %reduce-scatter.18.cloned.1.call-update) | async-done | bytes 147472 | tf_op jit(solution)/shard_map/reduce_scatter | solution.py:539
  1561.3 24.6 %reduce-scatter.20.cloned.1.call-done = bf16[96,768]{1,0:T(8,128)(2,1)} async-done(((bf16[384,768]{1,0:T(8,128)(2,1)}), bf16[96,768]{1,0:T(8,128)(2,1)}) %reduce-scatter.20.cloned.1.call-update) | async-done | bytes 147472 | tf_op jit(solution)/shard_map/reduce_scatter | solution.py:542
  1586.0 24.6 %reduce-scatter.14.cloned.1.call-done = bf16[96,3,192]{2,0,1:T(8,128)(2,1)} async-done(((bf16[384,3,192]{2,0,1:T(8,128)(2,1)}), bf16[96,3,192]{2,0,1:T(8,128)(2,1)}) %reduce-scatter.14.cloned.1.call-update) | async-done | bytes 110608 | tf_op jit(solution)/shard_map/reduce_scatter | solution.py:533
  1633.4 21.1 %psum.190 = bf16[96,192]{1,0:T(8,128)(2,1)S(1)} all-reduce(bf16[96,192]{1,0:T(8,128)(2,1)} %reduce-scatter.16.cloned.1.call-done), channel_id=1, replica_groups=mesh['clip'=4,'tok'=4,'head'=2] {'clip'}, use_global_device_ids=true, to_apply=%region_47.48 | all-reduce | flops 18432 | bytes 73728 | tf_op jit(solution)/shard_map/psum | solution.py:563
  1656.1 77.2 %all-reduce.36.cloned.1.call-done = (bf16[192,1536]{0,1:T(8,128)(2,1)}, bf16[96,3,192]{2,0,1:T(8,128)(2,1)}, bf16[96,768]{1,0:T(8,128)(2,1)}, bf16[96,768]{1,0:T...) async-done(((bf16[192,1536]{0,1:T(8,128)(2,1)}, bf16[96,3,192]{2,0,1:T(8,128)(2,1)}, ...) | async-done | bytes 2027536 | tf_op jit(solution)/shard_map/psum | solution.py:570
  1746.0 90.1 %all-reduce.38.cloned.1.call-done = (bf16[4,4,49,768]{3,2,1,0:T(8,128)(2,1)}, bf16[4,4,196,384]{3,2,1,0:T(8,128)(2,1)}) async-done(((bf16[4,4,49,768]{3,2,1,0:T(8,128)(2,1)}, bf16[4,4,196,384]{3,2,1,0:T(8,128)(2,1)}), (bf16[4,4,49,768]{3,2,1,0:T(8,128)(2,1)}, bf16[4,4,196,384]{3,2,1,0:T(8,128)(2,1)})) %all-reduce.38.cloned.1.call-update) | async-done | bytes 3612688 | tf_op jit(solution)/shard_map/psum | solution.py:63
  1850.8 62.0 %all-reduce.4 = (f32[3,384]{1,0:T(4,128)}, f32[768]{0:T(1024)}, f32[5,384]{1,0:T(8,128)}, f32[3,768]{1,0:T(4,128)}, f32[2,192]{1,0:T(2,128)}, /*index=5*/f32[2,384]{1,0:T(2,128)}, f32[768]{0:T(1024)}, f32[1536]{0:T(1024)}) all-reduce(f32[3,384]{1,0:T(4,128)S(1)} %pad_maximum_fusion.24, ...), channel_id=1, replica_groups=mesh['clip'=4,'tok'=4,'head'=2] {'clip','tok'}, use_global_device_ids=true, to_apply=%region_65.66 | all-reduce | flops 9600 | bytes 76800 | tf_op jit(solution)/shard_map/psum | solution.py:595
  (668 shorter events, 893.0 us)
Async XLA Ops:
  51.7 205.4 %all-reduce.20.cloned.1.call-start = ((), (), s32[]{:S(2)}) async-start(), calls=%async_computation.11 | async-start | bytes 4915200 | tf_op jit(solution)/shard_map/psum | solution.py:63
  187.9 159.7 %all-reduce.22.cloned.1.call-start = ((), (), s32[]{:S(2)}) async-start(), calls=%async_computation.12 | async-start | bytes 4915200 | tf_op jit(solution)/shard_map/psum | solution.py:63
  276.7 141.6 %all-gather.13.cloned.1.call-start = ((), (), s32[]{:S(2)}) async-start(), calls=%async_computation.14 | async-start | bytes 4014080 | tf_op jit(solution)/shard_map/all_gather | solution.py:86
  386.8 62.9 %all-gather.11.cloned.1.call-start = ((), (), s32[]{:S(2)}) async-start(), calls=%async_computation.13 | async-start | bytes 4014080 | tf_op jit(solution)/shard_map/all_gather | solution.py:87
  397.4 185.0 %all-reduce.24.cloned.1.call-start = ((), (), s32[]{:S(2)}) async-start(), calls=%async_computation.15 | async-start | bytes 2752512 | tf_op jit(solution)/shard_map/psum | solution.py:63
  428.0 78.9 %collective-permute-start.3 = (bf16[4,392,4,96]{1,0,3,2:T(4,128)(2,1)}, bf16[4,392,4,96]{1,0,3,2:T(4,128)(2,1)}, u32[]{:S(2)}, u32[]{:S(2)}) collective-permute-start(bf16[4,392,4,96]{1,0,3,2:T(4,128)(2,1)} %copy.426), channel_id=1, source_target_pairs={{0,8},{8,16},{16,24},{1,9},{9,17},{17,25},{2,10},{10,18},{18,26},{... | collective-permute-start | bytes 3612680 | tf_op jit(solution)/shard_map/ppermute | solution.py:21
  537.2 70.8 %all-gather.15.cloned.1.call-start = ((), (), s32[]{:S(2)}) async-start(), calls=%async_computation.16 | async-start | bytes 2949120 | tf_op jit(solution)/shard_map/all_gather | solution.py:472
  538.0 95.8 %all-gather.17.cloned.1.call-start = ((), (), s32[]{:S(2)}) async-start(), calls=%async_computation.17 | async-start | bytes 2949120 | tf_op jit(solution)/shard_map/all_gather | solution.py:473
  538.7 156.1 %all-reduce.26.cloned.1.call-start = ((), (), s32[]{:S(2)}) async-start(), calls=%async_computation.18 | async-start | bytes 2752512 | tf_op jit(solution)/shard_map/psum | solution.py:67
  647.5 304.1 %all-reduce.34.cloned.1.call-start = ((), (), s32[]{:S(2)}) async-start(), calls=%async_computation.31 | async-start | bytes 12845056
  830.5 231.8 %all-reduce.28.cloned.1.call-start = ((), (), s32[]{:S(2)}) async-start(), calls=%async_computation.19 | async-start | bytes 4915200 | tf_op jit(solution)/shard_map/psum | solution.py:67
  989.5 171.8 %all-reduce.30.cloned.1.call-start = ((), (), s32[]{:S(2)}) async-start(), calls=%async_computation.20 | async-start | bytes 4915200 | tf_op jit(solution)/shard_map/psum | solution.py:67
  1090.3 299.9 %all-reduce.32.cloned.1.call-start = ((), (), s32[]{:S(2)}) async-start(), calls=%async_computation.30 | async-start | bytes 6422528
  1321.0 104.9 %reduce-scatter.30.cloned.1.call-start = ((), (), s32[]{:S(2)}) async-start(), calls=%async_computation.29 | async-start | bytes 2949120
  1331.6 117.6 %reduce-scatter.26.cloned.1.call-start = ((), (), s32[]{:S(2)}) async-start(), calls=%async_computation.27 | async-start | bytes 491520 | tf_op jit(solution)/shard_map/reduce_scatter | solution.py:551
  1334.7 138.9 %reduce-scatter.24.cloned.1.call-start = ((), (), s32[]{:S(2)}) async-start(), calls=%async_computation.26 | async-start | bytes 737280 | tf_op jit(solution)/shard_map/reduce_scatter | solution.py:548
  1338.0 171.7 %reduce-scatter.28.cloned.1.call-start = ((), (), s32[]{:S(2)}) async-start(), calls=%async_computation.28 | async-start | bytes 2949120 | tf_op jit(solution)/shard_map/reduce_scatter | solution.py:554
  1344.7 192.2 %reduce-scatter.22.cloned.1.call-start = ((), (), s32[]{:S(2)}) async-start(), calls=%async_computation.25 | async-start | bytes 1105920 | tf_op jit(solution)/shard_map/reduce_scatter | solution.py:545
  1353.9 207.5 %reduce-scatter.18.cloned.1.call-start = ((), (), s32[]{:S(2)}) async-start(), calls=%async_computation.23 | async-start | bytes 737280 | tf_op jit(solution)/shard_map/reduce_scatter | solution.py:539
  1360.2 225.8 %reduce-scatter.20.cloned.1.call-start = ((), (), s32[]{:S(2)}) async-start(), calls=%async_computation.24 | async-start | bytes 737280 | tf_op jit(solution)/shard_map/reduce_scatter | solution.py:542
  1367.0 243.6 %reduce-scatter.14.cloned.1.call-start = ((), (), s32[]{:S(2)}) async-start(), calls=%async_computation.21 | async-start | bytes 737280 | tf_op jit(solution)/shard_map/reduce_scatter | solution.py:533
  1416.7 216.7 %reduce-scatter.16.cloned.1.call-start = ((), (), s32[]{:S(2)}) async-start(), calls=%async_computation.22 | async-start | bytes 245760 | tf_op jit(solution)/shard_map/reduce_scatter | solution.py:536
  1421.4 311.8 %all-reduce.36.cloned.1.call-start = ((), (), s32[]{:S(2)}) async-start(), calls=%async_computation.32 | async-start | bytes 4571136 | tf_op jit(solution)/shard_map/psum | solution.py:570
  1610.6 225.5 %all-reduce.38.cloned.1.call-start = ((), (), s32[]{:S(2)}) async-start(), calls=%async_computation.33 | async-start | bytes 7667712 | tf_op jit(solution)/shard_map/psum | solution.py:63
  (167 other events, 3737.2 us)
Sparse Core Ops, SparseCore 0:
  41.0 20.8 all-gather.6
  64.1 20.0 all-gather.8
  188.1 68.9 all-reduce.19
  276.8 70.7 all-reduce.21
  386.9 31.4 all-gather.12
  420.3 29.3 all-gather.10
  537.4 44.9 all-reduce.23
  584.0 24.0 all-gather.14
  609.7 24.0 all-gather.16
  647.6 47.1 all-reduce.25
  830.6 120.9 all-reduce.33
  989.5 72.7 all-reduce.27
  1090.5 70.7 all-reduce.29
  1321.2 69.0 all-reduce.31
  1392.8 33.1 reduce-scatter.29
  1428.3 20.8 reduce-scatter.25
  1451.5 22.0 reduce-scatter.23
  1476.6 33.0 reduce-scatter.27
  1513.0 23.8 reduce-scatter.21
  1539.3 22.0 reduce-scatter.17
  1563.8 22.0 reduce-scatter.19
  1588.5 22.0 reduce-scatter.13
  1636.8 96.3 all-reduce.35
  1736.2 99.8 all-reduce.37
  (1 shorter events, 19.7 us)
where the time goes:
time: 1930 us; the launch traced here: 1920 us
  waiting for transfers between devices  934 us (48%)
  local copies, waits for them, and re-layouts  298 us (15%)
  matrix products  285 us (15%)
  other arithmetic  220 us (11%)
  blocking collectives  141 us (7%)
  starting transfers between devices  26.1 us (1%)
    psum x4, waiting for transfers between devices, head_total(): lax.psum(partial_sum.astype(jnp.bfloat16), 'head').astype(jnp.float32)  248 us
    psum x3, waiting for transfers between devices, head_grad(): lax.psum(partial_sum.astype(jnp.bfloat16), 'head').astype(jnp.float32)  191 us
    unnamed x28, waiting for transfers between devices  113 us
    psum x1, waiting for transfers between devices, local(): lax.psum(shard_down_b.astype(jnp.bfloat16), 'clip').astype(jnp.float32)  77.2 us
    psum x1, blocking collectives, local(): lax.psum((gains_a_grad, gain_mlp_b, shifts_a_grad, shifts_b_grad, qv_grad...  62 us
  transfers between devices with their start and end apart: 33, of which 27 were waited for; matrix products, arithmetic and copies ran while one was open for 21% of the time, Pallas kernels for 0%

commit v1 on v0

v1 whole, which is shorter than its diff:
```python
import functools
import math
import jax
import jax.numpy as jnp
import numpy as np
from jax import lax
from jax.experimental import pallas as pl
from jax.experimental.pallas import tpu as pltpu
from jax.sharding import PartitionSpec as P
HD = 96
NEG = -1e30
VMEM_CAP = 60 * 2**20

def window(head):
    low = HD * head
    start = low // 128 * 128
    stop = -(-(low + HD) // 128) * 128
    return low, start, stop

def head_mask(head):
    low, start, stop = window(head)
    lane = lax.broadcasted_iota(jnp.int32, (1, stop - start), 1) + start
    return (lane >= low) & (lane < low + HD)

def attend_kernel(scaling, chunk, q_ref, kv_ref, mem_ref, bias_ref, out_ref, lse_ref, k_s, v_s, s_s, p_s):
    width = q_ref.shape[2]
    heads = width // HD
    nq = q_ref.shape[1]
    row = 0
    for ref in (kv_ref, mem_ref):
        rows = ref.shape[2]
        for t in range(ref.shape[0]):
            k_s[row:row + rows, :] = ref[t, 0, :, :width]
            v_s[row:row + rows, :] = ref[t, 0, :, width:]
            row += rows
    factor = scaling * math.log2(math.e)
    lane8 = lax.broadcasted_iota(jnp.int32, (chunk, 128), 1)
    for tile in range(width // 384):
        acc = q_ref[0, :, 384 * tile:384 * tile + 384].astype(jnp.float32)
        parts = [acc[:, :128], acc[:, 128:256], acc[:, 256:384]]
        for head in range(4 * tile, 4 * tile + 4):
            low, start, stop = window(head)
            mask = head_mask(head)
            qm = jnp.where(mask, q_ref[0, :, start:stop], jnp.bfloat16(0))
            s_s[...] = lax.dot_general(qm, k_s[:, start:stop], (((1,), (1,)), ((), ())), preferred_element_type=jnp.float32)

            def body(i, carry, head=head):
                rows = pl.ds(pl.multiple_of(i * chunk, chunk), chunk)
                s = s_s[rows, :] * factor + bias_ref[0]
                top = jnp.max(s, axis=1, keepdims=True)
                e = jnp.exp2(s - top)
                total = jnp.sum(e, axis=1, keepdims=True)
                p_s[rows, :] = (e * (1.0 / total)).astype(jnp.bfloat16)
                stat = top + jnp.log2(total)
                lse_ref[0, rows, :] = jnp.where(lane8 == head, stat, lse_ref[0, rows, :])
                return carry
            lax.fori_loop(0, nq // chunk, body, 0, unroll=nq // chunk)
            o = lax.dot_general(p_s[...], v_s[:, start:stop], (((1,), (0,)), ((), ())), preferred_element_type=jnp.float32)
            o = jnp.where(mask, o, 0.0)
            for w in range((stop - start) // 128):
                k = start // 128 - 3 * tile + w
                parts[k] = parts[k] + o[:, 128 * w:128 * w + 128]
        out_ref[0, :, 384 * tile:384 * tile + 384] = jnp.concatenate(parts, axis=1).astype(jnp.bfloat16)

def attend(q, kv, mem, bias):
    batches, nq, width = q.shape
    keys = kv.shape[0] * kv.shape[2] + mem.shape[0] * mem.shape[2]
    scaling = HD ** -0.5
    chunk = 112 if nq % 112 == 0 else 16
    return pl.pallas_call(
        functools.partial(attend_kernel, scaling, chunk),
        grid=(batches,),
        in_specs=[
            pl.BlockSpec((1, nq, width), lambda m: (m, 0, 0)),
            pl.BlockSpec((kv.shape[0], 1) + kv.shape[2:], lambda m: (0, m, 0, 0)),
            pl.BlockSpec((mem.shape[0], 1) + mem.shape[2:], lambda m: (0, m, 0, 0)),
            pl.BlockSpec((1, 1, keys), lambda m: (m, 0, 0)),
        ],
        out_specs=[
            pl.BlockSpec((1, nq, width), lambda m: (m, 0, 0)),
            pl.BlockSpec((1, nq, 128), lambda m: (m, 0, 0)),
        ],
        out_shape=[
            jax.ShapeDtypeStruct((batches, nq, width), jnp.bfloat16),
            jax.ShapeDtypeStruct((batches, nq, 128), jnp.float32),
        ],
        scratch_shapes=[
            pltpu.VMEM((keys, width), jnp.bfloat16),
            pltpu.VMEM((keys, width), jnp.bfloat16),
            pltpu.VMEM((nq, keys), jnp.float32),
            pltpu.VMEM((nq, keys), jnp.bfloat16),
        ],
        compiler_params=pltpu.CompilerParams(vmem_limit_bytes=VMEM_CAP),
        name="attend",
    )(q, kv, mem, bias)

def attend_back_kernel(scaling, chunk, q_ref, g_ref, kv_ref, mem_ref, bias_ref, lse_ref, dq_ref, dkv_ref, dmem_ref,
                       k_s, v_s, s_s, dp_s, p_s, ds_s, dkt_s, dvt_s):
    width = q_ref.shape[2]
    heads = width // HD
    nq = q_ref.shape[1]
    row = 0
    for ref in (kv_ref, mem_ref):
        rows = ref.shape[2]
        for t in range(ref.shape[0]):
            k_s[row:row + rows, :] = ref[t, 0, :, :width]
            v_s[row:row + rows, :] = ref[t, 0, :, width:]
            row += rows
    factor = scaling * math.log2(math.e)
    lane8 = lax.broadcasted_iota(jnp.int32, (chunk, 128), 1)
    nt = (((1,), (1,)), ((), ()))
    nn = (((1,), (0,)), ((), ()))
    for tile in range(width // 384):
        group = slice(384 * tile, 384 * tile + 384)
        qt = q_ref[0, :, group].astype(jnp.float32).T.astype(jnp.bfloat16)
        gt = g_ref[0, :, group].astype(jnp.float32).T.astype(jnp.bfloat16)
        parts = [None] * 3
        for head in range(4 * tile, 4 * tile + 4):
            low, start, stop = window(head)
            mask = head_mask(head)
            qm = jnp.where(mask, q_ref[0, :, start:stop], jnp.bfloat16(0))
            gm = jnp.where(mask, g_ref[0, :, start:stop], jnp.bfloat16(0))
            s_s[...] = lax.dot_general(qm, k_s[:, start:stop], nt, preferred_element_type=jnp.float32)
            dp_s[...] = lax.dot_general(gm, v_s[:, start:stop], nt, preferred_element_type=jnp.float32)

            def body(i, carry, head=head):
                rows = pl.ds(pl.multiple_of(i * chunk, chunk), chunk)
                lse = jnp.sum(jnp.where(lane8 == head, lse_ref[0, rows, :], 0.0), axis=1, keepdims=True)
                p = jnp.exp2(s_s[rows, :] * factor + bias_ref[0] - lse)
                dp = dp_s[rows, :]
                inner = jnp.sum(p * dp, axis=1, keepdims=True)
                p_s[rows, :] = p.astype(jnp.bfloat16)
                ds_s[rows, :] = (p * (dp - inner)).astype(jnp.bfloat16)
                return carry
            lax.fori_loop(0, nq // chunk, body, 0, unroll=nq // chunk)
            r = HD * (head - 4 * tile)
            dvt_s[r:r + HD, :] = lax.dot_general(gt[r:r + HD], p_s[...], nn, preferred_element_type=jnp.float32)
            dkt_s[r:r + HD, :] = lax.dot_general(qt[r:r + HD], ds_s[...], nn, preferred_element_type=jnp.float32) * scaling
            dq = lax.dot_general(ds_s[...], k_s[:, start:stop], nn, preferred_element_type=jnp.float32) * scaling
            dq = jnp.where(mask, dq, 0.0)
            for w in range((stop - start) // 128):
                k = start // 128 - 3 * tile + w
                part = dq[:, 128 * w:128 * w + 128]
                parts[k] = part if parts[k] is None else parts[k] + part
        dq_ref[0, :, group] = jnp.concatenate(parts, axis=1) + g_ref[0, :, group].astype(jnp.float32)
        for base, src in ((0, dkt_s), (width, dvt_s)):
            total = src[...].T.astype(jnp.bfloat16)
            lanes = slice(base + 384 * tile, base + 384 * tile + 384)
            row = 0
            for ref in (dkv_ref, dmem_ref):
                rows = ref.shape[2]
                for t in range(ref.shape[0]):
                    ref[t, 0, :, lanes] = total[row:row + rows]
                    row += rows

def attend_back(q, grad, kv, mem, bias, lse):
    batches, nq, width = q.shape
    keys = kv.shape[0] * kv.shape[2] + mem.shape[0] * mem.shape[2]
    scaling = HD ** -0.5
    chunk = 112 if nq % 112 == 0 else 16
    rows_spec = pl.BlockSpec((1, nq, width), lambda m: (m, 0, 0))
    kv_spec = pl.BlockSpec((kv.shape[0], 1) + kv.shape[2:], lambda m: (0, m, 0, 0))
    mem_spec = pl.BlockSpec((mem.shape[0], 1) + mem.shape[2:], lambda m: (0, m, 0, 0))
    return pl.pallas_call(
        functools.partial(attend_back_kernel, scaling, chunk),
        grid=(batches,),
        in_specs=[rows_spec, rows_spec, kv_spec, mem_spec,
            pl.BlockSpec((1, 1, keys), lambda m: (m, 0, 0)),
            pl.BlockSpec((1, nq, 128), lambda m: (m, 0, 0)),
        ],
        out_specs=[rows_spec, kv_spec, mem_spec],
        out_shape=[
            jax.ShapeDtypeStruct((batches, nq, width), jnp.float32),
            jax.ShapeDtypeStruct(kv.shape, jnp.bfloat16),
            jax.ShapeDtypeStruct(mem.shape, jnp.bfloat16),
        ],
        scratch_shapes=[
            pltpu.VMEM((keys, width), jnp.bfloat16),
            pltpu.VMEM((keys, width), jnp.bfloat16),
            pltpu.VMEM((nq, keys), jnp.float32),
            pltpu.VMEM((nq, keys), jnp.float32),
            pltpu.VMEM((nq, keys), jnp.bfloat16),
            pltpu.VMEM((nq, keys), jnp.bfloat16),
            pltpu.VMEM((384, keys), jnp.float32),
            pltpu.VMEM((384, keys), jnp.float32),
        ],
        compiler_params=pltpu.CompilerParams(vmem_limit_bytes=VMEM_CAP),
        name="attend_back",
    )(q, grad, kv, mem, bias, lse)


GRID = 14
PATCH = GRID * GRID
POOLED = PATCH // 4
eps = 1e-06
f32, bf16 = jnp.float32, jnp.bfloat16


def up16(n):
    return -(-n // 16) * 16


def dot(a, b, dims=((1,), (0,))):
    return lax.dot_general(a, b, (dims, ((), ())), preferred_element_type=f32)


def tokens_dot(a, b):
    return jnp.einsum("mnd,de->mne", a, b, preferred_element_type=f32)


def tokens_dot_t(a, b):
    return jnp.einsum("mne,de->mnd", a, b, preferred_element_type=f32)


def weight_grad(a, g):
    return jnp.einsum("mnd,mne->de", a, g, preferred_element_type=f32)


def pool_matrix(frames):
    rows, cols = up16(frames * POOLED), frames * PATCH
    out = np.zeros((rows, cols), np.float32)
    half = GRID // 2
    for f in range(frames):
        for p in range(PATCH):
            r, c = divmod(p, GRID)
            out[f * POOLED + (r // 2) * half + c // 2, f * PATCH + p] = 0.25
    return out


def pair_matrix(frames):
    rows, cols = up16(frames // 2 * POOLED), up16(frames * POOLED)
    out = np.zeros((rows, cols), np.float32)
    for j in range(frames // 2):
        for p in range(POOLED):
            out[j * POOLED + p, 2 * j * POOLED + p] = 0.5
            out[j * POOLED + p, (2 * j + 1) * POOLED + p] = 0.5
    return out


def pool(matrix, tensor):
    return jnp.einsum("pt,mtd->mpd", matrix, tensor, precision=lax.Precision.HIGHEST)


def unpool(matrix, tensor):
    return jnp.einsum("pt,mpd->mtd", matrix, tensor, precision=lax.Precision.HIGHEST)


def layer_norm(tensor, gain_row, shift_row):
    average = jnp.mean(tensor, axis=-1, keepdims=True)
    centred = tensor - average
    variance = jnp.mean(centred * centred, axis=-1, keepdims=True)
    return centred * lax.rsqrt(variance + eps) * gain_row + shift_row


def norm_back(tensor, gain_row, gradient):
    average = jnp.mean(tensor, axis=-1, keepdims=True)
    centred = tensor - average
    variance = jnp.mean(centred * centred, axis=-1, keepdims=True)
    inverse = lax.rsqrt(variance + eps)
    unit = centred * inverse
    scaled = gradient * gain_row
    back = inverse * (
        scaled
        - jnp.mean(scaled, axis=-1, keepdims=True)
        - unit * jnp.mean(scaled * unit, axis=-1, keepdims=True)
    )
    return back, jnp.sum(gradient * unit, axis=(0, 1)), jnp.sum(gradient, axis=(0, 1))


def gelu_back(pre_act, gradient):
    primal, pullback = jax.vjp(lambda v: jax.nn.gelu(v, approximate=True), pre_act)
    return pullback(gradient)[0]


def gelu(pre_act):
    return jax.nn.gelu(pre_act, approximate=True)


def grouped(pairs_of):
    clips, heads = lax.axis_size("clip"), lax.axis_size("head")
    return [
        (c * heads + h, c2 * heads + h2)
        for c in range(clips)
        for h in range(heads)
        for c2, h2 in [pairs_of(c, h)]
        if 0 <= c2 < clips
    ]


def send_memory(memory, by, heads):
    return [
        lax.ppermute(
            memory if not isinstance(memory, list) else memory[d],
            ("clip", "head"),
            grouped(lambda c, h, d=d: (c + by, (h + d) % heads)),
        )
        for d in range(heads)
    ]


def share_keys(kv, memory, slots, heads):
    received = send_memory(memory, 1, heads)
    own = lax.all_gather(kv, "tok")
    flat = jnp.stack(received).reshape((-1,) + memory.shape[1:])
    chosen = jnp.stack([lax.dynamic_index_in_dim(flat, slot, 0, keepdims=False) for slot in slots])
    return own, lax.all_gather(chosen, "tok")


def halve_over_tok(partial):
    size = lax.axis_size("tok")
    index = lax.axis_index("tok")
    bit = 1
    while bit < size:
        mine = (index // bit) % 2
        paired = partial.reshape((partial.shape[0] // 2, 2) + partial.shape[1:])
        keep = lax.dynamic_index_in_dim(paired, mine, 1, keepdims=False)
        give = lax.dynamic_index_in_dim(paired, 1 - mine, 1, keepdims=False)
        got = lax.ppermute(give, "tok", [(i, i ^ bit) for i in range(size)])
        partial = (keep.astype(f32) + got.astype(f32)).astype(bf16)
        bit *= 2
    return partial[0]


def return_keys(own_grad, mem_grad, slots, heads, pairing):
    mem = halve_over_tok(mem_grad)
    own = halve_over_tok(own_grad)
    routed = jnp.zeros((heads * mem.shape[0],) + mem.shape[1:], bf16)
    for m, slot in enumerate(slots):
        routed = lax.dynamic_update_index_in_dim(routed, mem[m], slot, 0)
    routed = routed.reshape((heads,) + mem.shape)
    back = send_memory([routed[(heads - d) % heads] for d in range(heads)], -1, heads)
    total = sum(piece.astype(f32) for piece in back)
    spread = jnp.einsum("jf,mjd->mfd", pairing, total, precision=lax.Precision.HIGHEST)
    return own.astype(f32) + spread


def padded(tensor, rows):
    return jnp.pad(tensor, ((0, 0), (0, rows - tensor.shape[1]), (0, 0)))


def local(
    clips_in, resets, assign, w_qkv_a, w_out_a, w_up_a, w_down_a, w_qkv_b, w_out_b, w_skip_b, w_up_b, w_down_b,
    gains_a, gains_b, shifts_a, shifts_b, qv_bias_a, qv_bias_b, up_bias_a, up_bias_b, cotangent,
):
    heads, toks = lax.axis_size("head"), lax.axis_size("tok")
    head = lax.axis_index("head")
    micro, frames = clips_in.shape[1], clips_in.shape[2]
    d1, d2 = clips_in.shape[-1], cotangent.shape[-1]
    share = micro // heads
    first = head * share
    pooling = jnp.asarray(pool_matrix(frames))
    pairing = jnp.asarray(pair_matrix(frames))
    own_rows, mem_rows = up16(frames * POOLED), up16(frames // 2 * POOLED)

    stream = lax.dynamic_slice_in_dim(clips_in[0], first, share, 0)
    stream = stream.reshape(share, frames * PATCH, d1).astype(f32)
    cot = lax.dynamic_slice_in_dim(cotangent[0], first, share, 0)
    cot = padded(cot.reshape(share, frames * POOLED, d2), own_rows)

    slots = []
    masks = []
    row_own = jnp.where(jnp.arange(own_rows) < frames * POOLED, 0.0, NEG)
    row_mem = jnp.arange(mem_rows) < frames // 2 * POOLED
    for m in range(share):
        source = lax.dynamic_index_in_dim(assign[0], first + m, 0, keepdims=False)
        flag = lax.dynamic_index_in_dim(resets[0], first + m, 0, keepdims=False)
        slots.append(((head - source // share + heads) % heads) * share + source % share)
        has = (flag == 0) & (lax.axis_index("clip") > 0)
        masks.append(jnp.concatenate([jnp.tile(row_own, toks), jnp.tile(jnp.where(row_mem & has, 0.0, NEG), toks)]))
    bias = jnp.stack(masks)[:, None, :].astype(f32)

    pack_a = jnp.concatenate([w_up_a, w_down_a, w_qkv_a.reshape(w_qkv_a.shape[0], -1), w_out_a], axis=1)
    pack_q = w_qkv_b.reshape(w_qkv_b.shape[0], -1)
    pack_b = jnp.concatenate([w_up_b, w_down_b, w_out_b, w_skip_b], axis=1)
    group = ("head", "tok")
    all_a = lax.all_gather(pack_a, group).reshape(heads, d1, -1)
    all_q = lax.all_gather(pack_q, group).reshape(heads, d1, -1)
    all_b = lax.all_gather(pack_b, group).reshape(heads, d2, -1)

    def lanes(pack, low, width):
        return jnp.concatenate([pack[h, :, low:low + width] for h in range(heads)], axis=1)

    fa, ha = w_up_a.shape[1], w_out_a.shape[1]
    fb, hb, hs = w_up_b.shape[1], w_out_b.shape[1], w_skip_b.shape[1]
    up_a, down_a = lanes(all_a, 0, fa), lanes(all_a, fa, fa)
    q_a, k_a, v_a = (lanes(all_a, 2 * fa + i * ha, ha) for i in range(3))
    kv_a = jnp.concatenate([k_a, v_a], axis=1)
    out_a = lanes(all_a, 2 * fa + 3 * ha, ha)
    qkv_b = jnp.concatenate([lanes(all_q, i * hb, hb) for i in range(3)], axis=1)
    up_b, down_b = lanes(all_b, 0, fb), lanes(all_b, fb, fb)
    out_b, skip_b = lanes(all_b, 2 * fb, hb), lanes(all_b, 2 * fb + hb, hs)

    bias_qv_a, bias_qv_b = (lax.all_gather(b, "head", axis=1, tiled=True) for b in (qv_bias_a, qv_bias_b))
    bias_up_a, bias_up_b = (lax.all_gather(b, "head", axis=0, tiled=True) for b in (up_bias_a, up_bias_b))

    normed1 = layer_norm(stream, gains_a[0], shifts_a[0])
    low1 = normed1.astype(bf16)
    pooled1 = pool(pooling, normed1).astype(bf16)
    zero1 = jnp.zeros((d1,), f32)
    kv1 = (tokens_dot(pooled1, kv_a) + jnp.concatenate([zero1, bias_qv_a[1]])).astype(bf16)
    q1 = (tokens_dot(low1, q_a) + bias_qv_a[0]).astype(bf16)
    mem1 = jnp.einsum("jf,mfd->mjd", pairing.astype(bf16), kv1, preferred_element_type=f32).astype(bf16)
    own_kv1, mem_kv1 = share_keys(kv1, mem1, slots, heads)
    comb1, lse1 = attend(q1, own_kv1, mem_kv1, bias)
    after1 = stream + tokens_dot_t(comb1, out_a) + shifts_a[1]
    normed2 = layer_norm(after1, gains_a[1], shifts_a[2]).astype(bf16)
    pre1 = tokens_dot(normed2, up_a) + bias_up_a
    hidden1 = gelu(pre1).astype(bf16)
    middle = after1 + tokens_dot_t(hidden1, down_a) + shifts_a[3]

    normed3 = layer_norm(middle, gains_a[2], shifts_a[4])
    pooled3 = pool(pooling, normed3).astype(bf16)
    zero2 = jnp.zeros((d2,), f32)
    proj2 = (tokens_dot(pooled3, qkv_b) + jnp.concatenate([bias_qv_b[0], zero2, bias_qv_b[1]])).astype(bf16)
    q2, kv2 = proj2[..., :d2], proj2[..., d2:]
    mem2 = jnp.einsum("jf,mfd->mjd", pairing.astype(bf16), kv2, preferred_element_type=f32).astype(bf16)
    own_kv2, mem_kv2 = share_keys(kv2, mem2, slots, heads)
    comb2, lse2 = attend(q2, own_kv2, mem_kv2, bias)
    after2 = tokens_dot_t(comb2, out_b) + tokens_dot_t(pooled3, skip_b) + shifts_b[0]
    normed4 = layer_norm(after2, gains_b, shifts_b[1]).astype(bf16)
    pre2 = tokens_dot(normed4, up_b) + bias_up_b
    hidden2 = gelu(pre2).astype(bf16)
    mixed = (after2 + tokens_dot_t(hidden2, down_b) + shifts_b[2]).astype(bf16)

    cot32 = cot.astype(f32)
    g_down_b = weight_grad(cot, hidden2)
    pre_grad = gelu_back(pre2, tokens_dot(cot, down_b))
    g_bias_up_b = jnp.sum(pre_grad, axis=(0, 1))
    pre_low = pre_grad.astype(bf16)
    g_up_b = weight_grad(normed4, pre_low)
    back, g_gain_b, g_shift_b1 = norm_back(after2, gains_b, tokens_dot_t(pre_low, up_b))
    res2 = back + cot32
    res2_low = res2.astype(bf16)
    g_out_b = weight_grad(res2_low, comb2)
    g_skip_b = weight_grad(res2_low, pooled3)
    g_shifts_b = jnp.stack([jnp.sum(res2, axis=(0, 1)), g_shift_b1, jnp.sum(cot32, axis=(0, 1))])
    comb2_grad = tokens_dot(res2_low, out_b).astype(bf16)
    skip_grad = tokens_dot(res2_low, skip_b)
    dq2, dkv2, dmem2 = attend_back(q2, comb2_grad, own_kv2, mem_kv2, bias, lse2)
    kv2_grad = return_keys(dkv2, dmem2, slots, heads, pairing)
    g_qv_b = jnp.stack([jnp.sum(dq2, axis=(0, 1)), jnp.sum(kv2_grad[..., d2:], axis=(0, 1))])
    proj2_low = jnp.concatenate([dq2.astype(bf16), kv2_grad.astype(bf16)], axis=-1)
    g_qkv_b = weight_grad(pooled3, proj2_low)
    normed3_grad = unpool(pooling, tokens_dot_t(proj2_low, qkv_b) + skip_grad)
    middle_grad, g_gain_a2, g_shift_a4 = norm_back(middle, gains_a[2], normed3_grad)

    mid_low = middle_grad.astype(bf16)
    g_down_a = weight_grad(mid_low, hidden1)
    pre_grad = gelu_back(pre1, tokens_dot(mid_low, down_a))
    g_bias_up_a = jnp.sum(pre_grad, axis=(0, 1))
    pre_low = pre_grad.astype(bf16)
    g_up_a = weight_grad(normed2, pre_low)
    back, g_gain_a1, g_shift_a2 = norm_back(after1, gains_a[1], tokens_dot_t(pre_low, up_a))
    res1 = back + middle_grad
    res1_low = res1.astype(bf16)
    g_out_a = weight_grad(res1_low, comb1)
    comb1_grad = tokens_dot(res1_low, out_a).astype(bf16)
    dq1, dkv1, dmem1 = attend_back(q1, comb1_grad, own_kv1, mem_kv1, bias, lse1)
    kv1_grad = return_keys(dkv1, dmem1, slots, heads, pairing)
    g_qv_a = jnp.stack([jnp.sum(dq1, axis=(0, 1)), jnp.sum(kv1_grad[..., d1:], axis=(0, 1))])
    dq1_low, kv1_low = dq1.astype(bf16), kv1_grad.astype(bf16)
    g_q_a = weight_grad(low1, dq1_low)
    g_kv_a = weight_grad(pooled1, kv1_low)
    normed1_grad = tokens_dot_t(dq1_low, q_a) + unpool(pooling, tokens_dot_t(kv1_low, kv_a))
    back, g_gain_a0, g_shift_a0 = norm_back(stream, gains_a[0], normed1_grad)
    stream_grad = (back + res1).astype(bf16)

    def by_head(grad, width):
        return grad.reshape(grad.shape[0], heads, width).transpose(1, 0, 2)

    grad_a = jnp.concatenate(
        [by_head(g_up_a, fa), by_head(g_down_a, fa), by_head(g_q_a, ha), by_head(g_kv_a[:, :d1], ha),
         by_head(g_kv_a[:, d1:], ha), by_head(g_out_a, ha)], axis=2).astype(bf16)
    grad_q = jnp.concatenate([by_head(g_qkv_b[:, i * d2:(i + 1) * d2], hb) for i in range(3)], axis=2).astype(bf16)
    grad_b = jnp.concatenate(
        [by_head(g_up_b, fb), by_head(g_down_b, fb), by_head(g_out_b, hb), by_head(g_skip_b, hs)], axis=2).astype(bf16)

    def reduce_grads(grad):
        blocks = grad.reshape((heads * toks, -1) + grad.shape[2:])
        shard = lax.psum_scatter(blocks, group, scatter_dimension=0, tiled=False)
        return lax.psum(shard, "clip").astype(f32)

    sum_b, sum_q, sum_a = reduce_grads(grad_b), reduce_grads(grad_q), reduce_grads(grad_a)

    small = [
        jnp.stack([g_gain_a0, g_gain_a1, g_gain_a2]), g_gain_b,
        jnp.stack([g_shift_a0, jnp.sum(res1, axis=(0, 1)), g_shift_a2, jnp.sum(middle_grad, axis=(0, 1)), g_shift_a4]),
        g_shifts_b, g_qv_a, g_qv_b, g_bias_up_a, g_bias_up_b,
    ]
    flat = lax.psum(jnp.concatenate([piece.reshape(-1) for piece in small]), ("clip", "tok", "head"))
    pieces, at = [], 0
    for piece in small:
        pieces.append(flat[at:at + piece.size].reshape(piece.shape))
        at += piece.size

    def mine(piece, axis):
        width = piece.shape[axis] // heads
        return lax.dynamic_slice_in_dim(piece, head * width, width, axis)

    mixed_all = lax.all_gather(mixed[:, :frames * POOLED], "head", axis=0, tiled=True)
    stream_all = lax.all_gather(stream_grad, "head", axis=0, tiled=True)
    return (
        mixed_all.reshape(cotangent.shape),
        stream_all.astype(f32).reshape(clips_in.shape),
        sum_a[:, 2 * fa:2 * fa + 3 * ha].reshape(w_qkv_a.shape),
        sum_a[:, 2 * fa + 3 * ha:],
        sum_a[:, :fa],
        sum_a[:, fa:2 * fa],
        sum_q.reshape(w_qkv_b.shape),
        sum_b[:, 2 * fb:2 * fb + hb],
        sum_b[:, 2 * fb + hb:],
        sum_b[:, :fb],
        sum_b[:, fb:2 * fb],
        pieces[0], pieces[1], pieces[2], pieces[3],
        mine(pieces[4], 1), mine(pieces[5], 1), mine(pieces[6], 0), mine(pieces[7], 0),
    )


def solution(mesh):
    in_specs = (
        P("clip", None, "tok", None, None),
        P("clip", None),
        P("clip", None),
        P("tok", None, "head"),
        P("tok", "head"),
        P("tok", "head"),
        P("tok", "head"),
        P("tok", None, "head"),
        P("tok", "head"),
        P("tok", "head"),
        P("tok", "head"),
        P("tok", "head"),
        P(),
        P(),
        P(),
        P(),
        P(None, "head"),
        P(None, "head"),
        P("head"),
        P("head"),
        P("clip", None, "tok", None, None),
    )
    out_specs = (
        P("clip", None, "tok", None, None),
        P("clip", None, "tok", None, None),
        P("tok", None, "head"),
        P("tok", "head"),
        P("tok", "head"),
        P("tok", "head"),
        P("tok", None, "head"),
        P("tok", "head"),
        P("tok", "head"),
        P("tok", "head"),
        P("tok", "head"),
        P(),
        P(),
        P(),
        P(),
        P(None, "head"),
        P(None, "head"),
        P("head"),
        P("head"),
    )
    return jax.shard_map(local, mesh=mesh, in_specs=in_specs, out_specs=out_specs, check_vma=False)
```

time: 1930 us -> 896 us (0.46)
  waiting for transfers between devices: 934 us -> 380 us
  other arithmetic: 220 us -> 43 us
  matrix products: 285 us -> 118 us
  local copies, waits for them, and re-layouts: 298 us -> 155 us
  blocking collectives: 141 us -> 58.7 us
  Pallas kernels: 0 us -> 79.6 us
    psum x8 -> x1, waiting for transfers between devices: 516 us -> 72.9 us  [reduce_grads(): return lax.psum(shard, 'clip').astype(f32)]
    dot_general x47 -> x38, matrix products: 285 us -> 118 us  [the longest x10 36.7 us: tokens_dot(): return jnp.einsum('mnd,de->mne', a, b, preferred_element_type=f32)]
    reduce_scatter x8 -> x3, waiting for transfers between devices: 191 us -> 74.2 us  [reduce_grads(): shard = lax.psum_scatter(blocks, group, scatter_dimension=0, tiled=False)]
    unnamed x28 -> x13, waiting for transfers between devices: 113 us -> 0.71 us
    reduce_sum x24 -> x8, other arithmetic: 90.8 us -> 8.91 us  [the longest x1 1.92 us: norm_back(): jnp.sum(gradient, axis=(0, 1))]
    pallas_call x0 -> x4, Pallas kernels: none -> 79.6 us  [the longest x2 47.3 us: attend_back(): pl.pallas_call(functools.partial(attend_back_kernel, scaling, chunk), gri...]
    convert_element_type x29 -> x10, other arithmetic: 89.2 us -> 15.8 us  [the longest x6 8.96 us: halve_over_tok(): partial = (keep.astype(f32) + got.astype(f32)).astype(bf16)]
    all_gather x6 -> x9, waiting for transfers between devices: 86.9 us -> 155 us  [the longest x2 68.4 us: share_keys(): own = lax.all_gather(kv, 'tok')]
  transfers between devices with their start and end apart: 33 -> 29, of which waited for: 27 -> 19; matrix products, arithmetic and copies ran while one was open for 21% -> 27% of each run, Pallas kernels for 0% -> 5%
where the time goes in v1:
time: 896 us; the launch traced here: 886 us
  waiting for transfers between devices  380 us (42%)
  local copies, waits for them, and re-layouts  155 us (17%)
  matrix products  118 us (13%)
  Pallas kernels  79.6 us (9%)
  blocking collectives  58.7 us (7%)
  other arithmetic  43 us (5%)
  starting transfers between devices  28.8 us (3%)
  between operations  23.2 us (3%)
    reduce_scatter x3, waiting for transfers between devices, reduce_grads(): shard = lax.psum_scatter(blocks, group, scatter_dimension=0, tiled=False)  74.2 us
    psum x1, waiting for transfers between devices, reduce_grads(): return lax.psum(shard, 'clip').astype(f32)  72.9 us
    all_gather x2, waiting for transfers between devices, share_keys(): own = lax.all_gather(kv, 'tok')  68.4 us
    ppermute x8, waiting for transfers between devices, send_memory(): lax.ppermute(memory if not isinstance(memory, list) else memory[d], ('cli...  57.6 us
    all_gather x1, waiting for transfers between devices, local(): all_b = lax.all_gather(pack_b, group).reshape(heads, d2, -1)  56.3 us
    pallas_call x2, Pallas kernels, attend_back(): pl.pallas_call(functools.partial(attend_back_kernel, scaling, chunk), gri...  47.3 us
    psum x1, blocking collectives, local(): lax.psum(jnp.concatenate([piece.reshape(-1) for piece in small]), ('clip'...  40.2 us
    dot_general x10, matrix products, tokens_dot(): return jnp.einsum('mnd,de->mne', a, b, preferred_element_type=f32)  36.7 us
  transfers between devices with their start and end apart: 29, of which 19 were waited for; matrix products, arithmetic and copies ran while one was open for 27% of the time, Pallas kernels for 5%

profile of v1, /device:TPU:0, one launch (start us, length us, event | category | flops | bytes accessed | tf_op | source)
XLA Modules:
  0.0 886.5 jit_solution(3755931646654115164)
XLA Ops:
  34.2 13.2 %all-gather.25.cloned.1.call-done = bf16[768,2304]{1,0:T(8,128)(2,1)} async-done(((bf16[96,2304]{1,0:T(8,128)(2,1)}), bf16[768,2304]{1,0:T(8,128)(2,1)}) %all-gather.25.cloned.1.call-update) | async-done | bytes 3538960 | tf_op jit(solution)/shard_map/all_gather | solution.py:376
  101.8 27.2 %all-gather.27.cloned.1.call-done = bf16[8,208,768]{2,1,0:T(8,128)(2,1)} async-done(((bf16[2,208,768]{2,1,0:T(8,128)(2,1)}), bf16[8,208,768]{2,1,0:T(8,128)(2,1)}) %all-gather.27.cloned.1.call-update) | async-done | bytes 2555920 | tf_op jit(solution)/shard_map/all_gather | solution.py:303
  129.0 19.0 %attend.2 = (bf16[2,784,384]{2,1,0:T(8,128)(2,1)}, f32[2,784,128]{2,1,0:T(8,128)}) custom-call(bf16[2,784,384]{2,1,0:T(8,128)(2,1)} %add_convert_fusion.4.q_ref, bf16[4,2,208,768]{3,2,1,0:T(8,128)(2,1)} %bitcast.400, bf16[4,2,112,768]{3,2,1,0:T(8,128)(2,1)} %bitcast.402, f32[2,1,1280]{2,1,0:T(1,128)} %broadcast_in_dim.35.bias_ref), custom_call_target="tpu_custom_call" | custom-call | tf_op jit(solution)/shard_map/attend/pallas_call | solution.py:70
  152.7 6.9 multiply_convert_fusion
  178.1 12.3 %collective-permute-done.3 = bf16[2,112,1536]{2,1,0:T(8,128)(2,1)S(1)} collective-permute-done((bf16[2,112,1536]{2,1,0:T(8,128)(2,1)S(1)}, bf16[2,112,1536]{2,1,0:T(8,128)(2,1)S(1)}, u32[]{:S(2)}, u32[]{:S(2)}) %collective-permute-start.3) | collective-permute-done | bytes 688160 | tf_op jit(solution)/shard_map/ppermute | solution.py:292
  190.4 14.1 %collective-permute-done.2 = bf16[2,112,1536]{2,1,0:T(8,128)(2,1)S(1)} collective-permute-done((bf16[2,112,1536]{2,1,0:T(8,128)(2,1)S(1)}, bf16[2,112,1536]{2,1,0:T(8,128)(2,1)S(1)}, u32[]{:S(2)}, u32[]{:S(2)}) %collective-permute-start.2) | collective-permute-done | bytes 688160 | tf_op jit(solution)/shard_map/ppermute | solution.py:292
  215.6 16.5 %all-gather.33.cloned.1.call-done = bf16[8,112,1536]{2,1,0:T(8,128)(2,1)} async-done(((bf16[2,112,1536]{2,1,0:T(8,128)(2,1)}), bf16[8,112,1536]{2,1,0:T(8,128)(2,1)}) %all-gather.33.cloned.1.call-update) | async-done | bytes 2752528 | tf_op jit(solution)/shard_map/all_gather | solution.py:306
  232.1 41.1 %all-gather.31.cloned.1.call-done = bf16[8,208,1536]{2,1,0:T(8,128)(2,1)} async-done(((bf16[2,208,1536]{2,1,0:T(8,128)(2,1)}), bf16[8,208,1536]{2,1,0:T(8,128)(2,1)}) %all-gather.31.cloned.1.call-update) | async-done | bytes 5111824 | tf_op jit(solution)/shard_map/all_gather | solution.py:303
  273.3 13.3 %attend.3 = (bf16[2,208,768]{2,1,0:T(8,128)(2,1)}, f32[2,208,128]{2,1,0:T(8,128)}) custom-call(bf16[2,208,768]{2,1,0:T(8,128)(2,1)} %slice.405.q_ref, bf16[4,2,208,1536]{3,2,1,0:T(8,128)(2,1)} %bitcast.387, bf16[4,2,112,1536]{3,2,1,0:T(8,128)(2,1)} %bitcast.398, f32[2,1,1280]{2,1,0:T(1,128)} %broadcast_in_dim.35.bias_ref), custom_call_target="tpu_custom_call" | custom-call | tf_op jit(solution)/shard_map/attend/pallas_call | solution.py:70
  286.6 56.3 %all-gather.35.cloned.1.call-done = bf16[1536,3648]{1,0:T(8,128)(2,1)} async-done(((bf16[192,3648]{1,0:T(8,128)(2,1)}), bf16[1536,3648]{1,0:T(8,128)(2,1)}) %all-gather.35.cloned.1.call-update) | async-done | bytes 11206672 | tf_op jit(solution)/shard_map/all_gather | solution.py:378
  354.8 6.8 fusion.149
  366.2 19.2 %attend_back.2 = (f32[2,208,768]{2,1,0:T(8,128)}, bf16[4,2,208,1536]{3,2,1,0:T(8,128)(2,1)}, bf16[4,2,112,1536]{3,2,1,0:T(8,128)(2,1)}) custom-call(bf16[2,208,768]{2,1,0:T(8,128)(2,1)} %slice.405.q_ref, bf16[2,208,768]{2,1,0:T(8,128)(2,1)} %convolution_convert_fusion.2.g_ref, bf16[4,2,208,1536]{3,2,1,0:T(8,128)(2,1)} %bitcast.388, ...), custom_call_target="tpu_custom_call" | custom-call | tf_op jit(solution)/shard_map/attend_back/pallas_call | solution.py:164
  404.5 8.9 %collective-permute-done.7 = bf16[1,2,112,1536]{3,2,1,0:T(8,128)(2,1)} collective-permute-done((bf16[1,2,112,1536]{3,2,1,0:T(8,128)(2,1)}, bf16[1,2,112,1536]{3,2,1,0:T(8,128)(2,1)}, u32[]{:S(2)}, u32[]{:S(2)}) %collective-permute-start.7) | collective-permute-done | bytes 688160 | tf_op jit(solution)/shard_map/ppermute | solution.py:318
  437.5 12.7 %collective-permute-done.8 = bf16[2,112,1536]{2,1,0:T(8,128)(2,1)} collective-permute-done((bf16[2,112,1536]{2,1,0:T(8,128)(2,1)S(1)}, bf16[2,112,1536]{2,1,0:T(8,128)(2,1)}, u32[]{:S(2)}, u32[]{:S(2)}) %collective-permute-start.8) | collective-permute-done | bytes 688160 | tf_op jit(solution)/shard_map/ppermute | solution.py:292
  454.4 6.0 fusion.147
  470.6 11.3 %fusion.148 = (f32[1536]{0:T(1024)S(1)}, bf16[2,784,1536]{2,1,0:T(8,128)(2,1)S(1)}) fusion(f32[2,784,1536]{2,1,0:T(8,128)} %get-tuple-element.247, f32[1536]{0:T(1024)S(1)} %copy-done.101, bf16[384,768]{1,0:T(8,128)(2,1)S(1)} %copy-done.62, bf16[384,768]{1,0:T(8,128)(2,1)S(1)} %copy-done.60, f32[2,784,384]{2,1,0:T(8,128)S(1)} %get-tuple-element.189), kind=kOutput, calls=%fused_computation.334 | convolution fusion | flops 1905633792 | bytes 18051072 | tf_op jit(solution)/shard_map/mnd,de->mne/dot_general | solution.py:208
  490.2 28.1 %attend_back.3 = (f32[2,784,384]{2,1,0:T(8,128)}, bf16[4,2,208,768]{3,2,1,0:T(8,128)(2,1)}, bf16[4,2,112,768]{3,2,1,0:T(8,128)(2,1)}) custom-call(bf16[2,784,384]{2,1,0:T(8,128)(2,1)} %add_convert_fusion.4.q_ref, bf16[2,784,384]{2,1,0:T(8,128)(2,1)} %convolution_convert_fusion.1.g_ref, bf16[4,2,208,768]{3,2,1,0:T(8,128)(2,1)} %bitcast.401, ...), custom_call_target="tpu_custom_call" | custom-call | tf_op jit(solution)/shard_map/attend_back/pallas_call | solution.py:164
  583.5 6.3 concatenate.118
  598.4 8.2 bitcast_convert_fusion
  606.6 11.7 %reshape.461 = bf16[768,2,1536]{2,1,0:T(2,128)(2,1)} reshape(bf16[768,3072]{1,0:T(8,128)(2,1)} %bitcast_convert_fusion) | data formatting | bytes 9437184 | tf_op jit(solution)/shard_map/reshape | solution.py:469
  628.6 11.6 %reshape.460 = bf16[768,2,1536]{2,1,0:T(2,128)(2,1)} reshape(bf16[768,3072]{1,0:T(8,128)(2,1)} %bitcast_convert_fusion.1) | data formatting | bytes 9437184 | tf_op jit(solution)/shard_map/reshape | solution.py:469
  662.6 74.2 %reduce-scatter.8.cloned.1.call-done = bf16[1,192,3648]{2,1,0:T(8,128)(2,1)} async-done(((bf16[8,192,3648]{2,1,0:T(8,128)(2,1)}), bf16[1,192,3648]{2,1,0:T(8,128)(2,1)}) %reduce-scatter.8.cloned.1.call-update) | async-done | bytes 1400848 | tf_op jit(solution)/shard_map/reduce_scatter | solution.py:480
  740.6 40.2 %psum.31 = f32[13056]{0:T(1024)S(1)} all-reduce(f32[13056]{0:T(1024)S(1)} %constant_dynamic-update-slice_fusion.3), channel_id=1, replica_groups=mesh['clip'=4,'tok'=4,'head'=2] {'clip','tok','head'}, use_global_device_ids=true, to_apply=%region_40.41 | all-reduce | flops 13056 | bytes 104448 | tf_op jit(solution)/shard_map/psum | solution.py:490
  796.4 72.9 %all-reduce.5.cloned.1.call-done = (bf16[96,2304]{1,0:T(8,128)(2,1)}, bf16[96,3,384]{2,1,0:T(4,128)(2,1)}, bf16[192,3648]{1,0:T(8,128)(2,1)}) async-done(((bf16[96,2304]{1,0:T(8,128)(2,1)}, bf16[96,3,384]{2,1,0:T(4,128)(2,1)}, bf16[192,3648]{1,0:T(8,128)(2,1)}), (bf16[96,2304]{1,0:T(8,128)(2,1)}, bf16[96,3,384]{2,1,0:T(4,128)(2,1)}, bf16[192,3648]{1,0:T(8,128)(2,1)})) %all-reduce.5.cloned.1.call-update) | async-done | bytes 2064400 | tf_op jit(solution)/shard_map/psum | solution.py:481
  (551 shorter events, 325.1 us)
Async XLA Ops:
  7.2 40.2 %all-gather.25.cloned.1.call-start = ((), (), s32[]{:S(2)}) async-start(), calls=%async_computation.9 | async-start | bytes 3981312 | tf_op jit(solution)/shard_map/all_gather | solution.py:376
  10.4 75.4 %all-gather.19.cloned.1.call-start = ((), (), s32[]{:S(2)}) async-start(), calls=%async_computation.3 | async-start | bytes 1990656 | tf_op jit(solution)/shard_map/all_gather | solution.py:377
  12.5 89.3 %all-gather.29.cloned.1.call-start = ((), (), s32[]{:S(2)}) async-start(), calls=%async_computation.11 | async-start | bytes 1720320 | tf_op jit(solution)/shard_map/all_gather | solution.py:306
  55.8 15.1 %collective-permute-start = (bf16[2,112,768]{2,1,0:T(8,128)(2,1)S(1)}, bf16[2,112,768]{2,1,0:T(8,128)(2,1)}, u32[]{:S(2)}, u32[]{:S(2)}) collective-permute-start(bf16[2,112,768]{2,1,0:T(8,128)(2,1)S(1)} %fusion.71), channel_id=1, source_target_pairs={{0,8},{1,9},{8,16},{9,17},{16,24},{17,25},{2,10},{3,11},{10,18},{1... | collective-permute-start | bytes 1032200 | tf_op jit(solution)/shard_map/ppermute | solution.py:292
  72.9 56.1 %all-gather.27.cloned.1.call-start = ((), (), s32[]{:S(2)}) async-start(), calls=%async_computation.10 | async-start | bytes 3194880 | tf_op jit(solution)/shard_map/all_gather | solution.py:303
  73.5 158.6 %all-gather.33.cloned.1.call-start = ((), (), s32[]{:S(2)}) async-start(), calls=%async_computation.13 | async-start | bytes 3440640 | tf_op jit(solution)/shard_map/all_gather | solution.py:306
  170.3 20.1 %collective-permute-start.3 = (bf16[2,112,1536]{2,1,0:T(8,128)(2,1)S(1)}, bf16[2,112,1536]{2,1,0:T(8,128)(2,1)S(1)}, u32[]{:S(2)}, u32[]{:S(2)}) collective-permute-start(bf16[2,112,1536]{2,1,0:T(8,128)(2,1)S(1)} %fusion.22), channel_id=1, source_target_pairs={{0,9},{1,8},{8,17},{9,16},{16,25},{17,24},{2,11},{3,10},{10,19},{1... | collective-permute-start | bytes 2064392 | tf_op jit(solution)/shard_map/ppermute | solution.py:292
  174.7 29.8 %collective-permute-start.2 = (bf16[2,112,1536]{2,1,0:T(8,128)(2,1)S(1)}, bf16[2,112,1536]{2,1,0:T(8,128)(2,1)S(1)}, u32[]{:S(2)}, u32[]{:S(2)}) collective-permute-start(bf16[2,112,1536]{2,1,0:T(8,128)(2,1)S(1)} %fusion.22), channel_id=1, source_target_pairs={{0,8},{1,9},{8,16},{9,17},{16,24},{17,25},{2,10},{3,11},{10,18},{1... | collective-permute-start | bytes 2064392 | tf_op jit(solution)/shard_map/ppermute | solution.py:292
  205.6 67.7 %all-gather.31.cloned.1.call-start = ((), (), s32[]{:S(2)}) async-start(), calls=%async_computation.12 | async-start | bytes 6389760 | tf_op jit(solution)/shard_map/all_gather | solution.py:303
  206.8 136.1 %all-gather.35.cloned.1.call-start = ((), (), s32[]{:S(2)}) async-start(), calls=%async_computation.14 | async-start | bytes 12828672 | tf_op jit(solution)/shard_map/all_gather | solution.py:378
  209.4 448.1 %all-gather.21.cloned.1.call-start = ((), (), s32[]{:S(2)}) async-start(), calls=%async_computation.4 | async-start | bytes 1843200 | tf_op jit(solution)/shard_map/all_gather | solution.py:500
  395.5 17.9 %collective-permute-start.7 = (bf16[1,2,112,1536]{3,2,1,0:T(8,128)(2,1)}, bf16[1,2,112,1536]{3,2,1,0:T(8,128)(2,1)}, u32[]{:S(2)}, u32[]{:S(2)}) collective-permute-start(bf16[1,2,112,1536]{3,2,1,0:T(8,128)(2,1)} %constant_dynamic-slice_fusion.4), channel_id=1, source_target_pairs={{0,4},{2,6},{4,0},{6,2},{1,5},{3,7},{5,1},{7,3},{8,12},{10,14},{12... | collective-permute-start | bytes 2064392 | tf_op jit(solution)/shard_map/ppermute | solution.py:318
  398.7 20.0 %collective-permute-start.4 = (bf16[2,2,208,1536]{3,2,1,0:T(8,128)(2,1)}, bf16[2,2,208,1536]{3,2,1,0:T(8,128)(2,1)}, u32[]{:S(2)}, u32[]{:S(2)}) collective-permute-start(bf16[2,2,208,1536]{3,2,1,0:T(8,128)(2,1)} %dynamic-slice_bitcast_fusion), channel_id=1, source_target_pairs={{0,2},{2,0},{4,6},{6,4},{1,3},{3,1},{5,7},{7,5},{8,10},{10,8},{12,... | collective-permute-start | bytes 7667720 | tf_op jit(solution)/shard_map/ppermute | solution.py:318
  416.1 21.5 %collective-permute-start.9 = (bf16[2,112,1536]{2,1,0:T(8,128)(2,1)}, bf16[2,112,1536]{2,1,0:T(8,128)(2,1)}, u32[]{:S(2)}, u32[]{:S(2)}) collective-permute-start(bf16[2,112,1536]{2,1,0:T(8,128)(2,1)} %get-tuple-element.221), channel_id=1, source_target_pairs={{8,1},{9,0},{16,9},{17,8},{24,17},{25,16},{10,3},{11,2},{18,11},{1... | collective-permute-start | bytes 2064392 | tf_op jit(solution)/shard_map/ppermute | solution.py:292
  417.3 32.8 %collective-permute-start.8 = (bf16[2,112,1536]{2,1,0:T(8,128)(2,1)S(1)}, bf16[2,112,1536]{2,1,0:T(8,128)(2,1)}, u32[]{:S(2)}, u32[]{:S(2)}) collective-permute-start(bf16[2,112,1536]{2,1,0:T(8,128)(2,1)S(1)} %get-tuple-element.220), channel_id=1, source_target_pairs={{8,0},{9,1},{16,8},{17,9},{24,16},{25,17},{10,2},{11,3},{18,10},{1... | collective-permute-start | bytes 2064392 | tf_op jit(solution)/shard_map/ppermute | solution.py:292
  424.6 29.7 %collective-permute-start.5 = (bf16[1,2,208,1536]{3,2,1,0:T(8,128)(2,1)}, bf16[1,2,208,1536]{3,2,1,0:T(8,128)(2,1)}, u32[]{:S(2)}, u32[]{:S(2)}) collective-permute-start(bf16[1,2,208,1536]{3,2,1,0:T(8,128)(2,1)} %constant_dynamic-slice_fusion.5), channel_id=1, source_target_pairs={{0,4},{2,6},{4,0},{6,2},{1,5},{3,7},{5,1},{7,3},{8,12},{10,14},{12... | collective-permute-start | bytes 3833864 | tf_op jit(solution)/shard_map/ppermute | solution.py:318
  432.8 228.0 %reduce-scatter.6.cloned.1.call-start = ((), (), s32[]{:S(2)}) async-start(), calls=%async_computation.7 | async-start | bytes 1990656 | tf_op jit(solution)/shard_map/reduce_scatter | solution.py:480
  523.0 23.1 %collective-permute-start.10 = (bf16[2,2,208,768]{3,2,1,0:T(8,128)(2,1)}, bf16[2,2,208,768]{3,2,1,0:T(8,128)(2,1)}, u32[]{:S(2)}, u32[]{:S(2)}) collective-permute-start(bf16[2,2,208,768]{3,2,1,0:T(8,128)(2,1)} %dynamic-slice_bitcast_fusion.2), channel_id=1, source_target_pairs={{0,2},{2,0},{4,6},{6,4},{1,3},{3,1},{5,7},{7,5},{8,10},{10,8},{12,... | collective-permute-start | bytes 3833864 | tf_op jit(solution)/shard_map/ppermute | solution.py:318
  529.8 132.8 %reduce-scatter.4.cloned.1.call-start = ((), (), s32[]{:S(2)}) async-start(), calls=%async_computation.6 | async-start | bytes 3981312 | tf_op jit(solution)/shard_map/reduce_scatter | solution.py:480
  548.9 22.0 %collective-permute-start.11 = (bf16[1,2,208,768]{3,2,1,0:T(8,128)(2,1)}, bf16[1,2,208,768]{3,2,1,0:T(8,128)(2,1)}, u32[]{:S(2)}, u32[]{:S(2)}) collective-permute-start(bf16[1,2,208,768]{3,2,1,0:T(8,128)(2,1)} %constant_dynamic-slice_fusion.3), channel_id=1, source_target_pairs={{0,4},{2,6},{4,0},{6,2},{1,5},{3,7},{5,1},{7,3},{8,12},{10,14},{12... | collective-permute-start | bytes 1916936 | tf_op jit(solution)/shard_map/ppermute | solution.py:318
  552.5 18.4 %collective-permute-start.14 = (bf16[2,112,768]{2,1,0:T(8,128)(2,1)}, bf16[2,112,768]{2,1,0:T(8,128)(2,1)}, u32[]{:S(2)}, u32[]{:S(2)}) collective-permute-start(bf16[2,112,768]{2,1,0:T(8,128)(2,1)} %get-tuple-element.226), channel_id=1, source_target_pairs={{8,0},{9,1},{16,8},{17,9},{24,16},{25,17},{10,2},{11,3},{18,10},{1... | collective-permute-start | bytes 1032200 | tf_op jit(solution)/shard_map/ppermute | solution.py:292
  589.9 147.0 %reduce-scatter.8.cloned.1.call-start = ((), (), s32[]{:S(2)}) async-start(), calls=%async_computation.8 | async-start | bytes 12828672 | tf_op jit(solution)/shard_map/reduce_scatter | solution.py:480
  648.9 137.0 %all-gather.23.cloned.1.call-start = ((), (), s32[]{:S(2)}) async-start(), calls=%async_computation.5 | async-start | bytes 3612672 | tf_op jit(solution)/shard_map/all_gather | solution.py:501
  657.3 211.9 %all-reduce.5.cloned.1.call-start = ((), (), s32[]{:S(2)}) async-start(), calls=%async_computation.15 | async-start | bytes 4325376 | tf_op jit(solution)/shard_map/psum | solution.py:481
  (130 other events, 1832.6 us)
Sparse Core Ops, SparseCore 0:
  10.6 36.7 all-gather.24
  49.8 31.1 all-gather.18
  83.2 18.5 all-gather.28
  103.8 25.1 all-gather.26
  205.7 26.3 all-gather.32
  233.5 39.6 all-gather.30
  275.7 67.1 all-gather.34
  433.0 26.8 all-gather.20
  529.9 49.2 reduce-scatter.5
  590.0 50.0 reduce-scatter.3
  649.0 87.7 reduce-scatter.7
  738.9 37.0 all-gather.22
  779.3 89.9 all-reduce.4

commit v2 on v1

v2 whole, which is shorter than its diff:
```python
import functools
import math

import jax
import jax.numpy as jnp
import numpy as np
from jax import lax
from jax.experimental import pallas as pl
from jax.experimental.pallas import tpu as pltpu
from jax.sharding import PartitionSpec as P

GRID = 14
PATCH = GRID * GRID
POOLED = PATCH // 4
HD = 96
NEG = -1e30
VMEM_CAP = 62 * 2**20
eps = 1e-06
f32, bf16 = jnp.float32, jnp.bfloat16
NN, NT, TN = ((1,), (0,)), ((1,), (1,)), ((0,), (0,))


def up16(n):
    return -(-n // 16) * 16


def pool_matrix(frames):
    rows, cols = up16(frames * POOLED), frames * PATCH
    out = np.zeros((rows, cols), np.float32)
    half = GRID // 2
    for f in range(frames):
        for p in range(PATCH):
            r, c = divmod(p, GRID)
            out[f * POOLED + (r // 2) * half + c // 2, f * PATCH + p] = 0.25
    return out


def pair_matrix(frames):
    rows, cols = up16(frames // 2 * POOLED), up16(frames * POOLED)
    out = np.zeros((rows, cols), np.float32)
    for j in range(frames // 2):
        for p in range(POOLED):
            out[j * POOLED + p, 2 * j * POOLED + p] = 0.5
            out[j * POOLED + p, (2 * j + 1) * POOLED + p] = 0.5
    return out


def dot(a, b, dims=NN):
    return lax.dot_general(a, b, (dims, ((), ())), preferred_element_type=f32)


def exact_dot(matrix, tensor):
    high = tensor.astype(bf16)
    low = (tensor - high.astype(f32)).astype(bf16)
    return dot(matrix, high) + dot(matrix, low)


def norm(x):
    average = jnp.mean(x, axis=-1, keepdims=True)
    centred = x - average
    inverse = lax.rsqrt(jnp.mean(centred * centred, axis=-1, keepdims=True) + eps)
    return centred * inverse, inverse


def norm_back(unit, inverse, gain, gradient):
    scaled = gradient * gain
    return inverse * (
        scaled
        - jnp.mean(scaled, axis=-1, keepdims=True)
        - unit * jnp.mean(scaled * unit, axis=-1, keepdims=True)
    )


GELU_A, GELU_B = math.sqrt(2.0 / math.pi), 0.044715


def gelu(x):
    t = jnp.tanh(GELU_A * (x + GELU_B * (x * x * x)))
    return 0.5 * x * (1.0 + t)


def gelu_both(x):
    square = x * x
    t = jnp.tanh(GELU_A * x * (1.0 + GELU_B * square))
    value = 0.5 * x * (1.0 + t)
    slope = 0.5 * (1.0 + t) + 0.5 * x * (1.0 - t * t) * (GELU_A * (1.0 + 3.0 * GELU_B * square))
    return value, slope


def sum_rows(x):
    return jnp.sum(x, axis=0, keepdims=True)


def add_rows(ref, rows):
    step = pl.program_id(0)

    @pl.when(step == 0)
    def _():
        ref[...] = jnp.zeros_like(ref)

    for i, row in enumerate(rows):
        ref[i:i + 1, :] += row


def transposed(x):
    return x.astype(f32).T.astype(bf16)


def window(head):
    low = HD * head
    return low // 128 * 128, -(-(low + HD) // 128) * 128


def head_mask(head):
    start, stop = window(head)
    lane = lax.broadcasted_iota(jnp.int32, (1, stop - start), 1) + start
    return (lane >= HD * head) & (lane < HD * head + HD)


def key_rows(own_ref, mem_ref):
    row = 0
    for ref in (own_ref, mem_ref):
        for t in range(ref.shape[0]):
            yield ref, t, slice(row, row + ref.shape[2])
            row += ref.shape[2]


def project_keys(own_ref, mem_ref, w_ref, bias_ref, x_s, k_s, v_s):
    for ref, t, rows in key_rows(own_ref, mem_ref):
        x_s[rows, :] = ref[t, 0]
    width = k_s.shape[1]
    for low in range(0, width, 384):
        k_s[:, low:low + 384] = dot(x_s[...], w_ref[:, width + low:width + low + 384]).astype(bf16)
    for low in range(0, width, 384):
        value = dot(x_s[...], w_ref[:, 2 * width + low:2 * width + low + 384])
        v_s[:, low:low + 384] = (value + bias_ref[1:2, low:low + 384]).astype(bf16)


def project_queries(x_ref, w_ref, bias_ref, q_s):
    width = q_s.shape[1]
    for low in range(0, width, 384):
        value = dot(x_ref[0], w_ref[:, low:low + 384])
        q_s[:, low:low + 384] = (value + bias_ref[0:1, low:low + 384]).astype(bf16)


def norm_pool_kernel(x_ref, vec_ref, pool_ref, pair_ref, low_ref, pooled_ref, mean_ref):
    unit, _ = norm(x_ref[0].astype(f32))
    normed = unit * vec_ref[0:1, :] + vec_ref[1:2, :]
    low_ref[0] = normed.astype(bf16)
    pooled = exact_dot(pool_ref[...], normed)
    pooled_ref[0] = pooled.astype(bf16)
    mean_ref[0] = exact_dot(pair_ref[...], pooled).astype(bf16)


def attend_kernel(chunk, x_ref, own_ref, mem_ref, w_ref, qv_ref, mask_ref, out_ref, lse_ref, x_s, q_s, k_s, v_s, s_s, p_s):
    nq, width = q_s.shape
    project_queries(x_ref, w_ref, qv_ref, q_s)
    project_keys(own_ref, mem_ref, w_ref, qv_ref, x_s, k_s, v_s)
    factor = HD**-0.5 * math.log2(math.e)
    lanes = lax.broadcasted_iota(jnp.int32, (chunk, 128), 1)
    for tile in range(width // 384):
        group = slice(384 * tile, 384 * tile + 384)
        base = q_s[:, group].astype(f32)
        parts = [base[:, :128], base[:, 128:256], base[:, 256:384]]
        for head in range(4 * tile, 4 * tile + 4):
            start, stop = window(head)
            mask = head_mask(head)
            query = jnp.where(mask, q_s[:, start:stop], jnp.zeros((), bf16))
            s_s[...] = dot(query, k_s[:, start:stop], NT)

            def body(i, carry, head=head):
                rows = pl.ds(pl.multiple_of(i * chunk, chunk), chunk)
                score = s_s[rows, :] * factor + mask_ref[0]
                top = jnp.max(score, axis=1, keepdims=True)
                power = jnp.exp2(score - top)
                total = jnp.sum(power, axis=1, keepdims=True)
                p_s[rows, :] = (power * (1.0 / total)).astype(bf16)
                lse_ref[0, rows, :] = jnp.where(lanes == head, top + jnp.log2(total), lse_ref[0, rows, :])
                return carry

            lax.fori_loop(0, nq // chunk, body, 0, unroll=nq // chunk)
            out = jnp.where(mask, dot(p_s[...], v_s[:, start:stop]), 0.0)
            for w in range((stop - start) // 128):
                k = start // 128 - 3 * tile + w
                parts[k] = parts[k] + out[:, 128 * w:128 * w + 128]
        out_ref[0, :, group] = jnp.concatenate(parts, axis=1).astype(bf16)


def attend_back_kernel(
    chunk, x_ref, g_ref, own_ref, mem_ref, w_ref, qv_ref, mask_ref, lse_ref,
    dx_ref, dpool_ref, gw_ref, row_ref,
    x_s, q_s, k_s, v_s, s_s, dp_s, p_s, ds_s, dk_s, dv_s, dq_s, gw_s,
):
    nq, width = q_s.shape
    step = pl.program_id(0)
    project_queries(x_ref, w_ref, qv_ref, q_s)
    project_keys(own_ref, mem_ref, w_ref, qv_ref, x_s, k_s, v_s)
    scaling = HD**-0.5
    factor = scaling * math.log2(math.e)
    lanes = lax.broadcasted_iota(jnp.int32, (chunk, 128), 1)

    @pl.when(step == 0)
    def _():
        gw_s[...] = jnp.zeros_like(gw_s)

    xt = transposed(x_ref[0])
    keys_t = transposed(x_s[...])
    dx = None
    dpool = None
    row_q, row_v = [], []
    for tile in range(width // 384):
        group = slice(384 * tile, 384 * tile + 384)
        qt = transposed(q_s[:, group])
        gt = transposed(g_ref[0, :, group])
        parts = [None] * 3
        for head in range(4 * tile, 4 * tile + 4):
            start, stop = window(head)
            mask = head_mask(head)
            query = jnp.where(mask, q_s[:, start:stop], jnp.zeros((), bf16))
            grad = jnp.where(mask, g_ref[0, :, start:stop], jnp.zeros((), bf16))
            s_s[...] = dot(query, k_s[:, start:stop], NT)
            dp_s[...] = dot(grad, v_s[:, start:stop], NT)

            def body(i, carry, head=head):
                rows = pl.ds(pl.multiple_of(i * chunk, chunk), chunk)
                lse = jnp.sum(jnp.where(lanes == head, lse_ref[0, rows, :], 0.0), axis=1, keepdims=True)
                p = jnp.exp2(s_s[rows, :] * factor + mask_ref[0] - lse)
                dp = dp_s[rows, :]
                inner = jnp.sum(p * dp, axis=1, keepdims=True)
                p_s[rows, :] = p.astype(bf16)
                ds_s[rows, :] = (p * (dp - inner)).astype(bf16)
                return carry

            lax.fori_loop(0, nq // chunk, body, 0, unroll=nq // chunk)
            r = slice(HD * (head - 4 * tile), HD * (head - 4 * tile) + HD)
            dv_s[r, :] = dot(gt[r], p_s[...])
            dk_s[r, :] = dot(qt[r], ds_s[...]) * scaling
            dq = jnp.where(mask, dot(ds_s[...], k_s[:, start:stop]) * scaling, 0.0)
            for w in range((stop - start) // 128):
                k = start // 128 - 3 * tile + w
                part = dq[:, 128 * w:128 * w + 128]
                parts[k] = part if parts[k] is None else parts[k] + part
        total = jnp.concatenate(parts, axis=1) + g_ref[0, :, group].astype(f32)
        row_q.append(sum_rows(total))
        low = total.astype(bf16)
        gw_s[:, group] += dot(xt, low)
        add = dot(low, w_ref[:, group], NT)
        dx = add if dx is None else dx + add
        for base, src in ((width, dk_s), (2 * width, dv_s)):
            grad = src[...].T
            if base == 2 * width:
                row_v.append(sum_rows(grad))
            low = grad.astype(bf16)
            here = slice(base + 384 * tile, base + 384 * tile + 384)
            gw_s[:, here] += dot(keys_t, low)
            add = dot(low, w_ref[:, here], NT)
            dpool = add if dpool is None else dpool + add
    dx_ref[0] = dx
    row = 0
    own, mem = own_ref.shape[2], mem_ref.shape[2]
    toks = own_ref.shape[0]
    for t in range(toks):
        dpool_ref[t, 0, :own, :] = dpool[t * own:(t + 1) * own].astype(bf16)
        dpool_ref[t, 0, own:, :] = dpool[toks * own + t * mem:toks * own + (t + 1) * mem].astype(bf16)
    add_rows(row_ref, [jnp.concatenate(row_q, axis=1), jnp.concatenate(row_v, axis=1)])

    @pl.when(step == pl.num_programs(0) - 1)
    def _():
        gw_ref[...] = gw_s[...].astype(bf16)


def first_mlp_kernel(x_ref, comb_ref, out_ref, up_ref, down_ref, ub_ref, vec_ref, pool_ref, pair_ref,
                     after_ref, middle_ref, pooled_ref, mean_ref):
    after = x_ref[0].astype(f32) + dot(comb_ref[0], out_ref[...], NT) + vec_ref[0:1, :]
    after_ref[0] = after
    unit, _ = norm(after)
    low = (unit * vec_ref[1:2, :] + vec_ref[2:3, :]).astype(bf16)
    total = after + vec_ref[3:4, :]
    for h in range(up_ref.shape[0]):
        hidden = gelu(dot(low, up_ref[h]) + ub_ref[h]).astype(bf16)
        total = total + dot(hidden, down_ref[h], NT)
    middle_ref[0] = total
    unit, _ = norm(total)
    pooled = exact_dot(pool_ref[...], unit * vec_ref[4:5, :] + vec_ref[5:6, :])
    pooled_ref[0] = pooled.astype(bf16)
    mean_ref[0] = exact_dot(pair_ref[...], pooled).astype(bf16)


def second_mlp_kernel(
    comb_ref, pooled_ref, cot_ref, out_ref, skip_ref, up_ref, down_ref, ub_ref, vec_ref,
    mixed_ref, dcomb_ref, dskip_ref, gup_ref, gdown_ref, gout_ref, gskip_ref, gub_ref, row_ref,
    after_s, low_s, lowt_s, cott_s, sum_s, dlow_s,
):
    step = pl.program_id(0)

    @pl.when(step == 0)
    def _():
        after = dot(comb_ref[...], out_ref[...], NT) + dot(pooled_ref[...], skip_ref[...], NT) + vec_ref[0:1, :]
        after_s[...] = after
        unit, _ = norm(after)
        low = (unit * vec_ref[1:2, :] + vec_ref[2:3, :]).astype(bf16)
        low_s[...] = low
        lowt_s[...] = transposed(low)
        cott_s[...] = transposed(cot_ref[...])
        sum_s[...] = after + vec_ref[3:4, :]
        dlow_s[...] = jnp.zeros_like(dlow_s)

    pre = dot(low_s[...], up_ref[0]) + ub_ref[...]
    hidden, slope = gelu_both(pre)
    hidden = hidden.astype(bf16)
    dpre = dot(cot_ref[...], down_ref[0]) * slope
    gub_ref[...] = sum_rows(dpre)
    dpre = dpre.astype(bf16)
    sum_s[...] += dot(hidden, down_ref[0], NT)
    dlow_s[...] += dot(dpre, up_ref[0], NT)
    gup_ref[0] = dot(lowt_s[...], dpre).astype(bf16)
    gdown_ref[0] = dot(cott_s[...], hidden).astype(bf16)

    @pl.when(step == pl.num_programs(0) - 1)
    def _():
        mixed_ref[...] = sum_s[...].astype(bf16)
        unit, inverse = norm(after_s[...])
        dlow = dlow_s[...]
        cot = cot_ref[...].astype(f32)
        res = norm_back(unit, inverse, vec_ref[1:2, :], dlow) + cot
        row_ref[...] = jnp.zeros_like(row_ref)
        for i, row in enumerate((res, dlow, cot, dlow * unit)):
            row_ref[i:i + 1, :] = sum_rows(row)
        res = res.astype(bf16)
        dcomb_ref[...] = dot(res, out_ref[...]).astype(bf16)
        dskip_ref[...] = dot(res, skip_ref[...])
        rest = transposed(res)
        gout_ref[...] = dot(rest, comb_ref[...]).astype(bf16)
        gskip_ref[...] = dot(rest, pooled_ref[...]).astype(bf16)


def first_back_kernel(
    middle_ref, after_ref, comb_ref, dskip_ref, dq_ref, own_ref, mem_ref, out_ref, up_ref, down_ref, ub_ref, vec_ref,
    unpool_ref, unpair_ref,
    res_ref, dcomb_ref, gup_ref, gdown_ref, gout_ref, gub_ref, row_ref,
    gup_s, gdown_s, gout_s,
):
    step = pl.program_id(0)

    @pl.when(step == 0)
    def _():
        gup_s[...] = jnp.zeros_like(gup_s)
        gdown_s[...] = jnp.zeros_like(gdown_s)
        gout_s[...] = jnp.zeros_like(gout_s)
        gub_ref[...] = jnp.zeros_like(gub_ref)

    memory = mem_ref[0, 0].astype(f32)
    for d in range(1, mem_ref.shape[0]):
        memory = memory + mem_ref[d, 0].astype(f32)
    dpool = dskip_ref[0] + dq_ref[0] + own_ref[0].astype(f32) + exact_dot(unpair_ref[...], memory)
    dnorm = exact_dot(unpool_ref[...], dpool)
    unit, inverse = norm(middle_ref[0])
    grad = norm_back(unit, inverse, vec_ref[2:3, :], dnorm)
    rows = [sum_rows(dnorm * unit), sum_rows(dnorm), sum_rows(grad)]
    low = grad.astype(bf16)
    lowt = transposed(low)
    unit, inverse = norm(after_ref[0])
    normed = (unit * vec_ref[0:1, :] + vec_ref[1:2, :]).astype(bf16)
    normedt = transposed(normed)
    dnormed = None
    for h in range(up_ref.shape[0]):
        hidden, slope = gelu_both(dot(normed, up_ref[h]) + ub_ref[h])
        hidden = hidden.astype(bf16)
        dpre = dot(low, down_ref[h]) * slope
        gub_ref[h] += sum_rows(dpre)
        dpre = dpre.astype(bf16)
        gdown_s[h] += dot(lowt, hidden)
        gup_s[h] += dot(normedt, dpre)
        add = dot(dpre, up_ref[h], NT)
        dnormed = add if dnormed is None else dnormed + add
    res = norm_back(unit, inverse, vec_ref[0:1, :], dnormed) + grad
    rows += [sum_rows(dnormed * unit), sum_rows(dnormed), sum_rows(res)]
    res_ref[0] = res
    res = res.astype(bf16)
    dcomb_ref[0] = dot(res, out_ref[...]).astype(bf16)
    gout_s[...] += dot(transposed(res), comb_ref[0])
    add_rows(row_ref, rows)

    @pl.when(step == pl.num_programs(0) - 1)
    def _():
        gup_ref[...] = gup_s[...].astype(bf16)
        gdown_ref[...] = gdown_s[...].astype(bf16)
        gout_ref[...] = gout_s[...].astype(bf16)


def last_back_kernel(x_ref, res_ref, dx_ref, own_ref, mem_ref, vec_ref, unpool_ref, unpair_ref, grad_ref, row_ref):
    memory = mem_ref[0, 0].astype(f32)
    for d in range(1, mem_ref.shape[0]):
        memory = memory + mem_ref[d, 0].astype(f32)
    dpool = own_ref[0].astype(f32) + exact_dot(unpair_ref[...], memory)
    dnorm = dx_ref[0] + exact_dot(unpool_ref[...], dpool)
    unit, inverse = norm(x_ref[0].astype(f32))
    grad_ref[0] = (norm_back(unit, inverse, vec_ref[0:1, :], dnorm) + res_ref[0]).astype(bf16)
    add_rows(row_ref, [sum_rows(dnorm * unit), sum_rows(dnorm)])


def whole(array):
    return pl.BlockSpec(array.shape, lambda i: (0,) * array.ndim)


def by_micro(array, axis=0):
    block = array.shape[:axis] + (1,) + array.shape[axis + 1:]
    return pl.BlockSpec(block, lambda i: (0,) * axis + (i,) + (0,) * (array.ndim - axis - 1))


def shape(dims, dtype):
    return jax.ShapeDtypeStruct(dims, dtype)


def call(kernel, steps, args, outs, scratch=(), name=None):
    def spec(array, how):
        if how is None:
            return whole(array)
        return by_micro(array, how) if isinstance(how, int) else how

    return pl.pallas_call(
        kernel,
        grid=(steps,),
        in_specs=[spec(a, how) for a, how in args],
        out_specs=[spec(a, how) for a, how in outs],
        out_shape=[a for a, _ in outs],
        scratch_shapes=[pltpu.VMEM(dims, dtype) for dims, dtype in scratch],
        compiler_params=pltpu.CompilerParams(vmem_limit_bytes=VMEM_CAP),
        name=name,
    )(*[a for a, _ in args])


def chunk_of(nq):
    return 112 if nq % 112 == 0 else 16


def attend(x, own, mem, w, qv, mask, width):
    batches, nq, d = x.shape
    keys = own.shape[0] * own.shape[2] + mem.shape[0] * mem.shape[2]
    return call(
        functools.partial(attend_kernel, chunk_of(nq)), batches,
        [(x, 0), (own, 1), (mem, 1), (w, None), (qv, None), (mask, 0)],
        [(shape((batches, nq, width), bf16), 0), (shape((batches, nq, 128), f32), 0)],
        [((keys, d), bf16), ((nq, width), bf16), ((keys, width), bf16), ((keys, width), bf16), ((nq, keys), f32), ((nq, keys), bf16)],
        name="attend",
    )


def attend_back(x, grad, own, mem, w, qv, mask, lse):
    batches, nq, d = x.shape
    width = grad.shape[2]
    keys = own.shape[0] * own.shape[2] + mem.shape[0] * mem.shape[2]
    both = (own.shape[0], batches, own.shape[2] + mem.shape[2], d)
    return call(
        functools.partial(attend_back_kernel, chunk_of(nq)), batches,
        [(x, 0), (grad, 0), (own, 1), (mem, 1), (w, None), (qv, None), (mask, 0), (lse, 0)],
        [(shape((batches, nq, d), f32), 0), (shape(both, bf16), 1), (shape(w.shape, bf16), None), (shape((8, width), f32), None)],
        [((keys, d), bf16), ((nq, width), bf16), ((keys, width), bf16), ((keys, width), bf16),
         ((nq, keys), f32), ((nq, keys), f32), ((nq, keys), bf16), ((nq, keys), bf16),
         ((384, keys), f32), ((384, keys), f32), ((8, 128), f32), (w.shape, f32)],
        name="attend_back",
    )


def grouped(pairs_of):
    clips, heads = lax.axis_size("clip"), lax.axis_size("head")
    return [
        (c * heads + h, c2 * heads + h2)
        for c in range(clips)
        for h in range(heads)
        for c2, h2 in [pairs_of(c, h)]
        if 0 <= c2 < clips
    ]


def to_clip(pieces, by, heads):
    return [
        lax.ppermute(pieces[d], ("clip", "head"), grouped(lambda c, h, d=d: (c + by, (h + d) % heads)))
        for d in range(heads)
    ]


def share_pooled(pooled, mean, slots, heads):
    received = to_clip([mean] * heads, 1, heads)
    own = lax.all_gather(pooled, "tok")
    flat = jnp.stack(received).reshape((-1,) + mean.shape[1:])
    chosen = jnp.stack([lax.dynamic_index_in_dim(flat, slot, 0, keepdims=False) for slot in slots])
    return own, lax.all_gather(chosen, "tok")


def halve_over_tok(partial):
    size = lax.axis_size("tok")
    index = lax.axis_index("tok")
    bit = 1
    while bit < size:
        mine = (index // bit) % 2
        paired = partial.reshape((partial.shape[0] // 2, 2) + partial.shape[1:])
        keep = lax.dynamic_index_in_dim(paired, mine, 1, keepdims=False)
        give = lax.dynamic_index_in_dim(paired, 1 - mine, 1, keepdims=False)
        got = lax.ppermute(give, "tok", [(i, i ^ bit) for i in range(size)])
        partial = (keep.astype(f32) + got.astype(f32)).astype(bf16)
        bit *= 2
    return partial[0]


def return_pooled(dpool, own_rows, slots, heads):
    total = halve_over_tok(dpool)
    own, mem = total[:, :own_rows], total[:, own_rows:]
    routed = jnp.zeros((heads * mem.shape[0],) + mem.shape[1:], bf16)
    for m, slot in enumerate(slots):
        routed = lax.dynamic_update_index_in_dim(routed, mem[m], slot, 0)
    routed = routed.reshape((heads,) + mem.shape)
    return own, jnp.stack(to_clip([routed[(heads - d) % heads] for d in range(heads)], -1, heads))


def padded_rows(*rows):
    return jnp.concatenate([jnp.stack(rows), jnp.zeros((-len(rows) % 8, rows[0].shape[0]), f32)])


def local(
    clips_in, resets, assign, w_qkv_a, w_out_a, w_up_a, w_down_a, w_qkv_b, w_out_b, w_skip_b, w_up_b, w_down_b,
    gains_a, gains_b, shifts_a, shifts_b, qv_bias_a, qv_bias_b, up_bias_a, up_bias_b, cotangent,
):
    heads, toks = lax.axis_size("head"), lax.axis_size("tok")
    head = lax.axis_index("head")
    micro, frames = clips_in.shape[1], clips_in.shape[2]
    d1, d2 = clips_in.shape[-1], cotangent.shape[-1]
    share = micro // heads
    first = head * share
    pool_np, pair_np = pool_matrix(frames), pair_matrix(frames)
    pooling, pairing = jnp.asarray(pool_np, bf16), jnp.asarray(pair_np, bf16)
    unpooling, unpairing = jnp.asarray(pool_np.T, bf16), jnp.asarray(pair_np.T, bf16)
    tokens, pooled_tokens = frames * PATCH, frames * POOLED
    own_rows, mem_rows = up16(pooled_tokens), up16(frames // 2 * POOLED)
    rows2 = share * own_rows

    stream = lax.dynamic_slice_in_dim(clips_in[0], first, share, 0).reshape(share, tokens, d1)
    cot = lax.dynamic_slice_in_dim(cotangent[0], first, share, 0).reshape(share, pooled_tokens, d2)
    cot = jnp.pad(cot, ((0, 0), (0, own_rows - pooled_tokens), (0, 0))).reshape(rows2, d2)

    slots, masks = [], []
    row_own = jnp.where(jnp.arange(own_rows) < pooled_tokens, 0.0, NEG)
    row_mem = jnp.arange(mem_rows) < frames // 2 * POOLED
    for m in range(share):
        source = lax.dynamic_index_in_dim(assign[0], first + m, 0, keepdims=False)
        flag = lax.dynamic_index_in_dim(resets[0], first + m, 0, keepdims=False)
        slots.append(((head - source // share + heads) % heads) * share + source % share)
        has = (flag == 0) & (lax.axis_index("clip") > 0)
        masks.append(jnp.concatenate([jnp.tile(row_own, toks), jnp.tile(jnp.where(row_mem & has, 0.0, NEG), toks)]))
    mask = jnp.stack(masks)[:, None, :].astype(f32)

    group = ("head", "tok")
    fa, ha = w_up_a.shape[1], w_out_a.shape[1]
    fb, hb, hs = w_up_b.shape[1], w_out_b.shape[1], w_skip_b.shape[1]
    pack_a = jnp.concatenate([w_up_a, w_down_a, w_qkv_a.reshape(w_qkv_a.shape[0], -1), w_out_a], axis=1)
    all_a = lax.all_gather(pack_a, group).reshape(heads, d1, -1)
    all_q = lax.all_gather(w_qkv_b.reshape(w_qkv_b.shape[0], -1), group).reshape(heads, d1, -1)
    all_o = lax.all_gather(jnp.concatenate([w_out_b, w_skip_b], axis=1), group).reshape(heads, d2, -1)
    all_b = lax.all_gather(jnp.concatenate([w_up_b, w_down_b], axis=1), group).reshape(heads, d2, -1)
    flat = jnp.concatenate([qv_bias_a.reshape(-1), qv_bias_b.reshape(-1), up_bias_a, up_bias_b])
    flat = lax.all_gather(flat, "head")
    qv_a = flat[:, :2 * ha].reshape(heads, 2, ha).transpose(1, 0, 2).reshape(2, d1)
    qv_b = flat[:, 2 * ha:2 * ha + 2 * hb].reshape(heads, 2, hb).transpose(1, 0, 2).reshape(2, d2)
    ub_a = flat[:, 2 * (ha + hb):2 * (ha + hb) + fa].reshape(heads, 1, fa)
    ub_b = flat[:, 2 * (ha + hb) + fa:].reshape(1, heads * fb)

    def lanes(pack, low, width):
        return jnp.concatenate([pack[h, :, low:low + width] for h in range(heads)], axis=1)

    up_a, down_a = all_a[:, :, :fa], all_a[:, :, fa:2 * fa]
    qkv_a = jnp.concatenate([lanes(all_a, 2 * fa + i * ha, ha) for i in range(3)], axis=1)
    out_a = lanes(all_a, 2 * fa + 3 * ha, ha)
    qkv_b = jnp.concatenate([lanes(all_q, i * hb, hb) for i in range(3)], axis=1)
    out_b, skip_b = lanes(all_o, 0, hb), lanes(all_o, hb, hs)

    low1, pooled1, mean1 = call(
        norm_pool_kernel, share,
        [(stream, 0), (padded_rows(gains_a[0], shifts_a[0]), None), (pooling, None), (pairing, None)],
        [(shape((share, tokens, d1), bf16), 0), (shape((share, own_rows, d1), bf16), 0), (shape((share, mem_rows, d1), bf16), 0)],
        name="norm_pool",
    )
    own1, mem1 = share_pooled(pooled1, mean1, slots, heads)
    comb1, lse1 = attend(low1, own1, mem1, qkv_a, qv_a, mask, d1)
    after1, middle, pooled3, mean3 = call(
        first_mlp_kernel, share,
        [(stream, 0), (comb1, 0), (out_a, None), (up_a, None), (down_a, None), (ub_a, None),
         (padded_rows(shifts_a[1], gains_a[1], shifts_a[2], shifts_a[3], gains_a[2], shifts_a[4]), None),
         (pooling, None), (pairing, None)],
        [(shape((share, tokens, d1), f32), 0), (shape((share, tokens, d1), f32), 0),
         (shape((share, own_rows, d1), bf16), 0), (shape((share, mem_rows, d1), bf16), 0)],
        name="first_mlp",
    )

    own2, mem2 = share_pooled(pooled3, mean3, slots, heads)
    comb2, lse2 = attend(pooled3, own2, mem2, qkv_b, qv_b, mask, d2)
    chunk = 768
    per_head = fb // chunk
    steps = heads * per_head
    rows_spec = pl.BlockSpec((1, d2, chunk), lambda j: (j // per_head, 0, j % per_head))
    mixed, dcomb2, dskip, g_up_b, g_down_b, g_out_b, g_skip_b, g_ub_b, rows_b = call(
        second_mlp_kernel, steps,
        [(comb2.reshape(rows2, d2), None), (pooled3.reshape(rows2, d1), None), (cot, None), (out_b, None), (skip_b, None),
         (all_b, rows_spec),
         (all_b, pl.BlockSpec((1, d2, chunk), lambda j: (j // per_head, 0, per_head + j % per_head))),
         (ub_b, pl.BlockSpec((1, chunk), lambda j: (0, j))),
         (padded_rows(shifts_b[0], gains_b, shifts_b[1], shifts_b[2]), None)],
        [(shape((rows2, d2), bf16), None), (shape((rows2, d2), bf16), None), (shape((rows2, d1), f32), None),
         (shape((heads, d2, fb), bf16), rows_spec), (shape((heads, d2, fb), bf16), rows_spec),
         (shape((d2, d2), bf16), None), (shape((d2, d1), bf16), None),
         (shape((1, heads * fb), f32), pl.BlockSpec((1, chunk), lambda j: (0, j))), (shape((8, d2), f32), None)],
        [((rows2, d2), f32), ((rows2, d2), bf16), ((d2, rows2), bf16), ((d2, rows2), bf16), ((rows2, d2), f32), ((rows2, d2), f32)],
        name="second_mlp",
    )

    def reduce_grad(blocks):
        blocks = blocks.reshape((heads * toks, -1) + blocks.shape[2:])
        shard = lax.psum_scatter(blocks, group, scatter_dimension=0, tiled=False)
        return lax.psum(shard, "clip").astype(f32)

    def by_head(grad, width):
        return grad.reshape(grad.shape[0], heads, width).transpose(1, 0, 2)

    dcomb2 = dcomb2.reshape(share, own_rows, d2)
    dq2, dpool2, g_qkv_b, rows_qv_b = attend_back(pooled3, dcomb2, own2, mem2, qkv_b, qv_b, mask, lse2)
    own_back2, mem_back2 = return_pooled(dpool2, own_rows, slots, heads)

    res1, dcomb1, g_up_a, g_down_a, g_out_a, g_ub_a, rows_a = call(
        first_back_kernel, share,
        [(middle, 0), (after1, 0), (comb1, 0), (dskip.reshape(share, own_rows, d1), 0), (dq2, 0), (own_back2, 0), (mem_back2, 1),
         (out_a, None), (up_a, None), (down_a, None), (ub_a, None),
         (padded_rows(gains_a[1], shifts_a[2], gains_a[2]), None), (unpooling, None), (unpairing, None)],
        [(shape((share, tokens, d1), f32), 0), (shape((share, tokens, d1), bf16), 0),
         (shape((heads, d1, fa), bf16), None), (shape((heads, d1, fa), bf16), None), (shape((d1, d1), bf16), None),
         (shape((heads, 1, fa), f32), None), (shape((8, d1), f32), None)],
        [((heads, d1, fa), f32), ((heads, d1, fa), f32), ((d1, d1), f32)],
        name="first_back",
    )
    dx1, dpool1, g_qkv_a, rows_qv_a = attend_back(low1, dcomb1, own1, mem1, qkv_a, qv_a, mask, lse1)
    own_back1, mem_back1 = return_pooled(dpool1, own_rows, slots, heads)
    stream_grad, rows_last = call(
        last_back_kernel, share,
        [(stream, 0), (res1, 0), (dx1, 0), (own_back1, 0), (mem_back1, 1), (padded_rows(gains_a[0]), None),
         (unpooling, None), (unpairing, None)],
        [(shape((share, tokens, d1), bf16), 0), (shape((8, d1), f32), None)],
        name="last_back",
    )

    sum_up_b, sum_down_b = reduce_grad(g_up_b), reduce_grad(g_down_b)
    grad_q = jnp.concatenate([by_head(g_qkv_b[:, i * d2:(i + 1) * d2], hb) for i in range(3)], axis=2)
    grad_o = jnp.concatenate([by_head(g_out_b, hb), by_head(g_skip_b, hs)], axis=2)
    sum_q, sum_o = reduce_grad(grad_q), reduce_grad(grad_o)
    grad_a = jnp.concatenate(
        [g_up_a, g_down_a] + [by_head(g_qkv_a[:, i * d1:(i + 1) * d1], ha) for i in range(3)] + [by_head(g_out_a, ha)], axis=2)
    sum_a = reduce_grad(grad_a)

    small = [
        jnp.stack([rows_last[0], rows_a[3], rows_a[0]]), rows_b[3],
        jnp.stack([rows_last[1], rows_a[5], rows_a[4], rows_a[2], rows_a[1]]),
        rows_b[:3], rows_qv_a[:2], rows_qv_b[:2], g_ub_a, g_ub_b,
    ]
    flat = lax.all_gather(jnp.concatenate([piece.reshape(-1) for piece in small]), ("clip", "tok", "head")).sum(axis=0)
    pieces, at = [], 0
    for piece in small:
        pieces.append(flat[at:at + piece.size].reshape(piece.shape))
        at += piece.size

    def mine(piece, axis):
        width = piece.shape[axis] // heads
        return lax.dynamic_slice_in_dim(piece, head * width, width, axis)

    mixed = mixed.reshape(share, own_rows, d2)[:, :pooled_tokens]
    mixed_all = lax.all_gather(mixed, "head", axis=0, tiled=True)
    stream_all = lax.all_gather(stream_grad, "head", axis=0, tiled=True)
    return (
        mixed_all.reshape(cotangent.shape),
        stream_all.astype(f32).reshape(clips_in.shape),
        sum_a[:, 2 * fa:2 * fa + 3 * ha].reshape(w_qkv_a.shape),
        sum_a[:, 2 * fa + 3 * ha:],
        sum_a[:, :fa],
        sum_a[:, fa:2 * fa],
        sum_q.reshape(w_qkv_b.shape),
        sum_o[:, :hb],
        sum_o[:, hb:],
        sum_up_b,
        sum_down_b,
        pieces[0], pieces[1], pieces[2], pieces[3],
        mine(pieces[4], 1), mine(pieces[5], 1), mine(pieces[6].reshape(-1), 0), mine(pieces[7].reshape(-1), 0),
    )


def solution(mesh):
    in_specs = (
        P("clip", None, "tok", None, None),
        P("clip", None),
        P("clip", None),
        P("tok", None, "head"),
        P("tok", "head"),
        P("tok", "head"),
        P("tok", "head"),
        P("tok", None, "head"),
        P("tok", "head"),
        P("tok", "head"),
        P("tok", "head"),
        P("tok", "head"),
        P(),
        P(),
        P(),
        P(),
        P(None, "head"),
        P(None, "head"),
        P("head"),
        P("head"),
        P("clip", None, "tok", None, None),
    )
    out_specs = (
        P("clip", None, "tok", None, None),
        P("clip", None, "tok", None, None),
        P("tok", None, "head"),
        P("tok", "head"),
        P("tok", "head"),
        P("tok", "head"),
        P("tok", None, "head"),
        P("tok", "head"),
        P("tok", "head"),
        P("tok", "head"),
        P("tok", "head"),
        P(),
        P(),
        P(),
        P(),
        P(None, "head"),
        P(None, "head"),
        P("head"),
        P("head"),
    )
    return jax.shard_map(local, mesh=mesh, in_specs=in_specs, out_specs=out_specs, check_vma=False)
```

time: 896 us -> 806 us (0.90)
  matrix products: 118 us -> 0 us
  Pallas kernels: 79.6 us -> 185 us
  local copies, waits for them, and re-layouts: 155 us -> 90.3 us
  waiting for transfers between devices: 380 us -> 434 us
  blocking collectives: 58.7 us -> 22.8 us
  other arithmetic: 43 us -> 19.7 us
    dot_general x38 -> x0, matrix products: 118 us -> none  [the longest x10 36.7 us: tokens_dot(): return jnp.einsum('mnd,de->mne', a, b, preferred_element_type=f32)]
    pallas_call x4 -> x9, Pallas kernels: 79.6 us -> 185 us  [call(): pl.pallas_call(kernel, grid=(steps,), in_specs=[spec(a, how) for a, how i...]
    reduce_scatter x3 -> x5, waiting for transfers between devices: 74.2 us -> 129 us  [reduce_grad(): shard = lax.psum_scatter(blocks, group, scatter_dimension=0, tiled=False)]
    psum x1 -> x0, blocking collectives: 40.2 us -> none  [local(): lax.psum(jnp.concatenate([piece.reshape(-1) for piece in small]), ('clip'...]
    ppermute x8, waiting for transfers between devices: 57.6 us -> 17.6 us  [to_clip(): lax.ppermute(pieces[d], ('clip', 'head'), grouped(lambda c, h, d=d: (c +...]
    all_gather x1, waiting for transfers between devices: 0.01 us -> 35 us  [local(): stream_all = lax.all_gather(stream_grad, 'head', axis=0, tiled=True)]
    reshape x8, local copies, waits for them, and re-layouts: 26 us -> 3.74 us  [by_head(): return grad.reshape(grad.shape[0], heads, width).transpose(1, 0, 2)]
    psum x1, waiting for transfers between devices: 72.9 us -> 90.3 us  [reduce_grad(): return lax.psum(shard, 'clip').astype(f32)]
  transfers between devices with their start and end apart: 29 -> 27, of which waited for: 19 -> 18; matrix products, arithmetic and copies ran while one was open for 27% -> 11% of each run, Pallas kernels for 5% -> 16%
where the time goes in v2:
time: 806 us; the launch traced here: 801 us
  waiting for transfers between devices  434 us (54%)
  Pallas kernels  185 us (23%)
  local copies, waits for them, and re-layouts  90.3 us (11%)
  starting transfers between devices  26.6 us (3%)
  blocking collectives  22.8 us (3%)
  between operations  21.8 us (3%)
  other arithmetic  19.7 us (2%)
    pallas_call x9, Pallas kernels, call(): pl.pallas_call(kernel, grid=(steps,), in_specs=[spec(a, how) for a, how i...  185 us
    reduce_scatter x5, waiting for transfers between devices, reduce_grad(): shard = lax.psum_scatter(blocks, group, scatter_dimension=0, tiled=False)  129 us
    psum x1, waiting for transfers between devices, reduce_grad(): return lax.psum(shard, 'clip').astype(f32)  90.3 us
    all_gather x1, waiting for transfers between devices, local(): lax.all_gather(jnp.concatenate([piece.reshape(-1) for piece in small]), (...  48.4 us
    all_gather x1, waiting for transfers between devices, local(): lax.all_gather(jnp.concatenate([w_up_b, w_down_b], axis=1), group)  39.9 us
    all_gather x1, waiting for transfers between devices, local(): stream_all = lax.all_gather(stream_grad, 'head', axis=0, tiled=True)  35 us
    ppermute x4, waiting for transfers between devices, halve_over_tok(): got = lax.ppermute(give, 'tok', [(i, i ^ bit) for i in range(size)])  28.6 us
    all_gather x1, waiting for transfers between devices, local(): mixed_all = lax.all_gather(mixed, 'head', axis=0, tiled=True)  25.3 us
  transfers between devices with their start and end apart: 27, of which 18 were waited for; matrix products, arithmetic and copies ran while one was open for 11% of the time, Pallas kernels for 16%

profile of v2, /device:TPU:0, one launch (start us, length us, event | category | flops | bytes accessed | tf_op | source)
XLA Modules:
  0.0 800.8 jit_solution(13454556327475657891)
XLA Ops:
  45.3 8.7 %all-gather.1 = bf16[8,112,384]{2,1,0:T(8,128)(2,1)} all-gather(bf16[2,112,384]{2,1,0:T(8,128)(2,1)S(1)} %pad_maximum_fusion.11), channel_id=3, replica_groups=mesh['clip'=4,'tok'=4,'head'=2] {'tok'}, dimensions={0}, use_global_device_ids=true | all-gather | bytes 860160 | tf_op jit(solution)/shard_map/all_gather | solution.py:488
  57.1 11.8 %all-gather.27.cloned.1.call-done = bf16[8,208,384]{2,1,0:T(8,128)(2,1)} async-done(((bf16[2,208,384]{2,1,0:T(8,128)(2,1)}), bf16[8,208,384]{2,1,0:T(8,128)(2,1)}) %all-gather.27.cloned.1.call-update) | async-done | bytes 1277968 | tf_op jit(solution)/shard_map/all_gather | solution.py:485
  69.0 20.9 %attend.2 = (bf16[2,784,384]{2,1,0:T(8,128)(2,1)}, f32[2,784,128]{2,1,0:T(8,128)}) custom-call(bf16[2,784,384]{2,1,0:T(8,128)(2,1)} %get-tuple-element.56.x_ref, bf16[4,2,208,384]{3,2,1,0:T(8,128)(2,1)} %bitcast.168, bf16[4,2,112,384]{3,2,1,0:T(8,128)(2,1)} %bitcast.163, bf16[384,1152]{1,0:T(8,128)(2,1)} %concatenate.62.w_ref, f32[2,384]{1,0:T(2,128)} %reshape.305.qv_ref, ...), custom_call_target="tpu_custom_call" | custom-call | tf_op jit(solution)/shard_map/attend/pallas_call | solution.py:421
  93.9 13.1 %first_mlp.1 = (f32[2,784,384]{2,1,0:T(8,128)}, f32[2,784,384]{2,1,0:T(8,128)}, bf16[2,208,384]{2,1,0:T(8,128)(2,1)}, bf16[2,112,384]{2,1,0:T(8,128)(2,1)}) custom-call(bf16[2,784,384]{2,1,0:T(8,128)(2,1)} %reshape.298.x_ref, bf16[2,784,384]{2,1,0:T(8,128)(2,1)} %get-tuple-element.59.comb_ref, bf16[384,384]{1,0:T(8,128)(2,1)} %pad_maximum_fusion.9.out_ref, ...), custom_call_target="tpu_custom_call" | custom-call | tf_op jit(solution)/shard_map/first_mlp/pallas_call | solution.py:421
  120.8 6.9 all-gather.33.cloned.1.call-done
  141.8 9.5 %all-gather.5 = bf16[8,112,384]{2,1,0:T(8,128)(2,1)} all-gather(bf16[2,112,384]{2,1,0:T(8,128)(2,1)S(1)} %pad_maximum_fusion.12), channel_id=7, replica_groups=mesh['clip'=4,'tok'=4,'head'=2] {'tok'}, dimensions={0}, use_global_device_ids=true | all-gather | bytes 860160 | tf_op jit(solution)/shard_map/all_gather | solution.py:488
  151.2 18.0 %attend.3 = (bf16[2,208,768]{2,1,0:T(8,128)(2,1)}, f32[2,208,128]{2,1,0:T(8,128)}) custom-call(bf16[2,208,384]{2,1,0:T(8,128)(2,1)} %get-tuple-element.60.x_ref, bf16[4,2,208,384]{3,2,1,0:T(8,128)(2,1)} %bitcast.166, bf16[4,2,112,384]{3,2,1,0:T(8,128)(2,1)} %bitcast.161, bf16[384,2304]{1,0:T(8,128)(2,1)} %fusion.4.w_ref, f32[2,768]{1,0:T(2,128)} %bitcast.228, ...), custom_call_target="tpu_custom_call" | custom-call | tf_op jit(solution)/shard_map/attend/pallas_call | solution.py:421
  169.2 39.9 %all-gather.35.cloned.1.call-done = bf16[1536,3072]{1,0:T(8,128)(2,1)} async-done(((bf16[192,3072]{1,0:T(8,128)(2,1)}), bf16[1536,3072]{1,0:T(8,128)(2,1)}) %all-gather.35.cloned.1.call-update) | async-done | bytes 9437200 | tf_op jit(solution)/shard_map/all_gather | solution.py:559
  209.1 25.9 %second_mlp.1 = (bf16[416,768]{1,0:T(8,128)(2,1)}, bf16[416,768]{1,0:T(8,128)(2,1)}, f32[416,384]{1,0:T(8,128)}, bf16[2,768,1536]{2,1,0:T(8,128)(2,1)}, bf16[2,7...) custom-call(bf16[416,768]{1,0:T(8,128)(2,1)} %bitcast.209, ...), custom_call_target="tpu_custom_call" | custom-call | tf_op jit(solution)/shard_map/second_mlp/pallas_call | solution.py:421
  235.0 34.3 %attend_back.2 = (f32[2,208,384]{2,1,0:T(8,128)}, bf16[4,2,320,384]{3,2,1,0:T(8,128)(2,1)}, bf16[384,2304]{1,0:T(8,128)(2,1)}, f32[8,768]{1,0:T(8,128)}) custom-call(bf16[2,208,384]{2,1,0:T(8,128)(2,1)} %get-tuple-element.60.x_ref, bf16[2,208,768]{2,1,0:T(8,128)(2,1)} %bitcast.210, bf16[4,2,208,384]{3,2,1,0:T(8,128)(2,1)} %bitcast.167, ...), custom_call_target="tpu_custom_call" | custom-call | tf_op jit(solution)/shard_map/attend_back/pallas_call | solution.py:421
  286.5 15.4 %collective-permute-done.5 = bf16[1,2,320,384]{3,2,1,0:T(8,128)(2,1)S(1)} collective-permute-done((bf16[1,2,320,384]{3,2,1,0:T(8,128)(2,1)S(1)}, bf16[1,2,320,384]{3,2,1,0:T(8,128)(2,1)S(1)}, u32[]{:S(2)}, u32[]{:S(2)}) %collective-permute-start.5) | collective-permute-done | bytes 491552 | tf_op jit(solution)/shard_map/ppermute | solution.py:500
  313.5 26.0 %first_back.1 = (f32[2,784,384]{2,1,0:T(8,128)}, bf16[2,784,384]{2,1,0:T(8,128)(2,1)}, bf16[2,384,768]{2,1,0:T(8,128)(2,1)}, bf16[2,384,768]{2,1,0:T(8,128)(2,1)...) custom-call(f32[2,784,384]{2,1,0:T(8,128)} %get-tuple-element.64.middle_ref, ...), custom_call_target="tpu_custom_call" | custom-call | tf_op jit(solution)/shard_map/first_back/pallas_call | solution.py:421
  339.5 37.0 %attend_back.3 = (f32[2,784,384]{2,1,0:T(8,128)}, bf16[4,2,320,384]{3,2,1,0:T(8,128)(2,1)}, bf16[384,1152]{1,0:T(8,128)(2,1)}, f32[8,384]{1,0:T(8,128)}) custom-call(bf16[2,784,384]{2,1,0:T(8,128)(2,1)} %get-tuple-element.56.x_ref, bf16[2,784,384]{2,1,0:T(8,128)(2,1)} %get-tuple-element.72.g_ref, bf16[4,2,208,384]{3,2,1,0:T(8,128)(2,1)} %bitcast.169, ...), custom_call_target="tpu_custom_call" | custom-call | tf_op jit(solution)/shard_map/attend_back/pallas_call | solution.py:421
  379.7 6.1 concatenate.76
  385.8 6.3 copy.103
  400.3 10.6 %collective-permute-done.9 = bf16[1,2,320,384]{3,2,1,0:T(8,128)(2,1)S(1)} collective-permute-done((bf16[1,2,320,384]{3,2,1,0:T(8,128)(2,1)S(1)}, bf16[1,2,320,384]{3,2,1,0:T(8,128)(2,1)S(1)}, u32[]{:S(2)}, u32[]{:S(2)}) %collective-permute-start.9) | collective-permute-done | bytes 491552 | tf_op jit(solution)/shard_map/ppermute | solution.py:500
  414.5 6.1 collective-permute-done.10
  435.6 13.7 %reduce-scatter.6.cloned.1.call-done = bf16[1,96,2304]{1,2,0:T(8,128)(2,1)} async-done(((bf16[8,96,2304]{1,2,0:T(8,128)(2,1)}), bf16[1,96,2304]{1,2,0:T(8,128)(2,1)}) %reduce-scatter.6.cloned.1.call-update) | async-done | bytes 442384 | tf_op jit(solution)/shard_map/reduce_scatter | solution.py:617
  449.3 57.8 %reduce-scatter.12.cloned.1.call-done = bf16[1,192,1536]{2,1,0:T(8,128)(2,1)} async-done(((bf16[8,192,1536]{2,1,0:T(8,128)(2,1)}), bf16[1,192,1536]{2,1,0:T(8,128)(2,1)}) %reduce-scatter.12.cloned.1.call-update) | async-done | bytes 589840 | tf_op jit(solution)/shard_map/reduce_scatter | solution.py:617
  507.1 57.7 %reduce-scatter.14.cloned.1.call-done = bf16[1,192,1536]{2,1,0:T(8,128)(2,1)} async-done(((bf16[8,192,1536]{2,1,0:T(8,128)(2,1)}), bf16[1,192,1536]{2,1,0:T(8,128)(2,1)}) %reduce-scatter.14.cloned.1.call-update) | async-done | bytes 589840 | tf_op jit(solution)/shard_map/reduce_scatter | solution.py:617
  564.9 25.3 %all-gather.23.cloned.1.call-done = bf16[4,196,768]{2,1,0:T(8,128)(2,1)} async-done(((bf16[2,196,768]{2,1,0:T(8,128)(2,1)}), bf16[4,196,768]{2,1,0:T(8,128)(2,1)}) %all-gather.23.cloned.1.call-update) | async-done | bytes 1204240 | tf_op jit(solution)/shard_map/all_gather | solution.py:672
  593.4 35.0 %all-gather.25.cloned.1.call-done = bf16[4,784,384]{2,1,0:T(8,128)(2,1)} async-done(((bf16[2,784,384]{2,1,0:T(8,128)(2,1)}), bf16[4,784,384]{2,1,0:T(8,128)(2,1)}) %all-gather.25.cloned.1.call-update) | async-done | bytes 2408464 | tf_op jit(solution)/shard_map/all_gather | solution.py:673
  638.7 48.4 %all-gather.37.cloned.1.call-done = f32[32,1,13056]{2,1,0:T(1,128)} async-done(((f32[1,1,13056]{2,1,0:T(1,128)}), f32[32,1,13056]{2,1,0:T(1,128)}) %all-gather.37.cloned.1.call-update) | async-done | bytes 1671184 | tf_op jit(solution)/shard_map/all_gather | solution.py:661
  694.5 90.3 %all-reduce.5.cloned.1.call-done = (bf16[96,2304]{0,1:T(8,128)(2,1)}, bf16[96,3,384]{2,1,0:T(4,128)(2,1)}, bf16[192,576]{1,0:T(8,128)(2,1)}, bf16[192,1536]{1,0:T(8,128)(2,1)}, bf16[192,1536]{1,0:T(8,128)(2,1)}) async-done(((bf16[96,2304]{0,1:T(8,128)(2,1)}, bf16[96,3,384]{2,1,0:T(4,128)(2,1)}, bf16[192,576]{1,0:T(8,128)(2,1)}, bf16[192,1536]{1,0:T(8,128)(2,1)}, bf16[192,1536]{1,0:T(8,128)(2,1)}), ...) | async-done | bytes 2064400 | tf_op jit(solution)/shard_map/psum | solution.py:618
  (307 shorter events, 154.3 us)
Async XLA Ops:
  7.2 46.8 %all-gather.29.cloned.1.call-start = ((), (), s32[]{:S(2)}) async-start(), calls=%async_computation.14 | async-start | bytes 3981312 | tf_op jit(solution)/shard_map/all_gather | solution.py:556
  10.4 58.5 %all-gather.27.cloned.1.call-start = ((), (), s32[]{:S(2)}) async-start(), calls=%async_computation.13 | async-start | bytes 1597440 | tf_op jit(solution)/shard_map/all_gather | solution.py:485
  18.7 94.3 %all-gather.21.cloned.1.call-start = ((), (), s32[]{:S(2)}) async-start(), calls=%async_computation.5 | async-start | bytes 1990656 | tf_op jit(solution)/shard_map/all_gather | solution.py:557
  19.9 107.8 %all-gather.33.cloned.1.call-start = ((), (), s32[]{:S(2)}) async-start(), calls=%async_computation.16 | async-start | bytes 2211840 | tf_op jit(solution)/shard_map/all_gather | solution.py:558
  20.7 130.6 %all-gather.31.cloned.1.call-start = ((), (), s32[]{:S(2)}) async-start(), calls=%async_computation.15 | async-start | bytes 1597440 | tf_op jit(solution)/shard_map/all_gather | solution.py:485
  20.7 24.4 %collective-permute-start = (bf16[2,112,384]{2,1,0:T(8,128)(2,1)S(1)}, bf16[2,112,384]{2,1,0:T(8,128)(2,1)S(1)}, u32[]{:S(2)}, u32[]{:S(2)}) collective-permute-start(bf16[2,112,384]{2,1,0:T(8,128)(2,1)S(1)} %copy-done.33), channel_id=1, source_target_pairs={{0,8},{1,9},{8,16},{9,17},{16,24},{17,25},{2,10},{3,11},{10,18},{1... | collective-permute-start | bytes 516104 | tf_op jit(solution)/shard_map/ppermute | solution.py:478
  25.7 19.5 %collective-permute-start.1 = (bf16[2,112,384]{2,1,0:T(8,128)(2,1)S(1)}, bf16[2,112,384]{2,1,0:T(8,128)(2,1)S(1)}, u32[]{:S(2)}, u32[]{:S(2)}) collective-permute-start(bf16[2,112,384]{2,1,0:T(8,128)(2,1)S(1)} %copy-done.33), channel_id=1, source_target_pairs={{0,9},{1,8},{8,17},{9,16},{16,25},{17,24},{2,11},{3,10},{10,19},{1... | collective-permute-start | bytes 516104 | tf_op jit(solution)/shard_map/ppermute | solution.py:478
  107.0 102.2 %all-gather.35.cloned.1.call-start = ((), (), s32[]{:S(2)}) async-start(), calls=%async_computation.17 | async-start | bytes 10616832 | tf_op jit(solution)/shard_map/all_gather | solution.py:559
  109.3 324.5 %reduce-scatter.8.cloned.1.call-start = ((), (), s32[]{:S(2)}) async-start(), calls=%async_computation.9 | async-start | bytes 1990656 | tf_op jit(solution)/shard_map/reduce_scatter | solution.py:617
  130.3 9.8 %collective-permute-start.2 = (bf16[2,112,384]{2,1,0:T(8,128)(2,1)S(1)}, bf16[2,112,384]{2,1,0:T(8,128)(2,1)S(1)}, u32[]{:S(2)}, u32[]{:S(2)}) collective-permute-start(bf16[2,112,384]{2,1,0:T(8,128)(2,1)S(1)} %copy-done.34), channel_id=1, source_target_pairs={{0,8},{1,9},{8,16},{9,17},{16,24},{17,25},{2,10},{3,11},{10,18},{1... | collective-permute-start | bytes 516104 | tf_op jit(solution)/shard_map/ppermute | solution.py:478
  272.5 163.1 %reduce-scatter.10.cloned.1.call-start = ((), (), s32[]{:S(2)}) async-start(), calls=%async_computation.10 | async-start | bytes 2211840 | tf_op jit(solution)/shard_map/reduce_scatter | solution.py:617
  281.7 167.6 %reduce-scatter.6.cloned.1.call-start = ((), (), s32[]{:S(2)}) async-start(), calls=%async_computation.8 | async-start | bytes 5308416 | tf_op jit(solution)/shard_map/reduce_scatter | solution.py:617
  284.9 17.0 %collective-permute-start.5 = (bf16[1,2,320,384]{3,2,1,0:T(8,128)(2,1)S(1)}, bf16[1,2,320,384]{3,2,1,0:T(8,128)(2,1)S(1)}, u32[]{:S(2)}, u32[]{:S(2)}) collective-permute-start(bf16[1,2,320,384]{3,2,1,0:T(8,128)(2,1)S(1)} %constant_dynamic-slice_fusion.3), channel_id=1, source_target_pairs={{0,4},{2,6},{4,0},{6,2},{1,5},{3,7},{5,1},{7,3},{8,12},{10,14},{12... | collective-permute-start | bytes 1474568 | tf_op jit(solution)/shard_map/ppermute | solution.py:500
  302.2 8.3 %collective-permute-start.6 = (bf16[2,112,384]{2,1,0:T(8,128)(2,1)S(1)}, bf16[2,112,384]{2,1,0:T(8,128)(2,1)S(1)}, u32[]{:S(2)}, u32[]{:S(2)}) collective-permute-start(bf16[2,112,384]{2,1,0:T(8,128)(2,1)S(1)} %get-tuple-element.179), channel_id=1, source_target_pairs={{8,0},{9,1},{16,8},{17,9},{24,16},{25,17},{10,2},{11,3},{18,10},{1... | collective-permute-start | bytes 516104 | tf_op jit(solution)/shard_map/ppermute | solution.py:478
  303.5 9.2 %collective-permute-start.7 = (bf16[2,112,384]{2,1,0:T(8,128)(2,1)S(1)}, bf16[2,112,384]{2,1,0:T(8,128)(2,1)S(1)}, u32[]{:S(2)}, u32[]{:S(2)}) collective-permute-start(bf16[2,112,384]{2,1,0:T(8,128)(2,1)S(1)} %get-tuple-element.180), channel_id=1, source_target_pairs={{8,1},{9,0},{16,9},{17,8},{24,17},{25,16},{10,3},{11,2},{18,11},{1... | collective-permute-start | bytes 516104 | tf_op jit(solution)/shard_map/ppermute | solution.py:478
  392.1 115.0 %reduce-scatter.12.cloned.1.call-start = ((), (), s32[]{:S(2)}) async-start(), calls=%async_computation.11 | async-start | bytes 5308416 | tf_op jit(solution)/shard_map/reduce_scatter | solution.py:617
  392.7 172.1 %reduce-scatter.14.cloned.1.call-start = ((), (), s32[]{:S(2)}) async-start(), calls=%async_computation.12 | async-start | bytes 5308416 | tf_op jit(solution)/shard_map/reduce_scatter | solution.py:617
  393.4 196.8 %all-gather.23.cloned.1.call-start = ((), (), s32[]{:S(2)}) async-start(), calls=%async_computation.6 | async-start | bytes 1843200 | tf_op jit(solution)/shard_map/all_gather | solution.py:672
  397.4 13.5 %collective-permute-start.9 = (bf16[1,2,320,384]{3,2,1,0:T(8,128)(2,1)S(1)}, bf16[1,2,320,384]{3,2,1,0:T(8,128)(2,1)S(1)}, u32[]{:S(2)}, u32[]{:S(2)}) collective-permute-start(bf16[1,2,320,384]{3,2,1,0:T(8,128)(2,1)S(1)} %constant_dynamic-slice_fusion.2), channel_id=1, source_target_pairs={{0,4},{2,6},{4,0},{6,2},{1,5},{3,7},{5,1},{7,3},{8,12},{10,14},{12... | collective-permute-start | bytes 1474568 | tf_op jit(solution)/shard_map/ppermute | solution.py:500
  400.2 228.2 %all-gather.25.cloned.1.call-start = ((), (), s32[]{:S(2)}) async-start(), calls=%async_computation.7 | async-start | bytes 3612672 | tf_op jit(solution)/shard_map/all_gather | solution.py:673
  411.1 9.4 %collective-permute-start.10 = (bf16[2,112,384]{2,1,0:T(8,128)(2,1)S(1)}, bf16[2,112,384]{2,1,0:T(8,128)(2,1)S(1)}, u32[]{:S(2)}, u32[]{:S(2)}) collective-permute-start(bf16[2,112,384]{2,1,0:T(8,128)(2,1)S(1)} %get-tuple-element.177), channel_id=1, source_target_pairs={{8,0},{9,1},{16,8},{17,9},{24,16},{25,17},{10,2},{11,3},{18,10},{1... | collective-permute-start | bytes 516104 | tf_op jit(solution)/shard_map/ppermute | solution.py:478
  412.4 11.6 %collective-permute-start.11 = (bf16[2,112,384]{2,1,0:T(8,128)(2,1)S(1)}, bf16[2,112,384]{2,1,0:T(8,128)(2,1)S(1)}, u32[]{:S(2)}, u32[]{:S(2)}) collective-permute-start(bf16[2,112,384]{2,1,0:T(8,128)(2,1)S(1)} %get-tuple-element.178), channel_id=1, source_target_pairs={{8,1},{9,0},{16,9},{17,8},{24,17},{25,16},{10,3},{11,2},{18,11},{1... | collective-permute-start | bytes 516104 | tf_op jit(solution)/shard_map/ppermute | solution.py:478
  430.5 256.6 %all-gather.37.cloned.1.call-start = ((), (), s32[]{:S(2)}) async-start(), calls=%async_computation.18 | async-start | bytes 1723392 | tf_op jit(solution)/shard_map/all_gather | solution.py:661
  433.8 351.0 %all-reduce.5.cloned.1.call-start = ((), (), s32[]{:S(2)}) async-start(), calls=%async_computation.19 | async-start | bytes 4620288 | tf_op jit(solution)/shard_map/psum | solution.py:618
  (39 other events, 360.1 us)
Sparse Core Ops, SparseCore 0:
  10.6 36.9 all-gather.28
  49.7 19.2 all-gather.26
  71.5 26.5 all-gather.20
  100.3 27.3 all-gather.32
  129.7 19.1 all-gather.30
  151.2 57.9 all-gather.34
  272.7 43.3 reduce-scatter.7
  319.4 40.1 reduce-scatter.9
  392.2 57.0 reduce-scatter.5
  453.2 53.8 reduce-scatter.11
  510.9 53.8 reduce-scatter.13
  566.8 23.3 all-gather.22
  591.7 36.6 all-gather.24
  631.7 55.3 all-gather.36
  690.2 94.5 all-reduce.4

commit v3 on v2

--- a/solution.py
+++ b/solution.py
@@ -288,7 +288,7 @@
 
 def second_mlp_kernel(
     comb_ref, pooled_ref, cot_ref, out_ref, skip_ref, up_ref, down_ref, ub_ref, vec_ref,
-    mixed_ref, dcomb_ref, dskip_ref, gup_ref, gdown_ref, gout_ref, gskip_ref, gub_ref, row_ref,
+    mixed_ref, dcomb_ref, dskip_ref, gmlp_ref, gout_ref, gskip_ref, gub_ref, row_ref,
     after_s, low_s, lowt_s, cott_s, sum_s, dlow_s,
 ):
     step = pl.program_id(0)
@@ -313,8 +313,10 @@
     dpre = dpre.astype(bf16)
     sum_s[...] += dot(hidden, down_ref[0], NT)
     dlow_s[...] += dot(dpre, up_ref[0], NT)
-    gup_ref[0] = dot(lowt_s[...], dpre).astype(bf16)
-    gdown_ref[0] = dot(cott_s[...], hidden).astype(bf16)
+    for n, grad in enumerate((dot(lowt_s[...], dpre), dot(cott_s[...], hidden))):
+        rows = gmlp_ref.shape[3]
+        for t in range(gmlp_ref.shape[1]):
+            gmlp_ref[0, t, n] = grad[t * rows:(t + 1) * rows].astype(bf16)
 
     @pl.when(step == pl.num_programs(0) - 1)
     def _():
@@ -349,10 +351,7 @@
         gout_s[...] = jnp.zeros_like(gout_s)
         gub_ref[...] = jnp.zeros_like(gub_ref)
 
-    memory = mem_ref[0, 0].astype(f32)
-    for d in range(1, mem_ref.shape[0]):
-        memory = memory + mem_ref[d, 0].astype(f32)
-    dpool = dskip_ref[0] + dq_ref[0] + own_ref[0].astype(f32) + exact_dot(unpair_ref[...], memory)
+    dpool = dskip_ref[0] + dq_ref[0] + own_ref[0] + exact_dot(unpair_ref[...], mem_ref[0])
     dnorm = exact_dot(unpool_ref[...], dpool)
     unit, inverse = norm(middle_ref[0])
     grad = norm_back(unit, inverse, vec_ref[2:3, :], dnorm)
@@ -389,10 +388,7 @@
 
 
 def last_back_kernel(x_ref, res_ref, dx_ref, own_ref, mem_ref, vec_ref, unpool_ref, unpair_ref, grad_ref, row_ref):
-    memory = mem_ref[0, 0].astype(f32)
-    for d in range(1, mem_ref.shape[0]):
-        memory = memory + mem_ref[d, 0].astype(f32)
-    dpool = own_ref[0].astype(f32) + exact_dot(unpair_ref[...], memory)
+    dpool = own_ref[0] + exact_dot(unpair_ref[...], mem_ref[0])
     dnorm = dx_ref[0] + exact_dot(unpool_ref[...], dpool)
     unit, inverse = norm(x_ref[0].astype(f32))
     grad_ref[0] = (norm_back(unit, inverse, vec_ref[0:1, :], dnorm) + res_ref[0]).astype(bf16)
@@ -462,55 +458,322 @@
     )
 
 
-def grouped(pairs_of):
+MESH = pl.DeviceIdType.MESH
+
+
+def places():
+    tok, toks = lax.axis_index("tok"), lax.axis_size("tok")
+    return lax.axis_index("clip"), lax.axis_index("head"), tok // 2, tok % 2, toks // 2
+
+
+def greet(copies_to_me, i_copy_to):
+    barrier = pltpu.get_barrier_semaphore()
+    for device, condition in copies_to_me:
+        if condition is None:
+            pl.semaphore_signal(barrier, inc=1, device_id=device, device_id_type=MESH)
+        else:
+            @pl.when(condition)
+            def _():
+                pl.semaphore_signal(barrier, inc=1, device_id=device, device_id_type=MESH)
+    count = 0
+    for _, condition in i_copy_to:
+        count = count + (1 if condition is None else jnp.where(condition, 1, 0))
+    pl.semaphore_wait(barrier, count)
+
+
+def remote(src, dst, send, recv, device):
+    return pltpu.make_async_remote_copy(
+        src_ref=src, dst_ref=dst, send_sem=send, recv_sem=recv, device_id=device, device_id_type=MESH
+    )
+
+
+def rem(a, n):
+    return lax.rem(a + n, n)
+
+
+def share_kernel(pooled_ref, mean_ref, pick_ref, own_ref, mem_ref, got_s, pick_s, local_sem, own_send, own_recv, mem_send, mem_recv,
+                 pass_send, pass_recv, clip_send, clip_recv):
+    clip, head, chip, core, chips = places()
     clips, heads = lax.axis_size("clip"), lax.axis_size("head")
-    return [
-        (c * heads + h, c2 * heads + h2)
-        for c in range(clips)
-        for h in range(heads)
-        for c2, h2 in [pairs_of(c, h)]
-        if 0 <= c2 < clips
+    share = pooled_ref.shape[0]
+    here = 2 * chip + core
+    partner = {"tok": 2 * chip + 1 - core}
+    across = [{"tok": 2 * rem(chip + k, chips) + core} for k in range(1, chips)]
+    heads_of = lambda by, sign: [{"clip": clip + by, "head": rem(head + sign * d, heads)} for d in range(heads)]
+    last, begun = clip < clips - 1, clip > 0
+    to = [(partner, None)] + [(d, None) for d in across] + [(d, last) for d in heads_of(1, 1)]
+    fro = [(partner, None)] + [(d, None) for d in across] + [(d, begun) for d in heads_of(-1, -1)]
+    greet(fro, to)
+
+    def spread(src, out, send, recv):
+        copies = [remote(src, out.at[here], send.at[0], recv.at[0], partner)]
+        copies += [remote(src, out.at[here], send.at[k + 1], recv.at[k + 1], across[k]) for k in range(chips - 1)]
+        return copies
+
+    def passed(out, k, row):
+        block = 2 * rem(chip - k, chips) + core
+        return remote(out.at[block], out.at[block], pass_send.at[row, k - 1], pass_recv.at[row, k - 1], partner)
+
+    clip_copies = [remote(mean_ref, got_s.at[d], clip_send.at[d], clip_recv.at[d], device) for d, device in enumerate(heads_of(1, 1))]
+
+    @pl.when(last)
+    def _():
+        for copy in clip_copies:
+            copy.start()
+
+    own_copies = spread(pooled_ref, own_ref, own_send, own_recv)
+    for copy in own_copies[1:] + own_copies[:1]:
+        copy.start()
+    own_local = pltpu.make_async_copy(pooled_ref, own_ref.at[here], local_sem.at[0])
+    own_local.start()
+
+    @pl.when(begun)
+    def _():
+        for copy in clip_copies:
+            copy.wait_recv()
+        for m in range(share):
+            total = None
+            for d in range(heads):
+                for s in range(share):
+                    piece = got_s[d, s].astype(f32) * pick_ref[m, d * share + s]
+                    total = piece if total is None else total + piece
+            pick_s[m] = total.astype(bf16)
+
+    @pl.when(jnp.logical_not(begun))
+    def _():
+        pick_s[...] = jnp.zeros_like(pick_s)
+
+    mem_copies = spread(pick_s, mem_ref, mem_send, mem_recv)
+    for copy in mem_copies[1:] + mem_copies[:1]:
+        copy.start()
+    mem_local = pltpu.make_async_copy(pick_s, mem_ref.at[here], local_sem.at[1])
+    mem_local.start()
+    forwards = []
+    for row, (copies, out) in enumerate(((own_copies, own_ref), (mem_copies, mem_ref))):
+        for k in range(1, chips):
+            copies[k].wait_recv()
+            forwards.append(passed(out, k, row))
+            forwards[-1].start()
+    own_copies[0].wait_recv()
+    mem_copies[0].wait_recv()
+    for copy in forwards:
+        copy.wait_recv()
+    for copy in own_copies + mem_copies + forwards:
+        copy.wait_send()
+    own_local.wait()
+    mem_local.wait()
+
+    @pl.when(last)
+    def _():
+        for copy in clip_copies:
+            copy.wait_send()
+
+
+ANY = pl.BlockSpec(memory_space=pl.ANY)
+INVMEM = pl.BlockSpec(memory_space=pltpu.VMEM)
+INSMEM = pl.BlockSpec(memory_space=pltpu.SMEM)
+
+
+def dma(*dims):
+    return pltpu.SemaphoreType.DMA(dims)
+
+
+def share_pooled(pooled, mean, pick, number):
+    toks, heads = lax.axis_size("tok"), lax.axis_size("head")
+    chips = toks // 2
+    return pl.pallas_call(
+        share_kernel,
+        in_specs=[INVMEM, INVMEM, INSMEM],
+        out_specs=[ANY, ANY],
+        out_shape=[shape((toks,) + pooled.shape, bf16), shape((toks,) + mean.shape, bf16)],
+        scratch_shapes=[
+            pltpu.VMEM((heads,) + mean.shape, bf16), pltpu.VMEM(mean.shape, bf16), dma(2),
+            dma(chips), dma(chips), dma(chips), dma(chips),
+            dma(2, max(chips - 1, 1)), dma(2, max(chips - 1, 1)), dma(heads), dma(heads),
+        ],
+        compiler_params=pltpu.CompilerParams(collective_id=number, has_side_effects=True, vmem_limit_bytes=VMEM_CAP),
+        name="share_pooled",
+    )(pooled, mean, pick)
+
+
+def give_back_kernel(part_ref, pick_ref, own_ref, back_ref, mine_s, core_s, sum_s, chip_s, route_s, got_s,
+                     local_sem, core_send, core_recv, mem_send, mem_recv, own_send, own_recv, clip_send, clip_recv):
+    clip, head, chip, core, chips = places()
+    clips, heads = lax.axis_size("clip"), lax.axis_size("head")
+    share, rows = own_ref.shape[0], own_ref.shape[1]
+    partner = {"tok": 2 * chip + 1 - core}
+    across = [{"tok": 2 * rem(chip + k, chips) + core} for k in range(1, chips)]
+    heads_of = lambda by, sign: [{"clip": clip + by, "head": rem(head + sign * d, heads)} for d in range(heads)]
+    last, begun = clip < clips - 1, clip > 0
+    to = [(partner, None)] + [(d, None) for d in across] + [(d, begun) for d in heads_of(-1, -1)]
+    fro = [(partner, None)] + [(d, None) for d in across] + [(d, last) for d in heads_of(1, 1)]
+    greet(fro, to)
+
+    order = [rem(chip + k, chips) for k in list(range(1, chips)) + [0]]
+    core_copies, local_copies = [], []
+    for n, other in enumerate(order):
+        core_copies.append(remote(part_ref.at[2 * other + 1 - core], core_s.at[n], core_send.at[n], core_recv.at[n], partner))
+        core_copies[-1].start()
+    for n, other in enumerate(order):
+        local_copies.append(pltpu.make_async_copy(part_ref.at[2 * other + core], mine_s.at[n], local_sem.at[n]))
+        local_copies[-1].start()
+    mem_copies, own_copies = [], []
+    for n in range(chips):
+        local_copies[n].wait()
+        core_copies[n].wait_recv()
+        if n == chips - 1:
+            break
+        sum_s[n] = (mine_s[n].astype(f32) + core_s[n].astype(f32)).astype(bf16)
+        low, high = pl.ds(0, rows), pl.ds(rows, sum_s.shape[2] - rows)
+        mem_copies.append(remote(sum_s.at[n, :, high, :], chip_s.at[n, :, high, :], mem_send.at[n], mem_recv.at[n], across[n]))
+        mem_copies[-1].start()
+        own_copies.append(remote(sum_s.at[n, :, low, :], chip_s.at[n, :, low, :], own_send.at[n], own_recv.at[n], across[n]))
+        own_copies[-1].start()
+    base = chips - 1
+    for copy in mem_copies:
+        copy.wait_recv()
+    memory = []
+    for m in range(share):
+        total = mine_s[base, m, rows:].astype(f32) + core_s[base, m, rows:].astype(f32)
+        for n in range(chips - 1):
+            total = total + chip_s[n, m, rows:].astype(f32)
+        memory.append(total)
+    clip_copies = [
+        remote(route_s.at[d], got_s.at[d], clip_send.at[d], clip_recv.at[d], device) for d, device in enumerate(heads_of(-1, -1))
     ]
 
-
-def to_clip(pieces, by, heads):
-    return [
-        lax.ppermute(pieces[d], ("clip", "head"), grouped(lambda c, h, d=d: (c + by, (h + d) % heads)))
-        for d in range(heads)
-    ]
-
-
-def share_pooled(pooled, mean, slots, heads):
-    received = to_clip([mean] * heads, 1, heads)
-    own = lax.all_gather(pooled, "tok")
-    flat = jnp.stack(received).reshape((-1,) + mean.shape[1:])
-    chosen = jnp.stack([lax.dynamic_index_in_dim(flat, slot, 0, keepdims=False) for slot in slots])
-    return own, lax.all_gather(chosen, "tok")
-
-
-def halve_over_tok(partial):
-    size = lax.axis_size("tok")
-    index = lax.axis_index("tok")
-    bit = 1
-    while bit < size:
-        mine = (index // bit) % 2
-        paired = partial.reshape((partial.shape[0] // 2, 2) + partial.shape[1:])
-        keep = lax.dynamic_index_in_dim(paired, mine, 1, keepdims=False)
-        give = lax.dynamic_index_in_dim(paired, 1 - mine, 1, keepdims=False)
-        got = lax.ppermute(give, "tok", [(i, i ^ bit) for i in range(size)])
-        partial = (keep.astype(f32) + got.astype(f32)).astype(bf16)
-        bit *= 2
-    return partial[0]
-
-
-def return_pooled(dpool, own_rows, slots, heads):
-    total = halve_over_tok(dpool)
-    own, mem = total[:, :own_rows], total[:, own_rows:]
-    routed = jnp.zeros((heads * mem.shape[0],) + mem.shape[1:], bf16)
-    for m, slot in enumerate(slots):
-        routed = lax.dynamic_update_index_in_dim(routed, mem[m], slot, 0)
-    routed = routed.reshape((heads,) + mem.shape)
-    return own, jnp.stack(to_clip([routed[(heads - d) % heads] for d in range(heads)], -1, heads))
+    @pl.when(begun)
+    def _():
+        for d in range(heads):
+            for s in range(share):
+                total = None
+                for m in range(share):
+                    piece = memory[m] * pick_ref[m, d * share + s]
+                    total = piece if total is None else total + piece
+                route_s[d, s] = total.astype(bf16)
+            clip_copies[d].start()
+
+    for copy in own_copies:
+        copy.wait_recv()
+    for m in range(share):
+        total = mine_s[base, m, :rows].astype(f32) + core_s[base, m, :rows].astype(f32)
+        for n in range(chips - 1):
+            total = total + chip_s[n, m, :rows].astype(f32)
+        own_ref[m] = total
+
+    @pl.when(last)
+    def _():
+        for copy in clip_copies:
+            copy.wait_recv()
+        total = got_s[0].astype(f32)
+        for d in range(1, heads):
+            total = total + got_s[d].astype(f32)
+        back_ref[...] = total
+
+    @pl.when(jnp.logical_not(last))
+    def _():
+        back_ref[...] = jnp.zeros_like(back_ref)
+
+    for copy in core_copies + mem_copies + own_copies:
+        copy.wait_send()
+
+    @pl.when(begun)
+    def _():
+        for copy in clip_copies:
+            copy.wait_send()
+
+
+def give_back(part, pick, own_rows, number):
+    toks, heads = lax.axis_size("tok"), lax.axis_size("head")
+    chips, few = toks // 2, max(toks // 2 - 1, 1)
+    share, rows, d = part.shape[1:]
+    return pl.pallas_call(
+        give_back_kernel,
+        in_specs=[ANY, INSMEM],
+        out_specs=[INVMEM, INVMEM],
+        out_shape=[shape((share, own_rows, d), f32), shape((share, rows - own_rows, d), f32)],
+        scratch_shapes=[
+            pltpu.VMEM((chips,) + part.shape[1:], bf16), pltpu.VMEM((chips,) + part.shape[1:], bf16),
+            pltpu.VMEM((few,) + part.shape[1:], bf16), pltpu.VMEM((few,) + part.shape[1:], bf16),
+            pltpu.VMEM((heads, share, rows - own_rows, d), bf16), pltpu.VMEM((heads, share, rows - own_rows, d), bf16),
+            dma(chips), dma(chips), dma(chips), dma(few), dma(few), dma(few), dma(few), dma(heads), dma(heads),
+        ],
+        compiler_params=pltpu.CompilerParams(collective_id=number, has_side_effects=True, vmem_limit_bytes=VMEM_CAP),
+        name="give_back",
+    )(part, pick)
+
+
+def finish_kernel(half_ref, small_ref, all_ref, total_ref, sum_s, core_s, chip_s, head_s, clip_s,
+                  local_sem, half_send, half_recv, core_send, core_recv, chip_send, chip_recv, head_send, head_recv, clip_send, clip_recv):
+    clip, head, chip, core, chips = places()
+    clips, heads = lax.axis_size("clip"), lax.axis_size("head")
+    partner = {"tok": 2 * chip + 1 - core}
+    across = [{"tok": 2 * rem(chip + k, chips) + core} for k in range(1, chips)]
+    beside = [{"head": rem(head + k, heads)} for k in range(1, heads)]
+    along = [{"clip": rem(clip + k, clips)} for k in range(1, clips)]
+    peers = [(d, None) for d in [partner] + across + beside + along]
+    greet(peers, peers)
+    halves = [remote(half_ref, all_ref.at[head], half_send.at[k], half_recv.at[k], d) for k, d in enumerate(beside)]
+    for copy in halves:
+        copy.start()
+    local_half = pltpu.make_async_copy(half_ref, all_ref.at[head], local_sem.at[0])
+    local_half.start()
+    first = remote(small_ref, core_s, core_send.at[0], core_recv.at[0], partner)
+    first.start()
+    first.wait_recv()
+    sum_s[0] = small_ref[...] + core_s[...]
+    waits = [first]
+    stages = ((across, chip, chips, chip_s, chip_send, chip_recv), (beside, head, heads, head_s, head_send, head_recv),
+              (along, clip, clips, clip_s, clip_send, clip_recv))
+    for n, (devices, index, size, slots, send, recv) in enumerate(stages):
+        copies = [remote(sum_s.at[n], slots.at[k], send.at[k], recv.at[k], d) for k, d in enumerate(devices)]
+        for copy in copies:
+            copy.start()
+        for copy in copies:
+            copy.wait_recv()
+        total = None
+        for i in range(size):
+            piece = jnp.zeros_like(sum_s[n])
+            piece = jnp.where(index == i, sum_s[n], piece)
+            for k in range(size - 1):
+                piece = jnp.where(rem(index - k - 1, size) == i, slots[k], piece)
+            total = piece if total is None else total + piece
+        if n + 1 < len(stages):
+            sum_s[n + 1] = total
+        else:
+            total_ref[...] = total
+        waits += copies
+    for copy in halves:
+        copy.wait_recv()
+    for copy in waits + halves:
+        copy.wait_send()
+    local_half.wait()
+
+
+def finish(half, small, number):
+    toks, heads, clips = lax.axis_size("tok"), lax.axis_size("head"), lax.axis_size("clip")
+    counts = [max(n, 1) for n in (toks // 2 - 1, heads - 1, clips - 1)]
+    return pl.pallas_call(
+        finish_kernel,
+        in_specs=[ANY, INVMEM],
+        out_specs=[ANY, INVMEM],
+        out_shape=[shape((heads,) + half.shape, half.dtype), shape(small.shape, f32)],
+        scratch_shapes=[pltpu.VMEM((3,) + small.shape, f32), pltpu.VMEM(small.shape, f32)]
+        + [pltpu.VMEM((n,) + small.shape, f32) for n in counts]
+        + [dma(1), dma(counts[1]), dma(counts[1]), dma(1), dma(1)] + [dma(n) for n in counts for _ in range(2)],
+        compiler_params=pltpu.CompilerParams(collective_id=number, has_side_effects=True, vmem_limit_bytes=VMEM_CAP),
+        name="finish",
+    )(half, small)
+
+
+def from_heads(piece, heads):
+    head = lax.axis_index("head")
+    out = jnp.zeros((heads,) + piece.shape, piece.dtype)
+    out = lax.dynamic_update_index_in_dim(out, piece, head, 0)
+    for d in range(1, heads):
+        got = lax.ppermute(piece, "head", [(i, (i + d) % heads) for i in range(heads)])
+        out = lax.dynamic_update_index_in_dim(out, got, (head - d + heads) % heads, 0)
+    return out.reshape((-1,) + piece.shape[1:])
 
 
 def padded_rows(*rows):
@@ -538,16 +801,18 @@
     cot = lax.dynamic_slice_in_dim(cotangent[0], first, share, 0).reshape(share, pooled_tokens, d2)
     cot = jnp.pad(cot, ((0, 0), (0, own_rows - pooled_tokens), (0, 0))).reshape(rows2, d2)
 
-    slots, masks = [], []
+    picks, masks = [], []
     row_own = jnp.where(jnp.arange(own_rows) < pooled_tokens, 0.0, NEG)
     row_mem = jnp.arange(mem_rows) < frames // 2 * POOLED
     for m in range(share):
         source = lax.dynamic_index_in_dim(assign[0], first + m, 0, keepdims=False)
         flag = lax.dynamic_index_in_dim(resets[0], first + m, 0, keepdims=False)
-        slots.append(((head - source // share + heads) % heads) * share + source % share)
+        slot = ((head - source // share + heads) % heads) * share + source % share
+        picks.append((jnp.arange(heads * share) == slot).astype(f32))
         has = (flag == 0) & (lax.axis_index("clip") > 0)
         masks.append(jnp.concatenate([jnp.tile(row_own, toks), jnp.tile(jnp.where(row_mem & has, 0.0, NEG), toks)]))
     mask = jnp.stack(masks)[:, None, :].astype(f32)
+    pick = jnp.stack(picks)
 
     group = ("head", "tok")
     fa, ha = w_up_a.shape[1], w_out_a.shape[1]
@@ -555,8 +820,7 @@
     pack_a = jnp.concatenate([w_up_a, w_down_a, w_qkv_a.reshape(w_qkv_a.shape[0], -1), w_out_a], axis=1)
     all_a = lax.all_gather(pack_a, group).reshape(heads, d1, -1)
     all_q = lax.all_gather(w_qkv_b.reshape(w_qkv_b.shape[0], -1), group).reshape(heads, d1, -1)
-    all_o = lax.all_gather(jnp.concatenate([w_out_b, w_skip_b], axis=1), group).reshape(heads, d2, -1)
-    all_b = lax.all_gather(jnp.concatenate([w_up_b, w_down_b], axis=1), group).reshape(heads, d2, -1)
+    all_b = lax.all_gather(jnp.concatenate([w_up_b, w_down_b, w_out_b, w_skip_b], axis=1), group).reshape(heads, d2, -1)
     flat = jnp.concatenate([qv_bias_a.reshape(-1), qv_bias_b.reshape(-1), up_bias_a, up_bias_b])
     flat = lax.all_gather(flat, "head")
     qv_a = flat[:, :2 * ha].reshape(heads, 2, ha).transpose(1, 0, 2).reshape(2, d1)
@@ -571,7 +835,7 @@
     qkv_a = jnp.concatenate([lanes(all_a, 2 * fa + i * ha, ha) for i in range(3)], axis=1)
     out_a = lanes(all_a, 2 * fa + 3 * ha, ha)
     qkv_b = jnp.concatenate([lanes(all_q, i * hb, hb) for i in range(3)], axis=1)
-    out_b, skip_b = lanes(all_o, 0, hb), lanes(all_o, hb, hs)
+    out_b, skip_b = lanes(all_b, 2 * fb, hb), lanes(all_b, 2 * fb + hb, hs)
 
     low1, pooled1, mean1 = call(
         norm_pool_kernel, share,
@@ -579,7 +843,7 @@
         [(shape((share, tokens, d1), bf16), 0), (shape((share, own_rows, d1), bf16), 0), (shape((share, mem_rows, d1), bf16), 0)],
         name="norm_pool",
     )
-    own1, mem1 = share_pooled(pooled1, mean1, slots, heads)
+    own1, mem1 = share_pooled(pooled1, mean1, pick, 0)
     comb1, lse1 = attend(low1, own1, mem1, qkv_a, qv_a, mask, d1)
     after1, middle, pooled3, mean3 = call(
         first_mlp_kernel, share,
@@ -591,13 +855,13 @@
         name="first_mlp",
     )
 
-    own2, mem2 = share_pooled(pooled3, mean3, slots, heads)
+    own2, mem2 = share_pooled(pooled3, mean3, pick, 1)
     comb2, lse2 = attend(pooled3, own2, mem2, qkv_b, qv_b, mask, d2)
     chunk = 768
     per_head = fb // chunk
     steps = heads * per_head
     rows_spec = pl.BlockSpec((1, d2, chunk), lambda j: (j // per_head, 0, j % per_head))
-    mixed, dcomb2, dskip, g_up_b, g_down_b, g_out_b, g_skip_b, g_ub_b, rows_b = call(
+    mixed, dcomb2, dskip, g_mlp_b, g_out_b, g_skip_b, g_ub_b, rows_b = call(
         second_mlp_kernel, steps,
         [(comb2.reshape(rows2, d2), None), (pooled3.reshape(rows2, d1), None), (cot, None), (out_b, None), (skip_b, None),
          (all_b, rows_spec),
@@ -605,7 +869,8 @@
          (ub_b, pl.BlockSpec((1, chunk), lambda j: (0, j))),
          (padded_rows(shifts_b[0], gains_b, shifts_b[1], shifts_b[2]), None)],
         [(shape((rows2, d2), bf16), None), (shape((rows2, d2), bf16), None), (shape((rows2, d1), f32), None),
-         (shape((heads, d2, fb), bf16), rows_spec), (shape((heads, d2, fb), bf16), rows_spec),
+         (shape((heads, toks, 2, d2 // toks, fb), bf16),
+          pl.BlockSpec((1, toks, 2, d2 // toks, chunk), lambda j: (j // per_head, 0, 0, 0, j % per_head))),
          (shape((d2, d2), bf16), None), (shape((d2, d1), bf16), None),
          (shape((1, heads * fb), f32), pl.BlockSpec((1, chunk), lambda j: (0, j))), (shape((8, d2), f32), None)],
         [((rows2, d2), f32), ((rows2, d2), bf16), ((d2, rows2), bf16), ((d2, rows2), bf16), ((rows2, d2), f32), ((rows2, d2), f32)],
@@ -613,20 +878,20 @@
     )
 
     def reduce_grad(blocks):
-        blocks = blocks.reshape((heads * toks, -1) + blocks.shape[2:])
-        shard = lax.psum_scatter(blocks, group, scatter_dimension=0, tiled=False)
-        return lax.psum(shard, "clip").astype(f32)
+        return lax.psum(lax.psum_scatter(blocks, group, scatter_dimension=0, tiled=False), "clip")
+
+    sum_mlp_b = reduce_grad(g_mlp_b.reshape((heads * toks,) + g_mlp_b.shape[2:]))
 
     def by_head(grad, width):
         return grad.reshape(grad.shape[0], heads, width).transpose(1, 0, 2)
 
     dcomb2 = dcomb2.reshape(share, own_rows, d2)
     dq2, dpool2, g_qkv_b, rows_qv_b = attend_back(pooled3, dcomb2, own2, mem2, qkv_b, qv_b, mask, lse2)
-    own_back2, mem_back2 = return_pooled(dpool2, own_rows, slots, heads)
+    own_back2, mem_back2 = give_back(dpool2, pick, own_rows, 2)
 
     res1, dcomb1, g_up_a, g_down_a, g_out_a, g_ub_a, rows_a = call(
         first_back_kernel, share,
-        [(middle, 0), (after1, 0), (comb1, 0), (dskip.reshape(share, own_rows, d1), 0), (dq2, 0), (own_back2, 0), (mem_back2, 1),
+        [(middle, 0), (after1, 0), (comb1, 0), (dskip.reshape(share, own_rows, d1), 0), (dq2, 0), (own_back2, 0), (mem_back2, 0),
          (out_a, None), (up_a, None), (down_a, None), (ub_a, None),
          (padded_rows(gains_a[1], shifts_a[2], gains_a[2]), None), (unpooling, None), (unpairing, None)],
         [(shape((share, tokens, d1), f32), 0), (shape((share, tokens, d1), bf16), 0),
@@ -636,29 +901,37 @@
         name="first_back",
     )
     dx1, dpool1, g_qkv_a, rows_qv_a = attend_back(low1, dcomb1, own1, mem1, qkv_a, qv_a, mask, lse1)
-    own_back1, mem_back1 = return_pooled(dpool1, own_rows, slots, heads)
+    own_back1, mem_back1 = give_back(dpool1, pick, own_rows, 3)
     stream_grad, rows_last = call(
         last_back_kernel, share,
-        [(stream, 0), (res1, 0), (dx1, 0), (own_back1, 0), (mem_back1, 1), (padded_rows(gains_a[0]), None),
+        [(stream, 0), (res1, 0), (dx1, 0), (own_back1, 0), (mem_back1, 0), (padded_rows(gains_a[0]), None),
          (unpooling, None), (unpairing, None)],
         [(shape((share, tokens, d1), bf16), 0), (shape((8, d1), f32), None)],
         name="last_back",
     )
 
-    sum_up_b, sum_down_b = reduce_grad(g_up_b), reduce_grad(g_down_b)
-    grad_q = jnp.concatenate([by_head(g_qkv_b[:, i * d2:(i + 1) * d2], hb) for i in range(3)], axis=2)
-    grad_o = jnp.concatenate([by_head(g_out_b, hb), by_head(g_skip_b, hs)], axis=2)
-    sum_q, sum_o = reduce_grad(grad_q), reduce_grad(grad_o)
-    grad_a = jnp.concatenate(
-        [g_up_a, g_down_a] + [by_head(g_qkv_a[:, i * d1:(i + 1) * d1], ha) for i in range(3)] + [by_head(g_out_a, ha)], axis=2)
-    sum_a = reduce_grad(grad_a)
+    def by_owner(grad):
+        return grad.reshape((heads * toks, -1) + grad.shape[2:])
+
+    grad_q = by_owner(jnp.concatenate([by_head(g_qkv_b[:, i * d2:(i + 1) * d2], hb) for i in range(3)], axis=2))
+    grad_o = by_owner(jnp.concatenate([by_head(g_out_b, hb), by_head(g_skip_b, hs)], axis=2))
+    grad_a = by_owner(jnp.concatenate(
+        [g_up_a, g_down_a] + [by_head(g_qkv_a[:, i * d1:(i + 1) * d1], ha) for i in range(3)] + [by_head(g_out_a, ha)], axis=2))
+    rest = jnp.concatenate([grad_a, grad_q], axis=2)
+    rest, grad_o, sum_mlp_b = lax.optimization_barrier((rest, grad_o, sum_mlp_b))
+    sum_rest, sum_o = reduce_grad(rest).astype(f32), reduce_grad(grad_o).astype(f32)
+    sum_mlp_b = sum_mlp_b.astype(f32)
+    sum_a, sum_q = sum_rest[:, :grad_a.shape[2]], sum_rest[:, grad_a.shape[2]:]
 
     small = [
         jnp.stack([rows_last[0], rows_a[3], rows_a[0]]), rows_b[3],
         jnp.stack([rows_last[1], rows_a[5], rows_a[4], rows_a[2], rows_a[1]]),
         rows_b[:3], rows_qv_a[:2], rows_qv_b[:2], g_ub_a, g_ub_b,
     ]
-    flat = lax.all_gather(jnp.concatenate([piece.reshape(-1) for piece in small]), ("clip", "tok", "head")).sum(axis=0)
+    flat = jnp.concatenate([piece.reshape(-1) for piece in small])
+    flat = jnp.pad(flat, (0, -flat.size % 1024)).reshape(-1, 128)
+    stream_all, flat = finish(stream_grad, flat, 4)
+    flat = flat.reshape(-1)
     pieces, at = [], 0
     for piece in small:
         pieces.append(flat[at:at + piece.size].reshape(piece.shape))
@@ -669,8 +942,7 @@
         return lax.dynamic_slice_in_dim(piece, head * width, width, axis)
 
     mixed = mixed.reshape(share, own_rows, d2)[:, :pooled_tokens]
-    mixed_all = lax.all_gather(mixed, "head", axis=0, tiled=True)
-    stream_all = lax.all_gather(stream_grad, "head", axis=0, tiled=True)
+    mixed_all = from_heads(mixed, heads)
     return (
         mixed_all.reshape(cotangent.shape),
         stream_all.astype(f32).reshape(clips_in.shape),
@@ -681,8 +953,8 @@
         sum_q.reshape(w_qkv_b.shape),
         sum_o[:, :hb],
         sum_o[:, hb:],
-        sum_up_b,
-        sum_down_b,
+        sum_mlp_b[0],
+        sum_mlp_b[1],
         pieces[0], pieces[1], pieces[2], pieces[3],
         mine(pieces[4], 1), mine(pieces[5], 1), mine(pieces[6].reshape(-1), 0), mine(pieces[7].reshape(-1), 0),
     )

time: 806 us -> 597 us (0.74)
  waiting for transfers between devices: 434 us -> 134 us
  Pallas kernels: 185 us -> 327 us
  starting transfers between devices: 26.6 us -> 1.89 us
  blocking collectives: 22.8 us -> 5.32 us
    all_gather x7 -> x1, waiting for transfers between devices: 167 us -> 0.01 us  [local(): lax.all_gather(jnp.concatenate([w_up_b, w_down_b, w_out_b, w_skip_b], axi...]
    pallas_call x0 -> x5, Pallas kernels: none -> 141 us  [the longest x2 49.8 us: share_pooled(): pl.pallas_call(share_kernel, in_specs=[INVMEM, INVMEM, INSMEM], out_specs...]
    reduce_scatter x5 -> x3, waiting for transfers between devices: 129 us -> 27.9 us  [reduce_grad(): lax.psum_scatter(blocks, group, scatter_dimension=0, tiled=False)]
    ppermute x12 -> x1, waiting for transfers between devices: 46.1 us -> 0.01 us  [from_heads(): lax.ppermute(piece, 'head', [(i, (i + d) % heads) for i in range(heads)])]
    ppermute x12 -> x1, starting transfers between devices: 26 us -> 1.56 us  [from_heads(): lax.ppermute(piece, 'head', [(i, (i + d) % heads) for i in range(heads)])]
    all_gather x2 -> x0, blocking collectives: 18.1 us -> none  [share_pooled(): return (own, lax.all_gather(chosen, 'tok'))]
    psum x1 -> x2, waiting for transfers between devices: 90.3 us -> 97.6 us  [reduce_grad(): lax.psum(lax.psum_scatter(blocks, group, scatter_dimension=0, tiled=False...]
    unnamed x97 -> x96, local copies, waits for them, and re-layouts: 24.6 us -> 23.7 us
  transfers between devices with their start and end apart: 27 -> 9, of which waited for: 18 -> 4; matrix products, arithmetic and copies ran while one was open for 11% -> 15% of each run, Pallas kernels for 16% -> 51%
where the time goes in v3:
time: 597 us; the launch traced here: 592 us
  Pallas kernels  327 us (55%)
  waiting for transfers between devices  134 us (22%)
  local copies, waits for them, and re-layouts  86.5 us (14%)
  between operations  22.1 us (4%)
  other arithmetic  15.3 us (3%)
    pallas_call x9, Pallas kernels, call(): pl.pallas_call(kernel, grid=(steps,), in_specs=[spec(a, how) for a, how i...  186 us
    psum x2, waiting for transfers between devices, reduce_grad(): lax.psum(lax.psum_scatter(blocks, group, scatter_dimension=0, tiled=False...  97.6 us
    pallas_call x2, Pallas kernels, share_pooled(): pl.pallas_call(share_kernel, in_specs=[INVMEM, INVMEM, INSMEM], out_specs...  49.8 us
    pallas_call x2, Pallas kernels, give_back(): pl.pallas_call(give_back_kernel, in_specs=[ANY, INSMEM], out_specs=[INVME...  49.8 us
    pallas_call x1, Pallas kernels, finish(): pl.pallas_call(finish_kernel, in_specs=[ANY, INVMEM], out_specs=[ANY, INV...  41.2 us
    reduce_scatter x3, waiting for transfers between devices, reduce_grad(): lax.psum_scatter(blocks, group, scatter_dimension=0, tiled=False)  27.9 us
    unnamed x96, local copies, waits for them, and re-layouts  23.7 us
  transfers between devices with their start and end apart: 9, of which 4 were waited for; matrix products, arithmetic and copies ran while one was open for 15% of the time, Pallas kernels for 51%

profile of v3, /device:TPU:0, one launch (start us, length us, event | category | flops | bytes accessed | tf_op | source)
XLA Modules:
  0.0 591.8 jit_solution(7777449452018250879)
XLA Ops:
  24.8 5.3 all-gather.3
  35.2 4.3 norm_pool.1
  40.1 21.8 %share_pooled.2 = (bf16[4,2,208,384]{3,2,1,0:T(8,128)(2,1)}, bf16[4,2,112,384]{3,2,1,0:T(8,128)(2,1)}) custom-call(bf16[2,208,384]{2,1,0:T(8,128)(2,1)} %get-tuple-element.69.pooled_ref, bf16[2,112,384]{2,1,0:T(8,128)(2,1)} %get-tuple-element.70.mean_ref, f32[2,4]{1,0:T(2,128)} %add_convert_fusion.pick_ref), custom_call_target="tpu_custom_call" | custom-call | tf_op jit(solution)/shard_map/share_pooled/pallas_call | solution.py:584
  71.1 7.7 %all-gather.10.cloned.1.call-done = bf16[768,2304]{1,0:T(8,128)(2,1)} async-done(((bf16[96,2304]{1,0:T(8,128)(2,1)}), bf16[768,2304]{1,0:T(8,128)(2,1)}) %all-gather.10.cloned.1.call-update) | async-done | bytes 3538960 | tf_op jit(solution)/shard_map/all_gather | solution.py:821
  81.9 20.9 %attend.2 = (bf16[2,784,384]{2,1,0:T(8,128)(2,1)}, f32[2,784,128]{2,1,0:T(8,128)}) custom-call(bf16[2,784,384]{2,1,0:T(8,128)(2,1)} %get-tuple-element.68.x_ref, bf16[4,2,208,384]{3,2,1,0:T(8,128)(2,1)} %get-tuple-element.71.own_ref, bf16[4,2,112,384]{3,2,1,0:T(8,128)(2,1)} %get-tuple-element.72.mem_ref, bf16[384,1152]{1,0:T(8,128)(2,1)} %concatenate.62.w_ref, ...), custom_call_target="tpu_custom_call" | custom-call | tf_op jit(solution)/shard_map/attend/pallas_call | solution.py:417
  106.8 13.1 %first_mlp.1 = (f32[2,784,384]{2,1,0:T(8,128)}, f32[2,784,384]{2,1,0:T(8,128)}, bf16[2,208,384]{2,1,0:T(8,128)(2,1)}, bf16[2,112,384]{2,1,0:T(8,128)(2,1)}) custom-call(bf16[2,784,384]{2,1,0:T(8,128)(2,1)} %reshape.253.x_ref, bf16[2,784,384]{2,1,0:T(8,128)(2,1)} %get-tuple-element.73.comb_ref, bf16[384,384]{1,0:T(8,128)(2,1)} %pad_maximum_fusion.6.out_ref, ...), custom_call_target="tpu_custom_call" | custom-call | tf_op jit(solution)/shard_map/first_mlp/pallas_call | solution.py:417
  119.9 28.0 %share_pooled.3 = (bf16[4,2,208,384]{3,2,1,0:T(8,128)(2,1)}, bf16[4,2,112,384]{3,2,1,0:T(8,128)(2,1)}) custom-call(bf16[2,208,384]{2,1,0:T(8,128)(2,1)} %get-tuple-element.74.pooled_ref.x_ref, bf16[2,112,384]{2,1,0:T(8,128)(2,1)} %get-tuple-element.75.mean_ref, f32[2,4]{1,0:T(2,128)} %add_convert_fusion.pick_ref), custom_call_target="tpu_custom_call" | custom-call | tf_op jit(solution)/shard_map/share_pooled/pallas_call | solution.py:584
  147.9 17.7 %attend.3 = (bf16[2,208,768]{2,1,0:T(8,128)(2,1)}, f32[2,208,128]{2,1,0:T(8,128)}) custom-call(bf16[2,208,384]{2,1,0:T(8,128)(2,1)} %get-tuple-element.74.pooled_ref.x_ref, bf16[4,2,208,384]{3,2,1,0:T(8,128)(2,1)} %get-tuple-element.76.own_ref, bf16[4,2,112,384]{3,2,1,0:T(8,128)(2,1)} %get-tuple-element.77.mem_ref, bf16[384,2304]{1,0:T(8,128)(2,1)} %fusion.w_ref, ...), custom_call_target="tpu_custom_call" | custom-call | tf_op jit(solution)/shard_map/attend/pallas_call | solution.py:417
  170.3 25.5 %second_mlp.1 = (bf16[416,768]{1,0:T(8,128)(2,1)}, bf16[416,768]{1,0:T(8,128)(2,1)}, f32[416,384]{1,0:T(8,128)}, bf16[2,4,2,192,1536]{4,3,2,1,0:T(8,128)(2,1)}, ...) custom-call(bf16[416,768]{1,0:T(8,128)(2,1)} %bitcast.182, ...), custom_call_target="tpu_custom_call" | custom-call | tf_op jit(solution)/shard_map/second_mlp/pallas_call | solution.py:417
  195.9 34.3 %attend_back.2 = (f32[2,208,384]{2,1,0:T(8,128)}, bf16[4,2,320,384]{3,2,1,0:T(8,128)(2,1)}, bf16[384,2304]{1,0:T(8,128)(2,1)}, f32[8,768]{1,0:T(8,128)}) custom-call(bf16[2,208,384]{2,1,0:T(8,128)(2,1)} %get-tuple-element.74.pooled_ref.x_ref, bf16[2,208,768]{2,1,0:T(8,128)(2,1)} %bitcast.181, bf16[4,2,208,384]{3,2,1,0:T(8,128)(2,1)} %get-tuple-element.76.own_ref, ...), custom_call_target="tpu_custom_call" | custom-call | tf_op jit(solution)/shard_map/attend_back/pallas_call | solution.py:417
  230.2 28.4 %give_back.2 = (f32[2,208,384]{2,1,0:T(8,128)}, f32[2,112,384]{2,1,0:T(8,128)}) custom-call(bf16[4,2,320,384]{3,2,1,0:T(8,128)(2,1)} %get-tuple-element.86.part_ref, f32[2,4]{1,0:T(2,128)} %add_convert_fusion.pick_ref), custom_call_target="tpu_custom_call" | custom-call | tf_op jit(solution)/shard_map/give_back/pallas_call | solution.py:690
  258.6 26.6 %first_back.1 = (f32[2,784,384]{2,1,0:T(8,128)}, bf16[2,784,384]{2,1,0:T(8,128)(2,1)}, bf16[2,384,768]{2,1,0:T(8,128)(2,1)}, bf16[2,384,768]{2,1,0:T(8,128)(2,1)...) custom-call(f32[2,784,384]{2,1,0:T(8,128)} %get-tuple-element.80.middle_ref, ...), custom_call_target="tpu_custom_call" | custom-call | tf_op jit(solution)/shard_map/first_back/pallas_call | solution.py:417
  285.2 37.0 %attend_back.3 = (f32[2,784,384]{2,1,0:T(8,128)}, bf16[4,2,320,384]{3,2,1,0:T(8,128)(2,1)}, bf16[384,1152]{1,0:T(8,128)(2,1)}, f32[8,384]{1,0:T(8,128)}) custom-call(bf16[2,784,384]{2,1,0:T(8,128)(2,1)} %get-tuple-element.68.x_ref, bf16[2,784,384]{2,1,0:T(8,128)(2,1)} %get-tuple-element.90.g_ref, bf16[4,2,208,384]{3,2,1,0:T(8,128)(2,1)} %get-tuple-element.71.own_ref, ...), custom_call_target="tpu_custom_call" | custom-call | tf_op jit(solution)/shard_map/attend_back/pallas_call | solution.py:417
  325.4 6.1 %concatenate.76 = bf16[2,384,2304]{2,1,0:T(8,128)(2,1)} concatenate(bf16[2,384,768]{2,1,0:T(8,128)(2,1)S(1)} %copy-done.7, bf16[2,384,768]{2,1,0:T(8,128)(2,1)} %get-tuple-element.106, bf16[2,384,192]{2,1,0:T(8,128)(2,1)S(1)} %bitcast.169, bf16[2,384,192]{2,1,0:T(8,128)(2,1)S(1)} %bitcast.170, bf16[2,384,192]{2,1,0:T(8,128)(2,1)S(1)} %bitcast.171, bf16[2,384,192]{2,1,0:T(8,128)(2,1)S(1)} %bitcast.172), dimensions={2} | concatenate | bytes 7077888 | tf_op jit(solution)/shard_map/concatenate | solution.py:918
  331.5 6.4 %copy.136 = bf16[8,96,2304]{1,2,0:T(8,128)(2,1)} copy(bf16[8,96,2304]{2,1,0:T(8,128)(2,1)} %bitcast.145) | data formatting | bytes 7077888 | tf_op jit(solution)/shard_map/reshape | solution.py:914
  346.7 6.8 %pad_maximum_fusion = bf16[8,96,3456]{1,2,0:T(8,128)(2,1)} fusion(bf16[8,96,1152]{1,2,0:T(8,128)(2,1)S(1)} %copy-done.2, bf16[8,96,2304]{1,2,0:T(8,128)(2,1)} %copy.136), kind=kLoop, calls=%fused_computation | loop fusion | flops 10616832 | bytes 10616832 | tf_op jit(solution)/shard_map/concatenate | solution.py:920
  353.4 45.1 %all-reduce.7.cloned.1.call-done = bf16[2,192,1536]{2,1,0:T(8,128)(2,1)} async-done(((bf16[2,192,1536]{2,1,0:T(8,128)(2,1)}), bf16[2,192,1536]{2,1,0:T(8,128)(2,1)}) %all-reduce.7.cloned.1.call-update) | async-done | bytes 1179664 | tf_op jit(solution)/shard_map/psum | solution.py:881
  399.3 21.4 %give_back.3 = (f32[2,208,384]{2,1,0:T(8,128)}, f32[2,112,384]{2,1,0:T(8,128)}) custom-call(bf16[4,2,320,384]{3,2,1,0:T(8,128)(2,1)} %get-tuple-element.93.part_ref, f32[2,4]{1,0:T(2,128)} %add_convert_fusion.pick_ref), custom_call_target="tpu_custom_call" | custom-call | tf_op jit(solution)/shard_map/give_back/pallas_call | solution.py:690
  420.8 6.5 %last_back.1 = (bf16[2,784,384]{2,1,0:T(8,128)(2,1)}, f32[8,384]{1,0:T(8,128)}) custom-call(bf16[2,784,384]{2,1,0:T(8,128)(2,1)} %reshape.253.x_ref, f32[2,784,384]{2,1,0:T(8,128)} %get-tuple-element.89.res_ref, f32[2,784,384]{2,1,0:T(8,128)} %get-tuple-element.92.dx_ref, f32[2,208,384]{2,1,0:T(8,128)} %get-tuple-element.94.own_ref, ...), custom_call_target="tpu_custom_call" | custom-call | tf_op jit(solution)/shard_map/last_back/pallas_call | solution.py:417
  430.5 41.2 %finish.1 = (bf16[2,2,784,384]{3,2,1,0:T(8,128)(2,1)}, f32[104,128]{1,0:T(8,128)}) custom-call(bf16[2,784,384]{2,1,0:T(8,128)(2,1)} %get-tuple-element.96.half_ref, f32[104,128]{1,0:T(8,128)} %pad_bitcast_fusion.small_ref), custom_call_target="tpu_custom_call" | custom-call | tf_op jit(solution)/shard_map/finish/pallas_call | solution.py:756
  473.8 4.6 reshape.304
  478.4 5.9 copy.143
  491.8 27.9 %reduce-scatter.6.cloned.1.call-done = bf16[1,96,3456]{1,2,0:T(8,128)(2,1)} async-done(((bf16[8,96,3456]{1,2,0:T(8,128)(2,1)}), bf16[1,96,3456]{1,2,0:T(8,128)(2,1)}) %reduce-scatter.6.cloned.1.call-update) | async-done | bytes 663568 | tf_op jit(solution)/shard_map/reduce_scatter | solution.py:881
  524.7 52.5 %all-reduce.9.cloned.1.call-done = (bf16[96,3456]{0,1:T(8,128)(2,1)}, bf16[192,576]{1,0:T(8,128)(2,1)}) async-done(((bf16[96,3456]{0,1:T(8,128)(2,1)}, bf16[192,576]{1,0:T(8,128)(2,1)}), (bf16[96,3456]{0,1:T(8,128)(2,1)}, bf16[192,576]{1,0:T(8,128)(2,1)})) %all-reduce.9.cloned.1.call-update) | async-done | bytes 884752 | tf_op jit(solution)/shard_map/psum | solution.py:881
  (247 shorter events, 74.8 us)
Async XLA Ops:
  7.2 24.9 %copy-start = (bf16[1,4,4,49,768]{4,2,3,1,0:T(4,128)(2,1)S(1)}, bf16[1,4,4,49,768]{4,2,3,1,0:T(4,128)(2,1)}, u32[]{:S(2)}) copy-start(bf16[1,4,4,49,768]{4,2,3,1,0:T(4,128)(2,1)} %param.45) | copy-start | bytes 3612676
  7.2 4.5 copy-start.15
  7.2 4.5 copy-start.18
  7.3 56.0 %all-gather.8.cloned.1.call-start = ((), (), s32[]{:S(2)}) async-start(), calls=%async_computation.3 | async-start | bytes 1990656 | tf_op jit(solution)/shard_map/all_gather | solution.py:822
  9.5 69.3 %all-gather.10.cloned.1.call-start = ((), (), s32[]{:S(2)}) async-start(), calls=%async_computation.8 | async-start | bytes 3981312 | tf_op jit(solution)/shard_map/all_gather | solution.py:821
  11.7 7.3 %copy-start.21 = (f32[3,768]{1,0:T(4,128)S(1)}, f32[3,768]{1,0:T(4,128)}, u32[]{:S(2)}) copy-start(f32[3,768]{1,0:T(4,128)} %param.40) | copy-start | bytes 27652
  11.7 153.9 %all-gather.12.cloned.1.call-start = ((), (), s32[]{:S(2)}) async-start(), calls=%async_computation.9 | async-start | bytes 12828672 | tf_op jit(solution)/shard_map/all_gather | solution.py:823
  13.1 329.4 %reduce-scatter.4.cloned.1.call-start = ((), (), s32[]{:S(2)}) async-start(), calls=%async_computation.4 | async-start | bytes 10616832 | tf_op jit(solution)/shard_map/reduce_scatter | solution.py:881
  21.0 9.9 %copy-start.25 = (f32[5,384]{1,0:T(8,128)S(1)}, f32[5,384]{1,0:T(8,128)}, u32[]{:S(2)}) copy-start(f32[5,384]{1,0:T(8,128)} %param.39) | copy-start | bytes 23044
  33.5 29.1 %slice-start = ((f32[3,768]{1,0:T(4,128)}), f32[1,768]{1,0:T(1,128)S(1)}, s32[]{:S(2)}) async-start(f32[3,768]{1,0:T(4,128)} %param.40), calls=%async_computation.11 | async-start | bytes 6144 | tf_op jit(solution)/shard_map/slice | solution.py:870
  63.2 5.5 copy-start.5
  195.9 202.6 %all-reduce.7.cloned.1.call-start = ((), (), s32[]{:S(2)}) async-start(), calls=%async_computation.5 | async-start | bytes 2359296 | tf_op jit(solution)/shard_map/psum | solution.py:881
  331.5 6.4 %copy-start.4 = (bf16[384,2304]{1,0:T(8,128)(2,1)S(1)}, bf16[384,2304]{1,0:T(8,128)(2,1)}, u32[]{:S(2)}) copy-start(bf16[384,2304]{1,0:T(8,128)(2,1)} %get-tuple-element.109) | copy-start | bytes 5308420
  342.5 149.3 %reduce-scatter.8.cloned.1.call-start = ((), (), s32[]{:S(2)}) async-start(), calls=%async_computation.7 | async-start | bytes 2211840 | tf_op jit(solution)/shard_map/reduce_scatter | solution.py:881
  398.5 121.2 %reduce-scatter.6.cloned.1.call-start = ((), (), s32[]{:S(2)}) async-start(), calls=%async_computation.6 | async-start | bytes 7962624 | tf_op jit(solution)/shard_map/reduce_scatter | solution.py:881
  399.2 178.0 %all-reduce.9.cloned.1.call-start = ((), (), s32[]{:S(2)}) async-start(), calls=%async_computation.10 | async-start | bytes 2260992 | tf_op jit(solution)/shard_map/psum | solution.py:881
  420.7 7.3 %copy-start.26 = (f32[8,384]{1,0:T(8,128)S(1)}, f32[8,384]{1,0:T(8,128)}, u32[]{:S(2)}) copy-start(f32[8,384]{1,0:T(8,128)} %get-tuple-element.98) | copy-start | bytes 36868
  420.7 7.4 %copy-start.23 = (f32[8,768]{1,0:T(8,128)S(1)}, f32[8,768]{1,0:T(8,128)}, u32[]{:S(2)}) copy-start(f32[8,768]{1,0:T(8,128)} %get-tuple-element.99) | copy-start | bytes 73732
  420.8 8.9 %copy-start.27 = (f32[2,1,768]{2,1,0:T(1,128)S(1)}, f32[2,1,768]{2,1,0:T(1,128)}, u32[]{:S(2)}) copy-start(f32[2,1,768]{2,1,0:T(1,128)} %get-tuple-element.102) | copy-start | bytes 18436
  420.8 9.1 %copy-start.22 = (f32[1,3072]{1,0:T(1,128)S(1)}, f32[1,3072]{1,0:T(1,128)}, u32[]{:S(2)}) copy-start(f32[1,3072]{1,0:T(1,128)} %get-tuple-element.103) | copy-start | bytes 36868
  478.4 5.9 %copy-start.19 = (f32[104,128]{1,0:T(8,128)S(1)}, f32[104,128]{1,0:T(8,128)}, u32[]{:S(2)}) copy-start(f32[104,128]{1,0:T(8,128)} %get-tuple-element.116) | copy-start | bytes 159748
  478.4 6.6 %copy-start.10 = (bf16[416,768]{1,0:T(8,128)(2,1)S(1)}, bf16[416,768]{1,0:T(8,128)(2,1)}, u32[]{:S(2)}) copy-start(bf16[416,768]{1,0:T(8,128)(2,1)} %get-tuple-element.79) | copy-start | bytes 1916932
  486.5 33.9 %collective-permute-start = (bf16[2,196,768]{2,0,1:T(2,128)(2,1)S(1)}, bf16[2,196,768]{2,0,1:T(2,128)(2,1)S(1)}, u32[]{:S(2)}, u32[]{:S(2)}) collective-permute-start(bf16[2,196,768]{2,0,1:T(2,128)(2,1)S(1)} %get-tuple-element.196), channel_id=1, source_target_pairs={{0,1},{1,0},{2,3},{3,2},{4,5},{5,4},{6,7},{7,6},{8,9},{9,8},{10,11... | collective-permute-start | bytes 1806344 | tf_op jit(solution)/shard_map/ppermute | solution.py:774
  578.7 5.8 copy-start.1
  (21 other events, 53.9 us)
Sparse Core Ops, SparseCore 0:
  10.6 29.2 all-gather.7
  42.3 36.3 all-gather.9
  80.6 77.1 all-gather.11
  196.0 86.2 reduce-scatter.3
  342.6 55.8 all-reduce.6
  401.7 42.5 reduce-scatter.7
  448.3 71.3 reduce-scatter.5
  522.2 55.0 all-reduce.8

commit v4 on v3

--- a/solution.py
+++ b/solution.py
@@ -130,16 +130,16 @@
         x_s[rows, :] = ref[t, 0]
     width = k_s.shape[1]
     for low in range(0, width, 384):
-        k_s[:, low:low + 384] = dot(x_s[...], w_ref[:, width + low:width + low + 384]).astype(bf16)
+        k_s[:, low:low + 384] = dot(x_s[...], w_ref[low // 384, :, 384:768]).astype(bf16)
     for low in range(0, width, 384):
-        value = dot(x_s[...], w_ref[:, 2 * width + low:2 * width + low + 384])
+        value = dot(x_s[...], w_ref[low // 384, :, 768:])
         v_s[:, low:low + 384] = (value + bias_ref[1:2, low:low + 384]).astype(bf16)
 
 
 def project_queries(x_ref, w_ref, bias_ref, q_s):
     width = q_s.shape[1]
     for low in range(0, width, 384):
-        value = dot(x_ref[0], w_ref[:, low:low + 384])
+        value = dot(x_ref[0], w_ref[low // 384, :, :384])
         q_s[:, low:low + 384] = (value + bias_ref[0:1, low:low + 384]).astype(bf16)
 
 
@@ -150,6 +150,14 @@
     pooled = exact_dot(pool_ref[...], normed)
     pooled_ref[0] = pooled.astype(bf16)
     mean_ref[0] = exact_dot(pair_ref[...], pooled).astype(bf16)
+
+
+def write_shares(gw_ref, h, gw_s):
+    wide = gw_ref.shape[2] // 3
+    for part in range(3):
+        low = wide * h
+        columns = gw_s[low // 384, :, 384 * part:384 * part + 384][:, low % 384:low % 384 + wide]
+        gw_ref[h, :, wide * part:wide * part + wide] = columns.astype(bf16)
 
 
 def attend_kernel(chunk, x_ref, own_ref, mem_ref, w_ref, qv_ref, mask_ref, out_ref, lse_ref, x_s, q_s, k_s, v_s, s_s, p_s):
@@ -243,17 +251,17 @@
         total = jnp.concatenate(parts, axis=1) + g_ref[0, :, group].astype(f32)
         row_q.append(sum_rows(total))
         low = total.astype(bf16)
-        gw_s[:, group] += dot(xt, low)
-        add = dot(low, w_ref[:, group], NT)
+        gw_s[tile, :, :384] += dot(xt, low)
+        add = dot(low, w_ref[tile, :, :384], NT)
         dx = add if dx is None else dx + add
-        for base, src in ((width, dk_s), (2 * width, dv_s)):
+        for part, src in ((1, dk_s), (2, dv_s)):
             grad = src[...].T
-            if base == 2 * width:
+            if part == 2:
                 row_v.append(sum_rows(grad))
             low = grad.astype(bf16)
-            here = slice(base + 384 * tile, base + 384 * tile + 384)
-            gw_s[:, here] += dot(keys_t, low)
-            add = dot(low, w_ref[:, here], NT)
+            here = slice(384 * part, 384 * part + 384)
+            gw_s[tile, :, here] += dot(keys_t, low)
+            add = dot(low, w_ref[tile, :, here], NT)
             dpool = add if dpool is None else dpool + add
     dx_ref[0] = dx
     row = 0
@@ -266,7 +274,8 @@
 
     @pl.when(step == pl.num_programs(0) - 1)
     def _():
-        gw_ref[...] = gw_s[...].astype(bf16)
+        for h in range(gw_ref.shape[0]):
+            write_shares(gw_ref, h, gw_s)
 
 
 def first_mlp_kernel(x_ref, comb_ref, out_ref, up_ref, down_ref, ub_ref, vec_ref, pool_ref, pair_ref,
@@ -295,7 +304,10 @@
 
     @pl.when(step == 0)
     def _():
-        after = dot(comb_ref[...], out_ref[...], NT) + dot(pooled_ref[...], skip_ref[...], NT) + vec_ref[0:1, :]
+        after = dot(pooled_ref[...], skip_ref[...], NT) + vec_ref[0:1, :]
+        wide = out_ref.shape[2]
+        for h in range(out_ref.shape[0]):
+            after = after + dot(comb_ref[:, wide * h:wide * h + wide], out_ref[h], NT)
         after_s[...] = after
         unit, _ = norm(after)
         low = (unit * vec_ref[1:2, :] + vec_ref[2:3, :]).astype(bf16)
@@ -329,17 +341,23 @@
         for i, row in enumerate((res, dlow, cot, dlow * unit)):
             row_ref[i:i + 1, :] = sum_rows(row)
         res = res.astype(bf16)
-        dcomb_ref[...] = dot(res, out_ref[...]).astype(bf16)
         dskip_ref[...] = dot(res, skip_ref[...])
         rest = transposed(res)
-        gout_ref[...] = dot(rest, comb_ref[...]).astype(bf16)
-        gskip_ref[...] = dot(rest, pooled_ref[...]).astype(bf16)
+        wide = out_ref.shape[2]
+        for h in range(out_ref.shape[0]):
+            here = slice(wide * h, wide * h + wide)
+            dcomb_ref[:, here] = dot(res, out_ref[h]).astype(bf16)
+            gout_ref[h] = dot(rest, comb_ref[:, here]).astype(bf16)
+        grad = dot(rest, pooled_ref[...])
+        wide = gskip_ref.shape[2]
+        for h in range(gskip_ref.shape[0]):
+            gskip_ref[h] = grad[:, wide * h:wide * h + wide].astype(bf16)
 
 
 def first_back_kernel(
     middle_ref, after_ref, comb_ref, dskip_ref, dq_ref, own_ref, mem_ref, out_ref, up_ref, down_ref, ub_ref, vec_ref,
     unpool_ref, unpair_ref,
-    res_ref, dcomb_ref, gup_ref, gdown_ref, gout_ref, gub_ref, row_ref,
+    res_ref, dcomb_ref, gmlp_ref, gout_ref, gub_ref, row_ref,
     gup_s, gdown_s, gout_s,
 ):
     step = pl.program_id(0)
@@ -382,16 +400,20 @@
 
     @pl.when(step == pl.num_programs(0) - 1)
     def _():
-        gup_ref[...] = gup_s[...].astype(bf16)
-        gdown_ref[...] = gdown_s[...].astype(bf16)
-        gout_ref[...] = gout_s[...].astype(bf16)
+        fa, ha = gmlp_ref.shape[2] // 2, gout_ref.shape[2]
+        for h in range(gmlp_ref.shape[0]):
+            gmlp_ref[h, :, :fa] = gup_s[h].astype(bf16)
+            gmlp_ref[h, :, fa:] = gdown_s[h].astype(bf16)
+            gout_ref[h] = gout_s[:, ha * h:ha * h + ha].astype(bf16)
 
 
 def last_back_kernel(x_ref, res_ref, dx_ref, own_ref, mem_ref, vec_ref, unpool_ref, unpair_ref, grad_ref, row_ref):
     dpool = own_ref[0] + exact_dot(unpair_ref[...], mem_ref[0])
     dnorm = dx_ref[0] + exact_dot(unpool_ref[...], dpool)
     unit, inverse = norm(x_ref[0].astype(f32))
-    grad_ref[0] = (norm_back(unit, inverse, vec_ref[0:1, :], dnorm) + res_ref[0]).astype(bf16)
+    grad = norm_back(unit, inverse, vec_ref[0:1, :], dnorm) + res_ref[0]
+    for f in range(grad_ref.shape[1]):
+        grad_ref[0, f] = grad[PATCH * f:PATCH * f + PATCH].astype(bf16)
     add_rows(row_ref, [sum_rows(dnorm * unit), sum_rows(dnorm)])
 
 
@@ -442,7 +464,7 @@
     )
 
 
-def attend_back(x, grad, own, mem, w, qv, mask, lse):
+def attend_back(x, grad, own, mem, w, qv, mask, lse, heads):
     batches, nq, d = x.shape
     width = grad.shape[2]
     keys = own.shape[0] * own.shape[2] + mem.shape[0] * mem.shape[2]
@@ -450,7 +472,7 @@
     return call(
         functools.partial(attend_back_kernel, chunk_of(nq)), batches,
         [(x, 0), (grad, 0), (own, 1), (mem, 1), (w, None), (qv, None), (mask, 0), (lse, 0)],
-        [(shape((batches, nq, d), f32), 0), (shape(both, bf16), 1), (shape(w.shape, bf16), None), (shape((8, width), f32), None)],
+        [(shape((batches, nq, d), f32), 0), (shape(both, bf16), 1), (shape((heads, d, 3 * width // heads), bf16), None), (shape((8, width), f32), None)],
         [((keys, d), bf16), ((nq, width), bf16), ((keys, width), bf16), ((keys, width), bf16),
          ((nq, keys), f32), ((nq, keys), f32), ((nq, keys), bf16), ((nq, keys), bf16),
          ((384, keys), f32), ((384, keys), f32), ((8, 128), f32), (w.shape, f32)],
@@ -703,67 +725,153 @@
     )(part, pick)
 
 
-def finish_kernel(half_ref, small_ref, all_ref, total_ref, sum_s, core_s, chip_s, head_s, clip_s,
-                  local_sem, half_send, half_recv, core_send, core_recv, chip_send, chip_recv, head_send, head_recv, clip_send, clip_recv):
+def finish_kernel(half_ref, small_ref, grad_ref, rest_ref, all_ref, total_ref, gtotal_ref, rtotal_ref, *scratch):
+    (small_s, small_core, small_chip, small_head, small_clip, part_s, part_core, chip_s, part_chip, head_s, part_head, mine_s, part_clip,
+     rest_in, rest_s, local_sem, half_send, half_recv, core_send, core_recv, chip_send, chip_recv, head_send, head_recv,
+     clip_send, clip_recv, rest_send, rest_recv, back_send, back_recv) = scratch
     clip, head, chip, core, chips = places()
     clips, heads = lax.axis_size("clip"), lax.axis_size("head")
+    share = half_ref.shape[0]
     partner = {"tok": 2 * chip + 1 - core}
     across = [{"tok": 2 * rem(chip + k, chips) + core} for k in range(1, chips)]
     beside = [{"head": rem(head + k, heads)} for k in range(1, heads)]
     along = [{"clip": rem(clip + k, clips)} for k in range(1, clips)]
     peers = [(d, None) for d in [partner] + across + beside + along]
     greet(peers, peers)
-    halves = [remote(half_ref, all_ref.at[head], half_send.at[k], half_recv.at[k], d) for k, d in enumerate(beside)]
-    for copy in halves:
-        copy.start()
+    pending = []
+
+    def go(copies):
+        for copy in copies:
+            copy.start()
+        pending.extend(copies)
+        return copies
+
+    def arrived(copies):
+        for copy in copies:
+            copy.wait_recv()
+
+    def in_order(index, size, own, slot):
+        total = None
+        for i in range(size):
+            piece = jnp.where(index == i, own, jnp.zeros_like(own))
+            for k in range(size - 1):
+                piece = jnp.where(rem(index - k - 1, size) == i, slot(k), piece)
+            total = piece if total is None else total + piece
+        return total
+
+    first = go([remote(small_ref, small_core, core_send.at[0], core_recv.at[0], partner)])
+    for h in range(heads):
+        for x in range(chips):
+            n = h * chips + x
+            first += go([remote(grad_ref.at[2 * n + 1 - core], part_core.at[n], core_send.at[n + 1], core_recv.at[n + 1], partner)])
+    gather = go([remote(rest_ref.at[rem(clip + k + 1, clips)], rest_in.at[k], rest_send.at[k], rest_recv.at[k], d) for k, d in enumerate(along)])
+    halves = [
+        [remote(half_ref.at[s], all_ref.at[head, s], half_send.at[k, s], half_recv.at[k, s], d) for k, d in enumerate(beside)]
+        for s in range(share)
+    ]
+    for s in range(share - 1):
+        go(halves[s])
     local_half = pltpu.make_async_copy(half_ref, all_ref.at[head], local_sem.at[0])
     local_half.start()
-    first = remote(small_ref, core_s, core_send.at[0], core_recv.at[0], partner)
-    first.start()
-    first.wait_recv()
-    sum_s[0] = small_ref[...] + core_s[...]
-    waits = [first]
-    stages = ((across, chip, chips, chip_s, chip_send, chip_recv), (beside, head, heads, head_s, head_send, head_recv),
-              (along, clip, clips, clip_s, clip_send, clip_recv))
-    for n, (devices, index, size, slots, send, recv) in enumerate(stages):
-        copies = [remote(sum_s.at[n], slots.at[k], send.at[k], recv.at[k], d) for k, d in enumerate(devices)]
-        for copy in copies:
-            copy.start()
-        for copy in copies:
-            copy.wait_recv()
-        total = None
-        for i in range(size):
-            piece = jnp.zeros_like(sum_s[n])
-            piece = jnp.where(index == i, sum_s[n], piece)
-            for k in range(size - 1):
-                piece = jnp.where(rem(index - k - 1, size) == i, slots[k], piece)
-            total = piece if total is None else total + piece
-        if n + 1 < len(stages):
-            sum_s[n + 1] = total
-        else:
-            total_ref[...] = total
-        waits += copies
-    for copy in halves:
-        copy.wait_recv()
-    for copy in waits + halves:
+    arrived(first)
+    small_s[0] = small_ref[...] + small_core[...]
+    for n in range(heads * chips):
+        part_s[n] = (grad_ref[2 * n + core].astype(f32) + part_core[n].astype(f32)).astype(bf16)
+    copies = []
+    for k, d in enumerate(across):
+        copies += go([remote(small_s.at[0], small_chip.at[k], chip_send.at[k, 0], chip_recv.at[k, 0], d)])
+        for h in range(heads):
+            block = h * chips + rem(chip + k + 1, chips)
+            copies += go([remote(part_s.at[block], part_chip.at[k, h], chip_send.at[k, h + 1], chip_recv.at[k, h + 1], d)])
+    arrived(copies)
+    small_s[1] = in_order(chip, chips, small_s[0], lambda k: small_chip[k])
+    for h in range(heads):
+        total = part_s[h * chips + chip].astype(f32)
+        for k in range(chips - 1):
+            total = total + part_chip[k, h].astype(f32)
+        chip_s[h] = total.astype(bf16)
+    copies = []
+    for k, d in enumerate(beside):
+        copies += go([remote(small_s.at[1], small_head.at[k], head_send.at[k, 0], head_recv.at[k, 0], d)])
+        copies += go([remote(chip_s.at[rem(head + k + 1, heads)], part_head.at[k], head_send.at[k, 1], head_recv.at[k, 1], d)])
+    go(halves[share - 1])
+    arrived(gather)
+    total = rest_ref[clip].astype(f32)
+    for k in range(clips - 1):
+        total = total + rest_in[k].astype(f32)
+    rest_s[clip] = total.astype(bf16)
+    spread = go([remote(rest_s.at[clip], rest_s.at[clip], back_send.at[k], back_recv.at[k], d) for k, d in enumerate(along)])
+    arrived(copies)
+    small_s[2] = in_order(head, heads, small_s[1], lambda k: small_head[k])
+    total = chip_s[head].astype(f32)
+    for k in range(heads - 1):
+        total = total + part_head[k].astype(f32)
+    mine_s[...] = total.astype(bf16)
+    copies = []
+    for k, d in enumerate(along):
+        copies += go([remote(small_s.at[2], small_clip.at[k], clip_send.at[k, 0], clip_recv.at[k, 0], d)])
+        copies += go([remote(mine_s, part_clip.at[k], clip_send.at[k, 1], clip_recv.at[k, 1], d)])
+    arrived(copies)
+    total_ref[...] = in_order(clip, clips, small_s[2], lambda k: small_clip[k])
+    gtotal_ref[...] = in_order(clip, clips, mine_s[...].astype(f32), lambda k: part_clip[k].astype(f32))
+    arrived(spread)
+    rtotal_ref[...] = rest_s[...].astype(f32)
+    for copies in halves:
+        arrived(copies)
+    for copy in pending:
         copy.wait_send()
     local_half.wait()
 
 
-def finish(half, small, number):
+def finish(half, small, grad, rest, number):
     toks, heads, clips = lax.axis_size("tok"), lax.axis_size("head"), lax.axis_size("clip")
-    counts = [max(n, 1) for n in (toks // 2 - 1, heads - 1, clips - 1)]
-    return pl.pallas_call(
+    chips = toks // 2
+    across, beside, along = (max(n, 1) for n in (chips - 1, heads - 1, clips - 1))
+    rows, lanes = rest.shape
+    rest = rest.reshape(clips, rows // clips, lanes)
+    pad = up16(rows // clips) - rows // clips
+    if pad:
+        rest = jnp.pad(rest, ((0, 0), (0, pad), (0, 0)))
+    block = grad.shape[1:]
+    low, full = lambda *dims: pltpu.VMEM(dims, bf16), lambda *dims: pltpu.VMEM(dims + small.shape, f32)
+    all_half, total, gtotal, rtotal = pl.pallas_call(
         finish_kernel,
-        in_specs=[ANY, INVMEM],
-        out_specs=[ANY, INVMEM],
-        out_shape=[shape((heads,) + half.shape, half.dtype), shape(small.shape, f32)],
-        scratch_shapes=[pltpu.VMEM((3,) + small.shape, f32), pltpu.VMEM(small.shape, f32)]
-        + [pltpu.VMEM((n,) + small.shape, f32) for n in counts]
-        + [dma(1), dma(counts[1]), dma(counts[1]), dma(1), dma(1)] + [dma(n) for n in counts for _ in range(2)],
+        in_specs=[ANY, INVMEM, INVMEM, INVMEM],
+        out_specs=[ANY, INVMEM, INVMEM, INVMEM],
+        out_shape=[shape((heads,) + half.shape, half.dtype), shape(small.shape, f32), shape(block, f32), shape(rest.shape, f32)],
+        scratch_shapes=[
+            full(3), full(), full(across), full(beside), full(along),
+            low(heads * chips, *block), low(heads * chips, *block), low(heads, *block), low(across, heads, *block),
+            low(heads, *block), low(beside, *block), low(*block), low(along, *block),
+            low(along, *rest.shape[1:]), low(*rest.shape),
+            dma(1), dma(beside, half.shape[0]), dma(beside, half.shape[0]), dma(heads * chips + 1), dma(heads * chips + 1),
+            dma(across, heads + 1), dma(across, heads + 1), dma(beside, 2), dma(beside, 2), dma(along, 2), dma(along, 2),
+            dma(along), dma(along), dma(along), dma(along),
+        ],
         compiler_params=pltpu.CompilerParams(collective_id=number, has_side_effects=True, vmem_limit_bytes=VMEM_CAP),
         name="finish",
-    )(half, small)
+    )(half, small, grad, rest)
+    return all_half, total, gtotal, rtotal[:, :rows // clips].reshape(rows, lanes)
+
+
+def reduce_clips(shard):
+    clips, clip = lax.axis_size("clip"), lax.axis_index("clip")
+    pieces = shard.reshape(clips, -1, shard.shape[-1])
+    total = lax.dynamic_index_in_dim(pieces, clip, 0, keepdims=False).astype(f32)
+    for k in range(1, clips):
+        give = lax.dynamic_index_in_dim(pieces, (clip + k) % clips, 0, keepdims=False)
+        total = total + lax.ppermute(give, "clip", [(i, (i + k) % clips) for i in range(clips)]).astype(f32)
+    return total.astype(bf16)
+
+
+def spread_clips(piece):
+    clips, clip = lax.axis_size("clip"), lax.axis_index("clip")
+    out = jnp.zeros((clips,) + piece.shape, piece.dtype)
+    out = lax.dynamic_update_index_in_dim(out, piece, clip, 0)
+    for k in range(1, clips):
+        got = lax.ppermute(piece, "clip", [(i, (i + k) % clips) for i in range(clips)])
+        out = lax.dynamic_update_index_in_dim(out, got, (clip - k + clips) % clips, 0)
+    return out.reshape((-1,) + piece.shape[1:])
 
 
 def from_heads(piece, heads):
@@ -819,23 +927,6 @@
     fb, hb, hs = w_up_b.shape[1], w_out_b.shape[1], w_skip_b.shape[1]
     pack_a = jnp.concatenate([w_up_a, w_down_a, w_qkv_a.reshape(w_qkv_a.shape[0], -1), w_out_a], axis=1)
     all_a = lax.all_gather(pack_a, group).reshape(heads, d1, -1)
-    all_q = lax.all_gather(w_qkv_b.reshape(w_qkv_b.shape[0], -1), group).reshape(heads, d1, -1)
-    all_b = lax.all_gather(jnp.concatenate([w_up_b, w_down_b, w_out_b, w_skip_b], axis=1), group).reshape(heads, d2, -1)
-    flat = jnp.concatenate([qv_bias_a.reshape(-1), qv_bias_b.reshape(-1), up_bias_a, up_bias_b])
-    flat = lax.all_gather(flat, "head")
-    qv_a = flat[:, :2 * ha].reshape(heads, 2, ha).transpose(1, 0, 2).reshape(2, d1)
-    qv_b = flat[:, 2 * ha:2 * ha + 2 * hb].reshape(heads, 2, hb).transpose(1, 0, 2).reshape(2, d2)
-    ub_a = flat[:, 2 * (ha + hb):2 * (ha + hb) + fa].reshape(heads, 1, fa)
-    ub_b = flat[:, 2 * (ha + hb) + fa:].reshape(1, heads * fb)
-
-    def lanes(pack, low, width):
-        return jnp.concatenate([pack[h, :, low:low + width] for h in range(heads)], axis=1)
-
-    up_a, down_a = all_a[:, :, :fa], all_a[:, :, fa:2 * fa]
-    qkv_a = jnp.concatenate([lanes(all_a, 2 * fa + i * ha, ha) for i in range(3)], axis=1)
-    out_a = lanes(all_a, 2 * fa + 3 * ha, ha)
-    qkv_b = jnp.concatenate([lanes(all_q, i * hb, hb) for i in range(3)], axis=1)
-    out_b, skip_b = lanes(all_b, 2 * fb, hb), lanes(all_b, 2 * fb + hb, hs)
 
     low1, pooled1, mean1 = call(
         norm_pool_kernel, share,
@@ -843,11 +934,34 @@
         [(shape((share, tokens, d1), bf16), 0), (shape((share, own_rows, d1), bf16), 0), (shape((share, mem_rows, d1), bf16), 0)],
         name="norm_pool",
     )
+    pooled1, pack_q, pack_b, flat, mask = lax.optimization_barrier((
+        pooled1, w_qkv_b.reshape(w_qkv_b.shape[0], -1), jnp.concatenate([w_up_b, w_down_b, w_out_b, w_skip_b], axis=1),
+        jnp.concatenate([qv_bias_a.reshape(-1), qv_bias_b.reshape(-1), up_bias_a, up_bias_b]), mask))
     own1, mem1 = share_pooled(pooled1, mean1, pick, 0)
+    all_q = lax.all_gather(pack_q, group).reshape(heads, d1, -1)
+    all_b = lax.all_gather(pack_b, group).reshape(heads, d2, -1)
+    flat = from_heads(flat[None], heads)
+    qv_a = flat[:, :2 * ha].reshape(heads, 2, ha).transpose(1, 0, 2).reshape(2, d1)
+    qv_b = flat[:, 2 * ha:2 * ha + 2 * hb].reshape(heads, 2, hb).transpose(1, 0, 2).reshape(2, d2)
+    ub_a = flat[:, 2 * (ha + hb):2 * (ha + hb) + fa].reshape(heads, 1, fa)
+    ub_b = flat[:, 2 * (ha + hb) + fa:].reshape(1, heads * fb)
+
+    def lanes(pack, low, width):
+        return jnp.concatenate([pack[h, :, low:low + width] for h in range(heads)], axis=1)
+
+    up_spec, down_spec = (pl.BlockSpec((heads, d1, fa), lambda i, n=n: (0, 0, n)) for n in range(2))
+    qkv_a = jnp.concatenate([lanes(all_a, 2 * fa + i * ha, ha) for i in range(3)], axis=1)[None]
+    out_a = lanes(all_a, 2 * fa + 3 * ha, ha)
+    qkv_b = all_q
+    if hb != 384:
+        parts = [lanes(all_q, i * hb, hb).reshape(d1, -1, 384).transpose(1, 0, 2) for i in range(3)]
+        qkv_b = jnp.concatenate(parts, axis=2)
+    skip_b = lanes(all_b, 2 * fb + hb, hs)
+
     comb1, lse1 = attend(low1, own1, mem1, qkv_a, qv_a, mask, d1)
     after1, middle, pooled3, mean3 = call(
         first_mlp_kernel, share,
-        [(stream, 0), (comb1, 0), (out_a, None), (up_a, None), (down_a, None), (ub_a, None),
+        [(stream, 0), (comb1, 0), (out_a, None), (all_a, up_spec), (all_a, down_spec), (ub_a, None),
          (padded_rows(shifts_a[1], gains_a[1], shifts_a[2], shifts_a[3], gains_a[2], shifts_a[4]), None),
          (pooling, None), (pairing, None)],
         [(shape((share, tokens, d1), f32), 0), (shape((share, tokens, d1), f32), 0),
@@ -860,10 +974,11 @@
     chunk = 768
     per_head = fb // chunk
     steps = heads * per_head
+    out_spec = pl.BlockSpec((heads, d2, hb), lambda j: (0, 0, 2 * fb // hb))
     rows_spec = pl.BlockSpec((1, d2, chunk), lambda j: (j // per_head, 0, j % per_head))
     mixed, dcomb2, dskip, g_mlp_b, g_out_b, g_skip_b, g_ub_b, rows_b = call(
         second_mlp_kernel, steps,
-        [(comb2.reshape(rows2, d2), None), (pooled3.reshape(rows2, d1), None), (cot, None), (out_b, None), (skip_b, None),
+        [(comb2.reshape(rows2, d2), None), (pooled3.reshape(rows2, d1), None), (cot, None), (all_b, out_spec), (skip_b, None),
          (all_b, rows_spec),
          (all_b, pl.BlockSpec((1, d2, chunk), lambda j: (j // per_head, 0, per_head + j % per_head))),
          (ub_b, pl.BlockSpec((1, chunk), lambda j: (0, j))),
@@ -871,57 +986,51 @@
         [(shape((rows2, d2), bf16), None), (shape((rows2, d2), bf16), None), (shape((rows2, d1), f32), None),
          (shape((heads, toks, 2, d2 // toks, fb), bf16),
           pl.BlockSpec((1, toks, 2, d2 // toks, chunk), lambda j: (j // per_head, 0, 0, 0, j % per_head))),
-         (shape((d2, d2), bf16), None), (shape((d2, d1), bf16), None),
+         (shape((heads, d2, hb), bf16), None), (shape((heads, d2, hs), bf16), None),
          (shape((1, heads * fb), f32), pl.BlockSpec((1, chunk), lambda j: (0, j))), (shape((8, d2), f32), None)],
         [((rows2, d2), f32), ((rows2, d2), bf16), ((d2, rows2), bf16), ((d2, rows2), bf16), ((rows2, d2), f32), ((rows2, d2), f32)],
         name="second_mlp",
     )
 
-    def reduce_grad(blocks):
-        return lax.psum(lax.psum_scatter(blocks, group, scatter_dimension=0, tiled=False), "clip")
-
-    sum_mlp_b = reduce_grad(g_mlp_b.reshape((heads * toks,) + g_mlp_b.shape[2:]))
-
-    def by_head(grad, width):
-        return grad.reshape(grad.shape[0], heads, width).transpose(1, 0, 2)
-
+    def by_owner(grad):
+        return grad.reshape((heads * toks, -1) + grad.shape[2:])
+
+    def scatter(grad):
+        return lax.psum_scatter(grad, group, scatter_dimension=0, tiled=False)
+
+    sum_mlp_b = scatter(g_mlp_b.reshape((heads * toks,) + g_mlp_b.shape[2:]))
     dcomb2 = dcomb2.reshape(share, own_rows, d2)
-    dq2, dpool2, g_qkv_b, rows_qv_b = attend_back(pooled3, dcomb2, own2, mem2, qkv_b, qv_b, mask, lse2)
+    dq2, dpool2, g_qkv_b, rows_qv_b = attend_back(pooled3, dcomb2, own2, mem2, qkv_b, qv_b, mask, lse2, heads)
     own_back2, mem_back2 = give_back(dpool2, pick, own_rows, 2)
 
-    res1, dcomb1, g_up_a, g_down_a, g_out_a, g_ub_a, rows_a = call(
+    res1, dcomb1, g_mlp_a, g_out_a, g_ub_a, rows_a = call(
         first_back_kernel, share,
         [(middle, 0), (after1, 0), (comb1, 0), (dskip.reshape(share, own_rows, d1), 0), (dq2, 0), (own_back2, 0), (mem_back2, 0),
-         (out_a, None), (up_a, None), (down_a, None), (ub_a, None),
+         (out_a, None), (all_a, up_spec), (all_a, down_spec), (ub_a, None),
          (padded_rows(gains_a[1], shifts_a[2], gains_a[2]), None), (unpooling, None), (unpairing, None)],
         [(shape((share, tokens, d1), f32), 0), (shape((share, tokens, d1), bf16), 0),
-         (shape((heads, d1, fa), bf16), None), (shape((heads, d1, fa), bf16), None), (shape((d1, d1), bf16), None),
+         (shape((heads, d1, 2 * fa), bf16), None), (shape((heads, d1, ha), bf16), None),
          (shape((heads, 1, fa), f32), None), (shape((8, d1), f32), None)],
         [((heads, d1, fa), f32), ((heads, d1, fa), f32), ((d1, d1), f32)],
         name="first_back",
     )
-    dx1, dpool1, g_qkv_a, rows_qv_a = attend_back(low1, dcomb1, own1, mem1, qkv_a, qv_a, mask, lse1)
+    g_out_b, g_skip_b = by_owner(g_out_b), by_owner(g_skip_b)
+    half = g_out_b.shape[1] // 2
+    rest_b = jnp.concatenate(
+        [by_owner(g_qkv_b), g_out_b[:, :half], g_out_b[:, half:], g_skip_b[:, :half], g_skip_b[:, half:]], axis=2)
+    rest_a = jnp.concatenate([by_owner(g_mlp_a), by_owner(g_out_a)], axis=2)
+    dcomb1, sum_mlp_b, rest_b, rest_a = lax.optimization_barrier((dcomb1, sum_mlp_b, rest_b, rest_a))
+    sum_rest_b, sum_rest_a = scatter(rest_b), scatter(rest_a)
+    sum_mlp_b = reduce_clips(sum_mlp_b)
+    dx1, dpool1, g_qkv_a, rows_qv_a = attend_back(low1, dcomb1, own1, mem1, qkv_a, qv_a, mask, lse1, heads)
     own_back1, mem_back1 = give_back(dpool1, pick, own_rows, 3)
     stream_grad, rows_last = call(
         last_back_kernel, share,
         [(stream, 0), (res1, 0), (dx1, 0), (own_back1, 0), (mem_back1, 0), (padded_rows(gains_a[0]), None),
          (unpooling, None), (unpairing, None)],
-        [(shape((share, tokens, d1), bf16), 0), (shape((8, d1), f32), None)],
+        [(shape((share, frames, PATCH, d1), bf16), 0), (shape((8, d1), f32), None)],
         name="last_back",
     )
-
-    def by_owner(grad):
-        return grad.reshape((heads * toks, -1) + grad.shape[2:])
-
-    grad_q = by_owner(jnp.concatenate([by_head(g_qkv_b[:, i * d2:(i + 1) * d2], hb) for i in range(3)], axis=2))
-    grad_o = by_owner(jnp.concatenate([by_head(g_out_b, hb), by_head(g_skip_b, hs)], axis=2))
-    grad_a = by_owner(jnp.concatenate(
-        [g_up_a, g_down_a] + [by_head(g_qkv_a[:, i * d1:(i + 1) * d1], ha) for i in range(3)] + [by_head(g_out_a, ha)], axis=2))
-    rest = jnp.concatenate([grad_a, grad_q], axis=2)
-    rest, grad_o, sum_mlp_b = lax.optimization_barrier((rest, grad_o, sum_mlp_b))
-    sum_rest, sum_o = reduce_grad(rest).astype(f32), reduce_grad(grad_o).astype(f32)
-    sum_mlp_b = sum_mlp_b.astype(f32)
-    sum_a, sum_q = sum_rest[:, :grad_a.shape[2]], sum_rest[:, grad_a.shape[2]:]
 
     small = [
         jnp.stack([rows_last[0], rows_a[3], rows_a[0]]), rows_b[3],
@@ -930,8 +1039,15 @@
     ]
     flat = jnp.concatenate([piece.reshape(-1) for piece in small])
     flat = jnp.pad(flat, (0, -flat.size % 1024)).reshape(-1, 128)
-    stream_all, flat = finish(stream_grad, flat, 4)
+    sum_rest_b = reduce_clips(sum_rest_b)
+    flat, sum_mlp_b, sum_rest_b = lax.optimization_barrier((flat, sum_mlp_b, sum_rest_b))
+    mlp_b, rest_b = spread_clips(sum_mlp_b), spread_clips(sum_rest_b)
+    mlp_b = mlp_b.reshape((2, -1, mlp_b.shape[-1])).astype(f32)
+    rest_b = rest_b.astype(f32)
+    stream_all, flat, grad_qkv_a, rest_a = finish(stream_grad, flat, by_owner(g_qkv_a), sum_rest_a, 4)
     flat = flat.reshape(-1)
+    out_lanes = rest_b[:, 3 * hb:5 * hb]
+    skip_lanes = rest_b[:, 5 * hb:]
     pieces, at = [], 0
     for piece in small:
         pieces.append(flat[at:at + piece.size].reshape(piece.shape))
@@ -946,15 +1062,15 @@
     return (
         mixed_all.reshape(cotangent.shape),
         stream_all.astype(f32).reshape(clips_in.shape),
-        sum_a[:, 2 * fa:2 * fa + 3 * ha].reshape(w_qkv_a.shape),
-        sum_a[:, 2 * fa + 3 * ha:],
-        sum_a[:, :fa],
-        sum_a[:, fa:2 * fa],
-        sum_q.reshape(w_qkv_b.shape),
-        sum_o[:, :hb],
-        sum_o[:, hb:],
-        sum_mlp_b[0],
-        sum_mlp_b[1],
+        grad_qkv_a.reshape(w_qkv_a.shape),
+        rest_a[:, 2 * fa:],
+        rest_a[:, :fa],
+        rest_a[:, fa:2 * fa],
+        rest_b[:, :3 * hb].reshape(w_qkv_b.shape),
+        jnp.concatenate([out_lanes[:, :hb], out_lanes[:, hb:]], axis=0),
+        jnp.concatenate([skip_lanes[:, :hs], skip_lanes[:, hs:]], axis=0),
+        mlp_b[0],
+        mlp_b[1],
         pieces[0], pieces[1], pieces[2], pieces[3],
         mine(pieces[4], 1), mine(pieces[5], 1), mine(pieces[6].reshape(-1), 0), mine(pieces[7].reshape(-1), 0),
     )

time: 597 us -> 508 us (0.85)
  waiting for transfers between devices: 134 us -> 37.7 us
  local copies, waits for them, and re-layouts: 86.5 us -> 55.2 us
  starting transfers between devices: 1.89 us -> 29.3 us
  Pallas kernels: 327 us -> 344 us
    psum x2 -> x0, waiting for transfers between devices: 97.6 us -> none  [reduce_grad(): lax.psum(lax.psum_scatter(blocks, group, scatter_dimension=0, tiled=False...]
    reduce_scatter x3, waiting for transfers between devices: 27.9 us -> 0.02 us  [scatter(): return lax.psum_scatter(grad, group, scatter_dimension=0, tiled=False)]
    ppermute x0 -> x12, starting transfers between devices: none -> 24.4 us  [the longest x6 15 us: spread_clips(): lax.ppermute(piece, 'clip', [(i, (i + k) % clips) for i in range(clips)])]
    pallas_call x1, Pallas kernels: 41.2 us -> 62.4 us  [finish(): pl.pallas_call(finish_kernel, in_specs=[ANY, INVMEM, INVMEM, INVMEM], out...]
    all_gather x2, waiting for transfers between devices: 0.01 us -> 16.3 us  [the longest x1 16.2 us: local(): all_b = lax.all_gather(pack_b, group).reshape(heads, d2, -1)]
    ppermute x1 -> x2, waiting for transfers between devices: 0.01 us -> 13.4 us  [from_heads(): lax.ppermute(piece, 'head', [(i, (i + d) % heads) for i in range(heads)])]
    reshape x11 -> x3, local copies, waits for them, and re-layouts: 14.7 us -> 1.51 us  [the longest x1 0.79 us: local(): rest_b[:, :3 * hb].reshape(w_qkv_b.shape)]
    unnamed x96 -> x68, local copies, waits for them, and re-layouts: 23.7 us -> 10.6 us
  transfers between devices with their start and end apart: 9 -> 20, of which waited for: 4 -> 5; matrix products, arithmetic and copies ran while one was open for 15% -> 12% of each run, Pallas kernels for 51% -> 63%
where the time goes in v4:
time: 508 us; the launch traced here: 502 us
  Pallas kernels  344 us (68%)
  local copies, waits for them, and re-layouts  55.2 us (11%)
  waiting for transfers between devices  37.7 us (7%)
  starting transfers between devices  29.3 us (6%)
  between operations  21.8 us (4%)
  other arithmetic  13.9 us (3%)
    pallas_call x9, Pallas kernels, call(): pl.pallas_call(kernel, grid=(steps,), in_specs=[spec(a, how) for a, how i...  187 us
    pallas_call x1, Pallas kernels, finish(): pl.pallas_call(finish_kernel, in_specs=[ANY, INVMEM, INVMEM, INVMEM], out...  62.4 us
    pallas_call x2, Pallas kernels, give_back(): pl.pallas_call(give_back_kernel, in_specs=[ANY, INSMEM], out_specs=[INVME...  51.2 us
    pallas_call x2, Pallas kernels, share_pooled(): pl.pallas_call(share_kernel, in_specs=[INVMEM, INVMEM, INSMEM], out_specs...  43.3 us
    all_gather x1, waiting for transfers between devices, local(): all_b = lax.all_gather(pack_b, group).reshape(heads, d2, -1)  16.2 us
    ppermute x6, starting transfers between devices, spread_clips(): lax.ppermute(piece, 'clip', [(i, (i + k) % clips) for i in range(clips)])  15 us
    ppermute x2, waiting for transfers between devices, from_heads(): lax.ppermute(piece, 'head', [(i, (i + d) % heads) for i in range(heads)])  13.4 us
    unnamed x68, local copies, waits for them, and re-layouts  10.6 us
  transfers between devices with their start and end apart: 20, of which 5 were waited for; matrix products, arithmetic and copies ran while one was open for 12% of the time, Pallas kernels for 63%

profile of v4, /device:TPU:0, one launch (start us, length us, event | category | flops | bytes accessed | tf_op | source)
XLA Modules:
  0.0 502.2 jit_solution(4473929869035830520)
XLA Ops:
  18.3 4.3 norm_pool.1
  25.8 3.1 collective-permute-start
  37.4 20.4 %share_pooled.2 = (bf16[4,2,208,384]{3,2,1,0:T(8,128)(2,1)}, bf16[4,2,112,384]{3,2,1,0:T(8,128)(2,1)}) custom-call(bf16[2,208,384]{2,1,0:T(8,128)(2,1)} %get-tuple-element.80.pooled_ref, bf16[2,112,384]{2,1,0:T(8,128)(2,1)} %get-tuple-element.81.mean_ref, f32[2,4]{1,0:T(2,128)} %add_convert_fusion.pick_ref), custom_call_target="tpu_custom_call" | custom-call | tf_op jit(solution)/shard_map/share_pooled/pallas_call | solution.py:606
  64.6 20.9 %attend.2 = (bf16[2,784,384]{2,1,0:T(8,128)(2,1)}, f32[2,784,128]{2,1,0:T(8,128)}) custom-call(bf16[2,784,384]{2,1,0:T(8,128)(2,1)} %get-tuple-element.78.x_ref, bf16[4,2,208,384]{3,2,1,0:T(8,128)(2,1)} %get-tuple-element.82.own_ref, bf16[4,2,112,384]{3,2,1,0:T(8,128)(2,1)} %get-tuple-element.83.mem_ref, bf16[1,384,1152]{2,1,0:T(8,128)(2,1)} %bitcast.135, ...), custom_call_target="tpu_custom_call" | custom-call | tf_op jit(solution)/shard_map/attend/pallas_call | solution.py:439
  86.3 13.0 %first_mlp.1 = (f32[2,784,384]{2,1,0:T(8,128)}, f32[2,784,384]{2,1,0:T(8,128)}, bf16[2,208,384]{2,1,0:T(8,128)(2,1)}, bf16[2,112,384]{2,1,0:T(8,128)(2,1)}) custom-call(bf16[2,784,384]{2,1,0:T(8,128)(2,1)} %reshape.266.x_ref, bf16[2,784,384]{2,1,0:T(8,128)(2,1)} %get-tuple-element.86.comb_ref, bf16[384,384]{1,0:T(8,128)(2,1)} %pad_maximum_fusion.3.out_ref, ...), custom_call_target="tpu_custom_call" | custom-call | tf_op jit(solution)/shard_map/first_mlp/pallas_call | solution.py:439
  99.3 22.9 %share_pooled.3 = (bf16[4,2,208,384]{3,2,1,0:T(8,128)(2,1)}, bf16[4,2,112,384]{3,2,1,0:T(8,128)(2,1)}) custom-call(bf16[2,208,384]{2,1,0:T(8,128)(2,1)} %get-tuple-element.87.pooled_ref.x_ref, bf16[2,112,384]{2,1,0:T(8,128)(2,1)} %get-tuple-element.88.mean_ref, f32[2,4]{1,0:T(2,128)} %add_convert_fusion.pick_ref), custom_call_target="tpu_custom_call" | custom-call | tf_op jit(solution)/shard_map/share_pooled/pallas_call | solution.py:606
  122.2 18.7 %attend.3 = (bf16[2,208,768]{2,1,0:T(8,128)(2,1)}, f32[2,208,128]{2,1,0:T(8,128)}) custom-call(bf16[2,208,384]{2,1,0:T(8,128)(2,1)} %get-tuple-element.87.pooled_ref.x_ref, bf16[4,2,208,384]{3,2,1,0:T(8,128)(2,1)} %get-tuple-element.89.own_ref, bf16[4,2,112,384]{3,2,1,0:T(8,128)(2,1)} %get-tuple-element.90.mem_ref, bf16[2,384,1152]{2,1,0:T(8,128)(2,1)} %bitcast.137, ...), custom_call_target="tpu_custom_call" | custom-call | tf_op jit(solution)/shard_map/attend/pallas_call | solution.py:439
  140.9 16.2 %all-gather.11.cloned.1.call-done = bf16[1536,3648]{1,0:T(8,128)(2,1)} async-done(((bf16[192,3648]{1,0:T(8,128)(2,1)}), bf16[1536,3648]{1,0:T(8,128)(2,1)}) %all-gather.11.cloned.1.call-update) | async-done | bytes 11206672 | tf_op jit(solution)/shard_map/all_gather | solution.py:942
  159.3 26.0 %second_mlp.1 = (bf16[416,768]{1,0:T(8,128)(2,1)}, bf16[416,768]{1,0:T(8,128)(2,1)}, f32[416,384]{1,0:T(8,128)}, bf16[2,4,2,192,1536]{4,3,2,1,0:T(8,128)(2,1)}, ...) custom-call(bf16[416,768]{1,0:T(8,128)(2,1)} %bitcast.157, ...), custom_call_target="tpu_custom_call" | custom-call | tf_op jit(solution)/shard_map/second_mlp/pallas_call | solution.py:439
  185.4 34.3 %attend_back.2 = (f32[2,208,384]{2,1,0:T(8,128)}, bf16[4,2,320,384]{3,2,1,0:T(8,128)(2,1)}, bf16[2,384,1152]{2,1,0:T(8,128)(2,1)}, f32[8,768]{1,0:T(8,128)}) custom-call(bf16[2,208,384]{2,1,0:T(8,128)(2,1)} %get-tuple-element.87.pooled_ref.x_ref, bf16[2,208,768]{2,1,0:T(8,128)(2,1)} %bitcast.159, bf16[4,2,208,384]{3,2,1,0:T(8,128)(2,1)} %get-tuple-element.89.own_ref, ...), custom_call_target="tpu_custom_call" | custom-call | tf_op jit(solution)/shard_map/attend_back/pallas_call | solution.py:439
  219.7 28.3 %give_back.2 = (f32[2,208,384]{2,1,0:T(8,128)}, f32[2,112,384]{2,1,0:T(8,128)}) custom-call(bf16[4,2,320,384]{3,2,1,0:T(8,128)(2,1)} %get-tuple-element.101.part_ref, f32[2,4]{1,0:T(2,128)} %add_convert_fusion.pick_ref), custom_call_target="tpu_custom_call" | custom-call | tf_op jit(solution)/shard_map/give_back/pallas_call | solution.py:712
  250.4 5.4 %concatenate.66 = bf16[8,96,2304]{2,1,0:T(8,128)(2,1)} concatenate(bf16[8,96,1152]{2,1,0:T(8,128)(2,1)S(1)} %bitcast.146, bf16[8,96,384]{2,1,0:T(8,128)(2,1)S(1)} %get-tuple-element.193, bf16[8,96,384]{2,1,0:T(8,128)(2,1)S(1)} %get-tuple-element.192, bf16[8,96,192]{2,1,0:T(8,128)(2,1)} %get-tuple-element.199, bf16[8,96,192]{2,1,0:T(8,128)(2,1)S(1)} %get-tuple-element.198), dimensions={2} | concatenate | bytes 7077888 | tf_op jit(solution)/shard_map/concatenate | solution.py:1019
  255.8 26.9 %first_back.1 = (f32[2,784,384]{2,1,0:T(8,128)}, bf16[2,784,384]{2,1,0:T(8,128)(2,1)}, bf16[2,384,1536]{2,1,0:T(8,128)(2,1)}, bf16[2,384,192]{2,1,0:T(8,128)(2,1...) custom-call(f32[2,784,384]{2,1,0:T(8,128)} %get-tuple-element.95.middle_ref, f32[2,784,384]{2,1,0:T(8,128)} %get-tuple-element.96.after_ref, ...), custom_call_target="tpu_custom_call" | custom-call | tf_op jit(solution)/shard_map/first_back/pallas_call | solution.py:439
  282.7 3.6 pad_maximum_fusion
  291.4 13.4 %collective-permute-done.1 = bf16[2,196,768]{2,0,1:T(2,128)(2,1)S(1)} collective-permute-done((bf16[2,196,768]{2,0,1:T(2,128)(2,1)S(1)}, bf16[2,196,768]{2,0,1:T(2,128)(2,1)S(1)}, u32[]{:S(2)}, u32[]{:S(2)}) %collective-permute-start.1) | collective-permute-done | bytes 602144 | tf_op jit(solution)/shard_map/ppermute | solution.py:882
  313.6 37.2 %attend_back.3 = (f32[2,784,384]{2,1,0:T(8,128)}, bf16[4,2,320,384]{3,2,1,0:T(8,128)(2,1)}, bf16[2,384,576]{2,1,0:T(8,128)(2,1)}, f32[8,384]{1,0:T(8,128)}) custom-call(bf16[2,784,384]{2,1,0:T(8,128)(2,1)} %get-tuple-element.78.x_ref, bf16[2,784,384]{2,1,0:T(8,128)(2,1)} %get-tuple-element.112.g_ref, bf16[4,2,208,384]{3,2,1,0:T(8,128)(2,1)} %get-tuple-element.82.own_ref, ...), custom_call_target="tpu_custom_call" | custom-call | tf_op jit(solution)/shard_map/attend_back/pallas_call | solution.py:439
  350.8 22.9 %give_back.3 = (f32[2,208,384]{2,1,0:T(8,128)}, f32[2,112,384]{2,1,0:T(8,128)}) custom-call(bf16[4,2,320,384]{3,2,1,0:T(8,128)(2,1)} %get-tuple-element.115.part_ref, f32[2,4]{1,0:T(2,128)} %add_convert_fusion.pick_ref), custom_call_target="tpu_custom_call" | custom-call | tf_op jit(solution)/shard_map/give_back/pallas_call | solution.py:712
  373.8 6.1 %last_back.1 = (bf16[2,4,196,384]{3,2,1,0:T(8,128)(2,1)}, f32[8,384]{1,0:T(8,128)}) custom-call(bf16[2,784,384]{2,1,0:T(8,128)(2,1)} %reshape.266.x_ref, f32[2,784,384]{2,1,0:T(8,128)} %get-tuple-element.104.res_ref, f32[2,784,384]{2,1,0:T(8,128)} %get-tuple-element.114.dx_ref, f32[2,208,384]{2,1,0:T(8,128)} %get-tuple-element.116.own_ref, ...), custom_call_target="tpu_custom_call" | custom-call | tf_op jit(solution)/shard_map/last_back/pallas_call | solution.py:439
  383.6 3.5 collective-permute-start.7
  391.1 3.5 collective-permute-done.6
  395.5 3.0 collective-permute-start.11
  403.4 62.4 %finish.1 = (bf16[2,2,4,196,384]{4,3,2,1,0:T(8,128)(2,1)}, f32[104,128]{1,0:T(8,128)}, f32[96,576]{1,0:T(8,128)}, f32[4,32,1728]{2,1,0:T(8,128)}) custom-call(bf16[2,4,196,384]{3,2,1,0:T(8,128)(2,1)} %get-tuple-element.118.half_ref, f32[104,128]{1,0:T(8,128)} %pad_bitcast_fusion.small_ref, bf16[8,96,576]{2,1,0:T(8,128)(2,1)} %bitcast.154, ...), custom_call_target="tpu_custom_call" | custom-call | tf_op jit(solution)/shard_map/finish/pallas_call | solution.py:837
  470.5 3.5 copy.60
  479.4 7.1 %collective-permute-start.10 = (bf16[24,2304]{1,0:T(8,128)(2,1)S(1)}, bf16[24,2304]{1,0:T(8,128)(2,1)S(1)}, u32[]{:S(2)}, u32[]{:S(2)}) collective-permute-start(bf16[24,2304]{1,0:T(8,128)(2,1)S(1)} %fusion.5), channel_id=1, source_target_pairs={{0,24},{8,0},{16,8},{24,16},{1,25},{9,1},{17,9},{25,17},{2,26},{10... | collective-permute-start | bytes 331784 | tf_op jit(solution)/shard_map/ppermute | solution.py:872
  (238 shorter events, 73.8 us)
Async XLA Ops:
  7.2 27.1 %copy-start = (bf16[1,4,4,49,768]{4,2,3,1,0:T(4,128)(2,1)S(1)}, bf16[1,4,4,49,768]{4,2,3,1,0:T(4,128)(2,1)}, u32[]{:S(2)}) copy-start(bf16[1,4,4,49,768]{4,2,3,1,0:T(4,128)(2,1)} %param.45) | copy-start | bytes 3612676
  7.2 54.1 %all-gather.7.cloned.1.call-start = ((), (), s32[]{:S(2)}) async-start(), calls=%async_computation.6 | async-start | bytes 3981312 | tf_op jit(solution)/shard_map/all_gather | solution.py:929
  10.5 111.7 %all-gather.9.cloned.1.call-start = ((), (), s32[]{:S(2)}) async-start(), calls=%async_computation.7 | async-start | bytes 1990656 | tf_op jit(solution)/shard_map/all_gather | solution.py:941
  24.9 9.2 %copy-start.21 = (f32[768]{0:T(1024)S(1)}, f32[768]{0:T(1024)}, u32[]{:S(2)}) copy-start(f32[768]{0:T(1024)} %param.38) | copy-start | bytes 9220
  25.0 9.6 %slice-start = ((f32[3,768]{1,0:T(4,128)}), f32[1,768]{1,0:T(1,128)S(1)}, s32[]{:S(2)}) async-start(f32[3,768]{1,0:T(4,128)} %param.40), calls=%async_computation.9 | async-start | bytes 6144 | tf_op jit(solution)/shard_map/slice | solution.py:985
  25.0 132.2 %all-gather.11.cloned.1.call-start = ((), (), s32[]{:S(2)}) async-start(), calls=%async_computation.8 | async-start | bytes 12828672 | tf_op jit(solution)/shard_map/all_gather | solution.py:942
  25.7 260.6 %reduce-scatter.4.cloned.1.call-start = ((), (), s32[]{:S(2)}) async-start(), calls=%async_computation.3 | async-start | bytes 10616832 | tf_op jit(solution)/shard_map/reduce_scatter | solution.py:999
  25.8 32.7 %collective-permute-start = (f32[1,3456]{1,0:T(1,128)S(1)}, f32[1,3456]{1,0:T(1,128)S(1)}, u32[]{:S(2)}, u32[]{:S(2)}) collective-permute-start(f32[1,3456]{1,0:T(1,128)S(1)} %reshape.272), channel_id=1, source_target_pairs={{0,1},{1,0},{2,3},{3,2},{4,5},{5,4},{6,7},{7,6},{8,9},{9,8},{10,11... | collective-permute-start | bytes 41480 | tf_op jit(solution)/shard_map/ppermute | solution.py:882
  185.4 196.8 %reduce-scatter.6.cloned.1.call-start = ((), (), s32[]{:S(2)}) async-start(), calls=%async_computation.4 | async-start | bytes 3981312 | tf_op jit(solution)/shard_map/reduce_scatter | solution.py:999
  219.7 28.3 %copy-start.6 = (bf16[2,768,192]{2,1,0:T(8,128)(2,1)S(1)}, bf16[2,768,192]{2,1,0:T(8,128)(2,1)}, u32[]{:S(2)}) copy-start(bf16[2,768,192]{2,1,0:T(8,128)(2,1)} %get-tuple-element.109) | copy-start | bytes 1769476
  286.3 102.1 %reduce-scatter.8.cloned.1.call-start = ((), (), s32[]{:S(2)}) async-start(), calls=%async_computation.5 | async-start | bytes 3096576 | tf_op jit(solution)/shard_map/reduce_scatter | solution.py:999
  288.9 15.8 %collective-permute-start.1 = (bf16[2,196,768]{2,0,1:T(2,128)(2,1)S(1)}, bf16[2,196,768]{2,0,1:T(2,128)(2,1)S(1)}, u32[]{:S(2)}, u32[]{:S(2)}) collective-permute-start(bf16[2,196,768]{2,0,1:T(2,128)(2,1)S(1)} %get-tuple-element.176), channel_id=1, source_target_pairs={{0,1},{1,0},{2,3},{3,2},{4,5},{5,4},{6,7},{7,6},{8,9},{9,8},{10,11... | collective-permute-start | bytes 1806344 | tf_op jit(solution)/shard_map/ppermute | solution.py:882
  308.1 75.5 %collective-permute-start.2 = (bf16[96,1536]{1,0:T(8,128)(2,1)}, bf16[96,1536]{1,0:T(8,128)(2,1)}, u32[]{:S(2)}, u32[]{:S(2)}) collective-permute-start(bf16[96,1536]{1,0:T(8,128)(2,1)} %get-tuple-element.189), channel_id=1, source_target_pairs={{0,8},{8,16},{16,24},{24,0},{1,9},{9,17},{17,25},{25,1},{2,10},{10... | collective-permute-start | bytes 884744 | tf_op jit(solution)/shard_map/ppermute | solution.py:863
  309.8 77.3 %collective-permute-start.3 = (bf16[96,1536]{1,0:T(8,128)(2,1)S(1)}, bf16[96,1536]{1,0:T(8,128)(2,1)}, u32[]{:S(2)}, u32[]{:S(2)}) collective-permute-start(bf16[96,1536]{1,0:T(8,128)(2,1)S(1)} %get-tuple-element.191), channel_id=1, source_target_pairs={{0,16},{8,24},{16,0},{24,8},{1,17},{9,25},{17,1},{25,9},{2,18},{10... | collective-permute-start | bytes 884744 | tf_op jit(solution)/shard_map/ppermute | solution.py:863
  312.1 74.9 %collective-permute-start.4 = (bf16[96,1536]{1,0:T(8,128)(2,1)S(1)}, bf16[96,1536]{1,0:T(8,128)(2,1)}, u32[]{:S(2)}, u32[]{:S(2)}) collective-permute-start(bf16[96,1536]{1,0:T(8,128)(2,1)S(1)} %get-tuple-element.190), channel_id=1, source_target_pairs={{0,24},{8,0},{16,8},{24,16},{1,25},{9,1},{17,9},{25,17},{2,26},{10... | collective-permute-start | bytes 884744 | tf_op jit(solution)/shard_map/ppermute | solution.py:863
  383.2 7.9 %collective-permute-start.5 = (bf16[24,2304]{1,0:T(8,128)(2,1)S(1)}, bf16[24,2304]{1,0:T(8,128)(2,1)S(1)}, u32[]{:S(2)}, u32[]{:S(2)}) collective-permute-start(bf16[24,2304]{1,0:T(8,128)(2,1)S(1)} %get-tuple-element.202), channel_id=1, source_target_pairs={{0,8},{8,16},{16,24},{24,0},{1,9},{9,17},{17,25},{25,1},{2,10},{10... | collective-permute-start | bytes 331784 | tf_op jit(solution)/shard_map/ppermute | solution.py:863
  383.6 11.0 %collective-permute-start.6 = (bf16[24,2304]{1,0:T(8,128)(2,1)S(1)}, bf16[24,2304]{1,0:T(8,128)(2,1)S(1)}, u32[]{:S(2)}, u32[]{:S(2)}) collective-permute-start(bf16[24,2304]{1,0:T(8,128)(2,1)S(1)} %get-tuple-element.204), channel_id=1, source_target_pairs={{0,16},{8,24},{16,0},{24,8},{1,17},{9,25},{17,1},{25,9},{2,18},{10... | collective-permute-start | bytes 331784 | tf_op jit(solution)/shard_map/ppermute | solution.py:863
  383.6 11.0 %collective-permute-start.7 = (bf16[24,2304]{1,0:T(8,128)(2,1)S(1)}, bf16[24,2304]{1,0:T(8,128)(2,1)S(1)}, u32[]{:S(2)}, u32[]{:S(2)}) collective-permute-start(bf16[24,2304]{1,0:T(8,128)(2,1)S(1)} %get-tuple-element.203), channel_id=1, source_target_pairs={{0,24},{8,0},{16,8},{24,16},{1,25},{9,1},{17,9},{25,17},{2,26},{10... | collective-permute-start | bytes 331784 | tf_op jit(solution)/shard_map/ppermute | solution.py:863
  395.5 95.8 %collective-permute-start.11 = (bf16[96,1536]{1,0:T(8,128)(2,1)S(1)}, bf16[96,1536]{1,0:T(8,128)(2,1)}, u32[]{:S(2)}, u32[]{:S(2)}) collective-permute-start(bf16[96,1536]{1,0:T(8,128)(2,1)S(1)} %fusion.2), channel_id=1, source_target_pairs={{0,8},{8,16},{16,24},{24,0},{1,9},{9,17},{17,25},{25,1},{2,10},{10... | collective-permute-start | bytes 884744 | tf_op jit(solution)/shard_map/ppermute | solution.py:872
  398.5 93.9 %collective-permute-start.12 = (bf16[96,1536]{1,0:T(8,128)(2,1)S(1)}, bf16[96,1536]{1,0:T(8,128)(2,1)}, u32[]{:S(2)}, u32[]{:S(2)}) collective-permute-start(bf16[96,1536]{1,0:T(8,128)(2,1)S(1)} %fusion.2), channel_id=1, source_target_pairs={{0,16},{8,24},{16,0},{24,8},{1,17},{9,25},{17,1},{25,9},{2,18},{10... | collective-permute-start | bytes 884744 | tf_op jit(solution)/shard_map/ppermute | solution.py:872
  398.8 94.5 %collective-permute-start.13 = (bf16[96,1536]{1,0:T(8,128)(2,1)S(1)}, bf16[96,1536]{1,0:T(8,128)(2,1)S(1)}, u32[]{:S(2)}, u32[]{:S(2)}) collective-permute-start(bf16[96,1536]{1,0:T(8,128)(2,1)S(1)} %fusion.2), channel_id=1, source_target_pairs={{0,24},{8,0},{16,8},{24,16},{1,25},{9,1},{17,9},{25,17},{2,26},{10... | collective-permute-start | bytes 884744 | tf_op jit(solution)/shard_map/ppermute | solution.py:872
  400.9 78.5 %collective-permute-start.8 = (bf16[24,2304]{1,0:T(8,128)(2,1)S(1)}, bf16[24,2304]{1,0:T(8,128)(2,1)S(1)}, u32[]{:S(2)}, u32[]{:S(2)}) collective-permute-start(bf16[24,2304]{1,0:T(8,128)(2,1)S(1)} %fusion.5), channel_id=1, source_target_pairs={{0,8},{8,16},{16,24},{24,0},{1,9},{9,17},{17,25},{25,1},{2,10},{10... | collective-permute-start | bytes 331784 | tf_op jit(solution)/shard_map/ppermute | solution.py:872
  400.9 85.6 %collective-permute-start.9 = (bf16[24,2304]{1,0:T(8,128)(2,1)S(1)}, bf16[24,2304]{1,0:T(8,128)(2,1)S(1)}, u32[]{:S(2)}, u32[]{:S(2)}) collective-permute-start(bf16[24,2304]{1,0:T(8,128)(2,1)S(1)} %fusion.5), channel_id=1, source_target_pairs={{0,16},{8,24},{16,0},{24,8},{1,17},{9,25},{17,1},{25,9},{2,18},{10... | collective-permute-start | bytes 331784 | tf_op jit(solution)/shard_map/ppermute | solution.py:872
  479.4 9.4 %collective-permute-start.10 = (bf16[24,2304]{1,0:T(8,128)(2,1)S(1)}, bf16[24,2304]{1,0:T(8,128)(2,1)S(1)}, u32[]{:S(2)}, u32[]{:S(2)}) collective-permute-start(bf16[24,2304]{1,0:T(8,128)(2,1)S(1)} %fusion.5), channel_id=1, source_target_pairs={{0,24},{8,0},{16,8},{24,16},{1,25},{9,1},{17,9},{25,17},{2,26},{10... | collective-permute-start | bytes 331784 | tf_op jit(solution)/shard_map/ppermute | solution.py:872
  (24 other events, 82.2 us)
Sparse Core Ops, SparseCore 0:
  10.6 40.3 all-gather.6
  53.4 27.7 all-gather.8
  83.7 73.3 all-gather.10
  185.5 86.9 reduce-scatter.3
  286.4 48.5 reduce-scatter.5
  338.2 47.5 reduce-scatter.7

commit v5 on v4

--- a/solution.py
+++ b/solution.py
@@ -143,8 +143,10 @@
         q_s[:, low:low + 384] = (value + bias_ref[0:1, low:low + 384]).astype(bf16)
 
 
-def norm_pool_kernel(x_ref, vec_ref, pool_ref, pair_ref, low_ref, pooled_ref, mean_ref):
-    unit, _ = norm(x_ref[0].astype(f32))
+def norm_pool_kernel(first_ref, clips_ref, vec_ref, pool_ref, pair_ref, x_ref, low_ref, pooled_ref, mean_ref):
+    x = jnp.concatenate([clips_ref[0, 0, f].astype(f32) for f in range(clips_ref.shape[2])], axis=0)
+    x_ref[0] = x.astype(bf16)
+    unit, _ = norm(x)
     normed = unit * vec_ref[0:1, :] + vec_ref[1:2, :]
     low_ref[0] = normed.astype(bf16)
     pooled = exact_dot(pool_ref[...], normed)
@@ -347,17 +349,22 @@
         for h in range(out_ref.shape[0]):
             here = slice(wide * h, wide * h + wide)
             dcomb_ref[:, here] = dot(res, out_ref[h]).astype(bf16)
-            gout_ref[h] = dot(rest, comb_ref[:, here]).astype(bf16)
+            grad = dot(rest, comb_ref[:, here])
+            half = gout_ref.shape[2]
+            for n in range(2 * gout_ref.shape[1]):
+                gout_ref[h, n // 2, :, wide * (n % 2):wide * (n % 2) + wide] = grad[half * n:half * n + half].astype(bf16)
         grad = dot(rest, pooled_ref[...])
-        wide = gskip_ref.shape[2]
+        wide = gskip_ref.shape[3] // 2
         for h in range(gskip_ref.shape[0]):
-            gskip_ref[h] = grad[:, wide * h:wide * h + wide].astype(bf16)
+            for t in range(gskip_ref.shape[1]):
+                low, high = (grad[half * n:half * n + half, wide * h:wide * h + wide] for n in (2 * t, 2 * t + 1))
+                gskip_ref[h, t] = jnp.concatenate([low, high], axis=1).astype(bf16)
 
 
 def first_back_kernel(
     middle_ref, after_ref, comb_ref, dskip_ref, dq_ref, own_ref, mem_ref, out_ref, up_ref, down_ref, ub_ref, vec_ref,
     unpool_ref, unpair_ref,
-    res_ref, dcomb_ref, gmlp_ref, gout_ref, gub_ref, row_ref,
+    res_ref, dcomb_ref, gmlp_ref, gub_ref, row_ref,
     gup_s, gdown_s, gout_s,
 ):
     step = pl.program_id(0)
@@ -400,11 +407,13 @@
 
     @pl.when(step == pl.num_programs(0) - 1)
     def _():
-        fa, ha = gmlp_ref.shape[2] // 2, gout_ref.shape[2]
+        fa, ha = gup_s.shape[2], gout_s.shape[1] // gmlp_ref.shape[0]
         for h in range(gmlp_ref.shape[0]):
             gmlp_ref[h, :, :fa] = gup_s[h].astype(bf16)
-            gmlp_ref[h, :, fa:] = gdown_s[h].astype(bf16)
-            gout_ref[h] = gout_s[:, ha * h:ha * h + ha].astype(bf16)
+            gmlp_ref[h, :, fa:2 * fa] = gdown_s[h].astype(bf16)
+            rest = gmlp_ref.shape[2] - 2 * fa - ha
+            gout = jnp.concatenate([gout_s[:, ha * h:ha * h + ha], jnp.zeros((gout_s.shape[0], rest), f32)], axis=1)
+            gmlp_ref[h, :, 2 * fa:] = gout.astype(bf16)
 
 
 def last_back_kernel(x_ref, res_ref, dx_ref, own_ref, mem_ref, vec_ref, unpool_ref, unpair_ref, grad_ref, row_ref):
@@ -513,19 +522,23 @@
     return lax.rem(a + n, n)
 
 
-def share_kernel(pooled_ref, mean_ref, pick_ref, own_ref, mem_ref, got_s, pick_s, local_sem, own_send, own_recv, mem_send, mem_recv,
-                 pass_send, pass_recv, clip_send, clip_recv):
+def share_kernel(gather, *refs):
+    if gather:
+        pooled_ref, mean_ref, pick_ref, w_ref, own_ref, mem_ref, all_ref, *refs = refs
+    else:
+        pooled_ref, mean_ref, pick_ref, own_ref, mem_ref, *refs = refs
+    (got_s, pick_s, local_sem, own_send, own_recv, mem_send, mem_recv, pass_send, pass_recv, clip_send, clip_recv, *refs) = refs
     clip, head, chip, core, chips = places()
     clips, heads = lax.axis_size("clip"), lax.axis_size("head")
     share = pooled_ref.shape[0]
     here = 2 * chip + core
     partner = {"tok": 2 * chip + 1 - core}
     across = [{"tok": 2 * rem(chip + k, chips) + core} for k in range(1, chips)]
+    beside = [{"head": rem(head + d, heads)} for d in range(1, heads)]
     heads_of = lambda by, sign: [{"clip": clip + by, "head": rem(head + sign * d, heads)} for d in range(heads)]
     last, begun = clip < clips - 1, clip > 0
-    to = [(partner, None)] + [(d, None) for d in across] + [(d, last) for d in heads_of(1, 1)]
-    fro = [(partner, None)] + [(d, None) for d in across] + [(d, begun) for d in heads_of(-1, -1)]
-    greet(fro, to)
+    near = [(d, None) for d in [partner] + across + (beside if gather else [])]
+    greet(near + [(d, begun) for d in heads_of(-1, -1)], near + [(d, last) for d in heads_of(1, 1)])
 
     def spread(src, out, send, recv):
         copies = [remote(src, out.at[here], send.at[0], recv.at[0], partner)]
@@ -542,12 +555,39 @@
     def _():
         for copy in clip_copies:
             copy.start()
+
+    w_first, w_diagonal, w_core = {}, {}, {}
+    if gather:
+        w_local, w_send, w_recv, d_send, d_recv, c_send, c_recv = refs
+        mine = all_ref.at[head, here]
+        for k in range(1, chips):
+            w_first[k, 0] = remote(w_ref, mine, w_send.at[k - 1], w_recv.at[k - 1], across[k - 1])
+        for d in range(1, heads):
+            w_first[0, d] = remote(w_ref, mine, w_send.at[chips - 2 + d], w_recv.at[chips - 2 + d], beside[d - 1])
+        w_core[0, 0] = remote(w_ref, mine, c_send.at[0, 0], c_recv.at[0, 0], partner)
+        for copy in [*w_first.values(), w_core[0, 0]]:
+            copy.start()
+        w_copy = pltpu.make_async_copy(w_ref, mine, w_local.at[0])
+        w_copy.start()
+
+        def forward(k, d):
+            block = all_ref.at[rem(head - d, heads), 2 * rem(chip - k, chips) + core]
+            w_core[k, d] = remote(block, block, c_send.at[k, d], c_recv.at[k, d], partner)
+            w_core[k, d].start()
 
     own_copies = spread(pooled_ref, own_ref, own_send, own_recv)
     for copy in own_copies[1:] + own_copies[:1]:
         copy.start()
     own_local = pltpu.make_async_copy(pooled_ref, own_ref.at[here], local_sem.at[0])
     own_local.start()
+    if gather:
+        for k in range(1, chips):
+            w_first[k, 0].wait_recv()
+            block = all_ref.at[head, 2 * rem(chip - k, chips) + core]
+            for d in range(1, heads):
+                w_diagonal[k, d] = remote(block, block, d_send.at[k - 1, d - 1], d_recv.at[k - 1, d - 1], beside[d - 1])
+                w_diagonal[k, d].start()
+            forward(k, 0)
 
     @pl.when(begun)
     def _():
@@ -571,19 +611,34 @@
     mem_local = pltpu.make_async_copy(pick_s, mem_ref.at[here], local_sem.at[1])
     mem_local.start()
     forwards = []
-    for row, (copies, out) in enumerate(((own_copies, own_ref), (mem_copies, mem_ref))):
-        for k in range(1, chips):
-            copies[k].wait_recv()
-            forwards.append(passed(out, k, row))
-            forwards[-1].start()
+    for k in range(1, chips):
+        own_copies[k].wait_recv()
+        forwards.append(passed(own_ref, k, 0))
+        forwards[-1].start()
+    if gather:
+        for d in range(1, heads):
+            w_first[0, d].wait_recv()
+            forward(0, d)
+    for k in range(1, chips):
+        mem_copies[k].wait_recv()
+        forwards.append(passed(mem_ref, k, 1))
+        forwards[-1].start()
+    if gather:
+        for k, d in w_diagonal:
+            w_diagonal[k, d].wait_recv()
+            forward(k, d)
+        for copy in w_core.values():
+            copy.wait_recv()
     own_copies[0].wait_recv()
     mem_copies[0].wait_recv()
     for copy in forwards:
         copy.wait_recv()
-    for copy in own_copies + mem_copies + forwards:
+    for copy in own_copies + mem_copies + forwards + [*w_first.values(), *w_diagonal.values(), *w_core.values()]:
         copy.wait_send()
     own_local.wait()
     mem_local.wait()
+    if gather:
+        w_copy.wait()
 
     @pl.when(last)
     def _():
@@ -600,36 +655,49 @@
     return pltpu.SemaphoreType.DMA(dims)
 
 
-def share_pooled(pooled, mean, pick, number):
+def share_pooled(pooled, mean, pick, number, block=None):
     toks, heads = lax.axis_size("tok"), lax.axis_size("head")
     chips = toks // 2
+    few = max(chips - 1, 1)
+    args, specs = [pooled, mean, pick], [INVMEM, INVMEM, INSMEM]
+    outs = [shape((toks,) + pooled.shape, bf16), shape((toks,) + mean.shape, bf16)]
+    scratch = [
+        pltpu.VMEM((heads,) + mean.shape, bf16), pltpu.VMEM(mean.shape, bf16), dma(2),
+        dma(chips), dma(chips), dma(chips), dma(chips), dma(2, few), dma(2, few), dma(heads), dma(heads),
+    ]
+    if block is not None:
+        args, specs, outs = args + [block], specs + [ANY], outs + [shape((heads, toks) + block.shape, bf16)]
+        firsts = max(chips + heads - 2, 1)
+        scratch += [dma(1), dma(firsts), dma(firsts), dma(few, max(heads - 1, 1)), dma(few, max(heads - 1, 1)), dma(chips, heads), dma(chips, heads)]
     return pl.pallas_call(
-        share_kernel,
-        in_specs=[INVMEM, INVMEM, INSMEM],
-        out_specs=[ANY, ANY],
-        out_shape=[shape((toks,) + pooled.shape, bf16), shape((toks,) + mean.shape, bf16)],
-        scratch_shapes=[
-            pltpu.VMEM((heads,) + mean.shape, bf16), pltpu.VMEM(mean.shape, bf16), dma(2),
-            dma(chips), dma(chips), dma(chips), dma(chips),
-            dma(2, max(chips - 1, 1)), dma(2, max(chips - 1, 1)), dma(heads), dma(heads),
-        ],
+        functools.partial(share_kernel, block is not None),
+        in_specs=specs,
+        out_specs=[ANY] * len(outs),
+        out_shape=outs,
+        scratch_shapes=scratch,
         compiler_params=pltpu.CompilerParams(collective_id=number, has_side_effects=True, vmem_limit_bytes=VMEM_CAP),
         name="share_pooled",
-    )(pooled, mean, pick)
-
-
-def give_back_kernel(part_ref, pick_ref, own_ref, back_ref, mine_s, core_s, sum_s, chip_s, route_s, got_s,
-                     local_sem, core_send, core_recv, mem_send, mem_recv, own_send, own_recv, clip_send, clip_recv):
+    )(*args)
+
+
+def give_back_kernel(exchange, *refs):
+    if exchange:
+        part_ref, pick_ref, half_ref, own_ref, back_ref, all_ref, *refs = refs
+        *refs, half_local, half_send, half_recv = refs
+    else:
+        part_ref, pick_ref, own_ref, back_ref, *refs = refs
+    (mine_s, core_s, sum_s, chip_s, route_s, got_s,
+     local_sem, core_send, core_recv, mem_send, mem_recv, own_send, own_recv, clip_send, clip_recv) = refs
     clip, head, chip, core, chips = places()
     clips, heads = lax.axis_size("clip"), lax.axis_size("head")
     share, rows = own_ref.shape[0], own_ref.shape[1]
     partner = {"tok": 2 * chip + 1 - core}
     across = [{"tok": 2 * rem(chip + k, chips) + core} for k in range(1, chips)]
+    beside = [{"head": rem(head + d, heads)} for d in range(1, heads)]
     heads_of = lambda by, sign: [{"clip": clip + by, "head": rem(head + sign * d, heads)} for d in range(heads)]
     last, begun = clip < clips - 1, clip > 0
-    to = [(partner, None)] + [(d, None) for d in across] + [(d, begun) for d in heads_of(-1, -1)]
-    fro = [(partner, None)] + [(d, None) for d in across] + [(d, last) for d in heads_of(1, 1)]
-    greet(fro, to)
+    near = [(d, None) for d in [partner] + across + (beside if exchange else [])]
+    greet(near + [(d, last) for d in heads_of(1, 1)], near + [(d, begun) for d in heads_of(-1, -1)])
 
     order = [rem(chip + k, chips) for k in list(range(1, chips)) + [0]]
     core_copies, local_copies = [], []
@@ -639,6 +707,13 @@
     for n, other in enumerate(order):
         local_copies.append(pltpu.make_async_copy(part_ref.at[2 * other + core], mine_s.at[n], local_sem.at[n]))
         local_copies[-1].start()
+    halves = []
+    if exchange:
+        halves = [remote(half_ref, all_ref.at[head], half_send.at[k], half_recv.at[k], d) for k, d in enumerate(beside)]
+        for copy in halves:
+            copy.start()
+        half_copy = pltpu.make_async_copy(half_ref, all_ref.at[head], half_local.at[0])
+        half_copy.start()
     mem_copies, own_copies = [], []
     for n in range(chips):
         local_copies[n].wait()
@@ -696,8 +771,12 @@
     def _():
         back_ref[...] = jnp.zeros_like(back_ref)
 
-    for copy in core_copies + mem_copies + own_copies:
+    for copy in halves:
+        copy.wait_recv()
+    for copy in core_copies + mem_copies + own_copies + halves:
         copy.wait_send()
+    if exchange:
+        half_copy.wait()
 
     @pl.when(begun)
     def _():
@@ -705,28 +784,36 @@
             copy.wait_send()
 
 
-def give_back(part, pick, own_rows, number):
+def give_back(part, pick, own_rows, number, half=None):
     toks, heads = lax.axis_size("tok"), lax.axis_size("head")
     chips, few = toks // 2, max(toks // 2 - 1, 1)
     share, rows, d = part.shape[1:]
+    args, specs = [part, pick], [ANY, INSMEM]
+    outs, out_specs = [shape((share, own_rows, d), f32), shape((share, rows - own_rows, d), f32)], [INVMEM, INVMEM]
+    scratch = [
+        pltpu.VMEM((chips,) + part.shape[1:], bf16), pltpu.VMEM((chips,) + part.shape[1:], bf16),
+        pltpu.VMEM((few,) + part.shape[1:], bf16), pltpu.VMEM((few,) + part.shape[1:], bf16),
+        pltpu.VMEM((heads, share, rows - own_rows, d), bf16), pltpu.VMEM((heads, share, rows - own_rows, d), bf16),
+        dma(chips), dma(chips), dma(chips), dma(few), dma(few), dma(few), dma(few), dma(heads), dma(heads),
+    ]
+    if half is not None:
+        args, specs = args + [half], specs + [ANY]
+        outs, out_specs = outs + [shape((heads,) + half.shape, half.dtype)], out_specs + [ANY]
+        scratch += [dma(1), dma(max(heads - 1, 1)), dma(max(heads - 1, 1))]
     return pl.pallas_call(
-        give_back_kernel,
-        in_specs=[ANY, INSMEM],
-        out_specs=[INVMEM, INVMEM],
-        out_shape=[shape((share, own_rows, d), f32), shape((share, rows - own_rows, d), f32)],
-        scratch_shapes=[
-            pltpu.VMEM((chips,) + part.shape[1:], bf16), pltpu.VMEM((chips,) + part.shape[1:], bf16),
-            pltpu.VMEM((few,) + part.shape[1:], bf16), pltpu.VMEM((few,) + part.shape[1:], bf16),
-            pltpu.VMEM((heads, share, rows - own_rows, d), bf16), pltpu.VMEM((heads, share, rows - own_rows, d), bf16),
-            dma(chips), dma(chips), dma(chips), dma(few), dma(few), dma(few), dma(few), dma(heads), dma(heads),
-        ],
+        functools.partial(give_back_kernel, half is not None),
+        in_specs=specs,
+        out_specs=out_specs,
+        out_shape=outs,
+        scratch_shapes=scratch,
         compiler_params=pltpu.CompilerParams(collective_id=number, has_side_effects=True, vmem_limit_bytes=VMEM_CAP),
         name="give_back",
-    )(part, pick)
-
-
-def finish_kernel(half_ref, small_ref, grad_ref, rest_ref, all_ref, total_ref, gtotal_ref, rtotal_ref, *scratch):
-    (small_s, small_core, small_chip, small_head, small_clip, part_s, part_core, chip_s, part_chip, head_s, part_head, mine_s, part_clip,
+    )(*args)
+
+
+def finish_kernel(sizes, half_ref, early_ref, last_ref, qv_ref, grad_ref, rest_ref, all_ref, gains_a_ref, gains_b_ref, shifts_a_ref,
+                  shifts_b_ref, qv_a_ref, qv_b_ref, ub_a_ref, ub_b_ref, gtotal_ref, up_ref, down_ref, out_ref, *scratch):
+    (small_ref, small_s, small_core, small_chip, small_head, small_clip, part_s, part_core, chip_s, part_chip, head_s, part_head, mine_s, part_clip,
      rest_in, rest_s, local_sem, half_send, half_recv, core_send, core_recv, chip_send, chip_recv, head_send, head_recv,
      clip_send, clip_recv, rest_send, rest_recv, back_send, back_recv) = scratch
     clip, head, chip, core, chips = places()
@@ -739,6 +826,13 @@
     peers = [(d, None) for d in [partner] + across + beside + along]
     greet(peers, peers)
     pending = []
+    small_ref[...] = early_ref[...]
+    small_ref[0:2, :] = last_ref[0:2, :]
+    small_ref[2:4, :] = qv_ref[0:2, :]
+    wide = rest_ref.shape[1] // clips
+
+    def lanes(c):
+        return pl.ds(pl.multiple_of(wide * c, wide), wide)
 
     def go(copies):
         for copy in copies:
@@ -764,7 +858,7 @@
         for x in range(chips):
             n = h * chips + x
             first += go([remote(grad_ref.at[2 * n + 1 - core], part_core.at[n], core_send.at[n + 1], core_recv.at[n + 1], partner)])
-    gather = go([remote(rest_ref.at[rem(clip + k + 1, clips)], rest_in.at[k], rest_send.at[k], rest_recv.at[k], d) for k, d in enumerate(along)])
+    gather = go([remote(rest_ref.at[:, lanes(rem(clip + k + 1, clips))], rest_in.at[k], rest_send.at[k], rest_recv.at[k], d) for k, d in enumerate(along)])
     halves = [
         [remote(half_ref.at[s], all_ref.at[head, s], half_send.at[k, s], half_recv.at[k, s], d) for k, d in enumerate(beside)]
         for s in range(share)
@@ -796,11 +890,11 @@
         copies += go([remote(chip_s.at[rem(head + k + 1, heads)], part_head.at[k], head_send.at[k, 1], head_recv.at[k, 1], d)])
     go(halves[share - 1])
     arrived(gather)
-    total = rest_ref[clip].astype(f32)
+    total = rest_ref[:, lanes(clip)].astype(f32)
     for k in range(clips - 1):
         total = total + rest_in[k].astype(f32)
-    rest_s[clip] = total.astype(bf16)
-    spread = go([remote(rest_s.at[clip], rest_s.at[clip], back_send.at[k], back_recv.at[k], d) for k, d in enumerate(along)])
+    rest_s[:, lanes(clip)] = total.astype(bf16)
+    spread = go([remote(rest_s.at[:, lanes(clip)], rest_s.at[:, lanes(clip)], back_send.at[k], back_recv.at[k], d) for k, d in enumerate(along)])
     arrived(copies)
     small_s[2] = in_order(head, heads, small_s[1], lambda k: small_head[k])
     total = chip_s[head].astype(f32)
@@ -812,10 +906,42 @@
         copies += go([remote(small_s.at[2], small_clip.at[k], clip_send.at[k, 0], clip_recv.at[k, 0], d)])
         copies += go([remote(mine_s, part_clip.at[k], clip_send.at[k, 1], clip_recv.at[k, 1], d)])
     arrived(copies)
-    total_ref[...] = in_order(clip, clips, small_s[2], lambda k: small_clip[k])
+    total = in_order(clip, clips, small_s[2], lambda k: small_clip[k])
+    at = [4]
+
+    def rows(width):
+        first = at[0]
+        at[0] += width // total.shape[1]
+        return jnp.concatenate([total[r:r + 1] for r in range(first, at[0])], axis=1)
+
+    def share_of(row):
+        width = row.shape[1] // heads
+        piece = row[:, :width]
+        for h in range(1, heads):
+            piece = jnp.where(head == h, row[:, width * h:width * h + width], piece)
+        return piece
+
+    gains_a_ref[0:1, :] = total[0:1]
+    gains_a_ref[1:3, :] = total[4:6]
+    shifts_a_ref[0:1, :] = total[1:2]
+    shifts_a_ref[1:5, :] = total[6:10]
+    qv_a_ref[0:1, :] = share_of(total[2:3])
+    qv_a_ref[1:2, :] = share_of(total[3:4])
+    at[0] = 10
+    d2, fa, fb = sizes
+    gains_b_ref[...] = rows(d2)
+    for i in range(3):
+        shifts_b_ref[i:i + 1, :] = rows(d2)
+    for i in range(2):
+        qv_b_ref[i:i + 1, :] = share_of(rows(d2))
+    ub_a_ref[...] = share_of(rows(fa))
+    ub_b_ref[...] = share_of(rows(fb))
     gtotal_ref[...] = in_order(clip, clips, mine_s[...].astype(f32), lambda k: part_clip[k].astype(f32))
     arrived(spread)
-    rtotal_ref[...] = rest_s[...].astype(f32)
+    wide = up_ref.shape[1]
+    up_ref[...] = rest_s[:, :wide].astype(f32)
+    down_ref[...] = rest_s[:, wide:2 * wide].astype(f32)
+    out_ref[...] = rest_s[:, 2 * wide:2 * wide + out_ref.shape[1]].astype(f32)
     for copies in halves:
         arrived(copies)
     for copy in pending:
@@ -823,35 +949,31 @@
     local_half.wait()
 
 
-def finish(half, small, grad, rest, number):
+def finish(half, early, last, qv, grad, rest, d2, fa, fb, ha, number):
     toks, heads, clips = lax.axis_size("tok"), lax.axis_size("head"), lax.axis_size("clip")
     chips = toks // 2
     across, beside, along = (max(n, 1) for n in (chips - 1, heads - 1, clips - 1))
-    rows, lanes = rest.shape
-    rest = rest.reshape(clips, rows // clips, lanes)
-    pad = up16(rows // clips) - rows // clips
-    if pad:
-        rest = jnp.pad(rest, ((0, 0), (0, pad), (0, 0)))
-    block = grad.shape[1:]
-    low, full = lambda *dims: pltpu.VMEM(dims, bf16), lambda *dims: pltpu.VMEM(dims + small.shape, f32)
-    all_half, total, gtotal, rtotal = pl.pallas_call(
-        finish_kernel,
-        in_specs=[ANY, INVMEM, INVMEM, INVMEM],
-        out_specs=[ANY, INVMEM, INVMEM, INVMEM],
-        out_shape=[shape((heads,) + half.shape, half.dtype), shape(small.shape, f32), shape(block, f32), shape(rest.shape, f32)],
+    block, rows, d1 = grad.shape[1:], rest.shape[0], early.shape[1]
+    low, full = lambda *dims: pltpu.VMEM(dims, bf16), lambda *dims: pltpu.VMEM(dims + early.shape, f32)
+    sums = [(3, d1), (1, d2), (5, d1), (3, d2), (2, d1 // heads), (2, d2 // heads), (1, fa // heads), (1, fb // heads),
+            block, (rows, fa // heads), (rows, fa // heads), (rows, ha)]
+    return pl.pallas_call(
+        functools.partial(finish_kernel, (d2, fa, fb)),
+        in_specs=[ANY] + [INVMEM] * 5,
+        out_specs=[ANY] + [INVMEM] * len(sums),
+        out_shape=[shape((heads,) + half.shape, half.dtype)] + [shape(dims, f32) for dims in sums],
         scratch_shapes=[
-            full(3), full(), full(across), full(beside), full(along),
+            full(), full(3), full(), full(across), full(beside), full(along),
             low(heads * chips, *block), low(heads * chips, *block), low(heads, *block), low(across, heads, *block),
             low(heads, *block), low(beside, *block), low(*block), low(along, *block),
-            low(along, *rest.shape[1:]), low(*rest.shape),
+            low(along, rows, rest.shape[1] // clips), low(*rest.shape),
             dma(1), dma(beside, half.shape[0]), dma(beside, half.shape[0]), dma(heads * chips + 1), dma(heads * chips + 1),
             dma(across, heads + 1), dma(across, heads + 1), dma(beside, 2), dma(beside, 2), dma(along, 2), dma(along, 2),
             dma(along), dma(along), dma(along), dma(along),
         ],
         compiler_params=pltpu.CompilerParams(collective_id=number, has_side_effects=True, vmem_limit_bytes=VMEM_CAP),
         name="finish",
-    )(half, small, grad, rest)
-    return all_half, total, gtotal, rtotal[:, :rows // clips].reshape(rows, lanes)
+    )(half, early, last, qv, grad, rest)
 
 
 def reduce_clips(shard):
@@ -892,7 +1014,7 @@
     clips_in, resets, assign, w_qkv_a, w_out_a, w_up_a, w_down_a, w_qkv_b, w_out_b, w_skip_b, w_up_b, w_down_b,
     gains_a, gains_b, shifts_a, shifts_b, qv_bias_a, qv_bias_b, up_bias_a, up_bias_b, cotangent,
 ):
-    heads, toks = lax.axis_size("head"), lax.axis_size("tok")
+    heads, toks, clips = lax.axis_size("head"), lax.axis_size("tok"), lax.axis_size("clip")
     head = lax.axis_index("head")
     micro, frames = clips_in.shape[1], clips_in.shape[2]
     d1, d2 = clips_in.shape[-1], cotangent.shape[-1]
@@ -905,7 +1027,6 @@
     own_rows, mem_rows = up16(pooled_tokens), up16(frames // 2 * POOLED)
     rows2 = share * own_rows
 
-    stream = lax.dynamic_slice_in_dim(clips_in[0], first, share, 0).reshape(share, tokens, d1)
     cot = lax.dynamic_slice_in_dim(cotangent[0], first, share, 0).reshape(share, pooled_tokens, d2)
     cot = jnp.pad(cot, ((0, 0), (0, own_rows - pooled_tokens), (0, 0))).reshape(rows2, d2)
 
@@ -926,18 +1047,28 @@
     fa, ha = w_up_a.shape[1], w_out_a.shape[1]
     fb, hb, hs = w_up_b.shape[1], w_out_b.shape[1], w_skip_b.shape[1]
     pack_a = jnp.concatenate([w_up_a, w_down_a, w_qkv_a.reshape(w_qkv_a.shape[0], -1), w_out_a], axis=1)
-    all_a = lax.all_gather(pack_a, group).reshape(heads, d1, -1)
-
-    low1, pooled1, mean1 = call(
-        norm_pool_kernel, share,
-        [(stream, 0), (padded_rows(gains_a[0], shifts_a[0]), None), (pooling, None), (pairing, None)],
-        [(shape((share, tokens, d1), bf16), 0), (shape((share, own_rows, d1), bf16), 0), (shape((share, mem_rows, d1), bf16), 0)],
+    pack_q = w_qkv_b.reshape(w_qkv_b.shape[0], -1)
+    pack_b = jnp.concatenate([w_up_b, w_down_b, w_out_b, w_skip_b], axis=1)
+    vec1 = padded_rows(gains_a[0], shifts_a[0])
+    fixed = lambda *dims: pl.BlockSpec(dims, lambda i, first: (0,) * len(dims))
+    micro_spec = lambda rows: pl.BlockSpec((1, rows, d1), lambda i, first: (i, 0, 0))
+    stream, low1, pooled1, mean1 = pl.pallas_call(
+        norm_pool_kernel,
+        grid_spec=pltpu.PrefetchScalarGridSpec(
+            num_scalar_prefetch=1,
+            grid=(share,),
+            in_specs=[pl.BlockSpec((1, 1) + clips_in.shape[2:], lambda i, first: (0, first[0] + i, 0, 0, 0)),
+                      fixed(*vec1.shape), fixed(*pooling.shape), fixed(*pairing.shape)],
+            out_specs=[micro_spec(rows) for rows in (tokens, tokens, own_rows, mem_rows)],
+        ),
+        out_shape=[shape((share, rows, d1), bf16) for rows in (tokens, tokens, own_rows, mem_rows)],
+        compiler_params=pltpu.CompilerParams(vmem_limit_bytes=VMEM_CAP),
         name="norm_pool",
-    )
-    pooled1, pack_q, pack_b, flat, mask = lax.optimization_barrier((
-        pooled1, w_qkv_b.reshape(w_qkv_b.shape[0], -1), jnp.concatenate([w_up_b, w_down_b, w_out_b, w_skip_b], axis=1),
-        jnp.concatenate([qv_bias_a.reshape(-1), qv_bias_b.reshape(-1), up_bias_a, up_bias_b]), mask))
-    own1, mem1 = share_pooled(pooled1, mean1, pick, 0)
+    )(first.astype(jnp.int32)[None], clips_in, vec1, pooling, pairing)
+    own1, mem1, all_a = share_pooled(pooled1, mean1, pick, 0, pack_a)
+    all_a = all_a.reshape(heads, d1, -1)
+    own1, flat = lax.optimization_barrier((
+        own1, jnp.concatenate([qv_bias_a.reshape(-1), qv_bias_b.reshape(-1), up_bias_a, up_bias_b])))
     all_q = lax.all_gather(pack_q, group).reshape(heads, d1, -1)
     all_b = lax.all_gather(pack_b, group).reshape(heads, d2, -1)
     flat = from_heads(flat[None], heads)
@@ -986,7 +1117,7 @@
         [(shape((rows2, d2), bf16), None), (shape((rows2, d2), bf16), None), (shape((rows2, d1), f32), None),
          (shape((heads, toks, 2, d2 // toks, fb), bf16),
           pl.BlockSpec((1, toks, 2, d2 // toks, chunk), lambda j: (j // per_head, 0, 0, 0, j % per_head))),
-         (shape((heads, d2, hb), bf16), None), (shape((heads, d2, hs), bf16), None),
+         (shape((heads, toks, d2 // toks // 2, 2 * hb), bf16), None), (shape((heads, toks, d2 // toks // 2, 2 * hs), bf16), None),
          (shape((1, heads * fb), f32), pl.BlockSpec((1, chunk), lambda j: (0, j))), (shape((8, d2), f32), None)],
         [((rows2, d2), f32), ((rows2, d2), bf16), ((d2, rows2), bf16), ((d2, rows2), bf16), ((rows2, d2), f32), ((rows2, d2), f32)],
         name="second_mlp",
@@ -1001,28 +1132,30 @@
     sum_mlp_b = scatter(g_mlp_b.reshape((heads * toks,) + g_mlp_b.shape[2:]))
     dcomb2 = dcomb2.reshape(share, own_rows, d2)
     dq2, dpool2, g_qkv_b, rows_qv_b = attend_back(pooled3, dcomb2, own2, mem2, qkv_b, qv_b, mask, lse2, heads)
-    own_back2, mem_back2 = give_back(dpool2, pick, own_rows, 2)
-
-    res1, dcomb1, g_mlp_a, g_out_a, g_ub_a, rows_a = call(
+    own_back2, mem_back2, mixed_all = give_back(dpool2, pick, own_rows, 2, mixed.reshape(share, own_rows, d2))
+
+    merge = lambda grad: grad.reshape((heads * toks,) + grad.shape[2:])
+    sum_rest_b = scatter(jnp.concatenate([by_owner(g_qkv_b), merge(g_out_b), merge(g_skip_b)], axis=2))
+
+    res1, dcomb1, g_mlp_a, g_ub_a, rows_a = call(
         first_back_kernel, share,
         [(middle, 0), (after1, 0), (comb1, 0), (dskip.reshape(share, own_rows, d1), 0), (dq2, 0), (own_back2, 0), (mem_back2, 0),
          (out_a, None), (all_a, up_spec), (all_a, down_spec), (ub_a, None),
          (padded_rows(gains_a[1], shifts_a[2], gains_a[2]), None), (unpooling, None), (unpairing, None)],
         [(shape((share, tokens, d1), f32), 0), (shape((share, tokens, d1), bf16), 0),
-         (shape((heads, d1, 2 * fa), bf16), None), (shape((heads, d1, ha), bf16), None),
+         (shape((heads, d1, -(-(2 * fa + ha) // (128 * clips)) * 128 * clips), bf16), None),
          (shape((heads, 1, fa), f32), None), (shape((8, d1), f32), None)],
         [((heads, d1, fa), f32), ((heads, d1, fa), f32), ((d1, d1), f32)],
         name="first_back",
     )
-    g_out_b, g_skip_b = by_owner(g_out_b), by_owner(g_skip_b)
-    half = g_out_b.shape[1] // 2
-    rest_b = jnp.concatenate(
-        [by_owner(g_qkv_b), g_out_b[:, :half], g_out_b[:, half:], g_skip_b[:, :half], g_skip_b[:, half:]], axis=2)
-    rest_a = jnp.concatenate([by_owner(g_mlp_a), by_owner(g_out_a)], axis=2)
-    dcomb1, sum_mlp_b, rest_b, rest_a = lax.optimization_barrier((dcomb1, sum_mlp_b, rest_b, rest_a))
-    sum_rest_b, sum_rest_a = scatter(rest_b), scatter(rest_a)
+    rest_a = by_owner(g_mlp_a)
+    dcomb1, sum_mlp_b, rest_a = lax.optimization_barrier((dcomb1, sum_mlp_b, rest_a))
+    sum_rest_a = scatter(rest_a)
     sum_mlp_b = reduce_clips(sum_mlp_b)
     dx1, dpool1, g_qkv_a, rows_qv_a = attend_back(low1, dcomb1, own1, mem1, qkv_a, qv_a, mask, lse1, heads)
+    dpool1, sum_mlp_b, sum_rest_b = lax.optimization_barrier((dpool1, sum_mlp_b, sum_rest_b))
+    mlp_b = spread_clips(sum_mlp_b)
+    sum_rest_b = reduce_clips(sum_rest_b)
     own_back1, mem_back1 = give_back(dpool1, pick, own_rows, 3)
     stream_grad, rows_last = call(
         last_back_kernel, share,
@@ -1032,47 +1165,34 @@
         name="last_back",
     )
 
-    small = [
-        jnp.stack([rows_last[0], rows_a[3], rows_a[0]]), rows_b[3],
-        jnp.stack([rows_last[1], rows_a[5], rows_a[4], rows_a[2], rows_a[1]]),
-        rows_b[:3], rows_qv_a[:2], rows_qv_b[:2], g_ub_a, g_ub_b,
+    zero = jnp.zeros((4, d1), f32)
+    early = [
+        zero, rows_a[3:4], rows_a[0:1], rows_a[5:6], rows_a[4:5], rows_a[2:3], rows_a[1:2],
+        rows_b[3:4], rows_b[:3], rows_qv_b[:2], g_ub_a, g_ub_b,
     ]
-    flat = jnp.concatenate([piece.reshape(-1) for piece in small])
-    flat = jnp.pad(flat, (0, -flat.size % 1024)).reshape(-1, 128)
-    sum_rest_b = reduce_clips(sum_rest_b)
-    flat, sum_mlp_b, sum_rest_b = lax.optimization_barrier((flat, sum_mlp_b, sum_rest_b))
-    mlp_b, rest_b = spread_clips(sum_mlp_b), spread_clips(sum_rest_b)
+    early = jnp.concatenate([piece.reshape(-1, d1) for piece in early])
+    early = jnp.pad(early, ((0, -early.shape[0] % 8), (0, 0)))
+    rows_last, sum_rest_b, early = lax.optimization_barrier((rows_last, sum_rest_b, early))
+    rest_b = spread_clips(sum_rest_b).astype(f32)
     mlp_b = mlp_b.reshape((2, -1, mlp_b.shape[-1])).astype(f32)
-    rest_b = rest_b.astype(f32)
-    stream_all, flat, grad_qkv_a, rest_a = finish(stream_grad, flat, by_owner(g_qkv_a), sum_rest_a, 4)
-    flat = flat.reshape(-1)
+    stream_all, *sums = finish(
+        stream_grad, early, rows_last, rows_qv_a, by_owner(g_qkv_a), sum_rest_a, d2, heads * fa, heads * fb, ha, 4)
     out_lanes = rest_b[:, 3 * hb:5 * hb]
     skip_lanes = rest_b[:, 5 * hb:]
-    pieces, at = [], 0
-    for piece in small:
-        pieces.append(flat[at:at + piece.size].reshape(piece.shape))
-        at += piece.size
-
-    def mine(piece, axis):
-        width = piece.shape[axis] // heads
-        return lax.dynamic_slice_in_dim(piece, head * width, width, axis)
-
-    mixed = mixed.reshape(share, own_rows, d2)[:, :pooled_tokens]
-    mixed_all = from_heads(mixed, heads)
+    mixed_all = mixed_all.reshape(micro, own_rows, d2)[:, :pooled_tokens]
     return (
         mixed_all.reshape(cotangent.shape),
         stream_all.astype(f32).reshape(clips_in.shape),
-        grad_qkv_a.reshape(w_qkv_a.shape),
-        rest_a[:, 2 * fa:],
-        rest_a[:, :fa],
-        rest_a[:, fa:2 * fa],
+        sums[8].reshape(w_qkv_a.shape),
+        sums[11],
+        sums[9],
+        sums[10],
         rest_b[:, :3 * hb].reshape(w_qkv_b.shape),
         jnp.concatenate([out_lanes[:, :hb], out_lanes[:, hb:]], axis=0),
         jnp.concatenate([skip_lanes[:, :hs], skip_lanes[:, hs:]], axis=0),
         mlp_b[0],
         mlp_b[1],
-        pieces[0], pieces[1], pieces[2], pieces[3],
-        mine(pieces[4], 1), mine(pieces[5], 1), mine(pieces[6].reshape(-1), 0), mine(pieces[7].reshape(-1), 0),
+        sums[0], sums[1][0], sums[2], sums[3], sums[4], sums[5], sums[6][0], sums[7][0],
     )
 
 

time: 508 us -> 463 us (0.911)
  waiting for transfers between devices: 37.7 us -> 13.5 us
  local copies, waits for them, and re-layouts: 55.2 us -> 40.5 us
  starting transfers between devices: 29.3 us -> 17.6 us
    all_gather x1, waiting for transfers between devices: 16.2 us -> 0.01 us  [local(): all_b = lax.all_gather(pack_b, group).reshape(heads, d2, -1)]
    ppermute x2 -> x1, waiting for transfers between devices: 13.4 us -> 0.01 us  [from_heads(): lax.ppermute(piece, 'head', [(i, (i + d) % heads) for i in range(heads)])]
    ppermute x6, waiting for transfers between devices: 2.29 us -> 13.4 us  [spread_clips(): lax.ppermute(piece, 'clip', [(i, (i + k) % clips) for i in range(clips)])]
    ppermute x6, starting transfers between devices: 15 us -> 5.93 us  [spread_clips(): lax.ppermute(piece, 'clip', [(i, (i + k) % clips) for i in range(clips)])]
    unnamed x68 -> x90, local copies, waits for them, and re-layouts: 10.6 us -> 17.7 us
    pallas_call x5 -> x6, Pallas kernels: 157 us -> 164 us  [the longest x2 63.6 us: give_back(): pl.pallas_call(functools.partial(give_back_kernel, half is not None), in_...]
    slice x16 -> x3, local copies, waits for them, and re-layouts: 5.76 us -> 0.1 us  [the longest x1 0.08 us: local(): mixed_all = mixed_all.reshape(micro, own_rows, d2)[:, :pooled_tokens]]
    pallas_call x9 -> x8, Pallas kernels: 187 us -> 183 us  [call(): pl.pallas_call(kernel, grid=(steps,), in_specs=[spec(a, how) for a, how i...]
  transfers between devices with their start and end apart: 20 -> 18, of which waited for: 5 -> 3; matrix products, arithmetic and copies ran while one was open for 12% -> 9% of each run, Pallas kernels for 63% -> 61%
where the time goes in v5:
time: 463 us; the launch traced here: 458 us
  Pallas kernels  347 us (75%)
  local copies, waits for them, and re-layouts  40.5 us (9%)
  between operations  21.5 us (5%)
  other arithmetic  18.6 us (4%)
  starting transfers between devices  17.6 us (4%)
  waiting for transfers between devices  13.5 us (3%)
    pallas_call x8, Pallas kernels, call(): pl.pallas_call(kernel, grid=(steps,), in_specs=[spec(a, how) for a, how i...  183 us
    pallas_call x2, Pallas kernels, give_back(): pl.pallas_call(functools.partial(give_back_kernel, half is not None), in_...  63.6 us
    pallas_call x2, Pallas kernels, share_pooled(): pl.pallas_call(functools.partial(share_kernel, block is not None), in_spe...  53 us
    pallas_call x1, Pallas kernels, finish(): pl.pallas_call(functools.partial(finish_kernel, (d2, fa, fb)), in_specs=[...  42.6 us
    unnamed x90, local copies, waits for them, and re-layouts  17.7 us
    ppermute x6, waiting for transfers between devices, spread_clips(): lax.ppermute(piece, 'clip', [(i, (i + k) % clips) for i in range(clips)])  13.4 us
    ppermute x6, starting transfers between devices, reduce_clips(): lax.ppermute(give, 'clip', [(i, (i + k) % clips) for i in range(clips)])  10.8 us
  transfers between devices with their start and end apart: 18, of which 3 were waited for; matrix products, arithmetic and copies ran while one was open for 9% of the time, Pallas kernels for 61%

profile of v5, /device:TPU:0, one launch (start us, length us, event | category | flops | bytes accessed | tf_op | source)
XLA Modules:
  0.0 458.3 jit_solution(5932340271641449038)
XLA Ops:
  9.5 2.2 pad_maximum_fusion.1
  18.4 3.6 copy.62.clips_ref
  24.0 4.4 norm_pool.1
  29.1 32.6 %share_pooled.2 = (bf16[4,2,208,384]{3,2,1,0:T(8,128)(2,1)}, bf16[4,2,112,384]{3,2,1,0:T(8,128)(2,1)}, bf16[2,4,96,2304]{3,2,1,0:T(8,128)(2,1)}) custom-call(bf16[2,208,384]{2,1,0:T(8,128)(2,1)} %get-tuple-element.90.refs_0_, bf16[2,112,384]{2,1,0:T(8,128)(2,1)} %get-tuple-element.91.refs_1_, f32[2,4]{1,0:T(2,128)} %add_convert_fusion.refs_2_.refs_1_, ...), custom_call_target="tpu_custom_call" | custom-call | tf_op jit(solution)/shard_map/share_pooled/pallas_call | solution.py:672
  74.8 20.9 %attend.2 = (bf16[2,784,384]{2,1,0:T(8,128)(2,1)}, f32[2,784,128]{2,1,0:T(8,128)}) custom-call(bf16[2,784,384]{2,1,0:T(8,128)(2,1)} %get-tuple-element.89.x_ref, bf16[4,2,208,384]{3,2,1,0:T(8,128)(2,1)} %get-tuple-element.93.own_ref, bf16[4,2,112,384]{3,2,1,0:T(8,128)(2,1)} %get-tuple-element.94.mem_ref, bf16[1,384,1152]{2,1,0:T(8,128)(2,1)} %bitcast.118, ...), custom_call_target="tpu_custom_call" | custom-call | tf_op jit(solution)/shard_map/attend/pallas_call | solution.py:448
  95.7 13.1 %first_mlp.1 = (f32[2,784,384]{2,1,0:T(8,128)}, f32[2,784,384]{2,1,0:T(8,128)}, bf16[2,208,384]{2,1,0:T(8,128)(2,1)}, bf16[2,112,384]{2,1,0:T(8,128)(2,1)}) custom-call(bf16[2,784,384]{2,1,0:T(8,128)(2,1)} %get-tuple-element.88.x_ref, bf16[2,784,384]{2,1,0:T(8,128)(2,1)} %get-tuple-element.97.comb_ref, bf16[384,384]{1,0:T(8,128)(2,1)} %pad_maximum_fusion.3.out_ref, ...), custom_call_target="tpu_custom_call" | custom-call | tf_op jit(solution)/shard_map/first_mlp/pallas_call | solution.py:448
  108.8 20.3 %share_pooled.3 = (bf16[4,2,208,384]{3,2,1,0:T(8,128)(2,1)}, bf16[4,2,112,384]{3,2,1,0:T(8,128)(2,1)}) custom-call(bf16[2,208,384]{2,1,0:T(8,128)(2,1)} %get-tuple-element.98.refs_0_.x_ref, bf16[2,112,384]{2,1,0:T(8,128)(2,1)} %get-tuple-element.99.refs_1_, f32[2,4]{1,0:T(2,128)} %add_convert_fusion.refs_2_.refs_1_), custom_call_target="tpu_custom_call" | custom-call | tf_op jit(solution)/shard_map/share_pooled/pallas_call | solution.py:672
  129.2 17.7 %attend.3 = (bf16[2,208,768]{2,1,0:T(8,128)(2,1)}, f32[2,208,128]{2,1,0:T(8,128)}) custom-call(bf16[2,208,384]{2,1,0:T(8,128)(2,1)} %get-tuple-element.98.refs_0_.x_ref, bf16[4,2,208,384]{3,2,1,0:T(8,128)(2,1)} %get-tuple-element.100.own_ref, bf16[4,2,112,384]{3,2,1,0:T(8,128)(2,1)} %get-tuple-element.101.mem_ref, bf16[2,384,1152]{2,1,0:T(8,128)(2,1)} %bitcast.120, ...), custom_call_target="tpu_custom_call" | custom-call | tf_op jit(solution)/shard_map/attend/pallas_call | solution.py:448
  149.1 26.0 %second_mlp.1 = (bf16[416,768]{1,0:T(8,128)(2,1)}, bf16[416,768]{1,0:T(8,128)(2,1)}, f32[416,384]{1,0:T(8,128)}, bf16[2,4,2,192,1536]{4,3,2,1,0:T(8,128)(2,1)}, ...) custom-call(bf16[416,768]{1,0:T(8,128)(2,1)} %bitcast.138, ...), custom_call_target="tpu_custom_call" | custom-call | tf_op jit(solution)/shard_map/second_mlp/pallas_call | solution.py:448
  175.2 34.4 %attend_back.2 = (f32[2,208,384]{2,1,0:T(8,128)}, bf16[4,2,320,384]{3,2,1,0:T(8,128)(2,1)}, bf16[2,384,1152]{2,1,0:T(8,128)(2,1)}, f32[8,768]{1,0:T(8,128)}) custom-call(bf16[2,208,384]{2,1,0:T(8,128)(2,1)} %get-tuple-element.98.refs_0_.x_ref, bf16[2,208,768]{2,1,0:T(8,128)(2,1)} %bitcast.141, bf16[4,2,208,384]{3,2,1,0:T(8,128)(2,1)} %get-tuple-element.100.own_ref, ...), custom_call_target="tpu_custom_call" | custom-call | tf_op jit(solution)/shard_map/attend_back/pallas_call | solution.py:448
  209.7 3.1 pad_maximum_fusion
  212.9 35.8 %give_back.2 = (f32[2,208,384]{2,1,0:T(8,128)}, f32[2,112,384]{2,1,0:T(8,128)}, bf16[2,2,208,768]{3,2,1,0:T(8,128)(2,1)}) custom-call(bf16[4,2,320,384]{3,2,1,0:T(8,128)(2,1)} %get-tuple-element.105.refs_0_, f32[2,4]{1,0:T(2,128)} %add_convert_fusion.refs_2_.refs_1_, bf16[2,208,768]{2,1,0:T(8,128)(2,1)} %bitcast.140), custom_call_target="tpu_custom_call" | custom-call | tf_op jit(solution)/shard_map/give_back/pallas_call | solution.py:803
  248.8 27.5 %first_back.1 = (f32[2,784,384]{2,1,0:T(8,128)}, bf16[2,784,384]{2,1,0:T(8,128)(2,1)}, bf16[2,384,2048]{2,1,0:T(8,128)(2,1)}, f32[2,1,768]{2,1,0:T(1,128)}, f32[8,384]{1,0:T(8,128)}) custom-call(f32[2,784,384]{2,1,0:T(8,128)} %get-tuple-element.108.middle_ref, f32[2,784,384]{2,1,0:T(8,128)} %get-tuple-element.109.after_ref, ...), custom_call_target="tpu_custom_call" | custom-call | tf_op jit(solution)/shard_map/first_back/pallas_call | solution.py:448
  283.3 2.9 collective-permute-start.3
  289.4 37.2 %attend_back.3 = (f32[2,784,384]{2,1,0:T(8,128)}, bf16[4,2,320,384]{3,2,1,0:T(8,128)(2,1)}, bf16[2,384,576]{2,1,0:T(8,128)(2,1)}, f32[8,384]{1,0:T(8,128)}) custom-call(bf16[2,784,384]{2,1,0:T(8,128)(2,1)} %get-tuple-element.89.x_ref, bf16[2,784,384]{2,1,0:T(8,128)(2,1)} %get-tuple-element.118.g_ref, bf16[4,2,208,384]{3,2,1,0:T(8,128)(2,1)} %get-tuple-element.93.own_ref, ...), custom_call_target="tpu_custom_call" | custom-call | tf_op jit(solution)/shard_map/attend_back/pallas_call | solution.py:448
  330.9 3.4 collective-permute-start.4
  334.3 2.4 collective-permute-start.6
  336.8 27.9 %give_back.3 = (f32[2,208,384]{2,1,0:T(8,128)}, f32[2,112,384]{2,1,0:T(8,128)}) custom-call(bf16[4,2,320,384]{3,2,1,0:T(8,128)(2,1)} %get-tuple-element.126.refs_0_, f32[2,4]{1,0:T(2,128)} %add_convert_fusion.refs_2_.refs_1_), custom_call_target="tpu_custom_call" | custom-call | tf_op jit(solution)/shard_map/give_back/pallas_call | solution.py:803
  364.6 6.3 %last_back.1 = (bf16[2,4,196,384]{3,2,1,0:T(8,128)(2,1)}, f32[8,384]{1,0:T(8,128)}) custom-call(bf16[2,784,384]{2,1,0:T(8,128)(2,1)} %get-tuple-element.88.x_ref, f32[2,784,384]{2,1,0:T(8,128)} %get-tuple-element.114.res_ref, f32[2,784,384]{2,1,0:T(8,128)} %get-tuple-element.120.dx_ref, f32[2,208,384]{2,1,0:T(8,128)} %get-tuple-element.127.own_ref, ...), custom_call_target="tpu_custom_call" | custom-call | tf_op jit(solution)/shard_map/last_back/pallas_call | solution.py:448
  372.0 3.0 collective-permute-start.7
  376.6 7.6 %collective-permute-done.7 = bf16[24,2304]{1,0:T(8,128)(2,1)S(1)} collective-permute-done((bf16[24,2304]{1,0:T(8,128)(2,1)S(1)}, bf16[24,2304]{1,0:T(8,128)(2,1)S(1)}, u32[]{:S(2)}, u32[]{:S(2)}) %collective-permute-start.7) | collective-permute-done | bytes 110624 | tf_op jit(solution)/shard_map/ppermute | solution.py:994
  384.5 5.5 %collective-permute-done.8 = bf16[24,2304]{1,0:T(8,128)(2,1)S(1)} collective-permute-done((bf16[24,2304]{1,0:T(8,128)(2,1)S(1)}, bf16[24,2304]{1,0:T(8,128)(2,1)S(1)}, u32[]{:S(2)}, u32[]{:S(2)}) %collective-permute-start.8) | collective-permute-done | bytes 110624 | tf_op jit(solution)/shard_map/ppermute | solution.py:994
  395.5 42.6 %finish.1 = (bf16[2,2,4,196,384]{4,3,2,1,0:T(8,128)(2,1)}, f32[3,384]{1,0:T(4,128)}, f32[1,768]{1,0:T(1,128)}, f32[5,384]{1,0:T(8,128)}, f32[3,768]{1,0:T(4,128)...) custom-call(bf16[2,4,196,384]{3,2,1,0:T(8,128)(2,1)} %get-tuple-elem, ...), custom_call_target="tpu_custom_call" | custom-call | tf_op jit(solution)/shard_map/finish/pallas_call | solution.py:960
  440.1 3.5 copy.72
  (226 shorter events, 53.0 us)
Async XLA Ops:
  7.2 57.0 %copy-start = (bf16[1,4,4,49,768]{4,2,3,1,0:T(4,128)(2,1)S(1)}, bf16[1,4,4,49,768]{4,2,3,1,0:T(4,128)(2,1)}, u32[]{:S(2)}) copy-start(bf16[1,4,4,49,768]{4,2,3,1,0:T(4,128)(2,1)} %param.45) | copy-start | bytes 3612676
  7.2 121.9 %all-gather.4.cloned.1.call-start = ((), (), s32[]{:S(2)}) async-start(), calls=%async_computation.3 | async-start | bytes 1990656 | tf_op jit(solution)/shard_map/all_gather | solution.py:1072
  9.4 137.5 %all-gather.6.cloned.1.call-start = ((), (), s32[]{:S(2)}) async-start(), calls=%async_computation.7 | async-start | bytes 12828672 | tf_op jit(solution)/shard_map/all_gather | solution.py:1073
  11.8 267.4 %reduce-scatter.4.cloned.1.call-start = ((), (), s32[]{:S(2)}) async-start(), calls=%async_computation.4 | async-start | bytes 10616832 | tf_op jit(solution)/shard_map/reduce_scatter | solution.py:1130
  24.0 37.7 %copy-start.20 = (f32[1536]{0:T(1024)S(1)}, f32[1536]{0:T(1024)}, u32[]{:S(2)}) copy-start(f32[1536]{0:T(1024)} %param.44) | copy-start | bytes 18436
  24.0 37.7 %copy-start.25 = (f32[768]{0:T(1024)S(1)}, f32[768]{0:T(1024)}, u32[]{:S(2)}) copy-start(f32[768]{0:T(1024)} %param.43) | copy-start | bytes 9220
  24.0 38.4 %copy-start.15 = (f32[3,768]{1,0:T(4,128)S(1)}, f32[3,768]{1,0:T(4,128)}, u32[]{:S(2)}) copy-start(f32[3,768]{1,0:T(4,128)} %param.40) | copy-start | bytes 27652
  24.0 40.1 %copy-start.26 = (f32[768]{0:T(1024)S(1)}, f32[768]{0:T(1024)}, u32[]{:S(2)}) copy-start(f32[768]{0:T(1024)} %param.38) | copy-start | bytes 9220
  28.5 36.0 %slice-start = ((f32[3,768]{1,0:T(4,128)}), f32[1,768]{1,0:T(1,128)S(1)}, s32[]{:S(2)}) async-start(f32[3,768]{1,0:T(4,128)} %param.40), calls=%async_computation.8 | async-start | bytes 6144 | tf_op jit(solution)/shard_map/slice | solution.py:1116
  61.8 10.2 %collective-permute-start = (f32[1,3456]{1,0:T(1,128)S(1)}, f32[1,3456]{1,0:T(1,128)S(1)}, u32[]{:S(2)}, u32[]{:S(2)}) collective-permute-start(f32[1,3456]{1,0:T(1,128)S(1)} %reshape.227), channel_id=1, source_target_pairs={{0,1},{1,0},{2,3},{3,2},{4,5},{5,4},{6,7},{7,6},{8,9},{9,8},{10,11... | collective-permute-start | bytes 41480 | tf_op jit(solution)/shard_map/ppermute | solution.py:1004
  175.2 152.9 %reduce-scatter.6.cloned.1.call-start = ((), (), s32[]{:S(2)}) async-start(), calls=%async_computation.5 | async-start | bytes 3981312 | tf_op jit(solution)/shard_map/reduce_scatter | solution.py:1130
  212.9 182.6 %reduce-scatter.8.cloned.1.call-start = ((), (), s32[]{:S(2)}) async-start(), calls=%async_computation.6 | async-start | bytes 3538944 | tf_op jit(solution)/shard_map/reduce_scatter | solution.py:1130
  281.1 45.5 %collective-permute-start.1 = (bf16[96,1536]{1,0:T(8,128)(2,1)}, bf16[96,1536]{1,0:T(8,128)(2,1)}, u32[]{:S(2)}, u32[]{:S(2)}) collective-permute-start(bf16[96,1536]{1,0:T(8,128)(2,1)} %get-tuple-element.226), channel_id=1, source_target_pairs={{0,8},{8,16},{16,24},{24,0},{1,9},{9,17},{17,25},{25,1},{2,10},{10... | collective-permute-start | bytes 884744 | tf_op jit(solution)/shard_map/ppermute | solution.py:985
  282.4 44.2 %collective-permute-start.2 = (bf16[96,1536]{1,0:T(8,128)(2,1)S(1)}, bf16[96,1536]{1,0:T(8,128)(2,1)}, u32[]{:S(2)}, u32[]{:S(2)}) collective-permute-start(bf16[96,1536]{1,0:T(8,128)(2,1)S(1)} %get-tuple-element.228), channel_id=1, source_target_pairs={{0,16},{8,24},{16,0},{24,8},{1,17},{9,25},{17,1},{25,9},{2,18},{10... | collective-permute-start | bytes 884744 | tf_op jit(solution)/shard_map/ppermute | solution.py:985
  283.3 43.3 %collective-permute-start.3 = (bf16[96,1536]{1,0:T(8,128)(2,1)S(1)}, bf16[96,1536]{1,0:T(8,128)(2,1)}, u32[]{:S(2)}, u32[]{:S(2)}) collective-permute-start(bf16[96,1536]{1,0:T(8,128)(2,1)S(1)} %get-tuple-element.227), channel_id=1, source_target_pairs={{0,24},{8,0},{16,8},{24,16},{1,25},{9,1},{17,9},{25,17},{2,26},{10... | collective-permute-start | bytes 884744 | tf_op jit(solution)/shard_map/ppermute | solution.py:985
  328.0 64.6 %collective-permute-start.10 = (bf16[96,1536]{1,0:T(8,128)(2,1)S(1)}, bf16[96,1536]{1,0:T(8,128)(2,1)}, u32[]{:S(2)}, u32[]{:S(2)}) collective-permute-start(bf16[96,1536]{1,0:T(8,128)(2,1)S(1)} %fusion.2), channel_id=1, source_target_pairs={{0,8},{8,16},{16,24},{24,0},{1,9},{9,17},{17,25},{25,1},{2,10},{10... | collective-permute-start | bytes 884744 | tf_op jit(solution)/shard_map/ppermute | solution.py:994
  328.1 65.6 %collective-permute-start.11 = (bf16[96,1536]{1,0:T(8,128)(2,1)S(1)}, bf16[96,1536]{1,0:T(8,128)(2,1)S(1)}, u32[]{:S(2)}, u32[]{:S(2)}) collective-permute-start(bf16[96,1536]{1,0:T(8,128)(2,1)S(1)} %fusion.2), channel_id=1, source_target_pairs={{0,16},{8,24},{16,0},{24,8},{1,17},{9,25},{17,1},{25,9},{2,18},{10... | collective-permute-start | bytes 884744 | tf_op jit(solution)/shard_map/ppermute | solution.py:994
  330.9 40.0 %collective-permute-start.4 = (bf16[24,2304]{1,0:T(8,128)(2,1)}, bf16[24,2304]{1,0:T(8,128)(2,1)S(1)}, u32[]{:S(2)}, u32[]{:S(2)}) collective-permute-start(bf16[24,2304]{1,0:T(8,128)(2,1)} %get-tuple-element.233), channel_id=1, source_target_pairs={{0,8},{8,16},{16,24},{24,0},{1,9},{9,17},{17,25},{25,1},{2,10},{10... | collective-permute-start | bytes 331784 | tf_op jit(solution)/shard_map/ppermute | solution.py:985
  334.3 36.7 %collective-permute-start.5 = (bf16[24,2304]{1,0:T(8,128)(2,1)}, bf16[24,2304]{1,0:T(8,128)(2,1)S(1)}, u32[]{:S(2)}, u32[]{:S(2)}) collective-permute-start(bf16[24,2304]{1,0:T(8,128)(2,1)} %get-tuple-element.235), channel_id=1, source_target_pairs={{0,16},{8,24},{16,0},{24,8},{1,17},{9,25},{17,1},{25,9},{2,18},{10... | collective-permute-start | bytes 331784 | tf_op jit(solution)/shard_map/ppermute | solution.py:985
  334.3 36.7 %collective-permute-start.6 = (bf16[24,2304]{1,0:T(8,128)(2,1)}, bf16[24,2304]{1,0:T(8,128)(2,1)}, u32[]{:S(2)}, u32[]{:S(2)}) collective-permute-start(bf16[24,2304]{1,0:T(8,128)(2,1)} %get-tuple-element.234), channel_id=1, source_target_pairs={{0,24},{8,0},{16,8},{24,16},{1,25},{9,1},{17,9},{25,17},{2,26},{10... | collective-permute-start | bytes 331784 | tf_op jit(solution)/shard_map/ppermute | solution.py:985
  370.9 22.8 %collective-permute-start.12 = (bf16[96,1536]{1,0:T(8,128)(2,1)S(1)}, bf16[96,1536]{1,0:T(8,128)(2,1)S(1)}, u32[]{:S(2)}, u32[]{:S(2)}) collective-permute-start(bf16[96,1536]{1,0:T(8,128)(2,1)S(1)} %fusion.2), channel_id=1, source_target_pairs={{0,24},{8,0},{16,8},{24,16},{1,25},{9,1},{17,9},{25,17},{2,26},{10... | collective-permute-start | bytes 884744 | tf_op jit(solution)/shard_map/ppermute | solution.py:994
  372.0 12.2 %collective-permute-start.7 = (bf16[24,2304]{1,0:T(8,128)(2,1)S(1)}, bf16[24,2304]{1,0:T(8,128)(2,1)S(1)}, u32[]{:S(2)}, u32[]{:S(2)}) collective-permute-start(bf16[24,2304]{1,0:T(8,128)(2,1)S(1)} %fusion.5), channel_id=1, source_target_pairs={{0,8},{8,16},{16,24},{24,0},{1,9},{9,17},{17,25},{25,1},{2,10},{10... | collective-permute-start | bytes 331784 | tf_op jit(solution)/shard_map/ppermute | solution.py:994
  375.1 14.9 %collective-permute-start.8 = (bf16[24,2304]{1,0:T(8,128)(2,1)S(1)}, bf16[24,2304]{1,0:T(8,128)(2,1)S(1)}, u32[]{:S(2)}, u32[]{:S(2)}) collective-permute-start(bf16[24,2304]{1,0:T(8,128)(2,1)S(1)} %fusion.5), channel_id=1, source_target_pairs={{0,16},{8,24},{16,0},{24,8},{1,17},{9,25},{17,1},{25,9},{2,18},{10... | collective-permute-start | bytes 331784 | tf_op jit(solution)/shard_map/ppermute | solution.py:994
  384.3 5.9 %collective-permute-start.9 = (bf16[24,2304]{1,0:T(8,128)(2,1)S(1)}, bf16[24,2304]{1,0:T(8,128)(2,1)S(1)}, u32[]{:S(2)}, u32[]{:S(2)}) collective-permute-start(bf16[24,2304]{1,0:T(8,128)(2,1)S(1)} %fusion.5), channel_id=1, source_target_pairs={{0,24},{8,0},{16,8},{24,16},{1,25},{9,1},{17,9},{25,17},{2,26},{10... | collective-permute-start | bytes 331784 | tf_op jit(solution)/shard_map/ppermute | solution.py:994
  (31 other events, 257.9 us)
Sparse Core Ops, SparseCore 0:
  10.5 31.9 all-gather.3
  44.4 72.7 all-gather.5
  175.3 92.5 reduce-scatter.3
  271.8 48.0 reduce-scatter.5
  326.7 47.1 reduce-scatter.7

commit v6 on v5

--- a/solution.py
+++ b/solution.py
@@ -125,6 +125,29 @@
             row += ref.shape[2]
 
 
+def key_mask(own_ref, mem_ref, valid, has):
+    parts = []
+    for ref, rows, there in ((own_ref, valid[0], None), (mem_ref, valid[1], has)):
+        block = ref.shape[2]
+        lane = lax.rem(lax.broadcasted_iota(jnp.int32, (1, ref.shape[0] * block), 1), block)
+        limit = rows if there is None else jnp.where(there > 0, rows, 0)
+        parts.append(jnp.where(lane < limit, 0.0, NEG))
+    return jnp.concatenate(parts, axis=1)
+
+
+def assemble(w_ref, w_s):
+    wide = w_ref.shape[2] // 4
+    for part in range(3):
+        pieces = [w_ref[h, :, wide * part:wide * part + wide].astype(f32) for h in range(w_ref.shape[0])]
+        w_s[0, :, 384 * part:384 * part + 384] = jnp.concatenate(pieces, axis=1).astype(bf16)
+
+
+def assemble_out(w_ref, out_s):
+    wide = w_ref.shape[2] // 4
+    pieces = [w_ref[h, :, 3 * wide:].astype(f32) for h in range(w_ref.shape[0])]
+    out_s[...] = jnp.concatenate(pieces, axis=1).astype(bf16)
+
+
 def project_keys(own_ref, mem_ref, w_ref, bias_ref, x_s, k_s, v_s):
     for ref, t, rows in key_rows(own_ref, mem_ref):
         x_s[rows, :] = ref[t, 0]
@@ -143,8 +166,8 @@
         q_s[:, low:low + 384] = (value + bias_ref[0:1, low:low + 384]).astype(bf16)
 
 
-def norm_pool_kernel(first_ref, clips_ref, vec_ref, pool_ref, pair_ref, x_ref, low_ref, pooled_ref, mean_ref):
-    x = jnp.concatenate([clips_ref[0, 0, f].astype(f32) for f in range(clips_ref.shape[2])], axis=0)
+def norm_pool_kernel(clips_ref, vec_ref, pool_ref, pair_ref, x_ref, low_ref, pooled_ref, mean_ref):
+    x = jnp.concatenate([clips_ref[0, f].astype(f32) for f in range(clips_ref.shape[1])], axis=0)
     x_ref[0] = x.astype(bf16)
     unit, _ = norm(x)
     normed = unit * vec_ref[0:1, :] + vec_ref[1:2, :]
@@ -162,8 +185,14 @@
         gw_ref[h, :, wide * part:wide * part + wide] = columns.astype(bf16)
 
 
-def attend_kernel(chunk, x_ref, own_ref, mem_ref, w_ref, qv_ref, mask_ref, out_ref, lse_ref, x_s, q_s, k_s, v_s, s_s, p_s):
+def attend_kernel(chunk, valid, x_ref, own_ref, mem_ref, w_ref, qv_ref, has_ref, out_ref, lse_ref, w_s, x_s, q_s, k_s, v_s, s_s, p_s):
     nq, width = q_s.shape
+    columns = key_mask(own_ref, mem_ref, valid, has_ref[pl.program_id(0)])
+    if width == 384:
+        @pl.when(pl.program_id(0) == 0)
+        def _():
+            assemble(w_ref, w_s)
+        w_ref = w_s
     project_queries(x_ref, w_ref, qv_ref, q_s)
     project_keys(own_ref, mem_ref, w_ref, qv_ref, x_s, k_s, v_s)
     factor = HD**-0.5 * math.log2(math.e)
@@ -180,7 +209,7 @@
 
             def body(i, carry, head=head):
                 rows = pl.ds(pl.multiple_of(i * chunk, chunk), chunk)
-                score = s_s[rows, :] * factor + mask_ref[0]
+                score = s_s[rows, :] * factor + columns
                 top = jnp.max(score, axis=1, keepdims=True)
                 power = jnp.exp2(score - top)
                 total = jnp.sum(power, axis=1, keepdims=True)
@@ -197,12 +226,18 @@
 
 
 def attend_back_kernel(
-    chunk, x_ref, g_ref, own_ref, mem_ref, w_ref, qv_ref, mask_ref, lse_ref,
+    chunk, valid, x_ref, g_ref, own_ref, mem_ref, w_ref, qv_ref, has_ref, lse_ref,
     dx_ref, dpool_ref, gw_ref, row_ref,
-    x_s, q_s, k_s, v_s, s_s, dp_s, p_s, ds_s, dk_s, dv_s, dq_s, gw_s,
+    w_s, x_s, q_s, k_s, v_s, s_s, dp_s, p_s, ds_s, dk_s, dv_s, dq_s, gw_s,
 ):
     nq, width = q_s.shape
     step = pl.program_id(0)
+    columns = key_mask(own_ref, mem_ref, valid, has_ref[step])
+    if width == 384:
+        @pl.when(step == 0)
+        def _():
+            assemble(w_ref, w_s)
+        w_ref = w_s
     project_queries(x_ref, w_ref, qv_ref, q_s)
     project_keys(own_ref, mem_ref, w_ref, qv_ref, x_s, k_s, v_s)
     scaling = HD**-0.5
@@ -234,7 +269,7 @@
             def body(i, carry, head=head):
                 rows = pl.ds(pl.multiple_of(i * chunk, chunk), chunk)
                 lse = jnp.sum(jnp.where(lanes == head, lse_ref[0, rows, :], 0.0), axis=1, keepdims=True)
-                p = jnp.exp2(s_s[rows, :] * factor + mask_ref[0] - lse)
+                p = jnp.exp2(s_s[rows, :] * factor + columns - lse)
                 dp = dp_s[rows, :]
                 inner = jnp.sum(p * dp, axis=1, keepdims=True)
                 p_s[rows, :] = p.astype(bf16)
@@ -281,8 +316,12 @@
 
 
 def first_mlp_kernel(x_ref, comb_ref, out_ref, up_ref, down_ref, ub_ref, vec_ref, pool_ref, pair_ref,
-                     after_ref, middle_ref, pooled_ref, mean_ref):
-    after = x_ref[0].astype(f32) + dot(comb_ref[0], out_ref[...], NT) + vec_ref[0:1, :]
+                     after_ref, middle_ref, pooled_ref, mean_ref, out_s):
+    @pl.when(pl.program_id(0) == 0)
+    def _():
+        assemble_out(out_ref, out_s)
+
+    after = x_ref[0].astype(f32) + dot(comb_ref[0], out_s[...], NT) + vec_ref[0:1, :]
     after_ref[0] = after
     unit, _ = norm(after)
     low = (unit * vec_ref[1:2, :] + vec_ref[2:3, :]).astype(bf16)
@@ -365,7 +404,7 @@
     middle_ref, after_ref, comb_ref, dskip_ref, dq_ref, own_ref, mem_ref, out_ref, up_ref, down_ref, ub_ref, vec_ref,
     unpool_ref, unpair_ref,
     res_ref, dcomb_ref, gmlp_ref, gub_ref, row_ref,
-    gup_s, gdown_s, gout_s,
+    gup_s, gdown_s, gout_s, out_s,
 ):
     step = pl.program_id(0)
 
@@ -375,6 +414,7 @@
         gdown_s[...] = jnp.zeros_like(gdown_s)
         gout_s[...] = jnp.zeros_like(gout_s)
         gub_ref[...] = jnp.zeros_like(gub_ref)
+        assemble_out(out_ref, out_s)
 
     dpool = dskip_ref[0] + dq_ref[0] + own_ref[0] + exact_dot(unpair_ref[...], mem_ref[0])
     dnorm = exact_dot(unpool_ref[...], dpool)
@@ -401,7 +441,7 @@
     rows += [sum_rows(dnormed * unit), sum_rows(dnormed), sum_rows(res)]
     res_ref[0] = res
     res = res.astype(bf16)
-    dcomb_ref[0] = dot(res, out_ref[...]).astype(bf16)
+    dcomb_ref[0] = dot(res, out_s[...]).astype(bf16)
     gout_s[...] += dot(transposed(res), comb_ref[0])
     add_rows(row_ref, rows)
 
@@ -439,7 +479,11 @@
     return jax.ShapeDtypeStruct(dims, dtype)
 
 
-def call(kernel, steps, args, outs, scratch=(), name=None):
+def about(us):
+    return pl.CostEstimate(flops=int(us * 1e9), bytes_accessed=0, transcendentals=0)
+
+
+def call(kernel, steps, args, outs, scratch=(), name=None, us=10):
     def spec(array, how):
         if how is None:
             return whole(array)
@@ -453,6 +497,7 @@
         out_shape=[a for a, _ in outs],
         scratch_shapes=[pltpu.VMEM(dims, dtype) for dims, dtype in scratch],
         compiler_params=pltpu.CompilerParams(vmem_limit_bytes=VMEM_CAP),
+        cost_estimate=about(us),
         name=name,
     )(*[a for a, _ in args])
 
@@ -461,31 +506,34 @@
     return 112 if nq % 112 == 0 else 16
 
 
-def attend(x, own, mem, w, qv, mask, width):
+def attend(x, own, mem, w, qv, has, valid, width):
     batches, nq, d = x.shape
     keys = own.shape[0] * own.shape[2] + mem.shape[0] * mem.shape[2]
     return call(
-        functools.partial(attend_kernel, chunk_of(nq)), batches,
-        [(x, 0), (own, 1), (mem, 1), (w, None), (qv, None), (mask, 0)],
+        functools.partial(attend_kernel, chunk_of(nq), valid), batches,
+        [(x, 0), (own, 1), (mem, 1), w, (qv, None), (has, pl.BlockSpec(memory_space=pltpu.SMEM))],
         [(shape((batches, nq, width), bf16), 0), (shape((batches, nq, 128), f32), 0)],
-        [((keys, d), bf16), ((nq, width), bf16), ((keys, width), bf16), ((keys, width), bf16), ((nq, keys), f32), ((nq, keys), bf16)],
-        name="attend",
+        [((1, d, 1152 if width == 384 else 128), bf16),
+         ((keys, d), bf16), ((nq, width), bf16), ((keys, width), bf16), ((keys, width), bf16), ((nq, keys), f32), ((nq, keys), bf16)],
+        name="attend", us=20,
     )
 
 
-def attend_back(x, grad, own, mem, w, qv, mask, lse, heads):
+def attend_back(x, grad, own, mem, w, qv, has, valid, lse, heads):
     batches, nq, d = x.shape
     width = grad.shape[2]
     keys = own.shape[0] * own.shape[2] + mem.shape[0] * mem.shape[2]
     both = (own.shape[0], batches, own.shape[2] + mem.shape[2], d)
+    groups = (width // 384, d, 1152)
     return call(
-        functools.partial(attend_back_kernel, chunk_of(nq)), batches,
-        [(x, 0), (grad, 0), (own, 1), (mem, 1), (w, None), (qv, None), (mask, 0), (lse, 0)],
+        functools.partial(attend_back_kernel, chunk_of(nq), valid), batches,
+        [(x, 0), (grad, 0), (own, 1), (mem, 1), w, (qv, None), (has, pl.BlockSpec(memory_space=pltpu.SMEM)), (lse, 0)],
         [(shape((batches, nq, d), f32), 0), (shape(both, bf16), 1), (shape((heads, d, 3 * width // heads), bf16), None), (shape((8, width), f32), None)],
-        [((keys, d), bf16), ((nq, width), bf16), ((keys, width), bf16), ((keys, width), bf16),
+        [((1, d, 1152 if width == 384 else 128), bf16),
+         ((keys, d), bf16), ((nq, width), bf16), ((keys, width), bf16), ((keys, width), bf16),
          ((nq, keys), f32), ((nq, keys), f32), ((nq, keys), bf16), ((nq, keys), bf16),
-         ((384, keys), f32), ((384, keys), f32), ((8, 128), f32), (w.shape, f32)],
-        name="attend_back",
+         ((384, keys), f32), ((384, keys), f32), ((8, 128), f32), (groups, f32)],
+        name="attend_back", us=36,
     )
 
 
@@ -524,7 +572,9 @@
 
 def share_kernel(gather, *refs):
     if gather:
-        pooled_ref, mean_ref, pick_ref, w_ref, own_ref, mem_ref, all_ref, *refs = refs
+        pooled_ref, mean_ref, pick_ref, w_ref, *refs = refs
+        biases, (own_ref, mem_ref, all_ref, *refs) = refs[:4], refs[4:]
+        (qv_a_ref, qv_b_ref, ub_a_ref, ub_b_ref), refs = refs[:4], refs[4:]
     else:
         pooled_ref, mean_ref, pick_ref, own_ref, mem_ref, *refs = refs
     (got_s, pick_s, local_sem, own_send, own_recv, mem_send, mem_recv, pass_send, pass_recv, clip_send, clip_recv, *refs) = refs
@@ -558,7 +608,14 @@
 
     w_first, w_diagonal, w_core = {}, {}, {}
     if gather:
-        w_local, w_send, w_recv, d_send, d_recv, c_send, c_recv = refs
+        w_local, w_send, w_recv, d_send, d_recv, c_send, c_recv, b_send, b_recv, *bias_got = refs
+        bias_copies = [
+            remote(ref, got.at[d], b_send.at[d, n], b_recv.at[d, n], device)
+            for d, device in enumerate(beside)
+            for n, (ref, got) in enumerate(zip(biases, bias_got))
+        ]
+        for copy in bias_copies:
+            copy.start()
         mine = all_ref.at[head, here]
         for k in range(1, chips):
             w_first[k, 0] = remote(w_ref, mine, w_send.at[k - 1], w_recv.at[k - 1], across[k - 1])
@@ -629,6 +686,24 @@
             forward(k, d)
         for copy in w_core.values():
             copy.wait_recv()
+        for copy in bias_copies:
+            copy.wait_recv()
+        by_head = []
+        for ref, got in zip(biases, bias_got):
+            pieces = []
+            for h in range(heads):
+                piece = ref[...]
+                for d in range(1, heads):
+                    piece = jnp.where(rem(head - d, heads) == h, got[d - 1], piece)
+                pieces.append(piece)
+            by_head.append(pieces)
+        qv_a_ref[...] = jnp.concatenate(by_head[0], axis=1)
+        qv_b_ref[...] = jnp.concatenate(by_head[1], axis=1)
+        for h in range(heads):
+            ub_a_ref[h] = by_head[2][h]
+        ub_b_ref[...] = jnp.concatenate(by_head[3], axis=1)
+        for copy in bias_copies:
+            copy.wait_send()
     own_copies[0].wait_recv()
     mem_copies[0].wait_recv()
     for copy in forwards:
@@ -655,7 +730,7 @@
     return pltpu.SemaphoreType.DMA(dims)
 
 
-def share_pooled(pooled, mean, pick, number, block=None):
+def share_pooled(pooled, mean, pick, number, block=None, biases=()):
     toks, heads = lax.axis_size("tok"), lax.axis_size("head")
     chips = toks // 2
     few = max(chips - 1, 1)
@@ -666,24 +741,30 @@
         dma(chips), dma(chips), dma(chips), dma(chips), dma(2, few), dma(2, few), dma(heads), dma(heads),
     ]
     if block is not None:
-        args, specs, outs = args + [block], specs + [ANY], outs + [shape((heads, toks) + block.shape, bf16)]
+        args, specs = args + [block, *biases], specs + [ANY] + [INVMEM] * len(biases)
+        (_, wa), (_, wb), (_, fa), (_, fb) = (b.shape for b in biases)
+        outs = outs + [shape((heads, toks) + block.shape, bf16)]
+        outs += [shape(dims, f32) for dims in ((2, heads * wa), (2, heads * wb), (heads, 1, fa), (1, heads * fb))]
         firsts = max(chips + heads - 2, 1)
         scratch += [dma(1), dma(firsts), dma(firsts), dma(few, max(heads - 1, 1)), dma(few, max(heads - 1, 1)), dma(chips, heads), dma(chips, heads)]
+        scratch += [dma(max(heads - 1, 1), 4), dma(max(heads - 1, 1), 4)]
+        scratch += [pltpu.VMEM((max(heads - 1, 1),) + b.shape, f32) for b in biases]
     return pl.pallas_call(
         functools.partial(share_kernel, block is not None),
         in_specs=specs,
-        out_specs=[ANY] * len(outs),
+        out_specs=[ANY] * min(len(outs), 3) + [INVMEM] * (len(outs) - 3),
         out_shape=outs,
         scratch_shapes=scratch,
         compiler_params=pltpu.CompilerParams(collective_id=number, has_side_effects=True, vmem_limit_bytes=VMEM_CAP),
+        cost_estimate=about(20 if block is None else 30),
         name="share_pooled",
     )(*args)
 
 
 def give_back_kernel(exchange, *refs):
     if exchange:
-        part_ref, pick_ref, half_ref, own_ref, back_ref, all_ref, *refs = refs
-        *refs, half_local, half_send, half_recv = refs
+        part_ref, pick_ref, half_ref, piece_ref, shard_ref, own_ref, back_ref, all_ref, pieces_ref, sum_ref, *refs = refs
+        *refs, half_local, half_send, half_recv, piece_send, piece_recv, shard_send, shard_recv, shard_s = refs
     else:
         part_ref, pick_ref, own_ref, back_ref, *refs = refs
     (mine_s, core_s, sum_s, chip_s, route_s, got_s,
@@ -696,7 +777,8 @@
     beside = [{"head": rem(head + d, heads)} for d in range(1, heads)]
     heads_of = lambda by, sign: [{"clip": clip + by, "head": rem(head + sign * d, heads)} for d in range(heads)]
     last, begun = clip < clips - 1, clip > 0
-    near = [(d, None) for d in [partner] + across + (beside if exchange else [])]
+    along = [{"clip": rem(clip + k, clips)} for k in range(1, clips)]
+    near = [(d, None) for d in [partner] + across + (beside + along if exchange else [])]
     greet(near + [(d, last) for d in heads_of(1, 1)], near + [(d, begun) for d in heads_of(-1, -1)])
 
     order = [rem(chip + k, chips) for k in list(range(1, chips)) + [0]]
@@ -715,6 +797,7 @@
         half_copy = pltpu.make_async_copy(half_ref, all_ref.at[head], half_local.at[0])
         half_copy.start()
     mem_copies, own_copies = [], []
+    piece_copies, shard_copies = [], []
     for n in range(chips):
         local_copies[n].wait()
         core_copies[n].wait_recv()
@@ -750,6 +833,17 @@
                 route_s[d, s] = total.astype(bf16)
             clip_copies[d].start()
 
+    if exchange:
+        wide = sum_ref.shape[1]
+        lanes = lambda c: pl.ds(pl.multiple_of(wide * c, wide), wide)
+        for k, d in enumerate(along):
+            shard_copies.append(
+                remote(shard_ref.at[:, lanes(rem(clip + k + 1, clips))], shard_s.at[k], shard_send.at[k], shard_recv.at[k], d))
+            piece_copies.append(remote(piece_ref, pieces_ref.at[clip], piece_send.at[k], piece_recv.at[k], d))
+        for copy in shard_copies + piece_copies:
+            copy.start()
+        piece_copy = pltpu.make_async_copy(piece_ref, pieces_ref.at[clip], half_local.at[1])
+        piece_copy.start()
     for copy in own_copies:
         copy.wait_recv()
     for m in range(share):
@@ -771,12 +865,20 @@
     def _():
         back_ref[...] = jnp.zeros_like(back_ref)
 
-    for copy in halves:
+    if exchange:
+        for copy in shard_copies:
+            copy.wait_recv()
+        total = shard_ref[:, lanes(clip)].astype(f32)
+        for k in range(clips - 1):
+            total = total + shard_s[k].astype(f32)
+        sum_ref[...] = total.astype(bf16)
+    for copy in halves + piece_copies:
         copy.wait_recv()
-    for copy in core_copies + mem_copies + own_copies + halves:
+    for copy in core_copies + mem_copies + own_copies + halves + piece_copies + shard_copies:
         copy.wait_send()
     if exchange:
         half_copy.wait()
+        piece_copy.wait()
 
     @pl.when(begun)
     def _():
@@ -784,7 +886,7 @@
             copy.wait_send()
 
 
-def give_back(part, pick, own_rows, number, half=None):
+def give_back(part, pick, own_rows, number, half=None, piece=None, shard=None):
     toks, heads = lax.axis_size("tok"), lax.axis_size("head")
     chips, few = toks // 2, max(toks // 2 - 1, 1)
     share, rows, d = part.shape[1:]
@@ -797,9 +899,14 @@
         dma(chips), dma(chips), dma(chips), dma(few), dma(few), dma(few), dma(few), dma(heads), dma(heads),
     ]
     if half is not None:
-        args, specs = args + [half], specs + [ANY]
-        outs, out_specs = outs + [shape((heads,) + half.shape, half.dtype)], out_specs + [ANY]
-        scratch += [dma(1), dma(max(heads - 1, 1)), dma(max(heads - 1, 1))]
+        clips = lax.axis_size("clip")
+        wide = shard.shape[1] // clips
+        args, specs = args + [half, piece, shard], specs + [ANY, ANY, INVMEM]
+        outs += [shape((heads,) + half.shape, half.dtype), shape((clips,) + piece.shape, bf16), shape((shard.shape[0], wide), bf16)]
+        out_specs += [ANY, ANY, INVMEM]
+        along = max(clips - 1, 1)
+        scratch += [dma(2), dma(max(heads - 1, 1)), dma(max(heads - 1, 1)), dma(along), dma(along), dma(along), dma(along)]
+        scratch += [pltpu.VMEM((along, shard.shape[0], wide), bf16)]
     return pl.pallas_call(
         functools.partial(give_back_kernel, half is not None),
         in_specs=specs,
@@ -807,15 +914,17 @@
         out_shape=outs,
         scratch_shapes=scratch,
         compiler_params=pltpu.CompilerParams(collective_id=number, has_side_effects=True, vmem_limit_bytes=VMEM_CAP),
+        cost_estimate=about(25 if half is None else 35),
         name="give_back",
     )(*args)
 
 
-def finish_kernel(sizes, half_ref, early_ref, last_ref, qv_ref, grad_ref, rest_ref, all_ref, gains_a_ref, gains_b_ref, shifts_a_ref,
-                  shifts_b_ref, qv_a_ref, qv_b_ref, ub_a_ref, ub_b_ref, gtotal_ref, up_ref, down_ref, out_ref, *scratch):
+def finish_kernel(sizes, half_ref, last_ref, qv_a_rows, a_ref, b_ref, qv_b_rows, ub_a_rows, ub_b_rows, grad_ref, rest_ref, piece_ref, all_ref, gains_a_ref, gains_b_ref, shifts_a_ref,
+                  shifts_b_ref, qv_a_ref, qv_b_ref, ub_a_ref, ub_b_ref, gtotal_ref, up_ref, down_ref, out_ref,
+                  q_ref, out_b_ref, skip_ref, *scratch):
     (small_ref, small_s, small_core, small_chip, small_head, small_clip, part_s, part_core, chip_s, part_chip, head_s, part_head, mine_s, part_clip,
      rest_in, rest_s, local_sem, half_send, half_recv, core_send, core_recv, chip_send, chip_recv, head_send, head_recv,
-     clip_send, clip_recv, rest_send, rest_recv, back_send, back_recv) = scratch
+     clip_send, clip_recv, rest_send, rest_recv, back_send, back_recv, piece_s, piece_send, piece_recv) = scratch
     clip, head, chip, core, chips = places()
     clips, heads = lax.axis_size("clip"), lax.axis_size("head")
     share = half_ref.shape[0]
@@ -826,9 +935,18 @@
     peers = [(d, None) for d in [partner] + across + beside + along]
     greet(peers, peers)
     pending = []
-    small_ref[...] = early_ref[...]
+    d1 = small_ref.shape[1]
+    small_ref[...] = jnp.zeros_like(small_ref)
     small_ref[0:2, :] = last_ref[0:2, :]
-    small_ref[2:4, :] = qv_ref[0:2, :]
+    small_ref[2:4, :] = qv_a_rows[0:2, :]
+    for row, source in enumerate((3, 0, 5, 4, 2, 1)):
+        small_ref[4 + row:5 + row, :] = a_ref[source:source + 1, :]
+    row = 10
+    longer = [b_ref[n:n + 1, :] for n in (3, 0, 1, 2)] + [qv_b_rows[n:n + 1, :] for n in range(2)]
+    for values in longer + [ub_a_rows[h] for h in range(heads)] + [ub_b_rows[...]]:
+        for low in range(0, values.shape[1], d1):
+            small_ref[row:row + 1, :] = values[:, low:low + d1]
+            row += 1
     wide = rest_ref.shape[1] // clips
 
     def lanes(c):
@@ -859,6 +977,10 @@
             n = h * chips + x
             first += go([remote(grad_ref.at[2 * n + 1 - core], part_core.at[n], core_send.at[n + 1], core_recv.at[n + 1], partner)])
     gather = go([remote(rest_ref.at[:, lanes(rem(clip + k + 1, clips))], rest_in.at[k], rest_send.at[k], rest_recv.at[k], d) for k, d in enumerate(along)])
+    wider = piece_ref.shape[1]
+    group = pl.ds(pl.multiple_of(wider * clip, wider), wider)
+    piece_s[:, group] = piece_ref[...]
+    pieces = go([remote(piece_ref, piece_s.at[:, group], piece_send.at[k], piece_recv.at[k], d) for k, d in enumerate(along)])
     halves = [
         [remote(half_ref.at[s], all_ref.at[head, s], half_send.at[k, s], half_recv.at[k, s], d) for k, d in enumerate(beside)]
         for s in range(share)
@@ -942,6 +1064,13 @@
     up_ref[...] = rest_s[:, :wide].astype(f32)
     down_ref[...] = rest_s[:, wide:2 * wide].astype(f32)
     out_ref[...] = rest_s[:, 2 * wide:2 * wide + out_ref.shape[1]].astype(f32)
+    arrived(pieces)
+    wide, rows = q_ref.shape[1], piece_s.shape[0]
+    q_ref[...] = piece_s[:, :wide].astype(f32)
+    for ref in (out_b_ref, skip_ref):
+        for n in range(2):
+            ref[rows * n:rows * n + rows, :] = piece_s[:, wide:wide + ref.shape[1]].astype(f32)
+            wide += ref.shape[1]
     for copies in halves:
         arrived(copies)
     for copy in pending:
@@ -949,31 +1078,35 @@
     local_half.wait()
 
 
-def finish(half, early, last, qv, grad, rest, d2, fa, fb, ha, number):
+def finish(half, rows, grad, rest, piece, d2, fa, fb, ha, hs, number):
     toks, heads, clips = lax.axis_size("tok"), lax.axis_size("head"), lax.axis_size("clip")
     chips = toks // 2
     across, beside, along = (max(n, 1) for n in (chips - 1, heads - 1, clips - 1))
-    block, rows, d1 = grad.shape[1:], rest.shape[0], early.shape[1]
-    low, full = lambda *dims: pltpu.VMEM(dims, bf16), lambda *dims: pltpu.VMEM(dims + early.shape, f32)
+    block, depth, d1 = grad.shape[1:], rest.shape[0], rows[0].shape[1]
+    count = 4 + 6 + (6 * d2 + fa + fb) // d1
+    low, full = lambda *dims: pltpu.VMEM(dims, bf16), lambda *dims: pltpu.VMEM(dims + (-(-count // 8) * 8, d1), f32)
     sums = [(3, d1), (1, d2), (5, d1), (3, d2), (2, d1 // heads), (2, d2 // heads), (1, fa // heads), (1, fb // heads),
-            block, (rows, fa // heads), (rows, fa // heads), (rows, ha)]
+            block, (depth, fa // heads), (depth, fa // heads), (depth, ha),
+            (piece.shape[0], 3 * d2 // heads), (2 * piece.shape[0], d2 // heads), (2 * piece.shape[0], hs)]
     return pl.pallas_call(
         functools.partial(finish_kernel, (d2, fa, fb)),
-        in_specs=[ANY] + [INVMEM] * 5,
+        in_specs=[ANY] + [INVMEM] * (len(rows) + 3),
         out_specs=[ANY] + [INVMEM] * len(sums),
         out_shape=[shape((heads,) + half.shape, half.dtype)] + [shape(dims, f32) for dims in sums],
         scratch_shapes=[
             full(), full(3), full(), full(across), full(beside), full(along),
             low(heads * chips, *block), low(heads * chips, *block), low(heads, *block), low(across, heads, *block),
             low(heads, *block), low(beside, *block), low(*block), low(along, *block),
-            low(along, rows, rest.shape[1] // clips), low(*rest.shape),
+            low(along, depth, rest.shape[1] // clips), low(*rest.shape),
             dma(1), dma(beside, half.shape[0]), dma(beside, half.shape[0]), dma(heads * chips + 1), dma(heads * chips + 1),
             dma(across, heads + 1), dma(across, heads + 1), dma(beside, 2), dma(beside, 2), dma(along, 2), dma(along, 2),
             dma(along), dma(along), dma(along), dma(along),
+            low(piece.shape[0], clips * piece.shape[1]), dma(along), dma(along),
         ],
         compiler_params=pltpu.CompilerParams(collective_id=number, has_side_effects=True, vmem_limit_bytes=VMEM_CAP),
+        cost_estimate=about(40),
         name="finish",
-    )(half, early, last, qv, grad, rest)
+    )(half, *rows, grad, rest, piece)
 
 
 def reduce_clips(shard):
@@ -984,26 +1117,6 @@
         give = lax.dynamic_index_in_dim(pieces, (clip + k) % clips, 0, keepdims=False)
         total = total + lax.ppermute(give, "clip", [(i, (i + k) % clips) for i in range(clips)]).astype(f32)
     return total.astype(bf16)
-
-
-def spread_clips(piece):
-    clips, clip = lax.axis_size("clip"), lax.axis_index("clip")
-    out = jnp.zeros((clips,) + piece.shape, piece.dtype)
-    out = lax.dynamic_update_index_in_dim(out, piece, clip, 0)
-    for k in range(1, clips):
-        got = lax.ppermute(piece, "clip", [(i, (i + k) % clips) for i in range(clips)])
-        out = lax.dynamic_update_index_in_dim(out, got, (clip - k + clips) % clips, 0)
-    return out.reshape((-1,) + piece.shape[1:])
-
-
-def from_heads(piece, heads):
-    head = lax.axis_index("head")
-    out = jnp.zeros((heads,) + piece.shape, piece.dtype)
-    out = lax.dynamic_update_index_in_dim(out, piece, head, 0)
-    for d in range(1, heads):
-        got = lax.ppermute(piece, "head", [(i, (i + d) % heads) for i in range(heads)])
-        out = lax.dynamic_update_index_in_dim(out, got, (head - d + heads) % heads, 0)
-    return out.reshape((-1,) + piece.shape[1:])
 
 
 def padded_rows(*rows):
@@ -1030,78 +1143,54 @@
     cot = lax.dynamic_slice_in_dim(cotangent[0], first, share, 0).reshape(share, pooled_tokens, d2)
     cot = jnp.pad(cot, ((0, 0), (0, own_rows - pooled_tokens), (0, 0))).reshape(rows2, d2)
 
-    picks, masks = [], []
-    row_own = jnp.where(jnp.arange(own_rows) < pooled_tokens, 0.0, NEG)
-    row_mem = jnp.arange(mem_rows) < frames // 2 * POOLED
-    for m in range(share):
-        source = lax.dynamic_index_in_dim(assign[0], first + m, 0, keepdims=False)
-        flag = lax.dynamic_index_in_dim(resets[0], first + m, 0, keepdims=False)
-        slot = ((head - source // share + heads) % heads) * share + source % share
-        picks.append((jnp.arange(heads * share) == slot).astype(f32))
-        has = (flag == 0) & (lax.axis_index("clip") > 0)
-        masks.append(jnp.concatenate([jnp.tile(row_own, toks), jnp.tile(jnp.where(row_mem & has, 0.0, NEG), toks)]))
-    mask = jnp.stack(masks)[:, None, :].astype(f32)
-    pick = jnp.stack(picks)
+    source = lax.dynamic_slice_in_dim(assign[0], first, share, 0)
+    flags = lax.dynamic_slice_in_dim(resets[0], first, share, 0)
+    slot = ((head - source // share + heads) % heads) * share + source % share
+    pick = (jnp.arange(heads * share)[None, :] == slot[:, None]).astype(f32)
+    has = ((flags == 0) & (lax.axis_index("clip") > 0)).astype(jnp.int32)
+    valid = (pooled_tokens, frames // 2 * POOLED)
 
     group = ("head", "tok")
     fa, ha = w_up_a.shape[1], w_out_a.shape[1]
     fb, hb, hs = w_up_b.shape[1], w_out_b.shape[1], w_skip_b.shape[1]
+    mine = lax.dynamic_slice_in_dim(clips_in[0], first, share, 0)
+    stream, low1, pooled1, mean1 = call(
+        norm_pool_kernel, share,
+        [(mine, 0), (padded_rows(gains_a[0], shifts_a[0]), None), (pooling, None), (pairing, None)],
+        [(shape((share, tokens, d1), bf16), 0), (shape((share, tokens, d1), bf16), 0),
+         (shape((share, own_rows, d1), bf16), 0), (shape((share, mem_rows, d1), bf16), 0)],
+        name="norm_pool", us=5,
+    )
+    pooled1, w_qkv_b, w_up_b = lax.optimization_barrier((pooled1, w_qkv_b, w_up_b))
     pack_a = jnp.concatenate([w_up_a, w_down_a, w_qkv_a.reshape(w_qkv_a.shape[0], -1), w_out_a], axis=1)
     pack_q = w_qkv_b.reshape(w_qkv_b.shape[0], -1)
     pack_b = jnp.concatenate([w_up_b, w_down_b, w_out_b, w_skip_b], axis=1)
-    vec1 = padded_rows(gains_a[0], shifts_a[0])
-    fixed = lambda *dims: pl.BlockSpec(dims, lambda i, first: (0,) * len(dims))
-    micro_spec = lambda rows: pl.BlockSpec((1, rows, d1), lambda i, first: (i, 0, 0))
-    stream, low1, pooled1, mean1 = pl.pallas_call(
-        norm_pool_kernel,
-        grid_spec=pltpu.PrefetchScalarGridSpec(
-            num_scalar_prefetch=1,
-            grid=(share,),
-            in_specs=[pl.BlockSpec((1, 1) + clips_in.shape[2:], lambda i, first: (0, first[0] + i, 0, 0, 0)),
-                      fixed(*vec1.shape), fixed(*pooling.shape), fixed(*pairing.shape)],
-            out_specs=[micro_spec(rows) for rows in (tokens, tokens, own_rows, mem_rows)],
-        ),
-        out_shape=[shape((share, rows, d1), bf16) for rows in (tokens, tokens, own_rows, mem_rows)],
-        compiler_params=pltpu.CompilerParams(vmem_limit_bytes=VMEM_CAP),
-        name="norm_pool",
-    )(first.astype(jnp.int32)[None], clips_in, vec1, pooling, pairing)
-    own1, mem1, all_a = share_pooled(pooled1, mean1, pick, 0, pack_a)
-    all_a = all_a.reshape(heads, d1, -1)
-    own1, flat = lax.optimization_barrier((
-        own1, jnp.concatenate([qv_bias_a.reshape(-1), qv_bias_b.reshape(-1), up_bias_a, up_bias_b])))
     all_q = lax.all_gather(pack_q, group).reshape(heads, d1, -1)
     all_b = lax.all_gather(pack_b, group).reshape(heads, d2, -1)
-    flat = from_heads(flat[None], heads)
-    qv_a = flat[:, :2 * ha].reshape(heads, 2, ha).transpose(1, 0, 2).reshape(2, d1)
-    qv_b = flat[:, 2 * ha:2 * ha + 2 * hb].reshape(heads, 2, hb).transpose(1, 0, 2).reshape(2, d2)
-    ub_a = flat[:, 2 * (ha + hb):2 * (ha + hb) + fa].reshape(heads, 1, fa)
-    ub_b = flat[:, 2 * (ha + hb) + fa:].reshape(1, heads * fb)
+    own1, mem1, all_a, qv_a, qv_b, ub_a, ub_b = share_pooled(
+        pooled1, mean1, pick, 0, pack_a, [qv_bias_a, qv_bias_b, up_bias_a[None], up_bias_b[None]])
+    all_a = all_a.reshape(heads, d1, -1)
 
     def lanes(pack, low, width):
         return jnp.concatenate([pack[h, :, low:low + width] for h in range(heads)], axis=1)
 
-    up_spec, down_spec = (pl.BlockSpec((heads, d1, fa), lambda i, n=n: (0, 0, n)) for n in range(2))
-    qkv_a = jnp.concatenate([lanes(all_a, 2 * fa + i * ha, ha) for i in range(3)], axis=1)[None]
-    out_a = lanes(all_a, 2 * fa + 3 * ha, ha)
-    qkv_b = all_q
-    if hb != 384:
-        parts = [lanes(all_q, i * hb, hb).reshape(d1, -1, 384).transpose(1, 0, 2) for i in range(3)]
-        qkv_b = jnp.concatenate(parts, axis=2)
+    up_spec, down_spec, rest_spec = (pl.BlockSpec((heads, d1, fa), lambda i, n=n: (0, 0, n)) for n in range(3))
     skip_b = lanes(all_b, 2 * fb + hb, hs)
 
-    comb1, lse1 = attend(low1, own1, mem1, qkv_a, qv_a, mask, d1)
+    comb1, lse1 = attend(low1, own1, mem1, (all_a, rest_spec), qv_a, has, valid, d1)
     after1, middle, pooled3, mean3 = call(
         first_mlp_kernel, share,
-        [(stream, 0), (comb1, 0), (out_a, None), (all_a, up_spec), (all_a, down_spec), (ub_a, None),
+        [(stream, 0), (comb1, 0), (all_a, rest_spec), (all_a, up_spec), (all_a, down_spec), (ub_a, None),
          (padded_rows(shifts_a[1], gains_a[1], shifts_a[2], shifts_a[3], gains_a[2], shifts_a[4]), None),
          (pooling, None), (pairing, None)],
         [(shape((share, tokens, d1), f32), 0), (shape((share, tokens, d1), f32), 0),
          (shape((share, own_rows, d1), bf16), 0), (shape((share, mem_rows, d1), bf16), 0)],
-        name="first_mlp",
+        [((d1, d1), bf16)],
+        name="first_mlp", us=13,
     )
 
     own2, mem2 = share_pooled(pooled3, mean3, pick, 1)
-    comb2, lse2 = attend(pooled3, own2, mem2, qkv_b, qv_b, mask, d2)
+    comb2, lse2 = attend(pooled3, own2, mem2, (all_q, None), qv_b, has, valid, d2)
     chunk = 768
     per_head = fb // chunk
     steps = heads * per_head
@@ -1120,7 +1209,7 @@
          (shape((heads, toks, d2 // toks // 2, 2 * hb), bf16), None), (shape((heads, toks, d2 // toks // 2, 2 * hs), bf16), None),
          (shape((1, heads * fb), f32), pl.BlockSpec((1, chunk), lambda j: (0, j))), (shape((8, d2), f32), None)],
         [((rows2, d2), f32), ((rows2, d2), bf16), ((d2, rows2), bf16), ((d2, rows2), bf16), ((rows2, d2), f32), ((rows2, d2), f32)],
-        name="second_mlp",
+        name="second_mlp", us=26,
     )
 
     def by_owner(grad):
@@ -1131,54 +1220,44 @@
 
     sum_mlp_b = scatter(g_mlp_b.reshape((heads * toks,) + g_mlp_b.shape[2:]))
     dcomb2 = dcomb2.reshape(share, own_rows, d2)
-    dq2, dpool2, g_qkv_b, rows_qv_b = attend_back(pooled3, dcomb2, own2, mem2, qkv_b, qv_b, mask, lse2, heads)
-    own_back2, mem_back2, mixed_all = give_back(dpool2, pick, own_rows, 2, mixed.reshape(share, own_rows, d2))
+    dq2, dpool2, g_qkv_b, rows_qv_b = attend_back(pooled3, dcomb2, own2, mem2, (all_q, None), qv_b, has, valid, lse2, heads)
+    own_back2, mem_back2 = give_back(dpool2, pick, own_rows, 2)
 
     merge = lambda grad: grad.reshape((heads * toks,) + grad.shape[2:])
-    sum_rest_b = scatter(jnp.concatenate([by_owner(g_qkv_b), merge(g_out_b), merge(g_skip_b)], axis=2))
+    rest_b = jnp.concatenate([by_owner(g_qkv_b), merge(g_out_b), merge(g_skip_b)], axis=2)
+    rest_b = jnp.pad(rest_b, ((0, 0), (0, 0), (0, -rest_b.shape[2] % (128 * clips))))
+    sum_rest_b = scatter(rest_b)
 
     res1, dcomb1, g_mlp_a, g_ub_a, rows_a = call(
         first_back_kernel, share,
         [(middle, 0), (after1, 0), (comb1, 0), (dskip.reshape(share, own_rows, d1), 0), (dq2, 0), (own_back2, 0), (mem_back2, 0),
-         (out_a, None), (all_a, up_spec), (all_a, down_spec), (ub_a, None),
+         (all_a, rest_spec), (all_a, up_spec), (all_a, down_spec), (ub_a, None),
          (padded_rows(gains_a[1], shifts_a[2], gains_a[2]), None), (unpooling, None), (unpairing, None)],
         [(shape((share, tokens, d1), f32), 0), (shape((share, tokens, d1), bf16), 0),
          (shape((heads, d1, -(-(2 * fa + ha) // (128 * clips)) * 128 * clips), bf16), None),
          (shape((heads, 1, fa), f32), None), (shape((8, d1), f32), None)],
-        [((heads, d1, fa), f32), ((heads, d1, fa), f32), ((d1, d1), f32)],
-        name="first_back",
+        [((heads, d1, fa), f32), ((heads, d1, fa), f32), ((d1, d1), f32), ((d1, d1), bf16)],
+        name="first_back", us=26,
     )
     rest_a = by_owner(g_mlp_a)
     dcomb1, sum_mlp_b, rest_a = lax.optimization_barrier((dcomb1, sum_mlp_b, rest_a))
     sum_rest_a = scatter(rest_a)
     sum_mlp_b = reduce_clips(sum_mlp_b)
-    dx1, dpool1, g_qkv_a, rows_qv_a = attend_back(low1, dcomb1, own1, mem1, qkv_a, qv_a, mask, lse1, heads)
-    dpool1, sum_mlp_b, sum_rest_b = lax.optimization_barrier((dpool1, sum_mlp_b, sum_rest_b))
-    mlp_b = spread_clips(sum_mlp_b)
-    sum_rest_b = reduce_clips(sum_rest_b)
-    own_back1, mem_back1 = give_back(dpool1, pick, own_rows, 3)
+    dx1, dpool1, g_qkv_a, rows_qv_a = attend_back(low1, dcomb1, own1, mem1, (all_a, rest_spec), qv_a, has, valid, lse1, heads)
+    own_back1, mem_back1, mixed_all, mlp_b, piece_b = give_back(
+        dpool1, pick, own_rows, 3, mixed.reshape(share, own_rows, d2), sum_mlp_b, sum_rest_b)
     stream_grad, rows_last = call(
         last_back_kernel, share,
         [(stream, 0), (res1, 0), (dx1, 0), (own_back1, 0), (mem_back1, 0), (padded_rows(gains_a[0]), None),
          (unpooling, None), (unpairing, None)],
         [(shape((share, frames, PATCH, d1), bf16), 0), (shape((8, d1), f32), None)],
-        name="last_back",
+        name="last_back", us=6,
     )
 
-    zero = jnp.zeros((4, d1), f32)
-    early = [
-        zero, rows_a[3:4], rows_a[0:1], rows_a[5:6], rows_a[4:5], rows_a[2:3], rows_a[1:2],
-        rows_b[3:4], rows_b[:3], rows_qv_b[:2], g_ub_a, g_ub_b,
-    ]
-    early = jnp.concatenate([piece.reshape(-1, d1) for piece in early])
-    early = jnp.pad(early, ((0, -early.shape[0] % 8), (0, 0)))
-    rows_last, sum_rest_b, early = lax.optimization_barrier((rows_last, sum_rest_b, early))
-    rest_b = spread_clips(sum_rest_b).astype(f32)
     mlp_b = mlp_b.reshape((2, -1, mlp_b.shape[-1])).astype(f32)
+    rows = [rows_last, rows_qv_a, rows_a, rows_b, rows_qv_b, g_ub_a, g_ub_b]
     stream_all, *sums = finish(
-        stream_grad, early, rows_last, rows_qv_a, by_owner(g_qkv_a), sum_rest_a, d2, heads * fa, heads * fb, ha, 4)
-    out_lanes = rest_b[:, 3 * hb:5 * hb]
-    skip_lanes = rest_b[:, 5 * hb:]
+        stream_grad, rows, by_owner(g_qkv_a), sum_rest_a, piece_b, d2, heads * fa, heads * fb, ha, hs, 4)
     mixed_all = mixed_all.reshape(micro, own_rows, d2)[:, :pooled_tokens]
     return (
         mixed_all.reshape(cotangent.shape),
@@ -1187,9 +1266,9 @@
         sums[11],
         sums[9],
         sums[10],
-        rest_b[:, :3 * hb].reshape(w_qkv_b.shape),
-        jnp.concatenate([out_lanes[:, :hb], out_lanes[:, hb:]], axis=0),
-        jnp.concatenate([skip_lanes[:, :hs], skip_lanes[:, hs:]], axis=0),
+        sums[12].reshape(w_qkv_b.shape),
+        sums[13],
+        sums[14],
         mlp_b[0],
         mlp_b[1],
         sums[0], sums[1][0], sums[2], sums[3], sums[4], sums[5], sums[6][0], sums[7][0],

time: 463 us -> 457 us (0.987)
  Pallas kernels: 347 us -> 386 us
  starting transfers between devices: 17.6 us -> 4.7 us
  local copies, waits for them, and re-layouts: 40.5 us -> 28.8 us
  waiting for transfers between devices: 13.5 us -> 2.5 us
  between operations: 21.5 us -> 14.6 us
    pallas_call x2, Pallas kernels: 63.6 us -> 78.2 us  [give_back(): pl.pallas_call(functools.partial(give_back_kernel, half is not None), in_...]
    ppermute x7 -> x0, waiting for transfers between devices: 13.4 us -> none  [the longest x6 13.4 us: spread_clips(): lax.ppermute(piece, 'clip', [(i, (i + k) % clips) for i in range(clips)])]
    pallas_call x2, Pallas kernels: 53 us -> 65.9 us  [share_pooled(): pl.pallas_call(functools.partial(share_kernel, block is not None), in_spe...]
    pallas_call x1, Pallas kernels: 42.6 us -> 53.1 us  [finish(): pl.pallas_call(functools.partial(finish_kernel, (d2, fa, fb)), in_specs=[...]
    ppermute x7 -> x0, starting transfers between devices: 6.56 us -> none  [the longest x6 5.93 us: spread_clips(): lax.ppermute(piece, 'clip', [(i, (i + k) % clips) for i in range(clips)])]
    ppermute x6 -> x3, starting transfers between devices: 10.8 us -> 4.49 us  [reduce_clips(): lax.ppermute(give, 'clip', [(i, (i + k) % clips) for i in range(clips)])]
    pallas_call x8 -> x9, Pallas kernels: 183 us -> 189 us  [call(): pl.pallas_call(kernel, grid=(steps,), in_specs=[spec(a, how) for a, how i...]
    unnamed x90 -> x84, local copies, waits for them, and re-layouts: 17.7 us -> 13.1 us
  transfers between devices with their start and end apart: 18 -> 8, of which waited for: 3 -> 1; matrix products, arithmetic and copies ran while one was open for 9% -> 5% of each run, Pallas kernels for 61% -> 67%
where the time goes in v6:
time: 457 us; the launch traced here: 452 us
  Pallas kernels  386 us (84%)
  local copies, waits for them, and re-layouts  28.8 us (6%)
  other arithmetic  15.1 us (3%)
  between operations  14.6 us (3%)
  starting transfers between devices  4.7 us (1%)
    pallas_call x9, Pallas kernels, call(): pl.pallas_call(kernel, grid=(steps,), in_specs=[spec(a, how) for a, how i...  189 us
    pallas_call x2, Pallas kernels, give_back(): pl.pallas_call(functools.partial(give_back_kernel, half is not None), in_...  78.2 us
    pallas_call x2, Pallas kernels, share_pooled(): pl.pallas_call(functools.partial(share_kernel, block is not None), in_spe...  65.9 us
    pallas_call x1, Pallas kernels, finish(): pl.pallas_call(functools.partial(finish_kernel, (d2, fa, fb)), in_specs=[...  53.1 us
    unnamed x84, local copies, waits for them, and re-layouts  13.1 us
  transfers between devices with their start and end apart: 8, of which 1 were waited for; matrix products, arithmetic and copies ran while one was open for 5% of the time, Pallas kernels for 67%

profile of v6, /device:TPU:0, one launch (start us, length us, event | category | flops | bytes accessed | tf_op | source)
XLA Modules:
  0.0 451.9 jit_solution(6798545725246318159)
XLA Ops:
  7.3 1.8 constant_dynamic-slice_fusion.3
  11.1 4.5 norm_pool.1
  16.8 2.4 pad_maximum_fusion
  26.8 35.1 %share_pooled.2 = (bf16[4,2,208,384]{3,2,1,0:T(8,128)(2,1)}, bf16[4,2,112,384]{3,2,1,0:T(8,128)(2,1)}, bf16[2,4,96,2304]{3,2,1,0:T(8,128)(2,1)}, f32[2,384]{1,0:...) custom-call(bf16[2,208,384]{2,1,0:T(8,128)(2,1)} %get-tuple-element.95.refs_0_, ...), custom_call_target="tpu_custom_call" | custom-call | flops 30000001024 | tf_op jit(solution)/shard_map/share_pooled/pallas_call | solution.py:752
  61.9 21.9 %attend.2 = (bf16[2,784,384]{2,1,0:T(8,128)(2,1)}, f32[2,784,128]{2,1,0:T(8,128)}) custom-call(bf16[2,784,384]{2,1,0:T(8,128)(2,1)} %get-tuple-element.92.x_ref, bf16[4,2,208,384]{3,2,1,0:T(8,128)(2,1)} %get-tuple-element.97.own_ref, bf16[4,2,112,384]{3,2,1,0:T(8,128)(2,1)} %get-tuple-element.98.mem_ref, bf16[2,384,2304]{2,1,0:T(8,128)(2,1)} %bitcast.83, ...), custom_call_target="tpu_custom_call" | custom-call | flops 20000000000 | tf_op jit(solution)/shard_map/attend/pallas_call | solution.py:492
  83.8 13.4 %first_mlp.1 = (f32[2,784,384]{2,1,0:T(8,128)}, f32[2,784,384]{2,1,0:T(8,128)}, bf16[2,208,384]{2,1,0:T(8,128)(2,1)}, bf16[2,112,384]{2,1,0:T(8,128)(2,1)}) custom-call(bf16[2,784,384]{2,1,0:T(8,128)(2,1)} %get-tuple-element.93.x_ref, bf16[2,784,384]{2,1,0:T(8,128)(2,1)} %get-tuple-element.101.comb_ref, bf16[2,384,2304]{2,1,0:T(8,128)(2,1)} %bitcast.84, ...), custom_call_target="tpu_custom_call" | custom-call | flops 12999999488 | tf_op jit(solution)/shard_map/first_mlp/pallas_call | solution.py:492
  97.2 30.8 %share_pooled.3 = (bf16[4,2,208,384]{3,2,1,0:T(8,128)(2,1)}, bf16[4,2,112,384]{3,2,1,0:T(8,128)(2,1)}) custom-call(bf16[2,208,384]{2,1,0:T(8,128)(2,1)} %get-tuple-element.105.refs_0_.x_ref, bf16[2,112,384]{2,1,0:T(8,128)(2,1)} %get-tuple-element.106.refs_1_, f32[2,4]{1,0:T(2,128)} %compare_convert_fusion.refs_2_.refs_1_), custom_call_target="tpu_custom_call" | custom-call | flops 20000000000 | tf_op jit(solution)/shard_map/share_pooled/pallas_call | solution.py:752
  128.1 17.7 %attend.3 = (bf16[2,208,768]{2,1,0:T(8,128)(2,1)}, f32[2,208,128]{2,1,0:T(8,128)}) custom-call(bf16[2,208,384]{2,1,0:T(8,128)(2,1)} %get-tuple-element.105.refs_0_.x_ref, bf16[4,2,208,384]{3,2,1,0:T(8,128)(2,1)} %get-tuple-element.107.own_ref, bf16[4,2,112,384]{3,2,1,0:T(8,128)(2,1)} %get-tuple-element.108.mem_ref, bf16[2,384,1152]{2,1,0:T(8,128)(2,1)} %bitcast.79, ...), custom_call_target="tpu_custom_call" | custom-call | flops 20000000000 | tf_op jit(solution)/shard_map/attend/pallas_call | solution.py:492
  148.0 25.9 %second_mlp.1 = (bf16[416,768]{1,0:T(8,128)(2,1)}, bf16[416,768]{1,0:T(8,128)(2,1)}, f32[416,384]{1,0:T(8,128)}, bf16[2,4,2,192,1536]{4,3,2,1,0:T(8,128)(2,1)}, ...) custom-call(bf16[416,768]{1,0:T(8,128)(2,1)} %bitcast.95, ...), custom_call_target="tpu_custom_call" | custom-call | flops 25999998976 | tf_op jit(solution)/shard_map/second_mlp/pallas_call | solution.py:492
  174.1 34.4 %attend_back.2 = (f32[2,208,384]{2,1,0:T(8,128)}, bf16[4,2,320,384]{3,2,1,0:T(8,128)(2,1)}, bf16[2,384,1152]{2,1,0:T(8,128)(2,1)}, f32[8,768]{1,0:T(8,128)}) custom-call(bf16[2,208,384]{2,1,0:T(8,128)(2,1)} %get-tuple-element.105.refs_0_.x_ref, bf16[2,208,768]{2,1,0:T(8,128)(2,1)} %bitcast.94, bf16[4,2,208,384]{3,2,1,0:T(8,128)(2,1)} %get-tuple-element.107.own_ref, ...), custom_call_target="tpu_custom_call" | custom-call | flops 35999997952 | tf_op jit(solution)/shard_map/attend_back/pallas_call | solution.py:492
  208.6 3.3 fusion.4
  211.9 25.7 %give_back.2 = (f32[2,208,384]{2,1,0:T(8,128)}, f32[2,112,384]{2,1,0:T(8,128)}) custom-call(bf16[4,2,320,384]{3,2,1,0:T(8,128)(2,1)} %get-tuple-element.118.refs_0_, f32[2,4]{1,0:T(2,128)} %compare_convert_fusion.refs_2_.refs_1_), custom_call_target="tpu_custom_call" | custom-call | flops 24999999488 | tf_op jit(solution)/shard_map/give_back/pallas_call | solution.py:910
  237.6 27.1 %first_back.1 = (f32[2,784,384]{2,1,0:T(8,128)}, bf16[2,784,384]{2,1,0:T(8,128)(2,1)}, bf16[2,384,2048]{2,1,0:T(8,128)(2,1)}, f32[2,1,768]{2,1,0:T(1,128)}, f32[8,384]{1,0:T(8,128)}) custom-call(f32[2,784,384]{2,1,0:T(8,128)} %get-tuple-element.103.middle_ref, f32[2,784,384]{2,1,0:T(8,128)} %get-tuple-element.104.after_ref, ...), custom_call_target="tpu_custom_call" | custom-call | flops 25999998976 | tf_op jit(solution)/shard_map/first_back/pallas_call | solution.py:492
  265.9 3.4 collective-permute-start.2
  270.4 38.0 %attend_back.3 = (f32[2,784,384]{2,1,0:T(8,128)}, bf16[4,2,320,384]{3,2,1,0:T(8,128)(2,1)}, bf16[2,384,576]{2,1,0:T(8,128)(2,1)}, f32[8,384]{1,0:T(8,128)}) custom-call(bf16[2,784,384]{2,1,0:T(8,128)(2,1)} %get-tuple-element.92.x_ref, bf16[2,784,384]{2,1,0:T(8,128)(2,1)} %get-tuple-element.124.g_ref, bf16[4,2,208,384]{3,2,1,0:T(8,128)(2,1)} %get-tuple-element.97.own_ref, ...), custom_call_target="tpu_custom_call" | custom-call | flops 35999997952 | tf_op jit(solution)/shard_map/attend_back/pallas_call | solution.py:492
  308.5 1.9 fusion.7.refs_3_
  310.4 2.4 reduce-scatter.6.cloned.1.call-done
  312.8 52.5 %give_back.3 = (f32[2,208,384]{2,1,0:T(8,128)}, f32[2,112,384]{2,1,0:T(8,128)}, bf16[2,2,208,768]{3,2,1,0:T(8,128)(2,1)}, bf16[4,96,1536]{2,1,0:T(8,128)(2,1)}, bf16[96,640]{1,0:T(8,128)(2,1)}) custom-call(bf16[4,2,320,384]{3,2,1,0:T(8,128)(2,1)} %get-tuple-element.126.refs_0_, f32[2,4]{1,0:T(2,128)} %compare_convert_fusion.refs_2_.refs_1_, ...), custom_call_target="tpu_custom_call" | custom-call | flops 35000000512 | tf_op jit(solution)/shard_map/give_back/pallas_call | solution.py:910
  367.1 1.5 copy.69
  368.6 1.7 fusion.13
  370.3 6.0 %last_back.1 = (bf16[2,4,196,384]{3,2,1,0:T(8,128)(2,1)}, f32[8,384]{1,0:T(8,128)}) custom-call(bf16[2,784,384]{2,1,0:T(8,128)(2,1)} %get-tuple-element.93.x_ref, f32[2,784,384]{2,1,0:T(8,128)} %get-tuple-element.133.res_ref, f32[2,784,384]{2,1,0:T(8,128)} %get-tuple-element.134.dx_ref, f32[2,208,384]{2,1,0:T(8,128)} %get-tuple-element.135.own_ref, ...), custom_call_target="tpu_custom_call" | custom-call | flops 6000000000 | tf_op jit(solution)/shard_map/last_back/pallas_call | solution.py:492
  376.3 53.1 %finish.1 = (bf16[2,2,4,196,384]{4,3,2,1,0:T(8,128)(2,1)}, f32[3,384]{1,0:T(4,128)}, f32[1,768]{1,0:T(1,128)}, f32[5,384]{1,0:T(8,128)}, f32[3,768]{1,0:T(4,128)...) custom-call(bf16[2,4,196,384]{3,2,1,0:T(8,128)(2,1)} %get-tuple-elem, ...), custom_call_target="tpu_custom_call" | custom-call | flops 40000000000 | tf_op jit(solution)/shard_map/finish/pallas_call | solution.py:1091
  429.4 2.0 bitcast_convert_fusion
  431.5 3.5 copy.70
  (140 shorter events, 27.4 us)
Async XLA Ops:
  7.2 14.3 %copy-start = (bf16[1,4,4,49,768]{4,2,3,1,0:T(4,128)(2,1)S(1)}, bf16[1,4,4,49,768]{4,2,3,1,0:T(4,128)(2,1)}, u32[]{:S(2)}) copy-start(bf16[1,4,4,49,768]{4,2,3,1,0:T(4,128)(2,1)} %param.45) | copy-start | bytes 3612676
  7.2 120.9 %all-gather.4.cloned.1.call-start = ((), (), s32[]{:S(2)}) async-start(), calls=%async_computation.3 | async-start | bytes 1990656 | tf_op jit(solution)/shard_map/all_gather | solution.py:1168
  11.1 4.5 copy-start.11
  11.1 5.6 %copy-start.5 = (bf16[192,1536]{1,0:T(8,128)(2,1)S(1)}, bf16[192,1536]{1,0:T(8,128)(2,1)}, u32[]{:S(2)}) copy-start(bf16[192,1536]{1,0:T(8,128)(2,1)} %param.36) | copy-start | bytes 1769476
  16.7 129.1 %all-gather.6.cloned.1.call-start = ((), (), s32[]{:S(2)}) async-start(), calls=%async_computation.7 | async-start | bytes 12828672 | tf_op jit(solution)/shard_map/all_gather | solution.py:1169
  19.2 245.5 %reduce-scatter.4.cloned.1.call-start = ((), (), s32[]{:S(2)}) async-start(), calls=%async_computation.4 | async-start | bytes 10616832 | tf_op jit(solution)/shard_map/reduce_scatter | solution.py:1219
  174.0 138.8 %reduce-scatter.6.cloned.1.call-start = ((), (), s32[]{:S(2)}) async-start(), calls=%async_computation.5 | async-start | bytes 4423680 | tf_op jit(solution)/shard_map/reduce_scatter | solution.py:1219
  174.1 34.5 %copy-start.3 = (bf16[2,4,96,768]{3,2,1,0:T(8,128)(2,1)S(1)}, bf16[2,4,96,768]{3,2,1,0:T(8,128)(2,1)}, u32[]{:S(2)}) copy-start(bf16[2,4,96,768]{3,2,1,0:T(8,128)(2,1)} %get-tuple-element.130) | copy-start | bytes 3538948
  174.1 34.5 %copy-start.4 = (bf16[2,4,96,384]{3,2,1,0:T(8,128)(2,1)S(1)}, bf16[2,4,96,384]{3,2,1,0:T(8,128)(2,1)}, u32[]{:S(2)}) copy-start(bf16[2,4,96,384]{3,2,1,0:T(8,128)(2,1)} %get-tuple-element.131) | copy-start | bytes 1769476
  237.6 138.7 %reduce-scatter.8.cloned.1.call-start = ((), (), s32[]{:S(2)}) async-start(), calls=%async_computation.6 | async-start | bytes 3538944 | tf_op jit(solution)/shard_map/reduce_scatter | solution.py:1219
  265.9 42.5 %collective-permute-start.2 = (bf16[96,1536]{1,0:T(8,128)(2,1)S(1)}, bf16[96,1536]{1,0:T(8,128)(2,1)S(1)}, u32[]{:S(2)}, u32[]{:S(2)}) collective-permute-start(bf16[96,1536]{1,0:T(8,128)(2,1)S(1)} %get-tuple-element.227), channel_id=1, source_target_pairs={{0,24},{8,0},{16,8},{24,16},{1,25},{9,1},{17,9},{25,17},{2,26},{10... | collective-permute-start | bytes 884744 | tf_op jit(solution)/shard_map/ppermute | solution.py:1118
  269.3 39.2 %collective-permute-start.1 = (bf16[96,1536]{1,0:T(8,128)(2,1)S(1)}, bf16[96,1536]{1,0:T(8,128)(2,1)S(1)}, u32[]{:S(2)}, u32[]{:S(2)}) collective-permute-start(bf16[96,1536]{1,0:T(8,128)(2,1)S(1)} %get-tuple-element.228), channel_id=1, source_target_pairs={{0,16},{8,24},{16,0},{24,8},{1,17},{9,25},{17,1},{25,9},{2,18},{10... | collective-permute-start | bytes 884744 | tf_op jit(solution)/shard_map/ppermute | solution.py:1118
  269.3 39.2 %collective-permute-start = (bf16[96,1536]{1,0:T(8,128)(2,1)S(1)}, bf16[96,1536]{1,0:T(8,128)(2,1)S(1)}, u32[]{:S(2)}, u32[]{:S(2)}) collective-permute-start(bf16[96,1536]{1,0:T(8,128)(2,1)S(1)} %get-tuple-element.226), channel_id=1, source_target_pairs={{0,8},{8,16},{16,24},{24,0},{1,9},{9,17},{17,25},{25,1},{2,10},{10... | collective-permute-start | bytes 884744 | tf_op jit(solution)/shard_map/ppermute | solution.py:1118
  431.5 4.6 %copy-start.6 = (f32[96,1152]{1,0:T(8,128)S(1)}, f32[96,1152]{1,0:T(8,128)}, u32[]{:S(2)}) copy-start(f32[96,1152]{1,0:T(8,128)} %get-tuple-element.153) | copy-start | bytes 1327108
  434.9 4.4 copy-start.9
  434.9 5.1 %copy-start.8 = (f32[96,768]{1,0:T(8,128)S(1)}, f32[96,768]{1,0:T(8,128)}, u32[]{:S(2)}) copy-start(f32[96,768]{1,0:T(8,128)} %get-tuple-element.263) | copy-start | bytes 884740
  435.0 5.8 %copy-start.7 = (f32[192,384]{1,0:T(8,128)S(1)}, f32[192,384]{1,0:T(8,128)}, u32[]{:S(2)}) copy-start(f32[192,384]{1,0:T(8,128)} %get-tuple-element.265) | copy-start | bytes 884740
  435.0 6.5 %copy-start.12 = (f32[192,192]{1,0:T(8,128)S(1)}, f32[192,192]{1,0:T(8,128)}, u32[]{:S(2)}) copy-start(f32[192,192]{1,0:T(8,128)} %get-tuple-element.266) | copy-start | bytes 442372
  435.1 7.0 %copy-start.23 = (f32[3,384]{1,0:T(4,128)S(1)}, f32[3,384]{1,0:T(4,128)}, u32[]{:S(2)}) copy-start(f32[3,384]{1,0:T(4,128)} %get-tuple-element.269) | copy-start | bytes 13828
  435.1 7.6 %copy-start.20 = (f32[5,384]{1,0:T(8,128)S(1)}, f32[5,384]{1,0:T(8,128)}, u32[]{:S(2)}) copy-start(f32[5,384]{1,0:T(8,128)} %get-tuple-element.271) | copy-start | bytes 23044
  435.2 10.0 %copy-start.1 = (bf16[1,4,4,49,768]{4,2,3,1,0:T(4,128)(2,1)S(1)}, bf16[1,4,4,49,768]{4,2,3,1,0:T(4,128)(2,1)}, u32[]{:S(2)}) copy-start(bf16[1,4,4,49,768]{4,2,3,1,0:T(4,128)(2,1)} %param.45) | copy-start | bytes 3612676
  435.2 8.2 %copy-start.19 = (f32[3,768]{1,0:T(4,128)S(1)}, f32[3,768]{1,0:T(4,128)}, u32[]{:S(2)}) copy-start(f32[3,768]{1,0:T(4,128)} %get-tuple-element.272) | copy-start | bytes 27652
  435.2 8.8 %copy-start.31 = (f32[2,192]{1,0:T(2,128)S(1)}, f32[2,192]{1,0:T(2,128)}, u32[]{:S(2)}) copy-start(f32[2,192]{1,0:T(2,128)} %get-tuple-element.273) | copy-start | bytes 4612
  435.2 9.4 %copy-start.28 = (f32[2,384]{1,0:T(2,128)S(1)}, f32[2,384]{1,0:T(2,128)}, u32[]{:S(2)}) copy-start(f32[2,384]{1,0:T(2,128)} %get-tuple-element.274) | copy-start | bytes 9220
  (19 other events, 53.4 us)
Sparse Core Ops, SparseCore 0:
  16.8 34.4 all-gather.3
  53.7 78.5 all-gather.5
  174.1 84.5 reduce-scatter.3
  262.7 50.0 reduce-scatter.5
  316.4 46.2 reduce-scatter.7

commit v7 on v6

--- a/solution.py
+++ b/solution.py
@@ -339,13 +339,15 @@
 def second_mlp_kernel(
     comb_ref, pooled_ref, cot_ref, out_ref, skip_ref, up_ref, down_ref, ub_ref, vec_ref,
     mixed_ref, dcomb_ref, dskip_ref, gmlp_ref, gout_ref, gskip_ref, gub_ref, row_ref,
-    after_s, low_s, lowt_s, cott_s, sum_s, dlow_s,
+    after_s, low_s, lowt_s, cott_s, sum_s, dlow_s, skip_s,
 ):
     step = pl.program_id(0)
 
     @pl.when(step == 0)
     def _():
-        after = dot(pooled_ref[...], skip_ref[...], NT) + vec_ref[0:1, :]
+        share = skip_s.shape[1] // skip_ref.shape[0]
+        skip_s[...] = jnp.concatenate([skip_ref[h, :, :share].astype(f32) for h in range(skip_ref.shape[0])], axis=1).astype(bf16)
+        after = dot(pooled_ref[...], skip_s[...], NT) + vec_ref[0:1, :]
         wide = out_ref.shape[2]
         for h in range(out_ref.shape[0]):
             after = after + dot(comb_ref[:, wide * h:wide * h + wide], out_ref[h], NT)
@@ -382,7 +384,7 @@
         for i, row in enumerate((res, dlow, cot, dlow * unit)):
             row_ref[i:i + 1, :] = sum_rows(row)
         res = res.astype(bf16)
-        dskip_ref[...] = dot(res, skip_ref[...])
+        dskip_ref[...] = dot(res, skip_s[...])
         rest = transposed(res)
         wide = out_ref.shape[2]
         for h in range(out_ref.shape[0]):
@@ -568,6 +570,74 @@
 
 def rem(a, n):
     return lax.rem(a + n, n)
+
+
+class Chain:
+    def __init__(self, part_s, outer_s, inner_s, pieces, in_send, in_recv, mid_send, mid_recv, out_send, out_recv):
+        self.clip, clips = lax.axis_index("clip"), lax.axis_size("clip")
+        clip = self.clip
+        left = clip < clips // 2
+        inner, outer = jnp.where(left, clip + 1, clip - 1), jnp.where(left, clip - 1, clip + 1)
+        self.inner, self.outer = {"clip": inner}, {"clip": outer}
+        self.end = (clip == 0) | (clip == clips - 1)
+        self.middle = (clip == clips // 2 - 1) | (clip == clips // 2)
+        self.part, self.from_outer, self.from_inner, self.pieces = part_s, outer_s, inner_s, pieces
+        self.inward = [remote(part_s.at[p], outer_s.at[p], in_send.at[n], in_recv.at[n], self.inner) for n, p in enumerate(pieces)]
+        self.across = [remote(part_s.at[p], inner_s.at[p], mid_send.at[n], mid_recv.at[n], self.inner) for n, p in enumerate(pieces)]
+        self.outward = [remote(inner_s.at[p], inner_s.at[p], out_send.at[n], out_recv.at[n], self.outer) for n, p in enumerate(pieces)]
+
+    def greets(self):
+        both = [(self.inner, None), (self.outer, jnp.logical_not(self.end))]
+        return both
+
+    def send_ends(self, n):
+        @pl.when(self.end & jnp.logical_not(self.middle))
+        def _():
+            self.inward[n].start()
+
+    def send_parts(self, n):
+        here = self.pieces[n]
+
+        @pl.when(jnp.logical_not(self.end))
+        def _():
+            self.inward[n].wait_recv()
+            self.part[here] = (self.part[here].astype(f32) + self.from_outer[here].astype(f32)).astype(bf16)
+
+        @pl.when(jnp.logical_not(self.end) & jnp.logical_not(self.middle))
+        def _():
+            self.inward[n].start()
+
+        @pl.when(self.middle)
+        def _():
+            self.across[n].start()
+
+    def totals(self, n):
+        here = self.pieces[n]
+
+        @pl.when(self.middle)
+        def _():
+            self.across[n].wait_recv()
+            self.across[n].wait_send()
+            self.from_inner[here] = (self.part[here].astype(f32) + self.from_inner[here].astype(f32)).astype(bf16)
+
+        @pl.when(jnp.logical_not(self.middle))
+        def _():
+            self.inward[n].wait_send()
+            self.outward[n].wait_recv()
+
+        @pl.when(jnp.logical_not(self.end))
+        def _():
+            self.outward[n].start()
+
+    def close(self):
+        @pl.when(jnp.logical_not(self.end))
+        def _():
+            for copy in self.outward:
+                copy.wait_send()
+
+
+def chain_scratch(buffer, pieces):
+    return [pltpu.VMEM(buffer, bf16)] * 3 + [dma(pieces)] * 6
 
 
 def share_kernel(gather, *refs):
@@ -763,8 +833,11 @@
 
 def give_back_kernel(exchange, *refs):
     if exchange:
-        part_ref, pick_ref, half_ref, piece_ref, shard_ref, own_ref, back_ref, all_ref, pieces_ref, sum_ref, *refs = refs
-        *refs, half_local, half_send, half_recv, piece_send, piece_recv, shard_send, shard_recv, shard_s = refs
+        part_ref, pick_ref, half_ref, shard_ref, own_ref, back_ref, all_ref, up_ref, down_ref, *refs = refs
+        refs, (half_local, half_send, half_recv), chain = refs[:-12], refs[-12:-9], refs[-9:]
+        depth = chain[-1].shape[0]
+        rows_each = shard_ref.shape[0] // depth
+        chain = Chain(*chain[:3], [(pl.ds(rows_each * n, rows_each), slice(None)) for n in range(depth)], *chain[3:])
     else:
         part_ref, pick_ref, own_ref, back_ref, *refs = refs
     (mine_s, core_s, sum_s, chip_s, route_s, got_s,
@@ -777,9 +850,13 @@
     beside = [{"head": rem(head + d, heads)} for d in range(1, heads)]
     heads_of = lambda by, sign: [{"clip": clip + by, "head": rem(head + sign * d, heads)} for d in range(heads)]
     last, begun = clip < clips - 1, clip > 0
-    along = [{"clip": rem(clip + k, clips)} for k in range(1, clips)]
-    near = [(d, None) for d in [partner] + across + (beside + along if exchange else [])]
+    near = [(d, None) for d in [partner] + across + (beside if exchange else [])]
+    near += chain.greets() if exchange else []
     greet(near + [(d, last) for d in heads_of(1, 1)], near + [(d, begun) for d in heads_of(-1, -1)])
+    if exchange:
+        chain.part[...] = shard_ref[...]
+        for n in range(depth):
+            chain.send_ends(n)
 
     order = [rem(chip + k, chips) for k in list(range(1, chips)) + [0]]
     core_copies, local_copies = [], []
@@ -797,7 +874,6 @@
         half_copy = pltpu.make_async_copy(half_ref, all_ref.at[head], half_local.at[0])
         half_copy.start()
     mem_copies, own_copies = [], []
-    piece_copies, shard_copies = [], []
     for n in range(chips):
         local_copies[n].wait()
         core_copies[n].wait_recv()
@@ -833,17 +909,6 @@
                 route_s[d, s] = total.astype(bf16)
             clip_copies[d].start()
 
-    if exchange:
-        wide = sum_ref.shape[1]
-        lanes = lambda c: pl.ds(pl.multiple_of(wide * c, wide), wide)
-        for k, d in enumerate(along):
-            shard_copies.append(
-                remote(shard_ref.at[:, lanes(rem(clip + k + 1, clips))], shard_s.at[k], shard_send.at[k], shard_recv.at[k], d))
-            piece_copies.append(remote(piece_ref, pieces_ref.at[clip], piece_send.at[k], piece_recv.at[k], d))
-        for copy in shard_copies + piece_copies:
-            copy.start()
-        piece_copy = pltpu.make_async_copy(piece_ref, pieces_ref.at[clip], half_local.at[1])
-        piece_copy.start()
     for copy in own_copies:
         copy.wait_recv()
     for m in range(share):
@@ -866,19 +931,21 @@
         back_ref[...] = jnp.zeros_like(back_ref)
 
     if exchange:
-        for copy in shard_copies:
-            copy.wait_recv()
-        total = shard_ref[:, lanes(clip)].astype(f32)
-        for k in range(clips - 1):
-            total = total + shard_s[k].astype(f32)
-        sum_ref[...] = total.astype(bf16)
-    for copy in halves + piece_copies:
+        for n in range(depth):
+            chain.send_parts(n)
+            if n > 0:
+                chain.totals(n - 1)
+        chain.totals(depth - 1)
+        total = chain.from_inner[...].astype(f32)
+        up_ref[...] = total[:up_ref.shape[0]]
+        down_ref[...] = total[up_ref.shape[0]:]
+        chain.close()
+    for copy in halves:
         copy.wait_recv()
-    for copy in core_copies + mem_copies + own_copies + halves + piece_copies + shard_copies:
+    for copy in core_copies + mem_copies + own_copies + halves:
         copy.wait_send()
     if exchange:
         half_copy.wait()
-        piece_copy.wait()
 
     @pl.when(begun)
     def _():
@@ -886,7 +953,7 @@
             copy.wait_send()
 
 
-def give_back(part, pick, own_rows, number, half=None, piece=None, shard=None):
+def give_back(part, pick, own_rows, number, half=None, shard=None):
     toks, heads = lax.axis_size("tok"), lax.axis_size("head")
     chips, few = toks // 2, max(toks // 2 - 1, 1)
     share, rows, d = part.shape[1:]
@@ -899,14 +966,13 @@
         dma(chips), dma(chips), dma(chips), dma(few), dma(few), dma(few), dma(few), dma(heads), dma(heads),
     ]
     if half is not None:
-        clips = lax.axis_size("clip")
-        wide = shard.shape[1] // clips
-        args, specs = args + [half, piece, shard], specs + [ANY, ANY, INVMEM]
-        outs += [shape((heads,) + half.shape, half.dtype), shape((clips,) + piece.shape, bf16), shape((shard.shape[0], wide), bf16)]
-        out_specs += [ANY, ANY, INVMEM]
-        along = max(clips - 1, 1)
-        scratch += [dma(2), dma(max(heads - 1, 1)), dma(max(heads - 1, 1)), dma(along), dma(along), dma(along), dma(along)]
-        scratch += [pltpu.VMEM((along, shard.shape[0], wide), bf16)]
+        pair, depth, lanes = shard.shape
+        shard = shard.reshape(-1, lanes)
+        args, specs = args + [half, shard], specs + [ANY, INVMEM]
+        outs += [shape((heads,) + half.shape, half.dtype), shape((depth, lanes), f32), shape((depth, lanes), f32)]
+        out_specs += [ANY, INVMEM, INVMEM]
+        scratch += [dma(1), dma(max(heads - 1, 1)), dma(max(heads - 1, 1))]
+        scratch += chain_scratch(shard.shape, shard.shape[0] // 48)
     return pl.pallas_call(
         functools.partial(give_back_kernel, half is not None),
         in_specs=specs,
@@ -919,12 +985,15 @@
     )(*args)
 
 
-def finish_kernel(sizes, half_ref, last_ref, qv_a_rows, a_ref, b_ref, qv_b_rows, ub_a_rows, ub_b_rows, grad_ref, rest_ref, piece_ref, all_ref, gains_a_ref, gains_b_ref, shifts_a_ref,
+def finish_kernel(sizes, half_ref, last_ref, qv_a_rows, a_ref, b_ref, qv_b_rows, ub_a_rows, ub_b_rows, grad_ref, rest_ref, group_ref, all_ref, gains_a_ref, gains_b_ref, shifts_a_ref,
                   shifts_b_ref, qv_a_ref, qv_b_ref, ub_a_ref, ub_b_ref, gtotal_ref, up_ref, down_ref, out_ref,
                   q_ref, out_b_ref, skip_ref, *scratch):
-    (small_ref, small_s, small_core, small_chip, small_head, small_clip, part_s, part_core, chip_s, part_chip, head_s, part_head, mine_s, part_clip,
-     rest_in, rest_s, local_sem, half_send, half_recv, core_send, core_recv, chip_send, chip_recv, head_send, head_recv,
-     clip_send, clip_recv, rest_send, rest_recv, back_send, back_recv, piece_s, piece_send, piece_recv) = scratch
+    (small_ref, small_s, small_core, small_chip, small_head, small_clip, part_s, part_core, chip_s, part_chip, part_head,
+     local_sem, half_send, half_recv, core_send, core_recv, chip_send, chip_recv, head_send, head_recv,
+     clip_send, clip_recv, *chain) = scratch
+    first_lanes, next_lanes, deep = group_ref.shape[1], rest_ref.shape[1], grad_ref.shape[1]
+    bounds = [0, first_lanes // 2, first_lanes, first_lanes + next_lanes // 2, first_lanes + next_lanes, chain[0].shape[1]]
+    chain = Chain(*chain[:3], [(slice(None), pl.ds(low, high - low)) for low, high in zip(bounds, bounds[1:])], *chain[3:])
     clip, head, chip, core, chips = places()
     clips, heads = lax.axis_size("clip"), lax.axis_size("head")
     share = half_ref.shape[0]
@@ -934,6 +1003,10 @@
     along = [{"clip": rem(clip + k, clips)} for k in range(1, clips)]
     peers = [(d, None) for d in [partner] + across + beside + along]
     greet(peers, peers)
+    chain.part[:, :first_lanes] = group_ref[...]
+    chain.part[:, first_lanes:first_lanes + next_lanes] = rest_ref[...]
+    for n in range(4):
+        chain.send_ends(n)
     pending = []
     d1 = small_ref.shape[1]
     small_ref[...] = jnp.zeros_like(small_ref)
@@ -947,11 +1020,6 @@
         for low in range(0, values.shape[1], d1):
             small_ref[row:row + 1, :] = values[:, low:low + d1]
             row += 1
-    wide = rest_ref.shape[1] // clips
-
-    def lanes(c):
-        return pl.ds(pl.multiple_of(wide * c, wide), wide)
-
     def go(copies):
         for copy in copies:
             copy.start()
@@ -976,11 +1044,6 @@
         for x in range(chips):
             n = h * chips + x
             first += go([remote(grad_ref.at[2 * n + 1 - core], part_core.at[n], core_send.at[n + 1], core_recv.at[n + 1], partner)])
-    gather = go([remote(rest_ref.at[:, lanes(rem(clip + k + 1, clips))], rest_in.at[k], rest_send.at[k], rest_recv.at[k], d) for k, d in enumerate(along)])
-    wider = piece_ref.shape[1]
-    group = pl.ds(pl.multiple_of(wider * clip, wider), wider)
-    piece_s[:, group] = piece_ref[...]
-    pieces = go([remote(piece_ref, piece_s.at[:, group], piece_send.at[k], piece_recv.at[k], d) for k, d in enumerate(along)])
     halves = [
         [remote(half_ref.at[s], all_ref.at[head, s], half_send.at[k, s], half_recv.at[k, s], d) for k, d in enumerate(beside)]
         for s in range(share)
@@ -1011,22 +1074,24 @@
         copies += go([remote(small_s.at[1], small_head.at[k], head_send.at[k, 0], head_recv.at[k, 0], d)])
         copies += go([remote(chip_s.at[rem(head + k + 1, heads)], part_head.at[k], head_send.at[k, 1], head_recv.at[k, 1], d)])
     go(halves[share - 1])
-    arrived(gather)
-    total = rest_ref[:, lanes(clip)].astype(f32)
-    for k in range(clips - 1):
-        total = total + rest_in[k].astype(f32)
-    rest_s[:, lanes(clip)] = total.astype(bf16)
-    spread = go([remote(rest_s.at[:, lanes(clip)], rest_s.at[:, lanes(clip)], back_send.at[k], back_recv.at[k], d) for k, d in enumerate(along)])
+    for n in range(4):
+        chain.send_parts(n)
     arrived(copies)
     small_s[2] = in_order(head, heads, small_s[1], lambda k: small_head[k])
     total = chip_s[head].astype(f32)
     for k in range(heads - 1):
         total = total + part_head[k].astype(f32)
-    mine_s[...] = total.astype(bf16)
+    mine = first_lanes + next_lanes
+    chain.part[:, mine:mine + grad_ref.shape[2]] = total.astype(bf16)
     copies = []
     for k, d in enumerate(along):
         copies += go([remote(small_s.at[2], small_clip.at[k], clip_send.at[k, 0], clip_recv.at[k, 0], d)])
-        copies += go([remote(mine_s, part_clip.at[k], clip_send.at[k, 1], clip_recv.at[k, 1], d)])
+    chain.send_ends(4)
+    chain.totals(0)
+    chain.totals(1)
+    chain.send_parts(4)
+    for n in range(2, 5):
+        chain.totals(n)
     arrived(copies)
     total = in_order(clip, clips, small_s[2], lambda k: small_clip[k])
     at = [4]
@@ -1058,19 +1123,16 @@
         qv_b_ref[i:i + 1, :] = share_of(rows(d2))
     ub_a_ref[...] = share_of(rows(fa))
     ub_b_ref[...] = share_of(rows(fb))
-    gtotal_ref[...] = in_order(clip, clips, mine_s[...].astype(f32), lambda k: part_clip[k].astype(f32))
-    arrived(spread)
     wide = up_ref.shape[1]
-    up_ref[...] = rest_s[:, :wide].astype(f32)
-    down_ref[...] = rest_s[:, wide:2 * wide].astype(f32)
-    out_ref[...] = rest_s[:, 2 * wide:2 * wide + out_ref.shape[1]].astype(f32)
-    arrived(pieces)
-    wide, rows = q_ref.shape[1], piece_s.shape[0]
-    q_ref[...] = piece_s[:, :wide].astype(f32)
+    sums = chain.from_inner
+    for ref, low in ((q_ref, 0), (up_ref, first_lanes), (down_ref, first_lanes + wide), (out_ref, first_lanes + 2 * wide), (gtotal_ref, mine)):
+        ref[...] = sums[:, low:low + ref.shape[1]].astype(f32)
+    low, rows = q_ref.shape[1], q_ref.shape[0]
     for ref in (out_b_ref, skip_ref):
         for n in range(2):
-            ref[rows * n:rows * n + rows, :] = piece_s[:, wide:wide + ref.shape[1]].astype(f32)
-            wide += ref.shape[1]
+            ref[rows * n:rows * n + rows, :] = sums[:, low:low + ref.shape[1]].astype(f32)
+            low += ref.shape[1]
+    chain.close()
     for copies in halves:
         arrived(copies)
     for copy in pending:
@@ -1078,7 +1140,7 @@
     local_half.wait()
 
 
-def finish(half, rows, grad, rest, piece, d2, fa, fb, ha, hs, number):
+def finish(half, rows, grad, rest, first, d2, fa, fb, ha, hs, number):
     toks, heads, clips = lax.axis_size("tok"), lax.axis_size("head"), lax.axis_size("clip")
     chips = toks // 2
     across, beside, along = (max(n, 1) for n in (chips - 1, heads - 1, clips - 1))
@@ -1087,7 +1149,8 @@
     low, full = lambda *dims: pltpu.VMEM(dims, bf16), lambda *dims: pltpu.VMEM(dims + (-(-count // 8) * 8, d1), f32)
     sums = [(3, d1), (1, d2), (5, d1), (3, d2), (2, d1 // heads), (2, d2 // heads), (1, fa // heads), (1, fb // heads),
             block, (depth, fa // heads), (depth, fa // heads), (depth, ha),
-            (piece.shape[0], 3 * d2 // heads), (2 * piece.shape[0], d2 // heads), (2 * piece.shape[0], hs)]
+            (depth, 3 * d2 // heads), (2 * depth, d2 // heads), (2 * depth, hs)]
+    buffer = (depth, first.shape[1] + rest.shape[1] + -(-block[1] // 128) * 128)
     return pl.pallas_call(
         functools.partial(finish_kernel, (d2, fa, fb)),
         in_specs=[ANY] + [INVMEM] * (len(rows) + 3),
@@ -1095,28 +1158,15 @@
         out_shape=[shape((heads,) + half.shape, half.dtype)] + [shape(dims, f32) for dims in sums],
         scratch_shapes=[
             full(), full(3), full(), full(across), full(beside), full(along),
-            low(heads * chips, *block), low(heads * chips, *block), low(heads, *block), low(across, heads, *block),
-            low(heads, *block), low(beside, *block), low(*block), low(along, *block),
-            low(along, depth, rest.shape[1] // clips), low(*rest.shape),
+            low(heads * chips, *block), low(heads * chips, *block), low(heads, *block), low(across, heads, *block), low(beside, *block),
             dma(1), dma(beside, half.shape[0]), dma(beside, half.shape[0]), dma(heads * chips + 1), dma(heads * chips + 1),
-            dma(across, heads + 1), dma(across, heads + 1), dma(beside, 2), dma(beside, 2), dma(along, 2), dma(along, 2),
-            dma(along), dma(along), dma(along), dma(along),
-            low(piece.shape[0], clips * piece.shape[1]), dma(along), dma(along),
+            dma(across, heads + 1), dma(across, heads + 1), dma(beside, 2), dma(beside, 2), dma(along, 1), dma(along, 1),
+            *chain_scratch(buffer, 5),
         ],
         compiler_params=pltpu.CompilerParams(collective_id=number, has_side_effects=True, vmem_limit_bytes=VMEM_CAP),
         cost_estimate=about(40),
         name="finish",
-    )(half, *rows, grad, rest, piece)
-
-
-def reduce_clips(shard):
-    clips, clip = lax.axis_size("clip"), lax.axis_index("clip")
-    pieces = shard.reshape(clips, -1, shard.shape[-1])
-    total = lax.dynamic_index_in_dim(pieces, clip, 0, keepdims=False).astype(f32)
-    for k in range(1, clips):
-        give = lax.dynamic_index_in_dim(pieces, (clip + k) % clips, 0, keepdims=False)
-        total = total + lax.ppermute(give, "clip", [(i, (i + k) % clips) for i in range(clips)]).astype(f32)
-    return total.astype(bf16)
+    )(half, *rows, grad, rest, first)
 
 
 def padded_rows(*rows):
@@ -1141,7 +1191,6 @@
     rows2 = share * own_rows
 
     cot = lax.dynamic_slice_in_dim(cotangent[0], first, share, 0).reshape(share, pooled_tokens, d2)
-    cot = jnp.pad(cot, ((0, 0), (0, own_rows - pooled_tokens), (0, 0))).reshape(rows2, d2)
 
     source = lax.dynamic_slice_in_dim(assign[0], first, share, 0)
     flags = lax.dynamic_slice_in_dim(resets[0], first, share, 0)
@@ -1153,6 +1202,8 @@
     group = ("head", "tok")
     fa, ha = w_up_a.shape[1], w_out_a.shape[1]
     fb, hb, hs = w_up_b.shape[1], w_out_b.shape[1], w_skip_b.shape[1]
+    pack_a = jnp.concatenate([w_up_a, w_down_a, w_qkv_a.reshape(w_qkv_a.shape[0], -1), w_out_a], axis=1)
+    all_a = lax.all_gather(pack_a, group).reshape(heads, d1, -1)
     mine = lax.dynamic_slice_in_dim(clips_in[0], first, share, 0)
     stream, low1, pooled1, mean1 = call(
         norm_pool_kernel, share,
@@ -1162,20 +1213,17 @@
         name="norm_pool", us=5,
     )
     pooled1, w_qkv_b, w_up_b = lax.optimization_barrier((pooled1, w_qkv_b, w_up_b))
-    pack_a = jnp.concatenate([w_up_a, w_down_a, w_qkv_a.reshape(w_qkv_a.shape[0], -1), w_out_a], axis=1)
     pack_q = w_qkv_b.reshape(w_qkv_b.shape[0], -1)
-    pack_b = jnp.concatenate([w_up_b, w_down_b, w_out_b, w_skip_b], axis=1)
-    all_q = lax.all_gather(pack_q, group).reshape(heads, d1, -1)
+    own1, mem1, all_q, qv_a, qv_b, ub_a, ub_b = share_pooled(
+        pooled1, mean1, pick, 0, pack_q, [qv_bias_a, qv_bias_b, up_bias_a[None], up_bias_b[None]])
+    all_q = all_q.reshape(heads, d1, -1)
+    own1, w_up_b, cot = lax.optimization_barrier((own1, w_up_b, cot))
+    spare = jnp.zeros((w_up_b.shape[0], -(2 * fb + hb + hs) % hb), bf16)
+    pack_b = jnp.concatenate([w_up_b, w_down_b, w_out_b, w_skip_b, spare], axis=1)
     all_b = lax.all_gather(pack_b, group).reshape(heads, d2, -1)
-    own1, mem1, all_a, qv_a, qv_b, ub_a, ub_b = share_pooled(
-        pooled1, mean1, pick, 0, pack_a, [qv_bias_a, qv_bias_b, up_bias_a[None], up_bias_b[None]])
-    all_a = all_a.reshape(heads, d1, -1)
-
-    def lanes(pack, low, width):
-        return jnp.concatenate([pack[h, :, low:low + width] for h in range(heads)], axis=1)
+    cot = jnp.pad(cot, ((0, 0), (0, own_rows - pooled_tokens), (0, 0))).reshape(rows2, d2)
 
     up_spec, down_spec, rest_spec = (pl.BlockSpec((heads, d1, fa), lambda i, n=n: (0, 0, n)) for n in range(3))
-    skip_b = lanes(all_b, 2 * fb + hb, hs)
 
     comb1, lse1 = attend(low1, own1, mem1, (all_a, rest_spec), qv_a, has, valid, d1)
     after1, middle, pooled3, mean3 = call(
@@ -1194,11 +1242,11 @@
     chunk = 768
     per_head = fb // chunk
     steps = heads * per_head
-    out_spec = pl.BlockSpec((heads, d2, hb), lambda j: (0, 0, 2 * fb // hb))
+    out_spec, skip_spec = (pl.BlockSpec((heads, d2, hb), lambda j, n=n: (0, 0, 2 * fb // hb + n)) for n in range(2))
     rows_spec = pl.BlockSpec((1, d2, chunk), lambda j: (j // per_head, 0, j % per_head))
     mixed, dcomb2, dskip, g_mlp_b, g_out_b, g_skip_b, g_ub_b, rows_b = call(
         second_mlp_kernel, steps,
-        [(comb2.reshape(rows2, d2), None), (pooled3.reshape(rows2, d1), None), (cot, None), (all_b, out_spec), (skip_b, None),
+        [(comb2.reshape(rows2, d2), None), (pooled3.reshape(rows2, d1), None), (cot, None), (all_b, out_spec), (all_b, skip_spec),
          (all_b, rows_spec),
          (all_b, pl.BlockSpec((1, d2, chunk), lambda j: (j // per_head, 0, per_head + j % per_head))),
          (ub_b, pl.BlockSpec((1, chunk), lambda j: (0, j))),
@@ -1208,7 +1256,7 @@
           pl.BlockSpec((1, toks, 2, d2 // toks, chunk), lambda j: (j // per_head, 0, 0, 0, j % per_head))),
          (shape((heads, toks, d2 // toks // 2, 2 * hb), bf16), None), (shape((heads, toks, d2 // toks // 2, 2 * hs), bf16), None),
          (shape((1, heads * fb), f32), pl.BlockSpec((1, chunk), lambda j: (0, j))), (shape((8, d2), f32), None)],
-        [((rows2, d2), f32), ((rows2, d2), bf16), ((d2, rows2), bf16), ((d2, rows2), bf16), ((rows2, d2), f32), ((rows2, d2), f32)],
+        [((rows2, d2), f32), ((rows2, d2), bf16), ((d2, rows2), bf16), ((d2, rows2), bf16), ((rows2, d2), f32), ((rows2, d2), f32), ((d2, d1), bf16)],
         name="second_mlp", us=26,
     )
 
@@ -1225,7 +1273,6 @@
 
     merge = lambda grad: grad.reshape((heads * toks,) + grad.shape[2:])
     rest_b = jnp.concatenate([by_owner(g_qkv_b), merge(g_out_b), merge(g_skip_b)], axis=2)
-    rest_b = jnp.pad(rest_b, ((0, 0), (0, 0), (0, -rest_b.shape[2] % (128 * clips))))
     sum_rest_b = scatter(rest_b)
 
     res1, dcomb1, g_mlp_a, g_ub_a, rows_a = call(
@@ -1234,18 +1281,16 @@
          (all_a, rest_spec), (all_a, up_spec), (all_a, down_spec), (ub_a, None),
          (padded_rows(gains_a[1], shifts_a[2], gains_a[2]), None), (unpooling, None), (unpairing, None)],
         [(shape((share, tokens, d1), f32), 0), (shape((share, tokens, d1), bf16), 0),
-         (shape((heads, d1, -(-(2 * fa + ha) // (128 * clips)) * 128 * clips), bf16), None),
+         (shape((heads, d1, -(-(2 * fa + ha) // 256) * 256), bf16), None),
          (shape((heads, 1, fa), f32), None), (shape((8, d1), f32), None)],
         [((heads, d1, fa), f32), ((heads, d1, fa), f32), ((d1, d1), f32), ((d1, d1), bf16)],
         name="first_back", us=26,
     )
     rest_a = by_owner(g_mlp_a)
-    dcomb1, sum_mlp_b, rest_a = lax.optimization_barrier((dcomb1, sum_mlp_b, rest_a))
     sum_rest_a = scatter(rest_a)
-    sum_mlp_b = reduce_clips(sum_mlp_b)
     dx1, dpool1, g_qkv_a, rows_qv_a = attend_back(low1, dcomb1, own1, mem1, (all_a, rest_spec), qv_a, has, valid, lse1, heads)
-    own_back1, mem_back1, mixed_all, mlp_b, piece_b = give_back(
-        dpool1, pick, own_rows, 3, mixed.reshape(share, own_rows, d2), sum_mlp_b, sum_rest_b)
+    own_back1, mem_back1, mixed_all, grad_up_b, grad_down_b = give_back(
+        dpool1, pick, own_rows, 3, mixed.reshape(share, own_rows, d2), sum_mlp_b)
     stream_grad, rows_last = call(
         last_back_kernel, share,
         [(stream, 0), (res1, 0), (dx1, 0), (own_back1, 0), (mem_back1, 0), (padded_rows(gains_a[0]), None),
@@ -1254,10 +1299,9 @@
         name="last_back", us=6,
     )
 
-    mlp_b = mlp_b.reshape((2, -1, mlp_b.shape[-1])).astype(f32)
     rows = [rows_last, rows_qv_a, rows_a, rows_b, rows_qv_b, g_ub_a, g_ub_b]
     stream_all, *sums = finish(
-        stream_grad, rows, by_owner(g_qkv_a), sum_rest_a, piece_b, d2, heads * fa, heads * fb, ha, hs, 4)
+        stream_grad, rows, by_owner(g_qkv_a), sum_rest_a, sum_rest_b, d2, heads * fa, heads * fb, ha, hs, 4)
     mixed_all = mixed_all.reshape(micro, own_rows, d2)[:, :pooled_tokens]
     return (
         mixed_all.reshape(cotangent.shape),
@@ -1269,8 +1313,8 @@
         sums[12].reshape(w_qkv_b.shape),
         sums[13],
         sums[14],
-        mlp_b[0],
-        mlp_b[1],
+        grad_up_b,
+        grad_down_b,
         sums[0], sums[1][0], sums[2], sums[3], sums[4], sums[5], sums[6][0], sums[7][0],
     )
 

time: 457 us -> 464 us (1.015)
  Pallas kernels: 386 us -> 400 us
  local copies, waits for them, and re-layouts: 28.8 us -> 35.3 us
    pallas_call x2, Pallas kernels: 78.2 us -> 102 us  [give_back(): pl.pallas_call(functools.partial(give_back_kernel, half is not None), in_...]
    pallas_call x1, Pallas kernels: 53.1 us -> 46.8 us  [finish(): pl.pallas_call(functools.partial(finish_kernel, (d2, fa, fb)), in_specs=[...]
    unnamed x84, local copies, waits for them, and re-layouts: 13.1 us -> 18.6 us
  transfers between devices with their start and end apart: 8 -> 5, of which waited for: 1 -> 0; matrix products, arithmetic and copies ran while one was open for 5% -> 4% of each run, Pallas kernels for 67% -> 71%
where the time goes in v7:
time: 464 us; the launch traced here: 460 us
  Pallas kernels  400 us (86%)
  local copies, waits for them, and re-layouts  35.3 us (8%)
  between operations  14.4 us (3%)
  other arithmetic  10.5 us (2%)
    pallas_call x9, Pallas kernels, call(): pl.pallas_call(kernel, grid=(steps,), in_specs=[spec(a, how) for a, how i...  189 us
    pallas_call x2, Pallas kernels, give_back(): pl.pallas_call(functools.partial(give_back_kernel, half is not None), in_...  102 us
    pallas_call x2, Pallas kernels, share_pooled(): pl.pallas_call(functools.partial(share_kernel, block is not None), in_spe...  62.2 us
    pallas_call x1, Pallas kernels, finish(): pl.pallas_call(functools.partial(finish_kernel, (d2, fa, fb)), in_specs=[...  46.8 us
    unnamed x84, local copies, waits for them, and re-layouts  18.6 us
  transfers between devices with their start and end apart: 5, of which 0 were waited for; matrix products, arithmetic and copies ran while one was open for 4% of the time, Pallas kernels for 71%

profile of v7, /device:TPU:0, one launch (start us, length us, event | category | flops | bytes accessed | tf_op | source)
XLA Modules:
  0.0 460.3 jit_solution(938004608555348489)
XLA Ops:
  8.6 1.8 concatenate.25
  17.8 4.4 norm_pool.1
  23.7 35.0 %share_pooled.2 = (bf16[4,2,208,384]{3,2,1,0:T(8,128)(2,1)}, bf16[4,2,112,384]{3,2,1,0:T(8,128)(2,1)}, bf16[2,4,96,1152]{3,2,1,0:T(8,128)(2,1)}, f32[2,384]{1,0:...) custom-call(bf16[2,208,384]{2,1,0:T(8,128)(2,1)} %get-tuple-element.95.refs_0_, ...), custom_call_target="tpu_custom_call" | custom-call | flops 30000001024 | tf_op jit(solution)/shard_map/share_pooled/pallas_call | solution.py:822
  58.7 1.9 concatenate.27
  64.6 21.5 %attend.2 = (bf16[2,784,384]{2,1,0:T(8,128)(2,1)}, f32[2,784,128]{2,1,0:T(8,128)}) custom-call(bf16[2,784,384]{2,1,0:T(8,128)(2,1)} %get-tuple-element.92.x_ref, bf16[4,2,208,384]{3,2,1,0:T(8,128)(2,1)} %get-tuple-element.100.own_ref, bf16[4,2,112,384]{3,2,1,0:T(8,128)(2,1)} %get-tuple-element.101.mem_ref, bf16[2,384,2304]{2,1,0:T(8,128)(2,1)} %bitcast.63, ...), custom_call_target="tpu_custom_call" | custom-call | flops 20000000000 | tf_op jit(solution)/shard_map/attend/pallas_call | solution.py:494
  86.1 13.4 %first_mlp.1 = (f32[2,784,384]{2,1,0:T(8,128)}, f32[2,784,384]{2,1,0:T(8,128)}, bf16[2,208,384]{2,1,0:T(8,128)(2,1)}, bf16[2,112,384]{2,1,0:T(8,128)(2,1)}) custom-call(bf16[2,784,384]{2,1,0:T(8,128)(2,1)} %get-tuple-element.93.x_ref, bf16[2,784,384]{2,1,0:T(8,128)(2,1)} %get-tuple-element.103.comb_ref, bf16[2,384,2304]{2,1,0:T(8,128)(2,1)} %bitcast.64, ...), custom_call_target="tpu_custom_call" | custom-call | flops 12999999488 | tf_op jit(solution)/shard_map/first_mlp/pallas_call | solution.py:494
  99.5 27.2 %share_pooled.3 = (bf16[4,2,208,384]{3,2,1,0:T(8,128)(2,1)}, bf16[4,2,112,384]{3,2,1,0:T(8,128)(2,1)}) custom-call(bf16[2,208,384]{2,1,0:T(8,128)(2,1)} %get-tuple-element.107.refs_0_.x_ref, bf16[2,112,384]{2,1,0:T(8,128)(2,1)} %get-tuple-element.108.refs_1_, f32[2,4]{1,0:T(2,128)} %compare_convert_fusion.refs_2_.refs_1_), custom_call_target="tpu_custom_call" | custom-call | flops 20000000000 | tf_op jit(solution)/shard_map/share_pooled/pallas_call | solution.py:822
  126.8 17.7 %attend.3 = (bf16[2,208,768]{2,1,0:T(8,128)(2,1)}, f32[2,208,128]{2,1,0:T(8,128)}) custom-call(bf16[2,208,384]{2,1,0:T(8,128)(2,1)} %get-tuple-element.107.refs_0_.x_ref, bf16[4,2,208,384]{3,2,1,0:T(8,128)(2,1)} %get-tuple-element.109.own_ref, bf16[4,2,112,384]{3,2,1,0:T(8,128)(2,1)} %get-tuple-element.110.mem_ref, bf16[2,384,1152]{2,1,0:T(8,128)(2,1)} %bitcast.74, ...), custom_call_target="tpu_custom_call" | custom-call | flops 20000000000 | tf_op jit(solution)/shard_map/attend/pallas_call | solution.py:494
  144.5 26.5 %second_mlp.1 = (bf16[416,768]{1,0:T(8,128)(2,1)}, bf16[416,768]{1,0:T(8,128)(2,1)}, f32[416,384]{1,0:T(8,128)}, bf16[2,4,2,192,1536]{4,3,2,1,0:T(8,128)(2,1)}, ...) custom-call(bf16[416,768]{1,0:T(8,128)(2,1)} %bitcast.80, ...), custom_call_target="tpu_custom_call" | custom-call | flops 25999998976 | tf_op jit(solution)/shard_map/second_mlp/pallas_call | solution.py:494
  171.1 34.4 %attend_back.2 = (f32[2,208,384]{2,1,0:T(8,128)}, bf16[4,2,320,384]{3,2,1,0:T(8,128)(2,1)}, bf16[2,384,1152]{2,1,0:T(8,128)(2,1)}, f32[8,768]{1,0:T(8,128)}) custom-call(bf16[2,208,384]{2,1,0:T(8,128)(2,1)} %get-tuple-element.107.refs_0_.x_ref, bf16[2,208,768]{2,1,0:T(8,128)(2,1)} %bitcast.79, bf16[4,2,208,384]{3,2,1,0:T(8,128)(2,1)} %get-tuple-element.109.own_ref, ...), custom_call_target="tpu_custom_call" | custom-call | flops 35999997952 | tf_op jit(solution)/shard_map/attend_back/pallas_call | solution.py:494
  205.5 28.3 %give_back.2 = (f32[2,208,384]{2,1,0:T(8,128)}, f32[2,112,384]{2,1,0:T(8,128)}) custom-call(bf16[4,2,320,384]{3,2,1,0:T(8,128)(2,1)} %get-tuple-element.121.refs_0_, f32[2,4]{1,0:T(2,128)} %compare_convert_fusion.refs_2_.refs_1_), custom_call_target="tpu_custom_call" | custom-call | flops 24999999488 | tf_op jit(solution)/shard_map/give_back/pallas_call | solution.py:976
  233.8 27.1 %first_back.1 = (f32[2,784,384]{2,1,0:T(8,128)}, bf16[2,784,384]{2,1,0:T(8,128)(2,1)}, bf16[2,384,1792]{2,1,0:T(8,128)(2,1)}, f32[2,1,768]{2,1,0:T(1,128)}, f32[8,384]{1,0:T(8,128)}) custom-call(f32[2,784,384]{2,1,0:T(8,128)} %get-tuple-element.105.middle_ref, f32[2,784,384]{2,1,0:T(8,128)} %get-tuple-element.106.after_ref, ...), custom_call_target="tpu_custom_call" | custom-call | flops 25999998976 | tf_op jit(solution)/shard_map/first_back/pallas_call | solution.py:494
  261.0 1.4 copy-done.2
  262.5 1.9 pad_maximum_fusion
  264.4 37.7 %attend_back.3 = (f32[2,784,384]{2,1,0:T(8,128)}, bf16[4,2,320,384]{3,2,1,0:T(8,128)(2,1)}, bf16[2,384,576]{2,1,0:T(8,128)(2,1)}, f32[8,384]{1,0:T(8,128)}) custom-call(bf16[2,784,384]{2,1,0:T(8,128)(2,1)} %get-tuple-element.92.x_ref, bf16[2,784,384]{2,1,0:T(8,128)(2,1)} %get-tuple-element.124.g_ref, bf16[4,2,208,384]{3,2,1,0:T(8,128)(2,1)} %get-tuple-element.100.own_ref, ...), custom_call_target="tpu_custom_call" | custom-call | flops 35999997952 | tf_op jit(solution)/shard_map/attend_back/pallas_call | solution.py:494
  302.1 73.4 %give_back.3 = (f32[2,208,384]{2,1,0:T(8,128)}, f32[2,112,384]{2,1,0:T(8,128)}, bf16[2,2,208,768]{3,2,1,0:T(8,128)(2,1)}, f32[192,1536]{1,0:T(8,128)}, f32[192,1536]{1,0:T(8,128)}) custom-call(bf16[4,2,320,384]{3,2,1,0:T(8,128)(2,1)} %get-tuple-element.126.refs_0_, f32[2,4]{1,0:T(2,128)} %compare_convert_fusion.refs_2_.refs_1_, ...), custom_call_target="tpu_custom_call" | custom-call | flops 35000000512 | tf_op jit(solution)/shard_map/give_back/pallas_call | solution.py:976
  375.6 1.4 slice.51
  377.4 1.5 copy.58
  378.9 6.0 %last_back.1 = (bf16[2,4,196,384]{3,2,1,0:T(8,128)(2,1)}, f32[8,384]{1,0:T(8,128)}) custom-call(bf16[2,784,384]{2,1,0:T(8,128)(2,1)} %get-tuple-element.93.x_ref, f32[2,784,384]{2,1,0:T(8,128)} %get-tuple-element.130.res_ref, f32[2,784,384]{2,1,0:T(8,128)} %get-tuple-element.131.dx_ref, f32[2,208,384]{2,1,0:T(8,128)} %get-tuple-element.132.own_ref, ...), custom_call_target="tpu_custom_call" | custom-call | flops 6000000000 | tf_op jit(solution)/shard_map/last_back/pallas_call | solution.py:494
  385.0 46.8 %finish.1 = (bf16[2,2,4,196,384]{4,3,2,1,0:T(8,128)(2,1)}, f32[3,384]{1,0:T(4,128)}, f32[1,768]{1,0:T(1,128)}, f32[5,384]{1,0:T(8,128)}, f32[3,768]{1,0:T(4,128)...) custom-call(bf16[2,4,196,384]{3,2,1,0:T(8,128)(2,1)} %get-tuple-elem, ...), custom_call_target="tpu_custom_call" | custom-call | flops 40000000000 | tf_op jit(solution)/shard_map/finish/pallas_call | solution.py:1154
  434.4 1.3 reduce.2
  437.7 1.8 copy.69
  439.5 2.0 bitcast_convert_fusion
  441.5 3.5 copy.59
  (129 shorter events, 27.8 us)
Async XLA Ops:
  7.2 6.0 %copy-start = (bf16[1,4,4,49,768]{4,2,3,1,0:T(4,128)(2,1)S(1)}, bf16[1,4,4,49,768]{4,2,3,1,0:T(4,128)(2,1)}, u32[]{:S(2)}) copy-start(bf16[1,4,4,49,768]{4,2,3,1,0:T(4,128)(2,1)} %param.45) | copy-start | bytes 3612676
  7.2 57.4 %all-gather.5.cloned.1.call-start = ((), (), s32[]{:S(2)}) async-start(), calls=%async_computation.6 | async-start | bytes 3981312 | tf_op jit(solution)/shard_map/all_gather | solution.py:1206
  10.4 134.1 %all-gather.7.cloned.1.call-start = ((), (), s32[]{:S(2)}) async-start(), calls=%async_computation.7 | async-start | bytes 13271040 | tf_op jit(solution)/shard_map/all_gather | solution.py:1223
  17.8 4.4 copy-start.13
  17.8 5.1 %copy-start.31 = (s32[1,4]{1,0:T(1,128)S(1)}, s32[1,4]{1,0:T(1,128)}, u32[]{:S(2)}) copy-start(s32[1,4]{1,0:T(1,128)} %param.27) | copy-start | bytes 52
  23.7 35.0 %copy-start.8 = (bf16[192,1536]{1,0:T(8,128)(2,1)S(1)}, bf16[192,1536]{1,0:T(8,128)(2,1)}, u32[]{:S(2)}) copy-start(bf16[192,1536]{1,0:T(8,128)(2,1)} %param.35) | copy-start | bytes 1769476
  23.7 35.0 %copy-start.9 = (bf16[192,1536]{1,0:T(8,128)(2,1)S(1)}, bf16[192,1536]{1,0:T(8,128)(2,1)}, u32[]{:S(2)}) copy-start(bf16[192,1536]{1,0:T(8,128)(2,1)} %param.36) | copy-start | bytes 1769476
  23.7 35.0 %copy-start.15 = (bf16[192,384]{1,0:T(8,128)(2,1)S(1)}, bf16[192,384]{1,0:T(8,128)(2,1)}, u32[]{:S(2)}) copy-start(bf16[192,384]{1,0:T(8,128)(2,1)} %param.33) | copy-start | bytes 442372
  23.7 35.0 %copy-start.16 = (bf16[192,192]{1,0:T(8,128)(2,1)S(1)}, bf16[192,192]{1,0:T(8,128)(2,1)}, u32[]{:S(2)}) copy-start(bf16[192,192]{1,0:T(8,128)(2,1)} %param.34) | copy-start | bytes 221188
  60.6 3.3 slice-start
  60.6 241.5 %reduce-scatter.4.cloned.1.call-start = ((), (), s32[]{:S(2)}) async-start(), calls=%async_computation.3 | async-start | bytes 10616832 | tf_op jit(solution)/shard_map/reduce_scatter | solution.py:1267
  171.1 213.9 %reduce-scatter.6.cloned.1.call-start = ((), (), s32[]{:S(2)}) async-start(), calls=%async_computation.4 | async-start | bytes 3096576 | tf_op jit(solution)/shard_map/reduce_scatter | solution.py:1267
  233.8 27.2 %copy-start.3 = (bf16[2,4,96,768]{3,2,1,0:T(8,128)(2,1)S(1)}, bf16[2,4,96,768]{3,2,1,0:T(8,128)(2,1)}, u32[]{:S(2)}) copy-start(bf16[2,4,96,768]{3,2,1,0:T(8,128)(2,1)} %get-tuple-element.145) | copy-start | bytes 3538948
  260.9 124.1 %reduce-scatter.8.cloned.1.call-start = ((), (), s32[]{:S(2)}) async-start(), calls=%async_computation.5 | async-start | bytes 3981312 | tf_op jit(solution)/shard_map/reduce_scatter | solution.py:1267
  441.5 3.5 copy-start.17
  441.5 4.1 copy-start.12
  441.5 4.8 %copy-start.11 = (f32[96,768]{1,0:T(8,128)S(1)}, f32[96,768]{1,0:T(8,128)}, u32[]{:S(2)}) copy-start(f32[96,768]{1,0:T(8,128)} %get-tuple-element.237) | copy-start | bytes 884740
  441.5 5.6 %copy-start.10 = (f32[192,384]{1,0:T(8,128)S(1)}, f32[192,384]{1,0:T(8,128)}, u32[]{:S(2)}) copy-start(f32[192,384]{1,0:T(8,128)} %get-tuple-element.239) | copy-start | bytes 884740
  445.0 3.5 copy-start.5
  446.4 3.2 copy-start.4
  447.8 5.7 %copy-start.1 = (bf16[1,4,4,49,768]{4,2,3,1,0:T(4,128)(2,1)S(1)}, bf16[1,4,4,49,768]{4,2,3,1,0:T(4,128)(2,1)}, u32[]{:S(2)}) copy-start(bf16[1,4,4,49,768]{4,2,3,1,0:T(4,128)(2,1)} %param.45) | copy-start | bytes 3612676
  448.5 3.3 copy-start.21
  448.5 3.9 copy-start.30
  448.5 4.4 copy-start.29
  (15 other events, 31.5 us)
Sparse Core Ops, SparseCore 0:
  10.6 45.8 all-gather.4
  60.8 78.1 all-gather.6
  171.2 86.1 reduce-scatter.3
  261.0 44.3 reduce-scatter.5
  309.8 50.7 reduce-scatter.7

commit v8 on v7

--- a/solution.py
+++ b/solution.py
@@ -31,7 +31,7 @@
     for f in range(frames):
         for p in range(PATCH):
             r, c = divmod(p, GRID)
-            out[f * POOLED + (r // 2) * half + c // 2, f * PATCH + p] = 0.25
+            out[((r // 2) * half + c // 2) * frames + f, p * frames + f] = 0.25
     return out
 
 
@@ -40,9 +40,138 @@
     out = np.zeros((rows, cols), np.float32)
     for j in range(frames // 2):
         for p in range(POOLED):
-            out[j * POOLED + p, 2 * j * POOLED + p] = 0.5
-            out[j * POOLED + p, (2 * j + 1) * POOLED + p] = 0.5
+            out[p * (frames // 2) + j, p * frames + 2 * j] = 0.5
+            out[p * (frames // 2) + j, p * frames + 2 * j + 1] = 0.5
     return out
+
+
+MESH = pl.DeviceIdType.MESH
+
+
+def places():
+    tok, toks = lax.axis_index("tok"), lax.axis_size("tok")
+    return lax.axis_index("clip"), lax.axis_index("head"), tok // 2, tok % 2, toks // 2
+
+
+def greet(copies_to_me, i_copy_to):
+    barrier = pltpu.get_barrier_semaphore()
+    for device, condition in copies_to_me:
+        if condition is None:
+            pl.semaphore_signal(barrier, inc=1, device_id=device, device_id_type=MESH)
+        else:
+            @pl.when(condition)
+            def _():
+                pl.semaphore_signal(barrier, inc=1, device_id=device, device_id_type=MESH)
+    count = 0
+    for _, condition in i_copy_to:
+        count = count + (1 if condition is None else jnp.where(condition, 1, 0))
+    pl.semaphore_wait(barrier, count)
+
+
+def remote(src, dst, send, recv, device):
+    return pltpu.make_async_remote_copy(
+        src_ref=src, dst_ref=dst, send_sem=send, recv_sem=recv, device_id=device, device_id_type=MESH
+    )
+
+
+def rem(a, n):
+    return lax.rem(a + n, n)
+
+
+class Chain:
+    def __init__(self, part_s, outer_s, inner_s, pieces, in_send, in_recv, mid_send, mid_recv, out_send, out_recv):
+        self.clip, clips = lax.axis_index("clip"), lax.axis_size("clip")
+        clip = self.clip
+        left = clip < clips // 2
+        inner, outer = jnp.where(left, clip + 1, clip - 1), jnp.where(left, clip - 1, clip + 1)
+        self.inner, self.outer = {"clip": inner}, {"clip": outer}
+        self.end = (clip == 0) | (clip == clips - 1)
+        self.middle = (clip == clips // 2 - 1) | (clip == clips // 2)
+        self.part, self.from_outer, self.from_inner, self.pieces = part_s, outer_s, inner_s, pieces
+        self.inward = [remote(part_s.at[p], outer_s.at[p], in_send.at[n], in_recv.at[n], self.inner) for n, p in enumerate(pieces)]
+        self.across = [remote(part_s.at[p], inner_s.at[p], mid_send.at[n], mid_recv.at[n], self.inner) for n, p in enumerate(pieces)]
+        self.outward = [remote(inner_s.at[p], inner_s.at[p], out_send.at[n], out_recv.at[n], self.outer) for n, p in enumerate(pieces)]
+
+    def greet(self):
+        barrier = pltpu.get_barrier_semaphore()
+        pl.semaphore_signal(barrier, inc=1, device_id=self.inner, device_id_type=MESH)
+
+        @pl.when(jnp.logical_not(self.end))
+        def _():
+            pl.semaphore_signal(barrier, inc=1, device_id=self.outer, device_id_type=MESH)
+
+        pl.semaphore_wait(barrier, jnp.where(self.end, 1, 2))
+
+    def greets(self):
+        both = [(self.inner, None), (self.outer, jnp.logical_not(self.end))]
+        return both
+
+    def send_ends(self, n):
+        @pl.when(self.end & jnp.logical_not(self.middle))
+        def _():
+            self.inward[n].start()
+
+    def send_parts(self, n):
+        here = self.pieces[n]
+
+        @pl.when(jnp.logical_not(self.end))
+        def _():
+            self.inward[n].wait_recv()
+            self.part[here] = (self.part[here].astype(f32) + self.from_outer[here].astype(f32)).astype(bf16)
+
+        @pl.when(jnp.logical_not(self.end) & jnp.logical_not(self.middle))
+        def _():
+            self.inward[n].start()
+
+        @pl.when(self.middle)
+        def _():
+            self.across[n].start()
+
+    def totals(self, n):
+        self.middle_totals(n)
+        self.other_totals(n)
+
+    def middle_totals(self, n):
+        here = self.pieces[n]
+
+        @pl.when(self.middle)
+        def _():
+            self.across[n].wait_recv()
+            self.across[n].wait_send()
+            self.from_inner[here] = (self.part[here].astype(f32) + self.from_inner[here].astype(f32)).astype(bf16)
+
+        @pl.when(self.middle & jnp.logical_not(self.end))
+        def _():
+            self.outward[n].start()
+
+    def other_totals(self, n):
+        @pl.when(jnp.logical_not(self.middle))
+        def _():
+            self.inward[n].wait_send()
+            self.outward[n].wait_recv()
+
+        @pl.when(jnp.logical_not(self.middle) & jnp.logical_not(self.end))
+        def _():
+            self.outward[n].start()
+
+    def close(self):
+        @pl.when(jnp.logical_not(self.end))
+        def _():
+            for copy in self.outward:
+                copy.wait_send()
+
+
+def chain_scratch(buffer, pieces):
+    return [pltpu.VMEM(buffer, bf16)] * 3 + [dma(pieces)] * 6
+
+
+ANY = pl.BlockSpec(memory_space=pl.ANY)
+INVMEM = pl.BlockSpec(memory_space=pltpu.VMEM)
+INSMEM = pl.BlockSpec(memory_space=pltpu.SMEM)
+
+
+def dma(*dims):
+    return pltpu.SemaphoreType.DMA(dims)
 
 
 def dot(a, b, dims=NN):
@@ -166,10 +295,8 @@
         q_s[:, low:low + 384] = (value + bias_ref[0:1, low:low + 384]).astype(bf16)
 
 
-def norm_pool_kernel(clips_ref, vec_ref, pool_ref, pair_ref, x_ref, low_ref, pooled_ref, mean_ref):
-    x = jnp.concatenate([clips_ref[0, f].astype(f32) for f in range(clips_ref.shape[1])], axis=0)
-    x_ref[0] = x.astype(bf16)
-    unit, _ = norm(x)
+def norm_pool_kernel(x_ref, vec_ref, pool_ref, pair_ref, low_ref, pooled_ref, mean_ref):
+    unit, _ = norm(x_ref[0].astype(f32))
     normed = unit * vec_ref[0:1, :] + vec_ref[1:2, :]
     low_ref[0] = normed.astype(bf16)
     pooled = exact_dot(pool_ref[...], normed)
@@ -225,13 +352,41 @@
         out_ref[0, :, group] = jnp.concatenate(parts, axis=1).astype(bf16)
 
 
-def attend_back_kernel(
-    chunk, valid, x_ref, g_ref, own_ref, mem_ref, w_ref, qv_ref, has_ref, lse_ref,
-    dx_ref, dpool_ref, gw_ref, row_ref,
-    w_s, x_s, q_s, k_s, v_s, s_s, dp_s, p_s, ds_s, dk_s, dv_s, dq_s, gw_s,
-):
+def attend_back_kernel(chunk, valid, hosted, *refs):
+    if hosted:
+        *refs, copy_sem = refs
+        refs, shard_ref, refs_out, sum_ref, scratch, chain = refs[:8], refs[8], refs[9:13], refs[13], refs[14:26], refs[26:]
+        refs = (*refs, *refs_out, *scratch)
+        each = shard_ref.shape[0] // hosted
+        chain = Chain(*chain[:3], [(pl.ds(each * n, each), slice(None)) for n in range(hosted)], *chain[3:])
+    (x_ref, g_ref, own_ref, mem_ref, w_ref, qv_ref, has_ref, lse_ref, dx_ref, dpool_ref, gw_ref, row_ref,
+     w_s, x_s, q_s, k_s, v_s, s_s, dp_s, p_s, ds_s, dk_s, dv_s, gw_s) = refs
     nq, width = q_s.shape
     step = pl.program_id(0)
+    if hosted:
+        @pl.when(step == 0)
+        def _():
+            chain.greet()
+            load = pltpu.make_async_copy(shard_ref, chain.part, copy_sem.at[0])
+            load.start()
+            load.wait()
+            for n in range(hosted):
+                chain.send_ends(n)
+
+    def progress(head):
+        if hosted:
+            half = -(-hosted // 3)
+
+            @pl.when(step == 0)
+            def _():
+                for n in range(max(half * (head - 1), 0), min(half * head, hosted)):
+                    chain.send_parts(n)
+
+            @pl.when(step == 1)
+            def _():
+                for n in range(half * head, min(half * head + half, hosted)):
+                    chain.middle_totals(n)
+
     columns = key_mask(own_ref, mem_ref, valid, has_ref[step])
     if width == 384:
         @pl.when(step == 0)
@@ -285,6 +440,7 @@
                 k = start // 128 - 3 * tile + w
                 part = dq[:, 128 * w:128 * w + 128]
                 parts[k] = part if parts[k] is None else parts[k] + part
+            progress(head)
         total = jnp.concatenate(parts, axis=1) + g_ref[0, :, group].astype(f32)
         row_q.append(sum_rows(total))
         low = total.astype(bf16)
@@ -313,6 +469,13 @@
     def _():
         for h in range(gw_ref.shape[0]):
             write_shares(gw_ref, h, gw_s)
+        if hosted:
+            for n in range(hosted):
+                chain.other_totals(n)
+            chain.close()
+            store = pltpu.make_async_copy(chain.from_inner, sum_ref, copy_sem.at[0])
+            store.start()
+            store.wait()
 
 
 def first_mlp_kernel(x_ref, comb_ref, out_ref, up_ref, down_ref, ub_ref, vec_ref, pool_ref, pair_ref,
@@ -463,8 +626,7 @@
     dnorm = dx_ref[0] + exact_dot(unpool_ref[...], dpool)
     unit, inverse = norm(x_ref[0].astype(f32))
     grad = norm_back(unit, inverse, vec_ref[0:1, :], dnorm) + res_ref[0]
-    for f in range(grad_ref.shape[1]):
-        grad_ref[0, f] = grad[PATCH * f:PATCH * f + PATCH].astype(bf16)
+    grad_ref[0] = grad.astype(bf16)
     add_rows(row_ref, [sum_rows(dnorm * unit), sum_rows(dnorm)])
 
 
@@ -485,7 +647,7 @@
     return pl.CostEstimate(flops=int(us * 1e9), bytes_accessed=0, transcendentals=0)
 
 
-def call(kernel, steps, args, outs, scratch=(), name=None, us=10):
+def call(kernel, steps, args, outs, scratch=(), name=None, us=10, number=None):
     def spec(array, how):
         if how is None:
             return whole(array)
@@ -497,8 +659,8 @@
         in_specs=[spec(a, how) for a, how in args],
         out_specs=[spec(a, how) for a, how in outs],
         out_shape=[a for a, _ in outs],
-        scratch_shapes=[pltpu.VMEM(dims, dtype) for dims, dtype in scratch],
-        compiler_params=pltpu.CompilerParams(vmem_limit_bytes=VMEM_CAP),
+        scratch_shapes=[pltpu.VMEM(*one) if isinstance(one, tuple) else one for one in scratch],
+        compiler_params=pltpu.CompilerParams(vmem_limit_bytes=VMEM_CAP, collective_id=number, has_side_effects=number is not None),
         cost_estimate=about(us),
         name=name,
     )(*[a for a, _ in args])
@@ -521,123 +683,29 @@
     )
 
 
-def attend_back(x, grad, own, mem, w, qv, has, valid, lse, heads):
+def attend_back(x, grad, own, mem, w, qv, has, valid, lse, heads, shard=None, number=None):
     batches, nq, d = x.shape
     width = grad.shape[2]
     keys = own.shape[0] * own.shape[2] + mem.shape[0] * mem.shape[2]
     both = (own.shape[0], batches, own.shape[2] + mem.shape[2], d)
     groups = (width // 384, d, 1152)
+    args = [(x, 0), (grad, 0), (own, 1), (mem, 1), w, (qv, None), (has, INSMEM), (lse, 0)]
+    outs = [(shape((batches, nq, d), f32), 0), (shape(both, bf16), 1), (shape((heads, d, 3 * width // heads), bf16), None), (shape((8, width), f32), None)]
+    scratch = [
+        ((1, d, 1152 if width == 384 else 128), bf16),
+        ((keys, d), bf16), ((nq, width), bf16), ((keys, width), bf16), ((keys, width), bf16),
+        ((nq, keys), f32), ((nq, keys), f32), ((nq, keys), bf16), ((nq, keys), bf16),
+        ((384, keys), f32), ((384, keys), f32), (groups, f32),
+    ]
+    pieces = 0
+    if shard is not None:
+        pieces = shard.shape[0] // 48
+        args, outs = args + [(shard, ANY)], outs + [(shape(shard.shape, bf16), ANY)]
+        scratch += chain_scratch(shard.shape, pieces) + [dma(1)]
     return call(
-        functools.partial(attend_back_kernel, chunk_of(nq), valid), batches,
-        [(x, 0), (grad, 0), (own, 1), (mem, 1), w, (qv, None), (has, pl.BlockSpec(memory_space=pltpu.SMEM)), (lse, 0)],
-        [(shape((batches, nq, d), f32), 0), (shape(both, bf16), 1), (shape((heads, d, 3 * width // heads), bf16), None), (shape((8, width), f32), None)],
-        [((1, d, 1152 if width == 384 else 128), bf16),
-         ((keys, d), bf16), ((nq, width), bf16), ((keys, width), bf16), ((keys, width), bf16),
-         ((nq, keys), f32), ((nq, keys), f32), ((nq, keys), bf16), ((nq, keys), bf16),
-         ((384, keys), f32), ((384, keys), f32), ((8, 128), f32), (groups, f32)],
-        name="attend_back", us=36,
+        functools.partial(attend_back_kernel, chunk_of(nq), valid, pieces), batches, args, outs, scratch,
+        name="attend_back", us=36, number=number,
     )
-
-
-MESH = pl.DeviceIdType.MESH
-
-
-def places():
-    tok, toks = lax.axis_index("tok"), lax.axis_size("tok")
-    return lax.axis_index("clip"), lax.axis_index("head"), tok // 2, tok % 2, toks // 2
-
-
-def greet(copies_to_me, i_copy_to):
-    barrier = pltpu.get_barrier_semaphore()
-    for device, condition in copies_to_me:
-        if condition is None:
-            pl.semaphore_signal(barrier, inc=1, device_id=device, device_id_type=MESH)
-        else:
-            @pl.when(condition)
-            def _():
-                pl.semaphore_signal(barrier, inc=1, device_id=device, device_id_type=MESH)
-    count = 0
-    for _, condition in i_copy_to:
-        count = count + (1 if condition is None else jnp.where(condition, 1, 0))
-    pl.semaphore_wait(barrier, count)
-
-
-def remote(src, dst, send, recv, device):
-    return pltpu.make_async_remote_copy(
-        src_ref=src, dst_ref=dst, send_sem=send, recv_sem=recv, device_id=device, device_id_type=MESH
-    )
-
-
-def rem(a, n):
-    return lax.rem(a + n, n)
-
-
-class Chain:
-    def __init__(self, part_s, outer_s, inner_s, pieces, in_send, in_recv, mid_send, mid_recv, out_send, out_recv):
-        self.clip, clips = lax.axis_index("clip"), lax.axis_size("clip")
-        clip = self.clip
-        left = clip < clips // 2
-        inner, outer = jnp.where(left, clip + 1, clip - 1), jnp.where(left, clip - 1, clip + 1)
-        self.inner, self.outer = {"clip": inner}, {"clip": outer}
-        self.end = (clip == 0) | (clip == clips - 1)
-        self.middle = (clip == clips // 2 - 1) | (clip == clips // 2)
-        self.part, self.from_outer, self.from_inner, self.pieces = part_s, outer_s, inner_s, pieces
-        self.inward = [remote(part_s.at[p], outer_s.at[p], in_send.at[n], in_recv.at[n], self.inner) for n, p in enumerate(pieces)]
-        self.across = [remote(part_s.at[p], inner_s.at[p], mid_send.at[n], mid_recv.at[n], self.inner) for n, p in enumerate(pieces)]
-        self.outward = [remote(inner_s.at[p], inner_s.at[p], out_send.at[n], out_recv.at[n], self.outer) for n, p in enumerate(pieces)]
-
-    def greets(self):
-        both = [(self.inner, None), (self.outer, jnp.logical_not(self.end))]
-        return both
-
-    def send_ends(self, n):
-        @pl.when(self.end & jnp.logical_not(self.middle))
-        def _():
-            self.inward[n].start()
-
-    def send_parts(self, n):
-        here = self.pieces[n]
-
-        @pl.when(jnp.logical_not(self.end))
-        def _():
-            self.inward[n].wait_recv()
-            self.part[here] = (self.part[here].astype(f32) + self.from_outer[here].astype(f32)).astype(bf16)
-
-        @pl.when(jnp.logical_not(self.end) & jnp.logical_not(self.middle))
-        def _():
-            self.inward[n].start()
-
-        @pl.when(self.middle)
-        def _():
-            self.across[n].start()
-
-    def totals(self, n):
-        here = self.pieces[n]
-
-        @pl.when(self.middle)
-        def _():
-            self.across[n].wait_recv()
-            self.across[n].wait_send()
-            self.from_inner[here] = (self.part[here].astype(f32) + self.from_inner[here].astype(f32)).astype(bf16)
-
-        @pl.when(jnp.logical_not(self.middle))
-        def _():
-            self.inward[n].wait_send()
-            self.outward[n].wait_recv()
-
-        @pl.when(jnp.logical_not(self.end))
-        def _():
-            self.outward[n].start()
-
-    def close(self):
-        @pl.when(jnp.logical_not(self.end))
-        def _():
-            for copy in self.outward:
-                copy.wait_send()
-
-
-def chain_scratch(buffer, pieces):
-    return [pltpu.VMEM(buffer, bf16)] * 3 + [dma(pieces)] * 6
 
 
 def share_kernel(gather, *refs):
@@ -791,15 +859,6 @@
             copy.wait_send()
 
 
-ANY = pl.BlockSpec(memory_space=pl.ANY)
-INVMEM = pl.BlockSpec(memory_space=pltpu.VMEM)
-INSMEM = pl.BlockSpec(memory_space=pltpu.SMEM)
-
-
-def dma(*dims):
-    return pltpu.SemaphoreType.DMA(dims)
-
-
 def share_pooled(pooled, mean, pick, number, block=None, biases=()):
     toks, heads = lax.axis_size("tok"), lax.axis_size("head")
     chips = toks // 2
@@ -833,11 +892,7 @@
 
 def give_back_kernel(exchange, *refs):
     if exchange:
-        part_ref, pick_ref, half_ref, shard_ref, own_ref, back_ref, all_ref, up_ref, down_ref, *refs = refs
-        refs, (half_local, half_send, half_recv), chain = refs[:-12], refs[-12:-9], refs[-9:]
-        depth = chain[-1].shape[0]
-        rows_each = shard_ref.shape[0] // depth
-        chain = Chain(*chain[:3], [(pl.ds(rows_each * n, rows_each), slice(None)) for n in range(depth)], *chain[3:])
+        part_ref, pick_ref, half_ref, own_ref, back_ref, all_ref, *refs, half_local, half_send, half_recv = refs
     else:
         part_ref, pick_ref, own_ref, back_ref, *refs = refs
     (mine_s, core_s, sum_s, chip_s, route_s, got_s,
@@ -851,12 +906,7 @@
     heads_of = lambda by, sign: [{"clip": clip + by, "head": rem(head + sign * d, heads)} for d in range(heads)]
     last, begun = clip < clips - 1, clip > 0
     near = [(d, None) for d in [partner] + across + (beside if exchange else [])]
-    near += chain.greets() if exchange else []
     greet(near + [(d, last) for d in heads_of(1, 1)], near + [(d, begun) for d in heads_of(-1, -1)])
-    if exchange:
-        chain.part[...] = shard_ref[...]
-        for n in range(depth):
-            chain.send_ends(n)
 
     order = [rem(chip + k, chips) for k in list(range(1, chips)) + [0]]
     core_copies, local_copies = [], []
@@ -930,16 +980,6 @@
     def _():
         back_ref[...] = jnp.zeros_like(back_ref)
 
-    if exchange:
-        for n in range(depth):
-            chain.send_parts(n)
-            if n > 0:
-                chain.totals(n - 1)
-        chain.totals(depth - 1)
-        total = chain.from_inner[...].astype(f32)
-        up_ref[...] = total[:up_ref.shape[0]]
-        down_ref[...] = total[up_ref.shape[0]:]
-        chain.close()
     for copy in halves:
         copy.wait_recv()
     for copy in core_copies + mem_copies + own_copies + halves:
@@ -953,7 +993,7 @@
             copy.wait_send()
 
 
-def give_back(part, pick, own_rows, number, half=None, shard=None):
+def give_back(part, pick, own_rows, number, half=None):
     toks, heads = lax.axis_size("tok"), lax.axis_size("head")
     chips, few = toks // 2, max(toks // 2 - 1, 1)
     share, rows, d = part.shape[1:]
@@ -966,13 +1006,9 @@
         dma(chips), dma(chips), dma(chips), dma(few), dma(few), dma(few), dma(few), dma(heads), dma(heads),
     ]
     if half is not None:
-        pair, depth, lanes = shard.shape
-        shard = shard.reshape(-1, lanes)
-        args, specs = args + [half, shard], specs + [ANY, INVMEM]
-        outs += [shape((heads,) + half.shape, half.dtype), shape((depth, lanes), f32), shape((depth, lanes), f32)]
-        out_specs += [ANY, INVMEM, INVMEM]
+        args, specs = args + [half], specs + [ANY]
+        outs, out_specs = outs + [shape((heads,) + half.shape, half.dtype)], out_specs + [ANY]
         scratch += [dma(1), dma(max(heads - 1, 1)), dma(max(heads - 1, 1))]
-        scratch += chain_scratch(shard.shape, shard.shape[0] // 48)
     return pl.pallas_call(
         functools.partial(give_back_kernel, half is not None),
         in_specs=specs,
@@ -980,15 +1016,14 @@
         out_shape=outs,
         scratch_shapes=scratch,
         compiler_params=pltpu.CompilerParams(collective_id=number, has_side_effects=True, vmem_limit_bytes=VMEM_CAP),
-        cost_estimate=about(25 if half is None else 35),
+        cost_estimate=about(25),
         name="give_back",
     )(*args)
 
 
-def finish_kernel(sizes, half_ref, last_ref, qv_a_rows, a_ref, b_ref, qv_b_rows, ub_a_rows, ub_b_rows, grad_ref, rest_ref, group_ref, all_ref, gains_a_ref, gains_b_ref, shifts_a_ref,
-                  shifts_b_ref, qv_a_ref, qv_b_ref, ub_a_ref, ub_b_ref, gtotal_ref, up_ref, down_ref, out_ref,
-                  q_ref, out_b_ref, skip_ref, *scratch):
-    (small_ref, small_s, small_core, small_chip, small_head, small_clip, part_s, part_core, chip_s, part_chip, part_head,
+def finish_kernel(half_ref, last_ref, qv_a_rows, a_ref, b_ref, qv_b_rows, ub_a_rows, ub_b_rows, grad_ref, rest_ref, group_ref,
+                  all_ref, total_ref, sums_ref, *scratch):
+    (small_ref, small_s, small_core, small_chip, small_head, small_clip, part_s, part_core, head_s, part_chip, part_head,
      local_sem, half_send, half_recv, core_send, core_recv, chip_send, chip_recv, head_send, head_recv,
      clip_send, clip_recv, *chain) = scratch
     first_lanes, next_lanes, deep = group_ref.shape[1], rest_ref.shape[1], grad_ref.shape[1]
@@ -1048,8 +1083,6 @@
         [remote(half_ref.at[s], all_ref.at[head, s], half_send.at[k, s], half_recv.at[k, s], d) for k, d in enumerate(beside)]
         for s in range(share)
     ]
-    for s in range(share - 1):
-        go(halves[s])
     local_half = pltpu.make_async_copy(half_ref, all_ref.at[head], local_sem.at[0])
     local_half.start()
     arrived(first)
@@ -1057,81 +1090,50 @@
     for n in range(heads * chips):
         part_s[n] = (grad_ref[2 * n + core].astype(f32) + part_core[n].astype(f32)).astype(bf16)
     copies = []
+    for k, d in enumerate(beside):
+        copies += go([remote(small_s.at[0], small_head.at[k], head_send.at[k, 0], head_recv.at[k, 0], d)])
+        for x in range(chips):
+            block = rem(head + k + 1, heads) * chips + x
+            copies += go([remote(part_s.at[block], part_head.at[k, x], head_send.at[k, x + 1], head_recv.at[k, x + 1], d)])
+    for s in range(share):
+        go(halves[s])
+    chain.send_parts(0)
+    chain.send_parts(1)
+    arrived(copies)
+    small_s[1] = in_order(head, heads, small_s[0], lambda k: small_head[k])
+    for x in range(chips):
+        total = part_s[head * chips + x].astype(f32)
+        for k in range(heads - 1):
+            total = total + part_head[k, x].astype(f32)
+        head_s[x] = total.astype(bf16)
+    copies = []
     for k, d in enumerate(across):
-        copies += go([remote(small_s.at[0], small_chip.at[k], chip_send.at[k, 0], chip_recv.at[k, 0], d)])
-        for h in range(heads):
-            block = h * chips + rem(chip + k + 1, chips)
-            copies += go([remote(part_s.at[block], part_chip.at[k, h], chip_send.at[k, h + 1], chip_recv.at[k, h + 1], d)])
+        copies += go([remote(small_s.at[1], small_chip.at[k], chip_send.at[k, 0], chip_recv.at[k, 0], d)])
+        copies += go([remote(head_s.at[rem(chip + k + 1, chips)], part_chip.at[k], chip_send.at[k, 1], chip_recv.at[k, 1], d)])
+    chain.send_parts(2)
+    chain.middle_totals(0)
+    chain.send_parts(3)
     arrived(copies)
-    small_s[1] = in_order(chip, chips, small_s[0], lambda k: small_chip[k])
-    for h in range(heads):
-        total = part_s[h * chips + chip].astype(f32)
-        for k in range(chips - 1):
-            total = total + part_chip[k, h].astype(f32)
-        chip_s[h] = total.astype(bf16)
-    copies = []
-    for k, d in enumerate(beside):
-        copies += go([remote(small_s.at[1], small_head.at[k], head_send.at[k, 0], head_recv.at[k, 0], d)])
-        copies += go([remote(chip_s.at[rem(head + k + 1, heads)], part_head.at[k], head_send.at[k, 1], head_recv.at[k, 1], d)])
-    go(halves[share - 1])
-    for n in range(4):
-        chain.send_parts(n)
-    arrived(copies)
-    small_s[2] = in_order(head, heads, small_s[1], lambda k: small_head[k])
-    total = chip_s[head].astype(f32)
-    for k in range(heads - 1):
-        total = total + part_head[k].astype(f32)
+    small_s[2] = in_order(chip, chips, small_s[1], lambda k: small_chip[k])
+    total = head_s[chip].astype(f32)
+    for k in range(chips - 1):
+        total = total + part_chip[k].astype(f32)
     mine = first_lanes + next_lanes
     chain.part[:, mine:mine + grad_ref.shape[2]] = total.astype(bf16)
+    chain.send_ends(4)
     copies = []
     for k, d in enumerate(along):
         copies += go([remote(small_s.at[2], small_clip.at[k], clip_send.at[k, 0], clip_recv.at[k, 0], d)])
-    chain.send_ends(4)
-    chain.totals(0)
-    chain.totals(1)
+    chain.middle_totals(1)
+    chain.middle_totals(2)
     chain.send_parts(4)
-    for n in range(2, 5):
-        chain.totals(n)
+    chain.middle_totals(3)
+    chain.middle_totals(4)
+    for n in range(5):
+        chain.other_totals(n)
     arrived(copies)
-    total = in_order(clip, clips, small_s[2], lambda k: small_clip[k])
-    at = [4]
-
-    def rows(width):
-        first = at[0]
-        at[0] += width // total.shape[1]
-        return jnp.concatenate([total[r:r + 1] for r in range(first, at[0])], axis=1)
-
-    def share_of(row):
-        width = row.shape[1] // heads
-        piece = row[:, :width]
-        for h in range(1, heads):
-            piece = jnp.where(head == h, row[:, width * h:width * h + width], piece)
-        return piece
-
-    gains_a_ref[0:1, :] = total[0:1]
-    gains_a_ref[1:3, :] = total[4:6]
-    shifts_a_ref[0:1, :] = total[1:2]
-    shifts_a_ref[1:5, :] = total[6:10]
-    qv_a_ref[0:1, :] = share_of(total[2:3])
-    qv_a_ref[1:2, :] = share_of(total[3:4])
-    at[0] = 10
-    d2, fa, fb = sizes
-    gains_b_ref[...] = rows(d2)
-    for i in range(3):
-        shifts_b_ref[i:i + 1, :] = rows(d2)
-    for i in range(2):
-        qv_b_ref[i:i + 1, :] = share_of(rows(d2))
-    ub_a_ref[...] = share_of(rows(fa))
-    ub_b_ref[...] = share_of(rows(fb))
-    wide = up_ref.shape[1]
-    sums = chain.from_inner
-    for ref, low in ((q_ref, 0), (up_ref, first_lanes), (down_ref, first_lanes + wide), (out_ref, first_lanes + 2 * wide), (gtotal_ref, mine)):
-        ref[...] = sums[:, low:low + ref.shape[1]].astype(f32)
-    low, rows = q_ref.shape[1], q_ref.shape[0]
-    for ref in (out_b_ref, skip_ref):
-        for n in range(2):
-            ref[rows * n:rows * n + rows, :] = sums[:, low:low + ref.shape[1]].astype(f32)
-            low += ref.shape[1]
+    total_ref[...] = in_order(clip, clips, small_s[2], lambda k: small_clip[k])
+    sums_ref[...] = chain.from_inner[...]
     chain.close()
     for copies in halves:
         arrived(copies)
@@ -1140,33 +1142,83 @@
     local_half.wait()
 
 
-def finish(half, rows, grad, rest, first, d2, fa, fb, ha, hs, number):
+def finish(half, rows, grad, rest, first, count, number):
     toks, heads, clips = lax.axis_size("tok"), lax.axis_size("head"), lax.axis_size("clip")
     chips = toks // 2
     across, beside, along = (max(n, 1) for n in (chips - 1, heads - 1, clips - 1))
     block, depth, d1 = grad.shape[1:], rest.shape[0], rows[0].shape[1]
-    count = 4 + 6 + (6 * d2 + fa + fb) // d1
-    low, full = lambda *dims: pltpu.VMEM(dims, bf16), lambda *dims: pltpu.VMEM(dims + (-(-count // 8) * 8, d1), f32)
-    sums = [(3, d1), (1, d2), (5, d1), (3, d2), (2, d1 // heads), (2, d2 // heads), (1, fa // heads), (1, fb // heads),
-            block, (depth, fa // heads), (depth, fa // heads), (depth, ha),
-            (depth, 3 * d2 // heads), (2 * depth, d2 // heads), (2 * depth, hs)]
+    small = (-(-count // 8) * 8, d1)
+    low, full = lambda *dims: pltpu.VMEM(dims, bf16), lambda *dims: pltpu.VMEM(dims + small, f32)
     buffer = (depth, first.shape[1] + rest.shape[1] + -(-block[1] // 128) * 128)
     return pl.pallas_call(
-        functools.partial(finish_kernel, (d2, fa, fb)),
+        finish_kernel,
         in_specs=[ANY] + [INVMEM] * (len(rows) + 3),
-        out_specs=[ANY] + [INVMEM] * len(sums),
-        out_shape=[shape((heads,) + half.shape, half.dtype)] + [shape(dims, f32) for dims in sums],
+        out_specs=[ANY, INVMEM, INVMEM],
+        out_shape=[shape((heads,) + half.shape, half.dtype), shape(small, f32), shape(buffer, bf16)],
         scratch_shapes=[
             full(), full(3), full(), full(across), full(beside), full(along),
-            low(heads * chips, *block), low(heads * chips, *block), low(heads, *block), low(across, heads, *block), low(beside, *block),
+            low(heads * chips, *block), low(heads * chips, *block), low(chips, *block), low(across, *block), low(beside, chips, *block),
             dma(1), dma(beside, half.shape[0]), dma(beside, half.shape[0]), dma(heads * chips + 1), dma(heads * chips + 1),
-            dma(across, heads + 1), dma(across, heads + 1), dma(beside, 2), dma(beside, 2), dma(along, 1), dma(along, 1),
+            dma(across, 2), dma(across, 2), dma(beside, chips + 1), dma(beside, chips + 1), dma(along, 1), dma(along, 1),
             *chain_scratch(buffer, 5),
         ],
         compiler_params=pltpu.CompilerParams(collective_id=number, has_side_effects=True, vmem_limit_bytes=VMEM_CAP),
         cost_estimate=about(40),
         name="finish",
     )(half, *rows, grad, rest, first)
+
+
+def write_kernel(head_ref, total_ref, sums_ref, mlp_ref, qkv_a_ref, out_a_ref, up_a_ref, down_a_ref, qkv_b_ref, out_b_ref, skip_b_ref,
+                 up_b_ref, down_b_ref, gains_a_ref, gains_b_ref, shifts_a_ref, shifts_b_ref, qv_a_ref, qv_b_ref, ub_a_ref, ub_b_ref):
+    head, total = head_ref[0], total_ref[...]
+    at = [10]
+
+    def rows(width):
+        first = at[0]
+        at[0] += width // total.shape[1]
+        return jnp.concatenate([total[r:r + 1] for r in range(first, at[0])], axis=1)
+
+    def share_of(row, width):
+        piece = row[:, :width]
+        for h in range(1, row.shape[1] // width):
+            piece = jnp.where(head == h, row[:, width * h:width * h + width], piece)
+        return piece
+
+    gains_a_ref[0:1, :] = total[0:1]
+    gains_a_ref[1:3, :] = total[4:6]
+    shifts_a_ref[0:1, :] = total[1:2]
+    shifts_a_ref[1:5, :] = total[6:10]
+    d2, fa, fb = gains_b_ref.shape[1], ub_a_ref.shape[1], ub_b_ref.shape[1]
+    heads = total.shape[1] // qv_a_ref.shape[1]
+    for i in range(2):
+        qv_a_ref[i:i + 1, :] = share_of(total[2 + i:3 + i], qv_a_ref.shape[1])
+    gains_b_ref[...] = rows(d2)
+    for i in range(3):
+        shifts_b_ref[i:i + 1, :] = rows(d2)
+    for i in range(2):
+        qv_b_ref[i:i + 1, :] = share_of(rows(d2), qv_b_ref.shape[1])
+    ub_a_ref[...] = share_of(rows(heads * fa), fa)
+    ub_b_ref[...] = share_of(rows(heads * fb), fb)
+    low = 0
+    depth = sums_ref.shape[0]
+
+    def take(ref):
+        nonlocal low
+        ref[...] = sums_ref[:, low:low + ref.shape[1]].astype(f32)
+        low += ref.shape[1]
+
+    for part in range(3):
+        take(qkv_b_ref.at[part])
+    for ref in (out_b_ref, skip_b_ref):
+        for n in range(2):
+            take(ref.at[depth * n:depth * n + depth])
+    for ref in (up_a_ref, down_a_ref, out_a_ref):
+        take(ref)
+    low = -(-low // 256) * 256
+    for part in range(3):
+        take(qkv_a_ref.at[part])
+    up_b_ref[...] = mlp_ref[:up_b_ref.shape[0], :].astype(f32)
+    down_b_ref[...] = mlp_ref[up_b_ref.shape[0]:, :].astype(f32)
 
 
 def padded_rows(*rows):
@@ -1190,7 +1242,14 @@
     own_rows, mem_rows = up16(pooled_tokens), up16(frames // 2 * POOLED)
     rows2 = share * own_rows
 
-    cot = lax.dynamic_slice_in_dim(cotangent[0], first, share, 0).reshape(share, pooled_tokens, d2)
+
+    def by_patch(tensor):
+        return tensor.transpose(0, 2, 1, 3).reshape(tensor.shape[0], -1, tensor.shape[3])
+
+    def by_frame(rows, like):
+        return rows.reshape(like[:2] + (like[3], like[2], like[4])).transpose(0, 1, 3, 2, 4)
+
+    cot = by_patch(lax.dynamic_slice_in_dim(cotangent[0], first, share, 0))
 
     source = lax.dynamic_slice_in_dim(assign[0], first, share, 0)
     flags = lax.dynamic_slice_in_dim(resets[0], first, share, 0)
@@ -1202,18 +1261,17 @@
     group = ("head", "tok")
     fa, ha = w_up_a.shape[1], w_out_a.shape[1]
     fb, hb, hs = w_up_b.shape[1], w_out_b.shape[1], w_skip_b.shape[1]
-    pack_a = jnp.concatenate([w_up_a, w_down_a, w_qkv_a.reshape(w_qkv_a.shape[0], -1), w_out_a], axis=1)
+    pack_a = jnp.concatenate([w_up_a, w_down_a, *w_qkv_a.transpose(1, 0, 2), w_out_a], axis=1)
     all_a = lax.all_gather(pack_a, group).reshape(heads, d1, -1)
-    mine = lax.dynamic_slice_in_dim(clips_in[0], first, share, 0)
-    stream, low1, pooled1, mean1 = call(
+    stream = by_patch(lax.dynamic_slice_in_dim(clips_in[0], first, share, 0))
+    low1, pooled1, mean1 = call(
         norm_pool_kernel, share,
-        [(mine, 0), (padded_rows(gains_a[0], shifts_a[0]), None), (pooling, None), (pairing, None)],
-        [(shape((share, tokens, d1), bf16), 0), (shape((share, tokens, d1), bf16), 0),
-         (shape((share, own_rows, d1), bf16), 0), (shape((share, mem_rows, d1), bf16), 0)],
+        [(stream, 0), (padded_rows(gains_a[0], shifts_a[0]), None), (pooling, None), (pairing, None)],
+        [(shape((share, tokens, d1), bf16), 0), (shape((share, own_rows, d1), bf16), 0), (shape((share, mem_rows, d1), bf16), 0)],
         name="norm_pool", us=5,
     )
     pooled1, w_qkv_b, w_up_b = lax.optimization_barrier((pooled1, w_qkv_b, w_up_b))
-    pack_q = w_qkv_b.reshape(w_qkv_b.shape[0], -1)
+    pack_q = jnp.concatenate([*w_qkv_b.transpose(1, 0, 2)], axis=1)
     own1, mem1, all_q, qv_a, qv_b, ub_a, ub_b = share_pooled(
         pooled1, mean1, pick, 0, pack_q, [qv_bias_a, qv_bias_b, up_bias_a[None], up_bias_b[None]])
     all_q = all_q.reshape(heads, d1, -1)
@@ -1266,7 +1324,7 @@
     def scatter(grad):
         return lax.psum_scatter(grad, group, scatter_dimension=0, tiled=False)
 
-    sum_mlp_b = scatter(g_mlp_b.reshape((heads * toks,) + g_mlp_b.shape[2:]))
+    sum_mlp_b = scatter(g_mlp_b.reshape((heads * toks,) + g_mlp_b.shape[2:])).reshape(-1, fb)
     dcomb2 = dcomb2.reshape(share, own_rows, d2)
     dq2, dpool2, g_qkv_b, rows_qv_b = attend_back(pooled3, dcomb2, own2, mem2, (all_q, None), qv_b, has, valid, lse2, heads)
     own_back2, mem_back2 = give_back(dpool2, pick, own_rows, 2)
@@ -1288,34 +1346,39 @@
     )
     rest_a = by_owner(g_mlp_a)
     sum_rest_a = scatter(rest_a)
-    dx1, dpool1, g_qkv_a, rows_qv_a = attend_back(low1, dcomb1, own1, mem1, (all_a, rest_spec), qv_a, has, valid, lse1, heads)
-    own_back1, mem_back1, mixed_all, grad_up_b, grad_down_b = give_back(
-        dpool1, pick, own_rows, 3, mixed.reshape(share, own_rows, d2), sum_mlp_b)
+    args = (low1, dcomb1, own1, mem1, (all_a, rest_spec), qv_a, has, valid, lse1, heads)
+    if toks * (own_rows + mem_rows) <= 1536:
+        dx1, dpool1, g_qkv_a, rows_qv_a, sum_mlp_b = attend_back(*args, sum_mlp_b, 5)
+    else:
+        dx1, dpool1, g_qkv_a, rows_qv_a = attend_back(*args)
+        sum_mlp_b = lax.psum(sum_mlp_b, "clip")
+    own_back1, mem_back1, mixed_all = give_back(dpool1, pick, own_rows, 3, mixed.reshape(share, own_rows, d2))
     stream_grad, rows_last = call(
         last_back_kernel, share,
         [(stream, 0), (res1, 0), (dx1, 0), (own_back1, 0), (mem_back1, 0), (padded_rows(gains_a[0]), None),
          (unpooling, None), (unpairing, None)],
-        [(shape((share, frames, PATCH, d1), bf16), 0), (shape((8, d1), f32), None)],
+        [(shape((share, tokens, d1), bf16), 0), (shape((8, d1), f32), None)],
         name="last_back", us=6,
     )
 
     rows = [rows_last, rows_qv_a, rows_a, rows_b, rows_qv_b, g_ub_a, g_ub_b]
-    stream_all, *sums = finish(
-        stream_grad, rows, by_owner(g_qkv_a), sum_rest_a, sum_rest_b, d2, heads * fa, heads * fb, ha, hs, 4)
+    count = 10 + (6 * d2 + heads * (fa + fb)) // d1
+    stream_all, total, sums = finish(stream_grad, rows, by_owner(g_qkv_a), sum_rest_a, sum_rest_b, count, 4)
+    row1, row2 = w_up_a.shape[0], w_up_b.shape[0]
+    outs = [(3, row1, ha), (row1, ha), (row1, fa), (row1, fa), (3, row1, hb), (row2, hb), (row2, hs), (row2, fb), (row2, fb),
+            (3, d1), (1, d2), (5, d1), (3, d2), (2, ha), (2, hb), (1, fa), (1, fb)]
+    grads = call(
+        write_kernel, 1,
+        [(head.astype(jnp.int32)[None], INSMEM), (total, None), (sums, None), (sum_mlp_b, None)],
+        [(shape(dims, f32), None) for dims in outs],
+        name="write", us=4,
+    )
     mixed_all = mixed_all.reshape(micro, own_rows, d2)[:, :pooled_tokens]
     return (
-        mixed_all.reshape(cotangent.shape),
-        stream_all.astype(f32).reshape(clips_in.shape),
-        sums[8].reshape(w_qkv_a.shape),
-        sums[11],
-        sums[9],
-        sums[10],
-        sums[12].reshape(w_qkv_b.shape),
-        sums[13],
-        sums[14],
-        grad_up_b,
-        grad_down_b,
-        sums[0], sums[1][0], sums[2], sums[3], sums[4], sums[5], sums[6][0], sums[7][0],
+        by_frame(mixed_all, cotangent.shape),
+        by_frame(stream_all.astype(f32), clips_in.shape),
+        grads[0].transpose(1, 0, 2), *grads[1:4], grads[4].transpose(1, 0, 2), *grads[5:10],
+        grads[10][0], *grads[11:15], grads[15][0], grads[16][0],
     )
 
 

time: 464 us -> 442 us (0.953)
  local copies, waits for them, and re-layouts: 35.3 us -> 23.5 us
  Pallas kernels: 400 us -> 389 us
    pallas_call x2, Pallas kernels: 102 us -> 55.8 us  [give_back(): pl.pallas_call(functools.partial(give_back_kernel, half is not None), in_...]
    pallas_call x9 -> x10, Pallas kernels: 189 us -> 227 us  [call(): pl.pallas_call(kernel, grid=(steps,), in_specs=[spec(a, how) for a, how i...]
    unnamed x84 -> x33, local copies, waits for them, and re-layouts: 18.6 us -> 4.46 us
    transpose x0 -> x4, local copies, waits for them, and re-layouts: none -> 6.67 us  [the longest x1 5.58 us: by_frame(): rows.reshape(like[:2] + (like[3], like[2], like[4]))]
  transfers between devices with their start and end apart: 5 -> 5, of which waited for: 0 -> 0; matrix products, arithmetic and copies ran while one was open for 4% -> 4% of each run, Pallas kernels for 71% -> 72%
where the time goes in v8:
time: 442 us; the launch traced here: 437 us
  Pallas kernels  389 us (88%)
  local copies, waits for them, and re-layouts  23.5 us (5%)
  between operations  14.3 us (3%)
  other arithmetic  10.1 us (2%)
    pallas_call x10, Pallas kernels, call(): pl.pallas_call(kernel, grid=(steps,), in_specs=[spec(a, how) for a, how i...  227 us
    pallas_call x2, Pallas kernels, share_pooled(): pl.pallas_call(functools.partial(share_kernel, block is not None), in_spe...  62.1 us
    pallas_call x2, Pallas kernels, give_back(): pl.pallas_call(functools.partial(give_back_kernel, half is not None), in_...  55.8 us
    pallas_call x1, Pallas kernels, finish(): pl.pallas_call(finish_kernel, in_specs=[ANY] + [INVMEM] * (len(rows) + 3)...  44.4 us
  transfers between devices with their start and end apart: 5, of which 0 were waited for; matrix products, arithmetic and copies ran while one was open for 4% of the time, Pallas kernels for 72%

profile of v8, /device:TPU:0, one launch (start us, length us, event | category | flops | bytes accessed | tf_op | source)
XLA Modules:
  0.0 437.3 jit_solution(12502435874615518170)
XLA Ops:
  8.2 1.9 concatenate.29
  11.6 1.3 broadcast_in_dim.29.refs_7_
  16.9 4.3 norm_pool.1
  22.7 34.9 %share_pooled.2 = (bf16[4,2,208,384]{3,2,1,0:T(8,128)(2,1)}, bf16[4,2,112,384]{3,2,1,0:T(8,128)(2,1)}, bf16[2,4,96,1152]{3,2,1,0:T(8,128)(2,1)}, f32[2,384]{1,0:...) custom-call(bf16[2,208,384]{2,1,0:T(8,128)(2,1)} %get-tuple-element.96.refs_0_, ...), custom_call_target="tpu_custom_call" | custom-call | flops 30000001024 | tf_op jit(solution)/shard_map/share_pooled/pallas_call | solution.py:881
  57.7 2.6 concatenate.31
  63.5 21.5 %attend.2 = (bf16[2,784,384]{2,1,0:T(8,128)(2,1)}, f32[2,784,128]{2,1,0:T(8,128)}) custom-call(bf16[2,784,384]{2,1,0:T(8,128)(2,1)} %get-tuple-element.94.x_ref.refs_0_, bf16[4,2,208,384]{3,2,1,0:T(8,128)(2,1)} %get-tuple-element.101.own_ref.refs_2_, bf16[4,2,112,384]{3,2,1,0:T(8,128)(2,1)} %get-tuple-element.102.mem_ref.refs_3_, ...), custom_call_target="tpu_custom_call" | custom-call | flops 20000000000 | tf_op jit(solution)/shard_map/attend/pallas_call | solution.py:656
  85.0 13.5 %first_mlp.1 = (f32[2,784,384]{2,1,0:T(8,128)}, f32[2,784,384]{2,1,0:T(8,128)}, bf16[2,208,384]{2,1,0:T(8,128)(2,1)}, bf16[2,112,384]{2,1,0:T(8,128)(2,1)}) custom-call(bf16[2,784,384]{2,1,0:T(8,128)(2,1)} %reshape.172.x_ref, bf16[2,784,384]{2,1,0:T(8,128)(2,1)} %get-tuple-element.104.comb_ref, bf16[2,384,2304]{2,1,0:T(8,128)(2,1)} %bitcast.74, ...), custom_call_target="tpu_custom_call" | custom-call | flops 12999999488 | tf_op jit(solution)/shard_map/first_mlp/pallas_call | solution.py:656
  98.5 27.2 %share_pooled.3 = (bf16[4,2,208,384]{3,2,1,0:T(8,128)(2,1)}, bf16[4,2,112,384]{3,2,1,0:T(8,128)(2,1)}) custom-call(bf16[2,208,384]{2,1,0:T(8,128)(2,1)} %get-tuple-element.108.refs_0_.x_ref, bf16[2,112,384]{2,1,0:T(8,128)(2,1)} %get-tuple-element.109.refs_1_, f32[2,4]{1,0:T(2,128)} %compare_convert_fusion.refs_2_.refs_1_), custom_call_target="tpu_custom_call" | custom-call | flops 20000000000 | tf_op jit(solution)/shard_map/share_pooled/pallas_call | solution.py:881
  125.7 17.8 %attend.3 = (bf16[2,208,768]{2,1,0:T(8,128)(2,1)}, f32[2,208,128]{2,1,0:T(8,128)}) custom-call(bf16[2,208,384]{2,1,0:T(8,128)(2,1)} %get-tuple-element.108.refs_0_.x_ref, bf16[4,2,208,384]{3,2,1,0:T(8,128)(2,1)} %get-tuple-element.110.own_ref.refs_2_, bf16[4,2,112,384]{3,2,1,0:T(8,128)(2,1)} %get-tuple-element.111.mem_ref.refs_3_, ...), custom_call_target="tpu_custom_call" | custom-call | flops 20000000000 | tf_op jit(solution)/shard_map/attend/pallas_call | solution.py:656
  143.5 26.5 %second_mlp.1 = (bf16[416,768]{1,0:T(8,128)(2,1)}, bf16[416,768]{1,0:T(8,128)(2,1)}, f32[416,384]{1,0:T(8,128)}, bf16[2,4,2,192,1536]{4,3,2,1,0:T(8,128)(2,1)}, ...) custom-call(bf16[416,768]{1,0:T(8,128)(2,1)} %bitcast.90, ...), custom_call_target="tpu_custom_call" | custom-call | flops 25999998976 | tf_op jit(solution)/shard_map/second_mlp/pallas_call | solution.py:656
  170.1 34.4 %attend_back.2 = (f32[2,208,384]{2,1,0:T(8,128)}, bf16[4,2,320,384]{3,2,1,0:T(8,128)(2,1)}, bf16[2,384,1152]{2,1,0:T(8,128)(2,1)}, f32[8,768]{1,0:T(8,128)}) custom-call(bf16[2,208,384]{2,1,0:T(8,128)(2,1)} %get-tuple-element.108.refs_0_.x_ref, bf16[2,208,768]{2,1,0:T(8,128)(2,1)} %bitcast.89, bf16[4,2,208,384]{3,2,1,0:T(8,128)(2,1)} %get-tuple-element.110.own_ref.refs_2_, ...), custom_call_target="tpu_custom_call" | custom-call | flops 35999997952 | tf_op jit(solution)/shard_map/attend_back/pallas_call | solution.py:656
  204.5 28.2 %give_back.2 = (f32[2,208,384]{2,1,0:T(8,128)}, f32[2,112,384]{2,1,0:T(8,128)}) custom-call(bf16[4,2,320,384]{3,2,1,0:T(8,128)(2,1)} %get-tuple-element.122.refs_0_, f32[2,4]{1,0:T(2,128)} %compare_convert_fusion.refs_2_.refs_1_), custom_call_target="tpu_custom_call" | custom-call | flops 24999999488 | tf_op jit(solution)/shard_map/give_back/pallas_call | solution.py:1012
  232.7 27.1 %first_back.1 = (f32[2,784,384]{2,1,0:T(8,128)}, bf16[2,784,384]{2,1,0:T(8,128)(2,1)}, bf16[2,384,1792]{2,1,0:T(8,128)(2,1)}, f32[2,1,768]{2,1,0:T(1,128)}, f32[8,384]{1,0:T(8,128)}) custom-call(f32[2,784,384]{2,1,0:T(8,128)} %get-tuple-element.106.middle_ref, f32[2,784,384]{2,1,0:T(8,128)} %get-tuple-element.107.after_ref, ...), custom_call_target="tpu_custom_call" | custom-call | flops 25999998976 | tf_op jit(solution)/shard_map/first_back/pallas_call | solution.py:656
  259.9 1.4 copy-done.2
  261.3 2.9 pad_maximum_fusion
  264.2 71.8 %attend_back.3 = (f32[2,784,384]{2,1,0:T(8,128)}, bf16[4,2,320,384]{3,2,1,0:T(8,128)(2,1)}, bf16[2,384,576]{2,1,0:T(8,128)(2,1)}, f32[8,384]{1,0:T(8,128)}, bf16[384,1536]{1,0:T(8,128)(2,1)}) custom-call(bf16[2,784,384]{2,1,0:T(8,128)(2,1)} %get-tuple-element.94.x_ref.refs_0_, bf16[2,784,384]{2,1,0:T(8,128)(2,1)} %get-tuple-element.125.refs_1_, ...), custom_call_target="tpu_custom_call" | custom-call | flops 35999997952 | tf_op jit(solution)/shard_map/attend_back/pallas_call | solution.py:656
  336.0 27.6 %give_back.3 = (f32[2,208,384]{2,1,0:T(8,128)}, f32[2,112,384]{2,1,0:T(8,128)}, bf16[2,2,208,768]{3,2,1,0:T(8,128)(2,1)}) custom-call(bf16[4,2,320,384]{3,2,1,0:T(8,128)(2,1)} %get-tuple-element.128.refs_0_, f32[2,4]{1,0:T(2,128)} %compare_convert_fusion.refs_2_.refs_1_, bf16[2,208,768]{2,1,0:T(8,128)(2,1)} %bitcast.87), custom_call_target="tpu_custom_call" | custom-call | flops 24999999488 | tf_op jit(solution)/shard_map/give_back/pallas_call | solution.py:1012
  363.6 1.4 slice.51
  365.5 1.5 copy.50
  367.0 5.9 %last_back.1 = (bf16[2,784,384]{2,1,0:T(8,128)(2,1)}, f32[8,384]{1,0:T(8,128)}) custom-call(bf16[2,784,384]{2,1,0:T(8,128)(2,1)} %reshape.172.x_ref, f32[2,784,384]{2,1,0:T(8,128)} %get-tuple-element.131.res_ref, f32[2,784,384]{2,1,0:T(8,128)} %get-tuple-element.132.dx_ref, f32[2,208,384]{2,1,0:T(8,128)} %get-tuple-element.133.own_ref, ...), custom_call_target="tpu_custom_call" | custom-call | flops 6000000000 | tf_op jit(solution)/shard_map/last_back/pallas_call | solution.py:656
  372.9 44.4 %finish.1 = (bf16[2,2,784,384]{3,2,1,0:T(8,128)(2,1)}, f32[40,384]{1,0:T(8,128)}, bf16[96,4736]{1,0:T(8,128)(2,1)}) custom-call(bf16[2,784,384]{2,1,0:T(8,128)(2,1)} %get-tuple-element.135.half_ref, f32[8,384]{1,0:T(8,128)} %get-tuple-element.136.last_ref, f32[8,384]{1,0:T(8,128)} %get-tuple-element.137.qv_a_rows, f32[8,384]{1,0:T(8,128)} %get-tuple-element.138.a_ref, ...), custom_call_target="tpu_custom_call" | custom-call | flops 40000000000 | tf_op jit(solution)/shard_map/finish/pallas_call | solution.py:1153
  417.3 5.6 %reshape.193 = f32[1,4,196,4,384]{4,3,2,1,0:T(4,128)} reshape(bf16[2,2,784,384]{3,2,1,0:T(8,128)(2,1)} %get-tuple-element.148) | data formatting | bytes 7225344 | tf_op jit(solution)/shard_map/transpose | solution.py:1250
  422.9 3.8 write.1
  429.3 1.3 reduce.2
  (78 shorter events, 14.4 us)
Async XLA Ops:
  7.2 5.7 %copy-start = (bf16[1,4,4,49,768]{4,2,3,1,0:T(4,128)(2,1)S(1)}, bf16[1,4,4,49,768]{4,2,3,1,0:T(4,128)(2,1)}, u32[]{:S(2)}) copy-start(bf16[1,4,4,49,768]{4,2,3,1,0:T(4,128)(2,1)} %param.45) | copy-start | bytes 3612676
  7.2 56.3 %all-gather.5.cloned.1.call-start = ((), (), s32[]{:S(2)}) async-start(), calls=%async_computation.6 | async-start | bytes 3981312 | tf_op jit(solution)/shard_map/all_gather | solution.py:1265
  10.1 133.4 %all-gather.7.cloned.1.call-start = ((), (), s32[]{:S(2)}) async-start(), calls=%async_computation.7 | async-start | bytes 13271040 | tf_op jit(solution)/shard_map/all_gather | solution.py:1281
  12.9 1.7 copy-start.4
  15.0 1.2 copy-start.12
  15.0 1.2 copy-start.10
  16.9 4.4 copy-start.13
  16.9 5.1 %copy-start.7 = (bf16[96,3,384]{2,0,1:T(8,128)(2,1)S(1)}, bf16[96,3,384]{2,0,1:T(8,128)(2,1)}, u32[]{:S(2)}) copy-start(bf16[96,3,384]{2,0,1:T(8,128)(2,1)} %param.32) | copy-start | bytes 663556
  22.7 34.9 %copy-start.5 = (bf16[192,1536]{1,0:T(8,128)(2,1)S(1)}, bf16[192,1536]{1,0:T(8,128)(2,1)}, u32[]{:S(2)}) copy-start(bf16[192,1536]{1,0:T(8,128)(2,1)} %param.35) | copy-start | bytes 1769476
  22.7 34.9 %copy-start.6 = (bf16[192,1536]{1,0:T(8,128)(2,1)S(1)}, bf16[192,1536]{1,0:T(8,128)(2,1)}, u32[]{:S(2)}) copy-start(bf16[192,1536]{1,0:T(8,128)(2,1)} %param.36) | copy-start | bytes 1769476
  22.7 34.9 %copy-start.8 = (bf16[192,384]{1,0:T(8,128)(2,1)S(1)}, bf16[192,384]{1,0:T(8,128)(2,1)}, u32[]{:S(2)}) copy-start(bf16[192,384]{1,0:T(8,128)(2,1)} %param.33) | copy-start | bytes 442372
  57.7 2.9 copy-start.9
  57.7 3.0 copy-start.11
  60.3 2.0 copy-start.14
  60.3 2.6 slice-start
  60.3 203.9 %reduce-scatter.4.cloned.1.call-start = ((), (), s32[]{:S(2)}) async-start(), calls=%async_computation.3 | async-start | bytes 10616832 | tf_op jit(solution)/shard_map/reduce_scatter | solution.py:1325
  170.1 202.9 %reduce-scatter.6.cloned.1.call-start = ((), (), s32[]{:S(2)}) async-start(), calls=%async_computation.4 | async-start | bytes 3096576 | tf_op jit(solution)/shard_map/reduce_scatter | solution.py:1325
  232.7 27.2 %copy-start.3 = (bf16[2,4,96,768]{3,2,1,0:T(8,128)(2,1)S(1)}, bf16[2,4,96,768]{3,2,1,0:T(8,128)(2,1)}, u32[]{:S(2)}) copy-start(bf16[2,4,96,768]{3,2,1,0:T(8,128)(2,1)} %get-tuple-element.146) | copy-start | bytes 3538948
  259.8 1.5 copy-start.2
  259.8 113.1 %reduce-scatter.8.cloned.1.call-start = ((), (), s32[]{:S(2)}) async-start(), calls=%async_computation.5 | async-start | bytes 3981312 | tf_op jit(solution)/shard_map/reduce_scatter | solution.py:1325
  422.9 7.7 %copy-start.1 = (bf16[1,4,4,49,768]{4,2,3,1,0:T(4,128)(2,1)S(1)}, bf16[1,4,4,49,768]{4,2,3,1,0:T(4,128)(2,1)}, u32[]{:S(2)}) copy-start(bf16[1,4,4,49,768]{4,2,3,1,0:T(4,128)(2,1)} %param.45) | copy-start | bytes 3612676
Sparse Core Ops, SparseCore 0:
  10.5 45.4 all-gather.4
  60.4 78.1 all-gather.6
  170.2 86.0 reduce-scatter.3
  259.9 44.3 reduce-scatter.5
  308.6 56.6 reduce-scatter.7

commit v9 on v8

--- a/solution.py
+++ b/solution.py
@@ -240,8 +240,7 @@
     return low // 128 * 128, -(-(low + HD) // 128) * 128
 
 
-def head_mask(head):
-    start, stop = window(head)
+def head_mask(head, start, stop):
     lane = lax.broadcasted_iota(jnp.int32, (1, stop - start), 1) + start
     return (lane >= HD * head) & (lane < HD * head + HD)
 
@@ -265,15 +264,15 @@
 
 
 def assemble(w_ref, w_s):
-    wide = w_ref.shape[2] // 4
+    wide = w_ref.shape[2] // 3
     for part in range(3):
         pieces = [w_ref[h, :, wide * part:wide * part + wide].astype(f32) for h in range(w_ref.shape[0])]
         w_s[0, :, 384 * part:384 * part + 384] = jnp.concatenate(pieces, axis=1).astype(bf16)
 
 
 def assemble_out(w_ref, out_s):
-    wide = w_ref.shape[2] // 4
-    pieces = [w_ref[h, :, 3 * wide:].astype(f32) for h in range(w_ref.shape[0])]
+    wide = out_s.shape[1] // w_ref.shape[0]
+    pieces = [w_ref[h, :, :wide].astype(f32) for h in range(w_ref.shape[0])]
     out_s[...] = jnp.concatenate(pieces, axis=1).astype(bf16)
 
 
@@ -323,70 +322,48 @@
     project_queries(x_ref, w_ref, qv_ref, q_s)
     project_keys(own_ref, mem_ref, w_ref, qv_ref, x_s, k_s, v_s)
     factor = HD**-0.5 * math.log2(math.e)
+    stack = s_s.shape[0] // nq
     lanes = lax.broadcasted_iota(jnp.int32, (chunk, 128), 1)
     for tile in range(width // 384):
         group = slice(384 * tile, 384 * tile + 384)
         base = q_s[:, group].astype(f32)
         parts = [base[:, :128], base[:, 128:256], base[:, 256:384]]
-        for head in range(4 * tile, 4 * tile + 4):
-            start, stop = window(head)
-            mask = head_mask(head)
-            query = jnp.where(mask, q_s[:, start:stop], jnp.zeros((), bf16))
+        for first in range(4 * tile, 4 * tile + 4, stack):
+            start, stop = window(first)[0], window(first + stack - 1)[1]
+            masks = [head_mask(first + k, start, stop) for k in range(stack)]
+            base = q_s[:, start:stop]
+            query = jnp.concatenate([jnp.where(mask, base, jnp.zeros((), bf16)) for mask in masks], axis=0)
             s_s[...] = dot(query, k_s[:, start:stop], NT)
 
-            def body(i, carry, head=head):
+            def body(i, carry, k):
                 rows = pl.ds(pl.multiple_of(i * chunk, chunk), chunk)
-                score = s_s[rows, :] * factor + columns
+                here = pl.ds(pl.multiple_of(k * nq + i * chunk, chunk), chunk)
+                score = s_s[here, :] * factor + columns
                 top = jnp.max(score, axis=1, keepdims=True)
                 power = jnp.exp2(score - top)
                 total = jnp.sum(power, axis=1, keepdims=True)
-                p_s[rows, :] = (power * (1.0 / total)).astype(bf16)
-                lse_ref[0, rows, :] = jnp.where(lanes == head, top + jnp.log2(total), lse_ref[0, rows, :])
+                p_s[here, :] = (power * (1.0 / total)).astype(bf16)
+                lse_ref[0, rows, :] = jnp.where(lanes == first + k, top + jnp.log2(total), lse_ref[0, rows, :])
                 return carry
 
-            lax.fori_loop(0, nq // chunk, body, 0, unroll=nq // chunk)
-            out = jnp.where(mask, dot(p_s[...], v_s[:, start:stop]), 0.0)
-            for w in range((stop - start) // 128):
-                k = start // 128 - 3 * tile + w
-                parts[k] = parts[k] + out[:, 128 * w:128 * w + 128]
+            for k in range(stack):
+                lax.fori_loop(0, nq // chunk, functools.partial(body, k=k), 0, unroll=nq // chunk)
+            both = dot(p_s[...], v_s[:, start:stop])
+            for k, mask in enumerate(masks):
+                out = jnp.where(mask, both[k * nq:(k + 1) * nq], 0.0)
+                for w in range((stop - start) // 128):
+                    n = start // 128 - 3 * tile + w
+                    parts[n] = parts[n] + out[:, 128 * w:128 * w + 128]
         out_ref[0, :, group] = jnp.concatenate(parts, axis=1).astype(bf16)
 
 
-def attend_back_kernel(chunk, valid, hosted, *refs):
-    if hosted:
-        *refs, copy_sem = refs
-        refs, shard_ref, refs_out, sum_ref, scratch, chain = refs[:8], refs[8], refs[9:13], refs[13], refs[14:26], refs[26:]
-        refs = (*refs, *refs_out, *scratch)
-        each = shard_ref.shape[0] // hosted
-        chain = Chain(*chain[:3], [(pl.ds(each * n, each), slice(None)) for n in range(hosted)], *chain[3:])
-    (x_ref, g_ref, own_ref, mem_ref, w_ref, qv_ref, has_ref, lse_ref, dx_ref, dpool_ref, gw_ref, row_ref,
-     w_s, x_s, q_s, k_s, v_s, s_s, dp_s, p_s, ds_s, dk_s, dv_s, gw_s) = refs
+def attend_back_kernel(
+    chunk, valid, x_ref, g_ref, own_ref, mem_ref, w_ref, qv_ref, has_ref, lse_ref,
+    dx_ref, dpool_ref, gw_ref, row_ref,
+    w_s, x_s, q_s, k_s, v_s, s_s, dp_s, p_s, ds_s, dk_s, dv_s, gw_s,
+):
     nq, width = q_s.shape
     step = pl.program_id(0)
-    if hosted:
-        @pl.when(step == 0)
-        def _():
-            chain.greet()
-            load = pltpu.make_async_copy(shard_ref, chain.part, copy_sem.at[0])
-            load.start()
-            load.wait()
-            for n in range(hosted):
-                chain.send_ends(n)
-
-    def progress(head):
-        if hosted:
-            half = -(-hosted // 3)
-
-            @pl.when(step == 0)
-            def _():
-                for n in range(max(half * (head - 1), 0), min(half * head, hosted)):
-                    chain.send_parts(n)
-
-            @pl.when(step == 1)
-            def _():
-                for n in range(half * head, min(half * head + half, hosted)):
-                    chain.middle_totals(n)
-
     columns = key_mask(own_ref, mem_ref, valid, has_ref[step])
     if width == 384:
         @pl.when(step == 0)
@@ -397,6 +374,7 @@
     project_keys(own_ref, mem_ref, w_ref, qv_ref, x_s, k_s, v_s)
     scaling = HD**-0.5
     factor = scaling * math.log2(math.e)
+    stack = s_s.shape[0] // nq
     lanes = lax.broadcasted_iota(jnp.int32, (chunk, 128), 1)
 
     @pl.when(step == 0)
@@ -413,34 +391,39 @@
         qt = transposed(q_s[:, group])
         gt = transposed(g_ref[0, :, group])
         parts = [None] * 3
-        for head in range(4 * tile, 4 * tile + 4):
-            start, stop = window(head)
-            mask = head_mask(head)
-            query = jnp.where(mask, q_s[:, start:stop], jnp.zeros((), bf16))
-            grad = jnp.where(mask, g_ref[0, :, start:stop], jnp.zeros((), bf16))
+        for first in range(4 * tile, 4 * tile + 4, stack):
+            start, stop = window(first)[0], window(first + stack - 1)[1]
+            masks = [head_mask(first + k, start, stop) for k in range(stack)]
+            zero = jnp.zeros((), bf16)
+            query = jnp.concatenate([jnp.where(mask, q_s[:, start:stop], zero) for mask in masks], axis=0)
+            grad = jnp.concatenate([jnp.where(mask, g_ref[0, :, start:stop], zero) for mask in masks], axis=0)
             s_s[...] = dot(query, k_s[:, start:stop], NT)
             dp_s[...] = dot(grad, v_s[:, start:stop], NT)
 
-            def body(i, carry, head=head):
+            def body(i, carry, k):
                 rows = pl.ds(pl.multiple_of(i * chunk, chunk), chunk)
-                lse = jnp.sum(jnp.where(lanes == head, lse_ref[0, rows, :], 0.0), axis=1, keepdims=True)
-                p = jnp.exp2(s_s[rows, :] * factor + columns - lse)
-                dp = dp_s[rows, :]
+                here = pl.ds(pl.multiple_of(k * nq + i * chunk, chunk), chunk)
+                lse = jnp.sum(jnp.where(lanes == first + k, lse_ref[0, rows, :], 0.0), axis=1, keepdims=True)
+                p = jnp.exp2(s_s[here, :] * factor + columns - lse)
+                dp = dp_s[here, :]
                 inner = jnp.sum(p * dp, axis=1, keepdims=True)
-                p_s[rows, :] = p.astype(bf16)
-                ds_s[rows, :] = (p * (dp - inner)).astype(bf16)
+                p_s[here, :] = p.astype(bf16)
+                ds_s[here, :] = (p * (dp - inner)).astype(bf16)
                 return carry
 
-            lax.fori_loop(0, nq // chunk, body, 0, unroll=nq // chunk)
-            r = slice(HD * (head - 4 * tile), HD * (head - 4 * tile) + HD)
-            dv_s[r, :] = dot(gt[r], p_s[...])
-            dk_s[r, :] = dot(qt[r], ds_s[...]) * scaling
-            dq = jnp.where(mask, dot(ds_s[...], k_s[:, start:stop]) * scaling, 0.0)
-            for w in range((stop - start) // 128):
-                k = start // 128 - 3 * tile + w
-                part = dq[:, 128 * w:128 * w + 128]
-                parts[k] = part if parts[k] is None else parts[k] + part
-            progress(head)
+            for k in range(stack):
+                lax.fori_loop(0, nq // chunk, functools.partial(body, k=k), 0, unroll=nq // chunk)
+            dq_both = dot(ds_s[...], k_s[:, start:stop]) * scaling
+            for k, mask in enumerate(masks):
+                mine = slice(k * nq, (k + 1) * nq)
+                r = slice(HD * (first + k - 4 * tile), HD * (first + k - 4 * tile) + HD)
+                dv_s[r, :] = dot(gt[r], p_s[mine, :])
+                dk_s[r, :] = dot(qt[r], ds_s[mine, :]) * scaling
+                dq = jnp.where(mask, dq_both[mine], 0.0)
+                for w in range((stop - start) // 128):
+                    n = start // 128 - 3 * tile + w
+                    part = dq[:, 128 * w:128 * w + 128]
+                    parts[n] = part if parts[n] is None else parts[n] + part
         total = jnp.concatenate(parts, axis=1) + g_ref[0, :, group].astype(f32)
         row_q.append(sum_rows(total))
         low = total.astype(bf16)
@@ -469,13 +452,6 @@
     def _():
         for h in range(gw_ref.shape[0]):
             write_shares(gw_ref, h, gw_s)
-        if hosted:
-            for n in range(hosted):
-                chain.other_totals(n)
-            chain.close()
-            store = pltpu.make_async_copy(chain.from_inner, sum_ref, copy_sem.at[0])
-            store.start()
-            store.wait()
 
 
 def first_mlp_kernel(x_ref, comb_ref, out_ref, up_ref, down_ref, ub_ref, vec_ref, pool_ref, pair_ref,
@@ -666,6 +642,10 @@
     )(*[a for a, _ in args])
 
 
+def stacked(nq):
+    return 2 if nq < 512 else 1
+
+
 def chunk_of(nq):
     return 112 if nq % 112 == 0 else 16
 
@@ -678,41 +658,37 @@
         [(x, 0), (own, 1), (mem, 1), w, (qv, None), (has, pl.BlockSpec(memory_space=pltpu.SMEM))],
         [(shape((batches, nq, width), bf16), 0), (shape((batches, nq, 128), f32), 0)],
         [((1, d, 1152 if width == 384 else 128), bf16),
-         ((keys, d), bf16), ((nq, width), bf16), ((keys, width), bf16), ((keys, width), bf16), ((nq, keys), f32), ((nq, keys), bf16)],
+         ((keys, d), bf16), ((nq, width), bf16), ((keys, width), bf16), ((keys, width), bf16),
+         ((stacked(nq) * nq, keys), f32), ((stacked(nq) * nq, keys), bf16)],
         name="attend", us=20,
     )
 
 
-def attend_back(x, grad, own, mem, w, qv, has, valid, lse, heads, shard=None, number=None):
+def attend_back(x, grad, own, mem, w, qv, has, valid, lse, heads):
     batches, nq, d = x.shape
     width = grad.shape[2]
     keys = own.shape[0] * own.shape[2] + mem.shape[0] * mem.shape[2]
     both = (own.shape[0], batches, own.shape[2] + mem.shape[2], d)
     groups = (width // 384, d, 1152)
-    args = [(x, 0), (grad, 0), (own, 1), (mem, 1), w, (qv, None), (has, INSMEM), (lse, 0)]
-    outs = [(shape((batches, nq, d), f32), 0), (shape(both, bf16), 1), (shape((heads, d, 3 * width // heads), bf16), None), (shape((8, width), f32), None)]
-    scratch = [
-        ((1, d, 1152 if width == 384 else 128), bf16),
-        ((keys, d), bf16), ((nq, width), bf16), ((keys, width), bf16), ((keys, width), bf16),
-        ((nq, keys), f32), ((nq, keys), f32), ((nq, keys), bf16), ((nq, keys), bf16),
-        ((384, keys), f32), ((384, keys), f32), (groups, f32),
-    ]
-    pieces = 0
-    if shard is not None:
-        pieces = shard.shape[0] // 48
-        args, outs = args + [(shard, ANY)], outs + [(shape(shard.shape, bf16), ANY)]
-        scratch += chain_scratch(shard.shape, pieces) + [dma(1)]
+    rows = stacked(nq) * nq
     return call(
-        functools.partial(attend_back_kernel, chunk_of(nq), valid, pieces), batches, args, outs, scratch,
-        name="attend_back", us=36, number=number,
+        functools.partial(attend_back_kernel, chunk_of(nq), valid), batches,
+        [(x, 0), (grad, 0), (own, 1), (mem, 1), w, (qv, None), (has, INSMEM), (lse, 0)],
+        [(shape((batches, nq, d), f32), 0), (shape(both, bf16), 1), (shape((heads, d, 3 * width // heads), bf16), None), (shape((8, width), f32), None)],
+        [((1, d, 1152 if width == 384 else 128), bf16),
+         ((keys, d), bf16), ((nq, width), bf16), ((keys, width), bf16), ((keys, width), bf16),
+         ((rows, keys), f32), ((rows, keys), f32), ((rows, keys), bf16), ((rows, keys), bf16),
+         ((384, keys), f32), ((384, keys), f32), (groups, f32)],
+        name="attend_back", us=36,
     )
 
 
-def share_kernel(gather, *refs):
+def share_kernel(gather, count, *refs):
     if gather:
         pooled_ref, mean_ref, pick_ref, w_ref, *refs = refs
-        biases, (own_ref, mem_ref, all_ref, *refs) = refs[:4], refs[4:]
-        (qv_a_ref, qv_b_ref, ub_a_ref, ub_b_ref), refs = refs[:4], refs[4:]
+        biases, (own_ref, mem_ref, all_ref, *refs) = refs[:count], refs[count:]
+        if count:
+            (qv_a_ref, qv_b_ref, ub_a_ref, ub_b_ref), refs = refs[:4], refs[4:]
     else:
         pooled_ref, mean_ref, pick_ref, own_ref, mem_ref, *refs = refs
     (got_s, pick_s, local_sem, own_send, own_recv, mem_send, mem_recv, pass_send, pass_recv, clip_send, clip_recv, *refs) = refs
@@ -826,6 +802,7 @@
             copy.wait_recv()
         for copy in bias_copies:
             copy.wait_recv()
+    if count:
         by_head = []
         for ref, got in zip(biases, bias_got):
             pieces = []
@@ -837,9 +814,10 @@
             by_head.append(pieces)
         qv_a_ref[...] = jnp.concatenate(by_head[0], axis=1)
         qv_b_ref[...] = jnp.concatenate(by_head[1], axis=1)
+        fa = ub_a_ref.shape[2]
         for h in range(heads):
-            ub_a_ref[h] = by_head[2][h]
-        ub_b_ref[...] = jnp.concatenate(by_head[3], axis=1)
+            ub_a_ref[h] = by_head[2][h][:, :fa]
+        ub_b_ref[...] = jnp.concatenate([piece[:, fa:] for piece in by_head[2]], axis=1)
         for copy in bias_copies:
             copy.wait_send()
     own_copies[0].wait_recv()
@@ -859,7 +837,7 @@
             copy.wait_send()
 
 
-def share_pooled(pooled, mean, pick, number, block=None, biases=()):
+def share_pooled(pooled, mean, pick, number, block=None, biases=(), fa=0):
     toks, heads = lax.axis_size("tok"), lax.axis_size("head")
     chips = toks // 2
     few = max(chips - 1, 1)
@@ -871,15 +849,16 @@
     ]
     if block is not None:
         args, specs = args + [block, *biases], specs + [ANY] + [INVMEM] * len(biases)
-        (_, wa), (_, wb), (_, fa), (_, fb) = (b.shape for b in biases)
         outs = outs + [shape((heads, toks) + block.shape, bf16)]
-        outs += [shape(dims, f32) for dims in ((2, heads * wa), (2, heads * wb), (heads, 1, fa), (1, heads * fb))]
+        if biases:
+            (_, wa), (_, wb), (_, wide) = (b.shape for b in biases)
+            outs += [shape(dims, f32) for dims in ((2, heads * wa), (2, heads * wb), (heads, 1, fa), (1, heads * (wide - fa)))]
         firsts = max(chips + heads - 2, 1)
         scratch += [dma(1), dma(firsts), dma(firsts), dma(few, max(heads - 1, 1)), dma(few, max(heads - 1, 1)), dma(chips, heads), dma(chips, heads)]
-        scratch += [dma(max(heads - 1, 1), 4), dma(max(heads - 1, 1), 4)]
+        scratch += [dma(max(heads - 1, 1), max(len(biases), 1)), dma(max(heads - 1, 1), max(len(biases), 1))]
         scratch += [pltpu.VMEM((max(heads - 1, 1),) + b.shape, f32) for b in biases]
     return pl.pallas_call(
-        functools.partial(share_kernel, block is not None),
+        functools.partial(share_kernel, block is not None, len(biases)),
         in_specs=specs,
         out_specs=[ANY] * min(len(outs), 3) + [INVMEM] * (len(outs) - 3),
         out_shape=outs,
@@ -1221,6 +1200,26 @@
     down_b_ref[...] = mlp_ref[up_b_ref.shape[0]:, :].astype(f32)
 
 
+def reduce_clips(shard):
+    clips, clip = lax.axis_size("clip"), lax.axis_index("clip")
+    pieces = shard.reshape(clips, -1, shard.shape[-1])
+    total = lax.dynamic_index_in_dim(pieces, clip, 0, keepdims=False).astype(f32)
+    for k in range(1, clips):
+        give = lax.dynamic_index_in_dim(pieces, (clip + k) % clips, 0, keepdims=False)
+        total = total + lax.ppermute(give, "clip", [(i, (i + k) % clips) for i in range(clips)]).astype(f32)
+    return total.astype(bf16)
+
+
+def spread_clips(piece):
+    clips, clip = lax.axis_size("clip"), lax.axis_index("clip")
+    out = jnp.zeros((clips,) + piece.shape, piece.dtype)
+    out = lax.dynamic_update_index_in_dim(out, piece, clip, 0)
+    for k in range(1, clips):
+        got = lax.ppermute(piece, "clip", [(i, (i + k) % clips) for i in range(clips)])
+        out = lax.dynamic_update_index_in_dim(out, got, (clip - k + clips) % clips, 0)
+    return out.reshape((-1,) + piece.shape[1:])
+
+
 def padded_rows(*rows):
     return jnp.concatenate([jnp.stack(rows), jnp.zeros((-len(rows) % 8, rows[0].shape[0]), f32)])
 
@@ -1261,7 +1260,8 @@
     group = ("head", "tok")
     fa, ha = w_up_a.shape[1], w_out_a.shape[1]
     fb, hb, hs = w_up_b.shape[1], w_out_b.shape[1], w_skip_b.shape[1]
-    pack_a = jnp.concatenate([w_up_a, w_down_a, *w_qkv_a.transpose(1, 0, 2), w_out_a], axis=1)
+    spare_a = jnp.zeros((w_out_a.shape[0], -w_out_a.shape[1] % 256), bf16)
+    pack_a = jnp.concatenate([w_up_a, w_down_a, w_out_a, spare_a], axis=1)
     all_a = lax.all_gather(pack_a, group).reshape(heads, d1, -1)
     stream = by_patch(lax.dynamic_slice_in_dim(clips_in[0], first, share, 0))
     low1, pooled1, mean1 = call(
@@ -1270,23 +1270,24 @@
         [(shape((share, tokens, d1), bf16), 0), (shape((share, own_rows, d1), bf16), 0), (shape((share, mem_rows, d1), bf16), 0)],
         name="norm_pool", us=5,
     )
-    pooled1, w_qkv_b, w_up_b = lax.optimization_barrier((pooled1, w_qkv_b, w_up_b))
+    pack_w = jnp.concatenate([*w_qkv_a.transpose(1, 0, 2)], axis=1)
+    own1, mem1, all_w, qv_a, qv_b, ub_a, ub_b = share_pooled(
+        pooled1, mean1, pick, 0, pack_w, [qv_bias_a, qv_bias_b, jnp.concatenate([up_bias_a, up_bias_b])[None]], fa)
+    all_w = all_w.reshape(heads, d1, -1)
     pack_q = jnp.concatenate([*w_qkv_b.transpose(1, 0, 2)], axis=1)
-    own1, mem1, all_q, qv_a, qv_b, ub_a, ub_b = share_pooled(
-        pooled1, mean1, pick, 0, pack_q, [qv_bias_a, qv_bias_b, up_bias_a[None], up_bias_b[None]])
-    all_q = all_q.reshape(heads, d1, -1)
     own1, w_up_b, cot = lax.optimization_barrier((own1, w_up_b, cot))
     spare = jnp.zeros((w_up_b.shape[0], -(2 * fb + hb + hs) % hb), bf16)
     pack_b = jnp.concatenate([w_up_b, w_down_b, w_out_b, w_skip_b, spare], axis=1)
     all_b = lax.all_gather(pack_b, group).reshape(heads, d2, -1)
     cot = jnp.pad(cot, ((0, 0), (0, own_rows - pooled_tokens), (0, 0))).reshape(rows2, d2)
 
-    up_spec, down_spec, rest_spec = (pl.BlockSpec((heads, d1, fa), lambda i, n=n: (0, 0, n)) for n in range(3))
-
-    comb1, lse1 = attend(low1, own1, mem1, (all_a, rest_spec), qv_a, has, valid, d1)
+    up_spec, down_spec = (pl.BlockSpec((heads, d1, fa), lambda i, n=n: (0, 0, n)) for n in range(2))
+    out_a_spec = pl.BlockSpec((heads, d1, 256), lambda i: (0, 0, 2 * fa // 256))
+
+    comb1, lse1 = attend(low1, own1, mem1, (all_w, None), qv_a, has, valid, d1)
     after1, middle, pooled3, mean3 = call(
         first_mlp_kernel, share,
-        [(stream, 0), (comb1, 0), (all_a, rest_spec), (all_a, up_spec), (all_a, down_spec), (ub_a, None),
+        [(stream, 0), (comb1, 0), (all_a, out_a_spec), (all_a, up_spec), (all_a, down_spec), (ub_a, None),
          (padded_rows(shifts_a[1], gains_a[1], shifts_a[2], shifts_a[3], gains_a[2], shifts_a[4]), None),
          (pooling, None), (pairing, None)],
         [(shape((share, tokens, d1), f32), 0), (shape((share, tokens, d1), f32), 0),
@@ -1295,7 +1296,8 @@
         name="first_mlp", us=13,
     )
 
-    own2, mem2 = share_pooled(pooled3, mean3, pick, 1)
+    own2, mem2, all_q = share_pooled(pooled3, mean3, pick, 1, pack_q)
+    all_q = all_q.reshape(heads, d1, -1)
     comb2, lse2 = attend(pooled3, own2, mem2, (all_q, None), qv_b, has, valid, d2)
     chunk = 768
     per_head = fb // chunk
@@ -1336,7 +1338,7 @@
     res1, dcomb1, g_mlp_a, g_ub_a, rows_a = call(
         first_back_kernel, share,
         [(middle, 0), (after1, 0), (comb1, 0), (dskip.reshape(share, own_rows, d1), 0), (dq2, 0), (own_back2, 0), (mem_back2, 0),
-         (all_a, rest_spec), (all_a, up_spec), (all_a, down_spec), (ub_a, None),
+         (all_a, out_a_spec), (all_a, up_spec), (all_a, down_spec), (ub_a, None),
          (padded_rows(gains_a[1], shifts_a[2], gains_a[2]), None), (unpooling, None), (unpairing, None)],
         [(shape((share, tokens, d1), f32), 0), (shape((share, tokens, d1), bf16), 0),
          (shape((heads, d1, -(-(2 * fa + ha) // 256) * 256), bf16), None),
@@ -1345,13 +1347,12 @@
         name="first_back", us=26,
     )
     rest_a = by_owner(g_mlp_a)
+    dcomb1, sum_mlp_b, rest_a = lax.optimization_barrier((dcomb1, sum_mlp_b, rest_a))
     sum_rest_a = scatter(rest_a)
-    args = (low1, dcomb1, own1, mem1, (all_a, rest_spec), qv_a, has, valid, lse1, heads)
-    if toks * (own_rows + mem_rows) <= 1536:
-        dx1, dpool1, g_qkv_a, rows_qv_a, sum_mlp_b = attend_back(*args, sum_mlp_b, 5)
-    else:
-        dx1, dpool1, g_qkv_a, rows_qv_a = attend_back(*args)
-        sum_mlp_b = lax.psum(sum_mlp_b, "clip")
+    sum_mlp_b = reduce_clips(sum_mlp_b)
+    dx1, dpool1, g_qkv_a, rows_qv_a = attend_back(low1, dcomb1, own1, mem1, (all_w, None), qv_a, has, valid, lse1, heads)
+    dpool1, sum_mlp_b = lax.optimization_barrier((dpool1, sum_mlp_b))
+    sum_mlp_b = spread_clips(sum_mlp_b)
     own_back1, mem_back1, mixed_all = give_back(dpool1, pick, own_rows, 3, mixed.reshape(share, own_rows, d2))
     stream_grad, rows_last = call(
         last_back_kernel, share,

time: 442 us -> 430 us (0.973)
  Pallas kernels: 389 us -> 358 us
  starting transfers between devices: 0.38 us -> 9.65 us
  waiting for transfers between devices: 0.12 us -> 8.85 us
    pallas_call x10, Pallas kernels: 227 us -> 189 us  [call(): pl.pallas_call(kernel, grid=(steps,), in_specs=[spec(a, how) for a, how i...]
    ppermute x0 -> x6, starting transfers between devices: none -> 9.27 us  [the longest x3 4.78 us: spread_clips(): lax.ppermute(piece, 'clip', [(i, (i + k) % clips) for i in range(clips)])]
    reduce_scatter x3, waiting for transfers between devices: 0.04 us -> 8.75 us  [scatter(): return lax.psum_scatter(grad, group, scatter_dimension=0, tiled=False)]
    pallas_call x2, Pallas kernels: 62.1 us -> 67.2 us  [share_pooled(): pl.pallas_call(functools.partial(share_kernel, block is not None, len(bia...]
  transfers between devices with their start and end apart: 5 -> 11, of which waited for: 0 -> 1; matrix products, arithmetic and copies ran while one was open for 4% -> 6% of each run, Pallas kernels for 72% -> 66%
where the time goes in v9:
time: 430 us; the launch traced here: 426 us
  Pallas kernels  358 us (83%)
  local copies, waits for them, and re-layouts  23.5 us (5%)
  between operations  14.6 us (3%)
  other arithmetic  12.3 us (3%)
  starting transfers between devices  9.65 us (2%)
  waiting for transfers between devices  8.85 us (2%)
    pallas_call x10, Pallas kernels, call(): pl.pallas_call(kernel, grid=(steps,), in_specs=[spec(a, how) for a, how i...  189 us
    pallas_call x2, Pallas kernels, share_pooled(): pl.pallas_call(functools.partial(share_kernel, block is not None, len(bia...  67.2 us
    pallas_call x2, Pallas kernels, give_back(): pl.pallas_call(functools.partial(give_back_kernel, half is not None), in_...  55.1 us
    pallas_call x1, Pallas kernels, finish(): pl.pallas_call(finish_kernel, in_specs=[ANY] + [INVMEM] * (len(rows) + 3)...  46 us
    reduce_scatter x3, waiting for transfers between devices, scatter(): return lax.psum_scatter(grad, group, scatter_dimension=0, tiled=False)  8.75 us
  transfers between devices with their start and end apart: 11, of which 1 were waited for; matrix products, arithmetic and copies ran while one was open for 6% of the time, Pallas kernels for 66%

profile of v9, /device:TPU:0, one launch (start us, length us, event | category | flops | bytes accessed | tf_op | source)
XLA Modules:
  0.0 426.4 jit_solution(1883858813276373772)
XLA Ops:
  7.3 1.9 concatenate.36
  9.3 1.7 dynamic-slice_bitcast_fusion
  16.4 4.3 %norm_pool.1 = (bf16[2,784,384]{2,1,0:T(8,128)(2,1)}, bf16[2,208,384]{2,1,0:T(8,128)(2,1)}, bf16[2,112,384]{2,1,0:T(8,128)(2,1)}) custom-call(bf16[2,784,384]{2,1,0:T(8,128)(2,1)} %reshape.183.x_ref, f32[8,384]{1,0:T(8,128)} %get-tuple-element.228.vec_ref, bf16[208,784]{1,0:T(8,128)(2,1)} %constant.126.clone.pool_ref, bf16[112,208]{1,0:T(8,128)(2,1)} %constant.127.clone.pair_ref), custom_call_target="tpu_custom_call" | custom-call | flops 5000000000 | tf_op jit(solution)/shard_map/norm_pool/pallas_call | solution.py:632
  20.8 29.9 %share_pooled.2 = (bf16[4,2,208,384]{3,2,1,0:T(8,128)(2,1)}, bf16[4,2,112,384]{3,2,1,0:T(8,128)(2,1)}, bf16[2,4,96,576]{3,2,1,0:T(8,128)(2,1)}, f32[2,384]{1,0:T...) custom-call(bf16[2,208,384]{2,1,0:T(8,128)(2,1)} %get-tuple-element.97.refs_0_, ...), custom_call_target="tpu_custom_call" | custom-call | flops 30000001024 | tf_op jit(solution)/shard_map/share_pooled/pallas_call | solution.py:860
  50.7 1.8 concatenate.39
  57.3 21.8 %attend.2 = (bf16[2,784,384]{2,1,0:T(8,128)(2,1)}, f32[2,784,128]{2,1,0:T(8,128)}) custom-call(bf16[2,784,384]{2,1,0:T(8,128)(2,1)} %get-tuple-element.96.x_ref, bf16[4,2,208,384]{3,2,1,0:T(8,128)(2,1)} %get-tuple-element.100.own_ref, bf16[4,2,112,384]{3,2,1,0:T(8,128)(2,1)} %get-tuple-element.101.mem_ref, bf16[2,384,576]{2,1,0:T(8,128)(2,1)} %bitcast.106, ...), custom_call_target="tpu_custom_call" | custom-call | flops 20000000000 | tf_op jit(solution)/shard_map/attend/pallas_call | solution.py:632
  79.1 13.2 %first_mlp.1 = (f32[2,784,384]{2,1,0:T(8,128)}, f32[2,784,384]{2,1,0:T(8,128)}, bf16[2,208,384]{2,1,0:T(8,128)(2,1)}, bf16[2,112,384]{2,1,0:T(8,128)(2,1)}) custom-call(bf16[2,784,384]{2,1,0:T(8,128)(2,1)} %reshape.183.x_ref, bf16[2,784,384]{2,1,0:T(8,128)(2,1)} %get-tuple-element.104.comb_ref, bf16[2,384,1792]{2,1,0:T(8,128)(2,1)} %bitcast.96, ...), custom_call_target="tpu_custom_call" | custom-call | flops 12999999488 | tf_op jit(solution)/shard_map/first_mlp/pallas_call | solution.py:632
  92.3 37.3 %share_pooled.3 = (bf16[4,2,208,384]{3,2,1,0:T(8,128)(2,1)}, bf16[4,2,112,384]{3,2,1,0:T(8,128)(2,1)}, bf16[2,4,96,1152]{3,2,1,0:T(8,128)(2,1)}) custom-call(bf16[2,208,384]{2,1,0:T(8,128)(2,1)} %get-tuple-element.108.refs_0_.x_ref, bf16[2,112,384]{2,1,0:T(8,128)(2,1)} %get-tuple-element.109.refs_1_, f32[2,4]{1,0:T(2,128)} %compare_convert_fusion.refs_2_.refs_1_, ...), custom_call_target="tpu_custom_call" | custom-call | flops 30000001024 | tf_op jit(solution)/shard_map/share_pooled/pallas_call | solution.py:860
  129.6 16.2 %attend.3 = (bf16[2,208,768]{2,1,0:T(8,128)(2,1)}, f32[2,208,128]{2,1,0:T(8,128)}) custom-call(bf16[2,208,384]{2,1,0:T(8,128)(2,1)} %get-tuple-element.108.refs_0_.x_ref, bf16[4,2,208,384]{3,2,1,0:T(8,128)(2,1)} %get-tuple-element.110.own_ref, bf16[4,2,112,384]{3,2,1,0:T(8,128)(2,1)} %get-tuple-element.111.mem_ref, bf16[2,384,1152]{2,1,0:T(8,128)(2,1)} %bitcast.104, ...), custom_call_target="tpu_custom_call" | custom-call | flops 20000000000 | tf_op jit(solution)/shard_map/attend/pallas_call | solution.py:632
  145.8 26.5 %second_mlp.1 = (bf16[416,768]{1,0:T(8,128)(2,1)}, bf16[416,768]{1,0:T(8,128)(2,1)}, f32[416,384]{1,0:T(8,128)}, bf16[2,4,2,192,1536]{4,3,2,1,0:T(8,128)(2,1)}, ...) custom-call(bf16[416,768]{1,0:T(8,128)(2,1)} %bitcast.112, ...), custom_call_target="tpu_custom_call" | custom-call | flops 25999998976 | tf_op jit(solution)/shard_map/second_mlp/pallas_call | solution.py:632
  172.5 33.4 %attend_back.2 = (f32[2,208,384]{2,1,0:T(8,128)}, bf16[4,2,320,384]{3,2,1,0:T(8,128)(2,1)}, bf16[2,384,1152]{2,1,0:T(8,128)(2,1)}, f32[8,768]{1,0:T(8,128)}) custom-call(bf16[2,208,384]{2,1,0:T(8,128)(2,1)} %get-tuple-element.108.refs_0_.x_ref, bf16[2,208,768]{2,1,0:T(8,128)(2,1)} %bitcast.111, bf16[4,2,208,384]{3,2,1,0:T(8,128)(2,1)} %get-tuple-element.110.own_ref, ...), custom_call_target="tpu_custom_call" | custom-call | flops 35999997952 | tf_op jit(solution)/shard_map/attend_back/pallas_call | solution.py:632
  206.0 3.1 pad_maximum_fusion
  209.1 28.1 %give_back.2 = (f32[2,208,384]{2,1,0:T(8,128)}, f32[2,112,384]{2,1,0:T(8,128)}) custom-call(bf16[4,2,320,384]{3,2,1,0:T(8,128)(2,1)} %get-tuple-element.122.refs_0_, f32[2,4]{1,0:T(2,128)} %compare_convert_fusion.refs_2_.refs_1_), custom_call_target="tpu_custom_call" | custom-call | flops 24999999488 | tf_op jit(solution)/shard_map/give_back/pallas_call | solution.py:991
  237.2 26.7 %first_back.1 = (f32[2,784,384]{2,1,0:T(8,128)}, bf16[2,784,384]{2,1,0:T(8,128)(2,1)}, bf16[2,384,1792]{2,1,0:T(8,128)(2,1)}, f32[2,1,768]{2,1,0:T(1,128)}, f32[8,384]{1,0:T(8,128)}) custom-call(f32[2,784,384]{2,1,0:T(8,128)} %get-tuple-element.106.middle_ref, f32[2,784,384]{2,1,0:T(8,128)} %get-tuple-element.107.after_ref, ...), custom_call_target="tpu_custom_call" | custom-call | flops 25999998976 | tf_op jit(solution)/shard_map/first_back/pallas_call | solution.py:632
  265.1 3.4 collective-permute-start.2
  269.6 37.4 %attend_back.3 = (f32[2,784,384]{2,1,0:T(8,128)}, bf16[4,2,320,384]{3,2,1,0:T(8,128)(2,1)}, bf16[2,384,576]{2,1,0:T(8,128)(2,1)}, f32[8,384]{1,0:T(8,128)}) custom-call(bf16[2,784,384]{2,1,0:T(8,128)(2,1)} %get-tuple-element.96.x_ref, bf16[2,784,384]{2,1,0:T(8,128)(2,1)} %get-tuple-element.128.g_ref, bf16[4,2,208,384]{3,2,1,0:T(8,128)(2,1)} %get-tuple-element.100.own_ref, ...), custom_call_target="tpu_custom_call" | custom-call | flops 35999997952 | tf_op jit(solution)/shard_map/attend_back/pallas_call | solution.py:632
  308.3 2.3 collective-permute-start.3
  311.5 1.5 collective-permute-start.5
  313.0 27.1 %give_back.3 = (f32[2,208,384]{2,1,0:T(8,128)}, f32[2,112,384]{2,1,0:T(8,128)}, bf16[2,2,208,768]{3,2,1,0:T(8,128)(2,1)}) custom-call(bf16[4,2,320,384]{3,2,1,0:T(8,128)(2,1)} %get-tuple-element.132.refs_0_, f32[2,4]{1,0:T(2,128)} %compare_convert_fusion.refs_2_.refs_1_, bf16[2,208,768]{2,1,0:T(8,128)(2,1)} %bitcast.109), custom_call_target="tpu_custom_call" | custom-call | flops 24999999488 | tf_op jit(solution)/shard_map/give_back/pallas_call | solution.py:991
  343.5 6.0 %last_back.1 = (bf16[2,784,384]{2,1,0:T(8,128)(2,1)}, f32[8,384]{1,0:T(8,128)}) custom-call(bf16[2,784,384]{2,1,0:T(8,128)(2,1)} %reshape.183.x_ref, f32[2,784,384]{2,1,0:T(8,128)} %get-tuple-element.135.res_ref, f32[2,784,384]{2,1,0:T(8,128)} %get-tuple-element.136.dx_ref, f32[2,208,384]{2,1,0:T(8,128)} %get-tuple-element.137.own_ref, ...), custom_call_target="tpu_custom_call" | custom-call | flops 6000000000 | tf_op jit(solution)/shard_map/last_back/pallas_call | solution.py:632
  351.7 8.7 %reduce-scatter.6.cloned.1.call-done = bf16[1,96,1792]{2,1,0:T(8,128)(2,1)} async-done(((bf16[8,96,1792]{2,1,0:T(8,128)(2,1)}), bf16[1,96,1792]{2,1,0:T(8,128)(2,1)}) %reduce-scatter.6.cloned.1.call-update) | async-done | bytes 344080 | tf_op jit(solution)/shard_map/reduce_scatter | solution.py:1327
  360.4 46.0 %finish.1 = (bf16[2,2,784,384]{3,2,1,0:T(8,128)(2,1)}, f32[40,384]{1,0:T(8,128)}, bf16[96,4736]{1,0:T(8,128)(2,1)}) custom-call(bf16[2,784,384]{2,1,0:T(8,128)(2,1)} %get-tuple-element.139.half_ref, f32[8,384]{1,0:T(8,128)} %get-tuple-element.140.last_ref, f32[8,384]{1,0:T(8,128)} %get-tuple-element.141.qv_a_rows, f32[8,384]{1,0:T(8,128)} %get-tuple-element.142.a_ref, ...), custom_call_target="tpu_custom_call" | custom-call | flops 40000000000 | tf_op jit(solution)/shard_map/finish/pallas_call | solution.py:1132
  406.4 5.6 %reshape.208 = f32[1,4,196,4,384]{4,3,2,1,0:T(4,128)} reshape(bf16[2,2,784,384]{3,2,1,0:T(8,128)(2,1)} %get-tuple-element.152) | data formatting | bytes 7225344 | tf_op jit(solution)/shard_map/transpose | solution.py:1249
  412.0 3.8 write.1
  (115 shorter events, 24.2 us)
Async XLA Ops:
  7.2 5.8 %copy-start = (bf16[1,4,4,49,768]{4,2,3,1,0:T(4,128)(2,1)S(1)}, bf16[1,4,4,49,768]{4,2,3,1,0:T(4,128)(2,1)}, u32[]{:S(2)}) copy-start(bf16[1,4,4,49,768]{4,2,3,1,0:T(4,128)(2,1)} %param.45) | copy-start | bytes 3612676
  7.2 71.9 %all-gather.5.cloned.1.call-start = ((), (), s32[]{:S(2)}) async-start(), calls=%async_computation.6 | async-start | bytes 3096576 | tf_op jit(solution)/shard_map/all_gather | solution.py:1265
  9.2 136.6 %all-gather.7.cloned.1.call-start = ((), (), s32[]{:S(2)}) async-start(), calls=%async_computation.7 | async-start | bytes 13271040 | tf_op jit(solution)/shard_map/all_gather | solution.py:1281
  13.0 2.2 copy-start.15
  15.2 5.6 %copy-start.11 = (f32[1,384]{1,0:T(1,128)}, f32[1,384]{1,0:T(1,128)S(1)}, u32[]{:S(2)}) copy-start(f32[1,384]{1,0:T(1,128)S(1)} %get-tuple-element.226) | copy-start | bytes 4612
  20.7 29.9 %copy-start.5 = (bf16[192,1536]{1,0:T(8,128)(2,1)S(1)}, bf16[192,1536]{1,0:T(8,128)(2,1)}, u32[]{:S(2)}) copy-start(bf16[192,1536]{1,0:T(8,128)(2,1)} %param.35) | copy-start | bytes 1769476
  20.7 29.9 %copy-start.6 = (bf16[192,1536]{1,0:T(8,128)(2,1)S(1)}, bf16[192,1536]{1,0:T(8,128)(2,1)}, u32[]{:S(2)}) copy-start(bf16[192,1536]{1,0:T(8,128)(2,1)} %param.36) | copy-start | bytes 1769476
  20.7 29.9 %copy-start.8 = (bf16[192,384]{1,0:T(8,128)(2,1)S(1)}, bf16[192,384]{1,0:T(8,128)(2,1)}, u32[]{:S(2)}) copy-start(bf16[192,384]{1,0:T(8,128)(2,1)} %param.33) | copy-start | bytes 442372
  20.7 29.9 %copy-start.10 = (bf16[192,192]{1,0:T(8,128)(2,1)S(1)}, bf16[192,192]{1,0:T(8,128)(2,1)}, u32[]{:S(2)}) copy-start(bf16[192,192]{1,0:T(8,128)(2,1)} %param.34) | copy-start | bytes 221188
  52.5 211.4 %reduce-scatter.4.cloned.1.call-start = ((), (), s32[]{:S(2)}) async-start(), calls=%async_computation.3 | async-start | bytes 10616832 | tf_op jit(solution)/shard_map/reduce_scatter | solution.py:1327
  53.5 2.3 slice-start
  53.6 3.0 copy-start.7
  172.4 179.3 %reduce-scatter.8.cloned.1.call-start = ((), (), s32[]{:S(2)}) async-start(), calls=%async_computation.5 | async-start | bytes 3981312 | tf_op jit(solution)/shard_map/reduce_scatter | solution.py:1327
  172.5 33.5 %copy-start.2 = (bf16[2,4,96,768]{3,2,1,0:T(8,128)(2,1)S(1)}, bf16[2,4,96,768]{3,2,1,0:T(8,128)(2,1)}, u32[]{:S(2)}) copy-start(bf16[2,4,96,768]{3,2,1,0:T(8,128)(2,1)} %get-tuple-element.150) | copy-start | bytes 3538948
  172.5 33.5 %copy-start.4 = (bf16[2,4,96,384]{3,2,1,0:T(8,128)(2,1)S(1)}, bf16[2,4,96,384]{3,2,1,0:T(8,128)(2,1)}, u32[]{:S(2)}) copy-start(bf16[2,4,96,384]{3,2,1,0:T(8,128)(2,1)} %get-tuple-element.151) | copy-start | bytes 1769476
  237.1 123.2 %reduce-scatter.6.cloned.1.call-start = ((), (), s32[]{:S(2)}) async-start(), calls=%async_computation.4 | async-start | bytes 3096576 | tf_op jit(solution)/shard_map/reduce_scatter | solution.py:1327
  265.1 41.9 %collective-permute-start.2 = (bf16[96,1536]{1,0:T(8,128)(2,1)S(1)}, bf16[96,1536]{1,0:T(8,128)(2,1)S(1)}, u32[]{:S(2)}, u32[]{:S(2)}) collective-permute-start(bf16[96,1536]{1,0:T(8,128)(2,1)S(1)} %get-tuple-element.212), channel_id=1, source_target_pairs={{0,24},{8,0},{16,8},{24,16},{1,25},{9,1},{17,9},{25,17},{2,26},{10... | collective-permute-start | bytes 884744 | tf_op jit(solution)/shard_map/ppermute | solution.py:1209
  268.5 38.5 %collective-permute-start.1 = (bf16[96,1536]{1,0:T(8,128)(2,1)S(1)}, bf16[96,1536]{1,0:T(8,128)(2,1)S(1)}, u32[]{:S(2)}, u32[]{:S(2)}) collective-permute-start(bf16[96,1536]{1,0:T(8,128)(2,1)S(1)} %get-tuple-element.213), channel_id=1, source_target_pairs={{0,16},{8,24},{16,0},{24,8},{1,17},{9,25},{17,1},{25,9},{2,18},{10... | collective-permute-start | bytes 884744 | tf_op jit(solution)/shard_map/ppermute | solution.py:1209
  268.5 38.5 %collective-permute-start = (bf16[96,1536]{1,0:T(8,128)(2,1)S(1)}, bf16[96,1536]{1,0:T(8,128)(2,1)}, u32[]{:S(2)}, u32[]{:S(2)}) collective-permute-start(bf16[96,1536]{1,0:T(8,128)(2,1)S(1)} %get-tuple-element.211), channel_id=1, source_target_pairs={{0,8},{8,16},{16,24},{24,0},{1,9},{9,17},{17,25},{25,1},{2,10},{10... | collective-permute-start | bytes 884744 | tf_op jit(solution)/shard_map/ppermute | solution.py:1209
  308.3 41.3 %collective-permute-start.3 = (bf16[96,1536]{1,0:T(8,128)(2,1)S(1)}, bf16[96,1536]{1,0:T(8,128)(2,1)}, u32[]{:S(2)}, u32[]{:S(2)}) collective-permute-start(bf16[96,1536]{1,0:T(8,128)(2,1)S(1)} %fusion.2), channel_id=1, source_target_pairs={{0,8},{8,16},{16,24},{24,0},{1,9},{9,17},{17,25},{25,1},{2,10},{10... | collective-permute-start | bytes 884744 | tf_op jit(solution)/shard_map/ppermute | solution.py:1218
  310.6 40.0 %collective-permute-start.4 = (bf16[96,1536]{1,0:T(8,128)(2,1)S(1)}, bf16[96,1536]{1,0:T(8,128)(2,1)}, u32[]{:S(2)}, u32[]{:S(2)}) collective-permute-start(bf16[96,1536]{1,0:T(8,128)(2,1)S(1)} %fusion.2), channel_id=1, source_target_pairs={{0,16},{8,24},{16,0},{24,8},{1,17},{9,25},{17,1},{25,9},{2,18},{10... | collective-permute-start | bytes 884744 | tf_op jit(solution)/shard_map/ppermute | solution.py:1218
  311.5 40.1 %collective-permute-start.5 = (bf16[96,1536]{1,0:T(8,128)(2,1)S(1)}, bf16[96,1536]{1,0:T(8,128)(2,1)S(1)}, u32[]{:S(2)}, u32[]{:S(2)}) collective-permute-start(bf16[96,1536]{1,0:T(8,128)(2,1)S(1)} %fusion.2), channel_id=1, source_target_pairs={{0,24},{8,0},{16,8},{24,16},{1,25},{9,1},{17,9},{25,17},{2,26},{10... | collective-permute-start | bytes 884744 | tf_op jit(solution)/shard_map/ppermute | solution.py:1218
  351.6 54.8 %copy-start.3 = (bf16[4,96,1536]{2,1,0:T(8,128)(2,1)}, bf16[4,96,1536]{2,1,0:T(8,128)(2,1)S(1)}, u32[]{:S(2)}) copy-start(bf16[4,96,1536]{2,1,0:T(8,128)(2,1)S(1)} %bitcast_dynamic-update-slice_fusion) | copy-start | bytes 3538948
  412.0 7.7 %copy-start.1 = (bf16[1,4,4,49,768]{4,2,3,1,0:T(4,128)(2,1)S(1)}, bf16[1,4,4,49,768]{4,2,3,1,0:T(4,128)(2,1)}, u32[]{:S(2)}) copy-start(bf16[1,4,4,49,768]{4,2,3,1,0:T(4,128)(2,1)} %param.45) | copy-start | bytes 3612676
  (11 other events, 16.1 us)
Sparse Core Ops, SparseCore 0:
  10.5 39.6 all-gather.4
  52.7 82.7 all-gather.6
  172.5 86.4 reduce-scatter.3
  263.0 48.0 reduce-scatter.7
  314.3 46.0 reduce-scatter.5

commit v10 on v9

--- a/solution.py
+++ b/solution.py
@@ -294,9 +294,9 @@
         q_s[:, low:low + 384] = (value + bias_ref[0:1, low:low + 384]).astype(bf16)
 
 
-def norm_pool_kernel(x_ref, vec_ref, pool_ref, pair_ref, low_ref, pooled_ref, mean_ref):
+def norm_pool_kernel(x_ref, gains_ref, shifts_ref, pool_ref, pair_ref, low_ref, pooled_ref, mean_ref):
     unit, _ = norm(x_ref[0].astype(f32))
-    normed = unit * vec_ref[0:1, :] + vec_ref[1:2, :]
+    normed = unit * gains_ref[0:1, :] + shifts_ref[0:1, :]
     low_ref[0] = normed.astype(bf16)
     pooled = exact_dot(pool_ref[...], normed)
     pooled_ref[0] = pooled.astype(bf16)
@@ -454,29 +454,29 @@
             write_shares(gw_ref, h, gw_s)
 
 
-def first_mlp_kernel(x_ref, comb_ref, out_ref, up_ref, down_ref, ub_ref, vec_ref, pool_ref, pair_ref,
+def first_mlp_kernel(x_ref, comb_ref, out_ref, up_ref, down_ref, ub_ref, gains_ref, shifts_ref, pool_ref, pair_ref,
                      after_ref, middle_ref, pooled_ref, mean_ref, out_s):
     @pl.when(pl.program_id(0) == 0)
     def _():
         assemble_out(out_ref, out_s)
 
-    after = x_ref[0].astype(f32) + dot(comb_ref[0], out_s[...], NT) + vec_ref[0:1, :]
+    after = x_ref[0].astype(f32) + dot(comb_ref[0], out_s[...], NT) + shifts_ref[1:2, :]
     after_ref[0] = after
     unit, _ = norm(after)
-    low = (unit * vec_ref[1:2, :] + vec_ref[2:3, :]).astype(bf16)
-    total = after + vec_ref[3:4, :]
+    low = (unit * gains_ref[1:2, :] + shifts_ref[2:3, :]).astype(bf16)
+    total = after + shifts_ref[3:4, :]
     for h in range(up_ref.shape[0]):
         hidden = gelu(dot(low, up_ref[h]) + ub_ref[h]).astype(bf16)
         total = total + dot(hidden, down_ref[h], NT)
     middle_ref[0] = total
     unit, _ = norm(total)
-    pooled = exact_dot(pool_ref[...], unit * vec_ref[4:5, :] + vec_ref[5:6, :])
+    pooled = exact_dot(pool_ref[...], unit * gains_ref[2:3, :] + shifts_ref[4:5, :])
     pooled_ref[0] = pooled.astype(bf16)
     mean_ref[0] = exact_dot(pair_ref[...], pooled).astype(bf16)
 
 
 def second_mlp_kernel(
-    comb_ref, pooled_ref, cot_ref, out_ref, skip_ref, up_ref, down_ref, ub_ref, vec_ref,
+    comb_ref, pooled_ref, cot_ref, out_ref, skip_ref, up_ref, down_ref, ub_ref, gains_ref, shifts_ref,
     mixed_ref, dcomb_ref, dskip_ref, gmlp_ref, gout_ref, gskip_ref, gub_ref, row_ref,
     after_s, low_s, lowt_s, cott_s, sum_s, dlow_s, skip_s,
 ):
@@ -486,17 +486,17 @@
     def _():
         share = skip_s.shape[1] // skip_ref.shape[0]
         skip_s[...] = jnp.concatenate([skip_ref[h, :, :share].astype(f32) for h in range(skip_ref.shape[0])], axis=1).astype(bf16)
-        after = dot(pooled_ref[...], skip_s[...], NT) + vec_ref[0:1, :]
+        after = dot(pooled_ref[...], skip_s[...], NT) + shifts_ref[0:1, :]
         wide = out_ref.shape[2]
         for h in range(out_ref.shape[0]):
             after = after + dot(comb_ref[:, wide * h:wide * h + wide], out_ref[h], NT)
         after_s[...] = after
         unit, _ = norm(after)
-        low = (unit * vec_ref[1:2, :] + vec_ref[2:3, :]).astype(bf16)
+        low = (unit * gains_ref[...] + shifts_ref[1:2, :]).astype(bf16)
         low_s[...] = low
         lowt_s[...] = transposed(low)
         cott_s[...] = transposed(cot_ref[...])
-        sum_s[...] = after + vec_ref[3:4, :]
+        sum_s[...] = after + shifts_ref[2:3, :]
         dlow_s[...] = jnp.zeros_like(dlow_s)
 
     pre = dot(low_s[...], up_ref[0]) + ub_ref[...]
@@ -518,7 +518,7 @@
         unit, inverse = norm(after_s[...])
         dlow = dlow_s[...]
         cot = cot_ref[...].astype(f32)
-        res = norm_back(unit, inverse, vec_ref[1:2, :], dlow) + cot
+        res = norm_back(unit, inverse, gains_ref[...], dlow) + cot
         row_ref[...] = jnp.zeros_like(row_ref)
         for i, row in enumerate((res, dlow, cot, dlow * unit)):
             row_ref[i:i + 1, :] = sum_rows(row)
@@ -542,7 +542,7 @@
 
 
 def first_back_kernel(
-    middle_ref, after_ref, comb_ref, dskip_ref, dq_ref, own_ref, mem_ref, out_ref, up_ref, down_ref, ub_ref, vec_ref,
+    middle_ref, after_ref, comb_ref, dskip_ref, dq_ref, own_ref, mem_ref, out_ref, up_ref, down_ref, ub_ref, gains_ref, shifts_ref,
     unpool_ref, unpair_ref,
     res_ref, dcomb_ref, gmlp_ref, gub_ref, row_ref,
     gup_s, gdown_s, gout_s, out_s,
@@ -560,12 +560,12 @@
     dpool = dskip_ref[0] + dq_ref[0] + own_ref[0] + exact_dot(unpair_ref[...], mem_ref[0])
     dnorm = exact_dot(unpool_ref[...], dpool)
     unit, inverse = norm(middle_ref[0])
-    grad = norm_back(unit, inverse, vec_ref[2:3, :], dnorm)
+    grad = norm_back(unit, inverse, gains_ref[2:3, :], dnorm)
     rows = [sum_rows(dnorm * unit), sum_rows(dnorm), sum_rows(grad)]
     low = grad.astype(bf16)
     lowt = transposed(low)
     unit, inverse = norm(after_ref[0])
-    normed = (unit * vec_ref[0:1, :] + vec_ref[1:2, :]).astype(bf16)
+    normed = (unit * gains_ref[1:2, :] + shifts_ref[2:3, :]).astype(bf16)
     normedt = transposed(normed)
     dnormed = None
     for h in range(up_ref.shape[0]):
@@ -578,7 +578,7 @@
         gup_s[h] += dot(normedt, dpre)
         add = dot(dpre, up_ref[h], NT)
         dnormed = add if dnormed is None else dnormed + add
-    res = norm_back(unit, inverse, vec_ref[0:1, :], dnormed) + grad
+    res = norm_back(unit, inverse, gains_ref[1:2, :], dnormed) + grad
     rows += [sum_rows(dnormed * unit), sum_rows(dnormed), sum_rows(res)]
     res_ref[0] = res
     res = res.astype(bf16)
@@ -597,11 +597,11 @@
             gmlp_ref[h, :, 2 * fa:] = gout.astype(bf16)
 
 
-def last_back_kernel(x_ref, res_ref, dx_ref, own_ref, mem_ref, vec_ref, unpool_ref, unpair_ref, grad_ref, row_ref):
+def last_back_kernel(x_ref, res_ref, dx_ref, own_ref, mem_ref, gains_ref, unpool_ref, unpair_ref, grad_ref, row_ref):
     dpool = own_ref[0] + exact_dot(unpair_ref[...], mem_ref[0])
     dnorm = dx_ref[0] + exact_dot(unpool_ref[...], dpool)
     unit, inverse = norm(x_ref[0].astype(f32))
-    grad = norm_back(unit, inverse, vec_ref[0:1, :], dnorm) + res_ref[0]
+    grad = norm_back(unit, inverse, gains_ref[0:1, :], dnorm) + res_ref[0]
     grad_ref[0] = grad.astype(bf16)
     add_rows(row_ref, [sum_rows(dnorm * unit), sum_rows(dnorm)])
 
@@ -848,7 +848,7 @@
         dma(chips), dma(chips), dma(chips), dma(chips), dma(2, few), dma(2, few), dma(heads), dma(heads),
     ]
     if block is not None:
-        args, specs = args + [block, *biases], specs + [ANY] + [INVMEM] * len(biases)
+        args, specs = args + [block, *biases], specs + [INVMEM] * (1 + len(biases))
         outs = outs + [shape((heads, toks) + block.shape, bf16)]
         if biases:
             (_, wa), (_, wb), (_, wide) = (b.shape for b in biases)
@@ -871,7 +871,10 @@
 
 def give_back_kernel(exchange, *refs):
     if exchange:
-        part_ref, pick_ref, half_ref, own_ref, back_ref, all_ref, *refs, half_local, half_send, half_recv = refs
+        part_ref, pick_ref, half_ref, grad_ref, own_ref, back_ref, all_ref, sum_ref, *refs = refs
+        refs, hosted = refs[:-14], refs[-14:]
+        (half_local, half_send, half_recv, block_s, block_core, head_s, block_head, block_chip,
+         bc_send, bc_recv, bh_send, bh_recv, bx_send, bx_recv) = hosted
     else:
         part_ref, pick_ref, own_ref, back_ref, *refs = refs
     (mine_s, core_s, sum_s, chip_s, route_s, got_s,
@@ -895,8 +898,20 @@
     for n, other in enumerate(order):
         local_copies.append(pltpu.make_async_copy(part_ref.at[2 * other + core], mine_s.at[n], local_sem.at[n]))
         local_copies[-1].start()
-    halves = []
+    halves, block_copies = [], []
     if exchange:
+        for n in range(heads * chips):
+            block_copies.append(remote(grad_ref.at[2 * n + 1 - core], block_core.at[n], bc_send.at[n], bc_recv.at[n], partner))
+            block_copies[-1].start()
+        for n, copy in enumerate(block_copies):
+            copy.wait_recv()
+            block_s[n] = (grad_ref[2 * n + core].astype(f32) + block_core[n].astype(f32)).astype(bf16)
+        head_copies = [
+            remote(block_s.at[rem(head + k + 1, heads) * chips + x], block_head.at[k, x], bh_send.at[k, x], bh_recv.at[k, x], d)
+            for k, d in enumerate(beside) for x in range(chips)
+        ]
+        for copy in head_copies:
+            copy.start()
         halves = [remote(half_ref, all_ref.at[head], half_send.at[k], half_recv.at[k], d) for k, d in enumerate(beside)]
         for copy in halves:
             copy.start()
@@ -938,6 +953,19 @@
                 route_s[d, s] = total.astype(bf16)
             clip_copies[d].start()
 
+    if exchange:
+        for copy in head_copies:
+            copy.wait_recv()
+        for x in range(chips):
+            total = block_s[head * chips + x].astype(f32)
+            for k in range(heads - 1):
+                total = total + block_head[k, x].astype(f32)
+            head_s[x] = total.astype(bf16)
+        chip_copies = [
+            remote(head_s.at[rem(chip + k + 1, chips)], block_chip.at[k], bx_send.at[k], bx_recv.at[k], d) for k, d in enumerate(across)
+        ]
+        for copy in chip_copies:
+            copy.start()
     for copy in own_copies:
         copy.wait_recv()
     for m in range(share):
@@ -961,6 +989,16 @@
 
     for copy in halves:
         copy.wait_recv()
+    if exchange:
+        for copy in chip_copies:
+            copy.wait_recv()
+        total = head_s[chip].astype(f32)
+        for k in range(chips - 1):
+            total = total + block_chip[k].astype(f32)
+        sum_ref[...] = jnp.zeros_like(sum_ref)
+        sum_ref[:, :grad_ref.shape[2]] = total.astype(bf16)
+        for copy in block_copies + head_copies + chip_copies:
+            copy.wait_send()
     for copy in core_copies + mem_copies + own_copies + halves:
         copy.wait_send()
     if exchange:
@@ -972,7 +1010,7 @@
             copy.wait_send()
 
 
-def give_back(part, pick, own_rows, number, half=None):
+def give_back(part, pick, own_rows, number, half=None, grad=None):
     toks, heads = lax.axis_size("tok"), lax.axis_size("head")
     chips, few = toks // 2, max(toks // 2 - 1, 1)
     share, rows, d = part.shape[1:]
@@ -985,9 +1023,14 @@
         dma(chips), dma(chips), dma(chips), dma(few), dma(few), dma(few), dma(few), dma(heads), dma(heads),
     ]
     if half is not None:
-        args, specs = args + [half], specs + [ANY]
-        outs, out_specs = outs + [shape((heads,) + half.shape, half.dtype)], out_specs + [ANY]
-        scratch += [dma(1), dma(max(heads - 1, 1)), dma(max(heads - 1, 1))]
+        block = grad.shape[1:]
+        beside = max(heads - 1, 1)
+        args, specs = args + [half, grad], specs + [INVMEM, INVMEM]
+        outs += [shape((heads,) + half.shape, half.dtype), shape((block[0], -(-block[1] // 128) * 128), bf16)]
+        out_specs += [ANY, INVMEM]
+        low = lambda *dims: pltpu.VMEM(dims + block, bf16)
+        scratch += [dma(1), dma(beside), dma(beside), low(heads * chips), low(heads * chips), low(chips), low(beside, chips), low(few)]
+        scratch += [dma(heads * chips), dma(heads * chips), dma(beside, chips), dma(beside, chips), dma(few), dma(few)]
     return pl.pallas_call(
         functools.partial(give_back_kernel, half is not None),
         in_specs=specs,
@@ -995,17 +1038,17 @@
         out_shape=outs,
         scratch_shapes=scratch,
         compiler_params=pltpu.CompilerParams(collective_id=number, has_side_effects=True, vmem_limit_bytes=VMEM_CAP),
-        cost_estimate=about(25),
+        cost_estimate=about(1),
         name="give_back",
     )(*args)
 
 
 def finish_kernel(half_ref, last_ref, qv_a_rows, a_ref, b_ref, qv_b_rows, ub_a_rows, ub_b_rows, grad_ref, rest_ref, group_ref,
                   all_ref, total_ref, sums_ref, *scratch):
-    (small_ref, small_s, small_core, small_chip, small_head, small_clip, part_s, part_core, head_s, part_chip, part_head,
+    (small_ref, small_s, small_core, small_chip, small_head, small_clip,
      local_sem, half_send, half_recv, core_send, core_recv, chip_send, chip_recv, head_send, head_recv,
      clip_send, clip_recv, *chain) = scratch
-    first_lanes, next_lanes, deep = group_ref.shape[1], rest_ref.shape[1], grad_ref.shape[1]
+    first_lanes, next_lanes = group_ref.shape[1], rest_ref.shape[1]
     bounds = [0, first_lanes // 2, first_lanes, first_lanes + next_lanes // 2, first_lanes + next_lanes, chain[0].shape[1]]
     chain = Chain(*chain[:3], [(slice(None), pl.ds(low, high - low)) for low, high in zip(bounds, bounds[1:])], *chain[3:])
     clip, head, chip, core, chips = places()
@@ -1019,7 +1062,8 @@
     greet(peers, peers)
     chain.part[:, :first_lanes] = group_ref[...]
     chain.part[:, first_lanes:first_lanes + next_lanes] = rest_ref[...]
-    for n in range(4):
+    chain.part[:, first_lanes + next_lanes:] = grad_ref[...]
+    for n in range(5):
         chain.send_ends(n)
     pending = []
     d1 = small_ref.shape[1]
@@ -1054,60 +1098,40 @@
         return total
 
     first = go([remote(small_ref, small_core, core_send.at[0], core_recv.at[0], partner)])
-    for h in range(heads):
-        for x in range(chips):
-            n = h * chips + x
-            first += go([remote(grad_ref.at[2 * n + 1 - core], part_core.at[n], core_send.at[n + 1], core_recv.at[n + 1], partner)])
+    cuts, tokens = [], half_ref.shape[1]
+    for s in range(share):
+        early = tokens // 4 // 16 * 16 if s == 0 else 0
+        cuts += [(s, low, high) for low, high in ((0, early), (early, tokens)) if high > low]
     halves = [
-        [remote(half_ref.at[s], all_ref.at[head, s], half_send.at[k, s], half_recv.at[k, s], d) for k, d in enumerate(beside)]
-        for s in range(share)
+        [remote(half_ref.at[s, pl.ds(low, high - low)], all_ref.at[head, s, pl.ds(low, high - low)], half_send.at[k, n], half_recv.at[k, n], d)
+         for k, d in enumerate(beside)]
+        for n, (s, low, high) in enumerate(cuts)
     ]
+    go(halves[0])
     local_half = pltpu.make_async_copy(half_ref, all_ref.at[head], local_sem.at[0])
     local_half.start()
     arrived(first)
     small_s[0] = small_ref[...] + small_core[...]
-    for n in range(heads * chips):
-        part_s[n] = (grad_ref[2 * n + core].astype(f32) + part_core[n].astype(f32)).astype(bf16)
-    copies = []
-    for k, d in enumerate(beside):
-        copies += go([remote(small_s.at[0], small_head.at[k], head_send.at[k, 0], head_recv.at[k, 0], d)])
-        for x in range(chips):
-            block = rem(head + k + 1, heads) * chips + x
-            copies += go([remote(part_s.at[block], part_head.at[k, x], head_send.at[k, x + 1], head_recv.at[k, x + 1], d)])
-    for s in range(share):
+    copies = go([remote(small_s.at[0], small_head.at[k], head_send.at[k, 0], head_recv.at[k, 0], d) for k, d in enumerate(beside)])
+    for s in range(1, len(halves)):
         go(halves[s])
     chain.send_parts(0)
+    arrived(copies)
+    small_s[1] = in_order(head, heads, small_s[0], lambda k: small_head[k])
+    copies = go([remote(small_s.at[1], small_chip.at[k], chip_send.at[k, 0], chip_recv.at[k, 0], d) for k, d in enumerate(across)])
     chain.send_parts(1)
     arrived(copies)
-    small_s[1] = in_order(head, heads, small_s[0], lambda k: small_head[k])
-    for x in range(chips):
-        total = part_s[head * chips + x].astype(f32)
-        for k in range(heads - 1):
-            total = total + part_head[k, x].astype(f32)
-        head_s[x] = total.astype(bf16)
+    small_s[2] = in_order(chip, chips, small_s[1], lambda k: small_chip[k])
     copies = []
-    for k, d in enumerate(across):
-        copies += go([remote(small_s.at[1], small_chip.at[k], chip_send.at[k, 0], chip_recv.at[k, 0], d)])
-        copies += go([remote(head_s.at[rem(chip + k + 1, chips)], part_chip.at[k], chip_send.at[k, 1], chip_recv.at[k, 1], d)])
+    for k, d in enumerate(along):
+        copies += go([remote(small_s.at[2], small_clip.at[k], clip_send.at[k, 0], clip_recv.at[k, 0], d)])
     chain.send_parts(2)
     chain.middle_totals(0)
     chain.send_parts(3)
-    arrived(copies)
-    small_s[2] = in_order(chip, chips, small_s[1], lambda k: small_chip[k])
-    total = head_s[chip].astype(f32)
-    for k in range(chips - 1):
-        total = total + part_chip[k].astype(f32)
-    mine = first_lanes + next_lanes
-    chain.part[:, mine:mine + grad_ref.shape[2]] = total.astype(bf16)
-    chain.send_ends(4)
-    copies = []
-    for k, d in enumerate(along):
-        copies += go([remote(small_s.at[2], small_clip.at[k], clip_send.at[k, 0], clip_recv.at[k, 0], d)])
     chain.middle_totals(1)
-    chain.middle_totals(2)
     chain.send_parts(4)
-    chain.middle_totals(3)
-    chain.middle_totals(4)
+    for n in range(2, 5):
+        chain.middle_totals(n)
     for n in range(5):
         chain.other_totals(n)
     arrived(copies)
@@ -1125,20 +1149,19 @@
     toks, heads, clips = lax.axis_size("tok"), lax.axis_size("head"), lax.axis_size("clip")
     chips = toks // 2
     across, beside, along = (max(n, 1) for n in (chips - 1, heads - 1, clips - 1))
-    block, depth, d1 = grad.shape[1:], rest.shape[0], rows[0].shape[1]
+    depth, d1 = rest.shape[0], rows[0].shape[1]
     small = (-(-count // 8) * 8, d1)
-    low, full = lambda *dims: pltpu.VMEM(dims, bf16), lambda *dims: pltpu.VMEM(dims + small, f32)
-    buffer = (depth, first.shape[1] + rest.shape[1] + -(-block[1] // 128) * 128)
+    full = lambda *dims: pltpu.VMEM(dims + small, f32)
+    buffer = (depth, first.shape[1] + rest.shape[1] + grad.shape[1])
     return pl.pallas_call(
         finish_kernel,
-        in_specs=[ANY] + [INVMEM] * (len(rows) + 3),
+        in_specs=[INVMEM] * (len(rows) + 4),
         out_specs=[ANY, INVMEM, INVMEM],
         out_shape=[shape((heads,) + half.shape, half.dtype), shape(small, f32), shape(buffer, bf16)],
         scratch_shapes=[
             full(), full(3), full(), full(across), full(beside), full(along),
-            low(heads * chips, *block), low(heads * chips, *block), low(chips, *block), low(across, *block), low(beside, chips, *block),
-            dma(1), dma(beside, half.shape[0]), dma(beside, half.shape[0]), dma(heads * chips + 1), dma(heads * chips + 1),
-            dma(across, 2), dma(across, 2), dma(beside, chips + 1), dma(beside, chips + 1), dma(along, 1), dma(along, 1),
+            dma(1), dma(beside, half.shape[0] + 1), dma(beside, half.shape[0] + 1), dma(1), dma(1),
+            dma(across, 1), dma(across, 1), dma(beside, 1), dma(beside, 1), dma(along, 1), dma(along, 1),
             *chain_scratch(buffer, 5),
         ],
         compiler_params=pltpu.CompilerParams(collective_id=number, has_side_effects=True, vmem_limit_bytes=VMEM_CAP),
@@ -1220,10 +1243,6 @@
     return out.reshape((-1,) + piece.shape[1:])
 
 
-def padded_rows(*rows):
-    return jnp.concatenate([jnp.stack(rows), jnp.zeros((-len(rows) % 8, rows[0].shape[0]), f32)])
-
-
 def local(
     clips_in, resets, assign, w_qkv_a, w_out_a, w_up_a, w_down_a, w_qkv_b, w_out_b, w_skip_b, w_up_b, w_down_b,
     gains_a, gains_b, shifts_a, shifts_b, qv_bias_a, qv_bias_b, up_bias_a, up_bias_b, cotangent,
@@ -1266,15 +1285,16 @@
     stream = by_patch(lax.dynamic_slice_in_dim(clips_in[0], first, share, 0))
     low1, pooled1, mean1 = call(
         norm_pool_kernel, share,
-        [(stream, 0), (padded_rows(gains_a[0], shifts_a[0]), None), (pooling, None), (pairing, None)],
+        [(stream, 0), (gains_a, None), (shifts_a, None), (pooling, None), (pairing, None)],
         [(shape((share, tokens, d1), bf16), 0), (shape((share, own_rows, d1), bf16), 0), (shape((share, mem_rows, d1), bf16), 0)],
         name="norm_pool", us=5,
     )
-    pack_w = jnp.concatenate([*w_qkv_a.transpose(1, 0, 2)], axis=1)
+    pack_w = jnp.concatenate([*w_qkv_b.transpose(1, 0, 2), *w_qkv_a.transpose(1, 0, 2)], axis=1)
     own1, mem1, all_w, qv_a, qv_b, ub_a, ub_b = share_pooled(
         pooled1, mean1, pick, 0, pack_w, [qv_bias_a, qv_bias_b, jnp.concatenate([up_bias_a, up_bias_b])[None]], fa)
-    all_w = all_w.reshape(heads, d1, -1)
-    pack_q = jnp.concatenate([*w_qkv_b.transpose(1, 0, 2)], axis=1)
+    all_q = all_w.reshape(heads, d1, -1)
+    all_w = all_q[:, :, 3 * hb:]
+    q_spec = pl.BlockSpec((heads, d1, 3 * hb), lambda i: (0, 0, 0))
     own1, w_up_b, cot = lax.optimization_barrier((own1, w_up_b, cot))
     spare = jnp.zeros((w_up_b.shape[0], -(2 * fb + hb + hs) % hb), bf16)
     pack_b = jnp.concatenate([w_up_b, w_down_b, w_out_b, w_skip_b, spare], axis=1)
@@ -1288,7 +1308,7 @@
     after1, middle, pooled3, mean3 = call(
         first_mlp_kernel, share,
         [(stream, 0), (comb1, 0), (all_a, out_a_spec), (all_a, up_spec), (all_a, down_spec), (ub_a, None),
-         (padded_rows(shifts_a[1], gains_a[1], shifts_a[2], shifts_a[3], gains_a[2], shifts_a[4]), None),
+         (gains_a, None), (shifts_a, None),
          (pooling, None), (pairing, None)],
         [(shape((share, tokens, d1), f32), 0), (shape((share, tokens, d1), f32), 0),
          (shape((share, own_rows, d1), bf16), 0), (shape((share, mem_rows, d1), bf16), 0)],
@@ -1296,9 +1316,8 @@
         name="first_mlp", us=13,
     )
 
-    own2, mem2, all_q = share_pooled(pooled3, mean3, pick, 1, pack_q)
-    all_q = all_q.reshape(heads, d1, -1)
-    comb2, lse2 = attend(pooled3, own2, mem2, (all_q, None), qv_b, has, valid, d2)
+    own2, mem2 = share_pooled(pooled3, mean3, pick, 1)
+    comb2, lse2 = attend(pooled3, own2, mem2, (all_q, q_spec), qv_b, has, valid, d2)
     chunk = 768
     per_head = fb // chunk
     steps = heads * per_head
@@ -1310,7 +1329,7 @@
          (all_b, rows_spec),
          (all_b, pl.BlockSpec((1, d2, chunk), lambda j: (j // per_head, 0, per_head + j % per_head))),
          (ub_b, pl.BlockSpec((1, chunk), lambda j: (0, j))),
-         (padded_rows(shifts_b[0], gains_b, shifts_b[1], shifts_b[2]), None)],
+         (gains_b[None], None), (shifts_b, None)],
         [(shape((rows2, d2), bf16), None), (shape((rows2, d2), bf16), None), (shape((rows2, d1), f32), None),
          (shape((heads, toks, 2, d2 // toks, fb), bf16),
           pl.BlockSpec((1, toks, 2, d2 // toks, chunk), lambda j: (j // per_head, 0, 0, 0, j % per_head))),
@@ -1328,7 +1347,7 @@
 
     sum_mlp_b = scatter(g_mlp_b.reshape((heads * toks,) + g_mlp_b.shape[2:])).reshape(-1, fb)
     dcomb2 = dcomb2.reshape(share, own_rows, d2)
-    dq2, dpool2, g_qkv_b, rows_qv_b = attend_back(pooled3, dcomb2, own2, mem2, (all_q, None), qv_b, has, valid, lse2, heads)
+    dq2, dpool2, g_qkv_b, rows_qv_b = attend_back(pooled3, dcomb2, own2, mem2, (all_q, q_spec), qv_b, has, valid, lse2, heads)
     own_back2, mem_back2 = give_back(dpool2, pick, own_rows, 2)
 
     merge = lambda grad: grad.reshape((heads * toks,) + grad.shape[2:])
@@ -1339,7 +1358,7 @@
         first_back_kernel, share,
         [(middle, 0), (after1, 0), (comb1, 0), (dskip.reshape(share, own_rows, d1), 0), (dq2, 0), (own_back2, 0), (mem_back2, 0),
          (all_a, out_a_spec), (all_a, up_spec), (all_a, down_spec), (ub_a, None),
-         (padded_rows(gains_a[1], shifts_a[2], gains_a[2]), None), (unpooling, None), (unpairing, None)],
+         (gains_a, None), (shifts_a, None), (unpooling, None), (unpairing, None)],
         [(shape((share, tokens, d1), f32), 0), (shape((share, tokens, d1), bf16), 0),
          (shape((heads, d1, -(-(2 * fa + ha) // 256) * 256), bf16), None),
          (shape((heads, 1, fa), f32), None), (shape((8, d1), f32), None)],
@@ -1353,18 +1372,19 @@
     dx1, dpool1, g_qkv_a, rows_qv_a = attend_back(low1, dcomb1, own1, mem1, (all_w, None), qv_a, has, valid, lse1, heads)
     dpool1, sum_mlp_b = lax.optimization_barrier((dpool1, sum_mlp_b))
     sum_mlp_b = spread_clips(sum_mlp_b)
-    own_back1, mem_back1, mixed_all = give_back(dpool1, pick, own_rows, 3, mixed.reshape(share, own_rows, d2))
+    own_back1, mem_back1, mixed_all, sum_qkv_a = give_back(
+        dpool1, pick, own_rows, 3, mixed.reshape(share, own_rows, d2), by_owner(g_qkv_a))
     stream_grad, rows_last = call(
         last_back_kernel, share,
-        [(stream, 0), (res1, 0), (dx1, 0), (own_back1, 0), (mem_back1, 0), (padded_rows(gains_a[0]), None),
+        [(stream, 0), (res1, 0), (dx1, 0), (own_back1, 0), (mem_back1, 0), (gains_a, None),
          (unpooling, None), (unpairing, None)],
         [(shape((share, tokens, d1), bf16), 0), (shape((8, d1), f32), None)],
-        name="last_back", us=6,
+        name="last_back", us=1,
     )
 
     rows = [rows_last, rows_qv_a, rows_a, rows_b, rows_qv_b, g_ub_a, g_ub_b]
     count = 10 + (6 * d2 + heads * (fa + fb)) // d1
-    stream_all, total, sums = finish(stream_grad, rows, by_owner(g_qkv_a), sum_rest_a, sum_rest_b, count, 4)
+    stream_all, total, sums = finish(stream_grad, rows, sum_qkv_a, sum_rest_a, sum_rest_b, count, 4)
     row1, row2 = w_up_a.shape[0], w_up_b.shape[0]
     outs = [(3, row1, ha), (row1, ha), (row1, fa), (row1, fa), (3, row1, hb), (row2, hb), (row2, hs), (row2, fb), (row2, fb),
             (3, d1), (1, d2), (5, d1), (3, d2), (2, ha), (2, hb), (1, fa), (1, fb)]

time: 430 us -> 424 us (0.986)
  waiting for transfers between devices: 8.85 us -> 1.73 us
    reduce_scatter x3, waiting for transfers between devices: 8.75 us -> 1.63 us  [scatter(): return lax.psum_scatter(grad, group, scatter_dimension=0, tiled=False)]
    pallas_call x2, Pallas kernels: 55.1 us -> 61.9 us  [give_back(): pl.pallas_call(functools.partial(give_back_kernel, half is not None), in_...]
  transfers between devices with their start and end apart: 11 -> 11, of which waited for: 1 -> 1; matrix products, arithmetic and copies ran while one was open for 6% -> 5% of each run, Pallas kernels for 66% -> 68%
where the time goes in v10:
time: 424 us; the launch traced here: 420 us
  Pallas kernels  359 us (85%)
  local copies, waits for them, and re-layouts  25 us (6%)
  between operations  14.5 us (3%)
  starting transfers between devices  9.65 us (2%)
  other arithmetic  9.52 us (2%)
    pallas_call x10, Pallas kernels, call(): pl.pallas_call(kernel, grid=(steps,), in_specs=[spec(a, how) for a, how i...  189 us
    pallas_call x2, Pallas kernels, share_pooled(): pl.pallas_call(functools.partial(share_kernel, block is not None, len(bia...  64.5 us
    pallas_call x2, Pallas kernels, give_back(): pl.pallas_call(functools.partial(give_back_kernel, half is not None), in_...  61.9 us
    pallas_call x1, Pallas kernels, finish(): pl.pallas_call(finish_kernel, in_specs=[INVMEM] * (len(rows) + 4), out_sp...  44 us
  transfers between devices with their start and end apart: 11, of which 1 were waited for; matrix products, arithmetic and copies ran while one was open for 5% of the time, Pallas kernels for 68%

profile of v10, /device:TPU:0, one launch (start us, length us, event | category | flops | bytes accessed | tf_op | source)
XLA Modules:
  0.0 419.7 jit_solution(4294144945076588669)
XLA Ops:
  7.3 1.9 concatenate.17
  9.2 1.7 dynamic-slice_bitcast_fusion
  15.3 4.3 %norm_pool.1 = (bf16[2,784,384]{2,1,0:T(8,128)(2,1)}, bf16[2,208,384]{2,1,0:T(8,128)(2,1)}, bf16[2,112,384]{2,1,0:T(8,128)(2,1)}) custom-call(bf16[2,784,384]{2,1,0:T(8,128)(2,1)} %reshape.180.x_ref, f32[3,384]{1,0:T(4,128)} %gains_ref.7, f32[5,384]{1,0:T(8,128)} %shifts_ref.7, bf16[208,784]{1,0:T(8,128)(2,1)} %constant.120.clone.pool_ref, ...), custom_call_target="tpu_custom_call" | custom-call | flops 5000000000 | tf_op jit(solution)/shard_map/norm_pool/pallas_call | solution.py:632
  19.7 35.6 %share_pooled.2 = (bf16[4,2,208,384]{3,2,1,0:T(8,128)(2,1)}, bf16[4,2,112,384]{3,2,1,0:T(8,128)(2,1)}, bf16[2,4,96,1728]{3,2,1,0:T(8,128)(2,1)}, f32[2,384]{1,0:...) custom-call(bf16[2,208,384]{2,1,0:T(8,128)(2,1)} %get-tuple-element.97.refs_0_, ...), custom_call_target="tpu_custom_call" | custom-call | flops 30000001024 | tf_op jit(solution)/shard_map/share_pooled/pallas_call | solution.py:860
  55.3 1.8 concatenate.18
  57.4 2.2 slice.8.w_ref
  61.7 21.4 %attend.2 = (bf16[2,784,384]{2,1,0:T(8,128)(2,1)}, f32[2,784,128]{2,1,0:T(8,128)}) custom-call(bf16[2,784,384]{2,1,0:T(8,128)(2,1)} %get-tuple-element.96.x_ref, bf16[4,2,208,384]{3,2,1,0:T(8,128)(2,1)} %get-tuple-element.100.own_ref, bf16[4,2,112,384]{3,2,1,0:T(8,128)(2,1)} %get-tuple-element.101.mem_ref, bf16[2,384,576]{2,1,0:T(8,128)(2,1)} %slice.8.w_ref, ...), custom_call_target="tpu_custom_call" | custom-call | flops 20000000000 | tf_op jit(solution)/shard_map/attend/pallas_call | solution.py:632
  83.1 13.2 %first_mlp.1 = (f32[2,784,384]{2,1,0:T(8,128)}, f32[2,784,384]{2,1,0:T(8,128)}, bf16[2,208,384]{2,1,0:T(8,128)(2,1)}, bf16[2,112,384]{2,1,0:T(8,128)(2,1)}) custom-call(bf16[2,784,384]{2,1,0:T(8,128)(2,1)} %reshape.180.x_ref, bf16[2,784,384]{2,1,0:T(8,128)(2,1)} %get-tuple-element.104.comb_ref, bf16[2,384,1792]{2,1,0:T(8,128)(2,1)} %bitcast.98, ...), custom_call_target="tpu_custom_call" | custom-call | flops 12999999488 | tf_op jit(solution)/shard_map/first_mlp/pallas_call | solution.py:632
  96.3 28.9 %share_pooled.3 = (bf16[4,2,208,384]{3,2,1,0:T(8,128)(2,1)}, bf16[4,2,112,384]{3,2,1,0:T(8,128)(2,1)}) custom-call(bf16[2,208,384]{2,1,0:T(8,128)(2,1)} %get-tuple-element.108.refs_0_.x_ref, bf16[2,112,384]{2,1,0:T(8,128)(2,1)} %get-tuple-element.109.refs_1_, f32[2,4]{1,0:T(2,128)} %compare_convert_fusion.refs_2_.refs_1_), custom_call_target="tpu_custom_call" | custom-call | flops 20000000000 | tf_op jit(solution)/shard_map/share_pooled/pallas_call | solution.py:860
  125.2 16.2 %attend.3 = (bf16[2,208,768]{2,1,0:T(8,128)(2,1)}, f32[2,208,128]{2,1,0:T(8,128)}) custom-call(bf16[2,208,384]{2,1,0:T(8,128)(2,1)} %get-tuple-element.108.refs_0_.x_ref, bf16[4,2,208,384]{3,2,1,0:T(8,128)(2,1)} %get-tuple-element.110.own_ref, bf16[4,2,112,384]{3,2,1,0:T(8,128)(2,1)} %get-tuple-element.111.mem_ref, bf16[2,384,1728]{2,1,0:T(8,128)(2,1)} %bitcast.90, ...), custom_call_target="tpu_custom_call" | custom-call | flops 20000000000 | tf_op jit(solution)/shard_map/attend/pallas_call | solution.py:632
  141.5 26.5 %second_mlp.1 = (bf16[416,768]{1,0:T(8,128)(2,1)}, bf16[416,768]{1,0:T(8,128)(2,1)}, f32[416,384]{1,0:T(8,128)}, bf16[2,4,2,192,1536]{4,3,2,1,0:T(8,128)(2,1)}, ...) custom-call(bf16[416,768]{1,0:T(8,128)(2,1)} %bitcast.110, ...), custom_call_target="tpu_custom_call" | custom-call | flops 25999998976 | tf_op jit(solution)/shard_map/second_mlp/pallas_call | solution.py:632
  168.1 33.4 %attend_back.2 = (f32[2,208,384]{2,1,0:T(8,128)}, bf16[4,2,320,384]{3,2,1,0:T(8,128)(2,1)}, bf16[2,384,1152]{2,1,0:T(8,128)(2,1)}, f32[8,768]{1,0:T(8,128)}) custom-call(bf16[2,208,384]{2,1,0:T(8,128)(2,1)} %get-tuple-element.108.refs_0_.x_ref, bf16[2,208,768]{2,1,0:T(8,128)(2,1)} %bitcast.109, bf16[4,2,208,384]{3,2,1,0:T(8,128)(2,1)} %get-tuple-element.110.own_ref, ...), custom_call_target="tpu_custom_call" | custom-call | flops 35999997952 | tf_op jit(solution)/shard_map/attend_back/pallas_call | solution.py:632
  201.6 3.1 pad_maximum_fusion
  204.8 27.6 %give_back.2 = (f32[2,208,384]{2,1,0:T(8,128)}, f32[2,112,384]{2,1,0:T(8,128)}) custom-call(bf16[4,2,320,384]{3,2,1,0:T(8,128)(2,1)} %get-tuple-element.121.refs_0_, f32[2,4]{1,0:T(2,128)} %compare_convert_fusion.refs_2_.refs_1_), custom_call_target="tpu_custom_call" | custom-call | flops 1000000000 | tf_op jit(solution)/shard_map/give_back/pallas_call | solution.py:1034
  232.4 26.7 %first_back.1 = (f32[2,784,384]{2,1,0:T(8,128)}, bf16[2,784,384]{2,1,0:T(8,128)(2,1)}, bf16[2,384,1792]{2,1,0:T(8,128)(2,1)}, f32[2,1,768]{2,1,0:T(1,128)}, f32[8,384]{1,0:T(8,128)}) custom-call(f32[2,784,384]{2,1,0:T(8,128)} %get-tuple-element.106.middle_ref, f32[2,784,384]{2,1,0:T(8,128)} %get-tuple-element.107.after_ref, ...), custom_call_target="tpu_custom_call" | custom-call | flops 25999998976 | tf_op jit(solution)/shard_map/first_back/pallas_call | solution.py:632
  260.3 3.4 collective-permute-start.2
  264.8 37.4 %attend_back.3 = (f32[2,784,384]{2,1,0:T(8,128)}, bf16[4,2,320,384]{3,2,1,0:T(8,128)(2,1)}, bf16[2,384,576]{2,1,0:T(8,128)(2,1)}, f32[8,384]{1,0:T(8,128)}) custom-call(bf16[2,784,384]{2,1,0:T(8,128)(2,1)} %get-tuple-element.96.x_ref, bf16[2,784,384]{2,1,0:T(8,128)(2,1)} %get-tuple-element.127.g_ref, bf16[4,2,208,384]{3,2,1,0:T(8,128)(2,1)} %get-tuple-element.100.own_ref, ...), custom_call_target="tpu_custom_call" | custom-call | flops 35999997952 | tf_op jit(solution)/shard_map/attend_back/pallas_call | solution.py:632
  303.5 2.3 collective-permute-start.3
  308.3 34.3 %give_back.3 = (f32[2,208,384]{2,1,0:T(8,128)}, f32[2,112,384]{2,1,0:T(8,128)}, bf16[2,2,208,768]{3,2,1,0:T(8,128)(2,1)}, bf16[96,640]{1,0:T(8,128)(2,1)}) custom-call(bf16[4,2,320,384]{3,2,1,0:T(8,128)(2,1)} %get-tuple-element.131.refs_0_, f32[2,4]{1,0:T(2,128)} %compare_convert_fusion.refs_2_.refs_1_, bf16[2,208,768]{2,1,0:T(8,128)(2,1)} %bitcast.107, ...), custom_call_target="tpu_custom_call" | custom-call | flops 1000000000 | tf_op jit(solution)/shard_map/give_back/pallas_call | solution.py:1034
  345.9 6.0 %last_back.1 = (bf16[2,784,384]{2,1,0:T(8,128)(2,1)}, f32[8,384]{1,0:T(8,128)}) custom-call(bf16[2,784,384]{2,1,0:T(8,128)(2,1)} %reshape.180.x_ref, f32[2,784,384]{2,1,0:T(8,128)} %get-tuple-element.135.res_ref, f32[2,784,384]{2,1,0:T(8,128)} %get-tuple-element.136.dx_ref, f32[2,208,384]{2,1,0:T(8,128)} %get-tuple-element.137.own_ref, ...), custom_call_target="tpu_custom_call" | custom-call | flops 1000000000 | tf_op jit(solution)/shard_map/last_back/pallas_call | solution.py:632
  354.1 1.6 reduce-scatter.6.cloned.1.call-done
  355.7 44.0 %finish.1 = (bf16[2,2,784,384]{3,2,1,0:T(8,128)(2,1)}, f32[40,384]{1,0:T(8,128)}, bf16[96,4736]{1,0:T(8,128)(2,1)}) custom-call(bf16[2,784,384]{2,1,0:T(8,128)(2,1)} %get-tuple-element.139.half_ref, f32[8,384]{1,0:T(8,128)} %get-tuple-element.140.last_ref, f32[8,384]{1,0:T(8,128)} %get-tuple-element.141.qv_a_rows, f32[8,384]{1,0:T(8,128)} %get-tuple-element.142.a_ref, ...), custom_call_target="tpu_custom_call" | custom-call | flops 40000000000 | tf_op jit(solution)/shard_map/finish/pallas_call | solution.py:1156
  399.7 5.6 %reshape.204 = f32[1,4,196,4,384]{4,3,2,1,0:T(4,128)} reshape(bf16[2,2,784,384]{3,2,1,0:T(8,128)(2,1)} %get-tuple-element.152) | data formatting | bytes 7225344 | tf_op jit(solution)/shard_map/transpose | solution.py:1268
  405.3 3.8 write.1
  (85 shorter events, 22.3 us)
Async XLA Ops:
  7.2 5.6 %copy-start = (bf16[1,4,4,49,768]{4,2,3,1,0:T(4,128)(2,1)S(1)}, bf16[1,4,4,49,768]{4,2,3,1,0:T(4,128)(2,1)}, u32[]{:S(2)}) copy-start(bf16[1,4,4,49,768]{4,2,3,1,0:T(4,128)(2,1)} %param.45) | copy-start | bytes 3612676
  7.2 75.9 %all-gather.5.cloned.1.call-start = ((), (), s32[]{:S(2)}) async-start(), calls=%async_computation.6 | async-start | bytes 3096576 | tf_op jit(solution)/shard_map/all_gather | solution.py:1284
  9.2 132.3 %all-gather.7.cloned.1.call-start = ((), (), s32[]{:S(2)}) async-start(), calls=%async_computation.7 | async-start | bytes 13271040 | tf_op jit(solution)/shard_map/all_gather | solution.py:1301
  10.9 1.2 copy-start.11
  12.2 1.3 copy-start.9
  13.0 1.6 copy-start.14
  19.6 35.7 %copy-start.5 = (bf16[192,1536]{1,0:T(8,128)(2,1)S(1)}, bf16[192,1536]{1,0:T(8,128)(2,1)}, u32[]{:S(2)}) copy-start(bf16[192,1536]{1,0:T(8,128)(2,1)} %param.35) | copy-start | bytes 1769476
  19.6 35.7 %copy-start.6 = (bf16[192,1536]{1,0:T(8,128)(2,1)S(1)}, bf16[192,1536]{1,0:T(8,128)(2,1)}, u32[]{:S(2)}) copy-start(bf16[192,1536]{1,0:T(8,128)(2,1)} %param.36) | copy-start | bytes 1769476
  19.6 35.7 %copy-start.8 = (bf16[192,384]{1,0:T(8,128)(2,1)S(1)}, bf16[192,384]{1,0:T(8,128)(2,1)}, u32[]{:S(2)}) copy-start(bf16[192,384]{1,0:T(8,128)(2,1)} %param.33) | copy-start | bytes 442372
  19.7 35.7 %copy-start.10 = (bf16[192,192]{1,0:T(8,128)(2,1)S(1)}, bf16[192,192]{1,0:T(8,128)(2,1)}, u32[]{:S(2)}) copy-start(bf16[192,192]{1,0:T(8,128)(2,1)} %param.34) | copy-start | bytes 221188
  57.2 201.9 %reduce-scatter.4.cloned.1.call-start = ((), (), s32[]{:S(2)}) async-start(), calls=%async_computation.3 | async-start | bytes 10616832 | tf_op jit(solution)/shard_map/reduce_scatter | solution.py:1346
  59.6 1.5 copy-start.15
  168.0 186.1 %reduce-scatter.8.cloned.1.call-start = ((), (), s32[]{:S(2)}) async-start(), calls=%async_computation.5 | async-start | bytes 3981312 | tf_op jit(solution)/shard_map/reduce_scatter | solution.py:1346
  168.1 33.5 %copy-start.2 = (bf16[2,4,96,768]{3,2,1,0:T(8,128)(2,1)S(1)}, bf16[2,4,96,768]{3,2,1,0:T(8,128)(2,1)}, u32[]{:S(2)}) copy-start(bf16[2,4,96,768]{3,2,1,0:T(8,128)(2,1)} %get-tuple-element.150) | copy-start | bytes 3538948
  168.1 33.5 %copy-start.4 = (bf16[2,4,96,384]{3,2,1,0:T(8,128)(2,1)S(1)}, bf16[2,4,96,384]{3,2,1,0:T(8,128)(2,1)}, u32[]{:S(2)}) copy-start(bf16[2,4,96,384]{3,2,1,0:T(8,128)(2,1)} %get-tuple-element.151) | copy-start | bytes 1769476
  204.7 151.0 %reduce-scatter.6.cloned.1.call-start = ((), (), s32[]{:S(2)}) async-start(), calls=%async_computation.4 | async-start | bytes 3096576 | tf_op jit(solution)/shard_map/reduce_scatter | solution.py:1346
  260.3 41.9 %collective-permute-start.2 = (bf16[96,1536]{1,0:T(8,128)(2,1)S(1)}, bf16[96,1536]{1,0:T(8,128)(2,1)S(1)}, u32[]{:S(2)}, u32[]{:S(2)}) collective-permute-start(bf16[96,1536]{1,0:T(8,128)(2,1)S(1)} %get-tuple-element.212), channel_id=1, source_target_pairs={{0,24},{8,0},{16,8},{24,16},{1,25},{9,1},{17,9},{25,17},{2,26},{10... | collective-permute-start | bytes 884744 | tf_op jit(solution)/shard_map/ppermute | solution.py:1232
  263.7 38.6 %collective-permute-start.1 = (bf16[96,1536]{1,0:T(8,128)(2,1)S(1)}, bf16[96,1536]{1,0:T(8,128)(2,1)S(1)}, u32[]{:S(2)}, u32[]{:S(2)}) collective-permute-start(bf16[96,1536]{1,0:T(8,128)(2,1)S(1)} %get-tuple-element.213), channel_id=1, source_target_pairs={{0,16},{8,24},{16,0},{24,8},{1,17},{9,25},{17,1},{25,9},{2,18},{10... | collective-permute-start | bytes 884744 | tf_op jit(solution)/shard_map/ppermute | solution.py:1232
  263.7 38.6 %collective-permute-start = (bf16[96,1536]{1,0:T(8,128)(2,1)S(1)}, bf16[96,1536]{1,0:T(8,128)(2,1)}, u32[]{:S(2)}, u32[]{:S(2)}) collective-permute-start(bf16[96,1536]{1,0:T(8,128)(2,1)S(1)} %get-tuple-element.211), channel_id=1, source_target_pairs={{0,8},{8,16},{16,24},{24,0},{1,9},{9,17},{17,25},{25,1},{2,10},{10... | collective-permute-start | bytes 884744 | tf_op jit(solution)/shard_map/ppermute | solution.py:1232
  303.5 48.5 %collective-permute-start.3 = (bf16[96,1536]{1,0:T(8,128)(2,1)S(1)}, bf16[96,1536]{1,0:T(8,128)(2,1)}, u32[]{:S(2)}, u32[]{:S(2)}) collective-permute-start(bf16[96,1536]{1,0:T(8,128)(2,1)S(1)} %fusion.2), channel_id=1, source_target_pairs={{0,8},{8,16},{16,24},{24,0},{1,9},{9,17},{17,25},{25,1},{2,10},{10... | collective-permute-start | bytes 884744 | tf_op jit(solution)/shard_map/ppermute | solution.py:1241
  305.8 47.2 %collective-permute-start.4 = (bf16[96,1536]{1,0:T(8,128)(2,1)S(1)}, bf16[96,1536]{1,0:T(8,128)(2,1)}, u32[]{:S(2)}, u32[]{:S(2)}) collective-permute-start(bf16[96,1536]{1,0:T(8,128)(2,1)S(1)} %fusion.2), channel_id=1, source_target_pairs={{0,16},{8,24},{16,0},{24,8},{1,17},{9,25},{17,1},{25,9},{2,18},{10... | collective-permute-start | bytes 884744 | tf_op jit(solution)/shard_map/ppermute | solution.py:1241
  306.7 47.3 %collective-permute-start.5 = (bf16[96,1536]{1,0:T(8,128)(2,1)S(1)}, bf16[96,1536]{1,0:T(8,128)(2,1)S(1)}, u32[]{:S(2)}, u32[]{:S(2)}) collective-permute-start(bf16[96,1536]{1,0:T(8,128)(2,1)S(1)} %fusion.2), channel_id=1, source_target_pairs={{0,24},{8,0},{16,8},{24,16},{1,25},{9,1},{17,9},{25,17},{2,26},{10... | collective-permute-start | bytes 884744 | tf_op jit(solution)/shard_map/ppermute | solution.py:1241
  354.1 45.6 %copy-start.3 = (bf16[4,96,1536]{2,1,0:T(8,128)(2,1)}, bf16[4,96,1536]{2,1,0:T(8,128)(2,1)S(1)}, u32[]{:S(2)}) copy-start(bf16[4,96,1536]{2,1,0:T(8,128)(2,1)S(1)} %bitcast_dynamic-update-slice_fusion) | copy-start | bytes 3538948
  405.3 7.7 %copy-start.1 = (bf16[1,4,4,49,768]{4,2,3,1,0:T(4,128)(2,1)S(1)}, bf16[1,4,4,49,768]{4,2,3,1,0:T(4,128)(2,1)}, u32[]{:S(2)}) copy-start(bf16[1,4,4,49,768]{4,2,3,1,0:T(4,128)(2,1)} %param.45) | copy-start | bytes 3612676
  (3 other events, 3.1 us)
Sparse Core Ops, SparseCore 0:
  10.5 42.4 all-gather.4
  57.3 79.8 all-gather.6
  168.2 86.0 reduce-scatter.3
  258.2 48.1 reduce-scatter.7
  309.6 46.0 reduce-scatter.5

commit v11 on v10

--- a/solution.py
+++ b/solution.py
@@ -15,6 +15,7 @@
 HD = 96
 NEG = -1e30
 VMEM_CAP = 62 * 2**20
+PIECES = 9
 eps = 1e-06
 f32, bf16 = jnp.float32, jnp.bfloat16
 NN, NT, TN = ((1,), (0,)), ((1,), (1,)), ((0,), (0,))
@@ -514,7 +515,9 @@
 
     @pl.when(step == pl.num_programs(0) - 1)
     def _():
-        mixed_ref[...] = sum_s[...].astype(bf16)
+        padded = sum_s.shape[0] // mixed_ref.shape[0]
+        for m in range(mixed_ref.shape[0]):
+            mixed_ref[m] = sum_s[padded * m:padded * m + mixed_ref.shape[1], :].astype(bf16)
         unit, inverse = norm(after_s[...])
         dlow = dlow_s[...]
         cot = cot_ref[...].astype(f32)
@@ -1049,7 +1052,8 @@
      local_sem, half_send, half_recv, core_send, core_recv, chip_send, chip_recv, head_send, head_recv,
      clip_send, clip_recv, *chain) = scratch
     first_lanes, next_lanes = group_ref.shape[1], rest_ref.shape[1]
-    bounds = [0, first_lanes // 2, first_lanes, first_lanes + next_lanes // 2, first_lanes + next_lanes, chain[0].shape[1]]
+    tiles, count = chain[0].shape[1] // 128, chain[-1].shape[0]
+    bounds = [tiles * n // count * 128 for n in range(count + 1)]
     chain = Chain(*chain[:3], [(slice(None), pl.ds(low, high - low)) for low, high in zip(bounds, bounds[1:])], *chain[3:])
     clip, head, chip, core, chips = places()
     clips, heads = lax.axis_size("clip"), lax.axis_size("head")
@@ -1063,7 +1067,7 @@
     chain.part[:, :first_lanes] = group_ref[...]
     chain.part[:, first_lanes:first_lanes + next_lanes] = rest_ref[...]
     chain.part[:, first_lanes + next_lanes:] = grad_ref[...]
-    for n in range(5):
+    for n in range(count):
         chain.send_ends(n)
     pending = []
     d1 = small_ref.shape[1]
@@ -1125,14 +1129,12 @@
     copies = []
     for k, d in enumerate(along):
         copies += go([remote(small_s.at[2], small_clip.at[k], clip_send.at[k, 0], clip_recv.at[k, 0], d)])
-    chain.send_parts(2)
-    chain.middle_totals(0)
-    chain.send_parts(3)
-    chain.middle_totals(1)
-    chain.send_parts(4)
-    for n in range(2, 5):
+    for n in range(2, count):
+        chain.send_parts(n)
+        chain.middle_totals(n - 2)
+    for n in range(count - 2, count):
         chain.middle_totals(n)
-    for n in range(5):
+    for n in range(count):
         chain.other_totals(n)
     arrived(copies)
     total_ref[...] = in_order(clip, clips, small_s[2], lambda k: small_clip[k])
@@ -1162,7 +1164,7 @@
             full(), full(3), full(), full(across), full(beside), full(along),
             dma(1), dma(beside, half.shape[0] + 1), dma(beside, half.shape[0] + 1), dma(1), dma(1),
             dma(across, 1), dma(across, 1), dma(beside, 1), dma(beside, 1), dma(along, 1), dma(along, 1),
-            *chain_scratch(buffer, 5),
+            *chain_scratch(buffer, PIECES),
         ],
         compiler_params=pltpu.CompilerParams(collective_id=number, has_side_effects=True, vmem_limit_bytes=VMEM_CAP),
         cost_estimate=about(40),
@@ -1190,17 +1192,17 @@
     gains_a_ref[1:3, :] = total[4:6]
     shifts_a_ref[0:1, :] = total[1:2]
     shifts_a_ref[1:5, :] = total[6:10]
-    d2, fa, fb = gains_b_ref.shape[1], ub_a_ref.shape[1], ub_b_ref.shape[1]
+    d2, fa, fb = gains_b_ref.shape[0], ub_a_ref.shape[0], ub_b_ref.shape[0]
     heads = total.shape[1] // qv_a_ref.shape[1]
     for i in range(2):
         qv_a_ref[i:i + 1, :] = share_of(total[2 + i:3 + i], qv_a_ref.shape[1])
-    gains_b_ref[...] = rows(d2)
+    gains_b_ref[...] = rows(d2).reshape(d2)
     for i in range(3):
         shifts_b_ref[i:i + 1, :] = rows(d2)
     for i in range(2):
         qv_b_ref[i:i + 1, :] = share_of(rows(d2), qv_b_ref.shape[1])
-    ub_a_ref[...] = share_of(rows(heads * fa), fa)
-    ub_b_ref[...] = share_of(rows(heads * fb), fb)
+    ub_a_ref[...] = share_of(rows(heads * fa), fa).reshape(fa)
+    ub_b_ref[...] = share_of(rows(heads * fb), fb).reshape(fb)
     low = 0
     depth = sums_ref.shape[0]
 
@@ -1330,7 +1332,7 @@
          (all_b, pl.BlockSpec((1, d2, chunk), lambda j: (j // per_head, 0, per_head + j % per_head))),
          (ub_b, pl.BlockSpec((1, chunk), lambda j: (0, j))),
          (gains_b[None], None), (shifts_b, None)],
-        [(shape((rows2, d2), bf16), None), (shape((rows2, d2), bf16), None), (shape((rows2, d1), f32), None),
+        [(shape((share, pooled_tokens, d2), bf16), None), (shape((rows2, d2), bf16), None), (shape((rows2, d1), f32), None),
          (shape((heads, toks, 2, d2 // toks, fb), bf16),
           pl.BlockSpec((1, toks, 2, d2 // toks, chunk), lambda j: (j // per_head, 0, 0, 0, j % per_head))),
          (shape((heads, toks, d2 // toks // 2, 2 * hb), bf16), None), (shape((heads, toks, d2 // toks // 2, 2 * hs), bf16), None),
@@ -1373,7 +1375,7 @@
     dpool1, sum_mlp_b = lax.optimization_barrier((dpool1, sum_mlp_b))
     sum_mlp_b = spread_clips(sum_mlp_b)
     own_back1, mem_back1, mixed_all, sum_qkv_a = give_back(
-        dpool1, pick, own_rows, 3, mixed.reshape(share, own_rows, d2), by_owner(g_qkv_a))
+        dpool1, pick, own_rows, 3, mixed, by_owner(g_qkv_a))
     stream_grad, rows_last = call(
         last_back_kernel, share,
         [(stream, 0), (res1, 0), (dx1, 0), (own_back1, 0), (mem_back1, 0), (gains_a, None),
@@ -1387,19 +1389,19 @@
     stream_all, total, sums = finish(stream_grad, rows, sum_qkv_a, sum_rest_a, sum_rest_b, count, 4)
     row1, row2 = w_up_a.shape[0], w_up_b.shape[0]
     outs = [(3, row1, ha), (row1, ha), (row1, fa), (row1, fa), (3, row1, hb), (row2, hb), (row2, hs), (row2, fb), (row2, fb),
-            (3, d1), (1, d2), (5, d1), (3, d2), (2, ha), (2, hb), (1, fa), (1, fb)]
+            (3, d1), (d2,), (5, d1), (3, d2), (2, ha), (2, hb), (fa,), (fb,)]
     grads = call(
         write_kernel, 1,
         [(head.astype(jnp.int32)[None], INSMEM), (total, None), (sums, None), (sum_mlp_b, None)],
         [(shape(dims, f32), None) for dims in outs],
         name="write", us=4,
     )
-    mixed_all = mixed_all.reshape(micro, own_rows, d2)[:, :pooled_tokens]
+    mixed_all = mixed_all.reshape(micro, pooled_tokens, d2)
     return (
         by_frame(mixed_all, cotangent.shape),
         by_frame(stream_all.astype(f32), clips_in.shape),
         grads[0].transpose(1, 0, 2), *grads[1:4], grads[4].transpose(1, 0, 2), *grads[5:10],
-        grads[10][0], *grads[11:15], grads[15][0], grads[16][0],
+        *grads[10:],
     )
 
 

time: 424 us -> 419 us (0.988)
  transfers between devices with their start and end apart: 11 -> 11, of which waited for: 1 -> 1; matrix products, arithmetic and copies ran while one was open for 5% -> 6% of each run, Pallas kernels for 68% -> 69%
where the time goes in v11:
time: 419 us; the launch traced here: 414 us
  Pallas kernels  356 us (85%)
  local copies, waits for them, and re-layouts  24.9 us (6%)
  between operations  14.5 us (3%)
  starting transfers between devices  9.69 us (2%)
  other arithmetic  5.66 us (1%)
    pallas_call x10, Pallas kernels, call(): pl.pallas_call(kernel, grid=(steps,), in_specs=[spec(a, how) for a, how i...  189 us
    pallas_call x2, Pallas kernels, share_pooled(): pl.pallas_call(functools.partial(share_kernel, block is not None, len(bia...  64.5 us
    pallas_call x2, Pallas kernels, give_back(): pl.pallas_call(functools.partial(give_back_kernel, half is not None), in_...  61 us
    pallas_call x1, Pallas kernels, finish(): pl.pallas_call(finish_kernel, in_specs=[INVMEM] * (len(rows) + 4), out_sp...  41.6 us
  transfers between devices with their start and end apart: 11, of which 1 were waited for; matrix products, arithmetic and copies ran while one was open for 6% of the time, Pallas kernels for 69%

profile of v11, /device:TPU:0, one launch (start us, length us, event | category | flops | bytes accessed | tf_op | source)
XLA Modules:
  0.0 414.3 jit_solution(3743878730962788622)
XLA Ops:
  7.3 1.9 concatenate.17
  15.3 4.3 %norm_pool.1 = (bf16[2,784,384]{2,1,0:T(8,128)(2,1)}, bf16[2,208,384]{2,1,0:T(8,128)(2,1)}, bf16[2,112,384]{2,1,0:T(8,128)(2,1)}) custom-call(bf16[2,784,384]{2,1,0:T(8,128)(2,1)} %reshape.171.x_ref, f32[3,384]{1,0:T(4,128)} %gains_ref.7, f32[5,384]{1,0:T(8,128)} %shifts_ref.7, bf16[208,784]{1,0:T(8,128)(2,1)} %constant.120.clone.pool_ref, ...), custom_call_target="tpu_custom_call" | custom-call | flops 5000000000 | tf_op jit(solution)/shard_map/norm_pool/pallas_call | solution.py:635
  19.6 35.6 %share_pooled.2 = (bf16[4,2,208,384]{3,2,1,0:T(8,128)(2,1)}, bf16[4,2,112,384]{3,2,1,0:T(8,128)(2,1)}, bf16[2,4,96,1728]{3,2,1,0:T(8,128)(2,1)}, f32[2,384]{1,0:...) custom-call(bf16[2,208,384]{2,1,0:T(8,128)(2,1)} %get-tuple-element.97.refs_0_, ...), custom_call_target="tpu_custom_call" | custom-call | flops 30000001024 | tf_op jit(solution)/shard_map/share_pooled/pallas_call | solution.py:863
  55.3 2.6 concatenate.18
  58.2 2.2 slice.4.w_ref
  62.6 21.4 %attend.2 = (bf16[2,784,384]{2,1,0:T(8,128)(2,1)}, f32[2,784,128]{2,1,0:T(8,128)}) custom-call(bf16[2,784,384]{2,1,0:T(8,128)(2,1)} %get-tuple-element.96.x_ref, bf16[4,2,208,384]{3,2,1,0:T(8,128)(2,1)} %get-tuple-element.100.own_ref, bf16[4,2,112,384]{3,2,1,0:T(8,128)(2,1)} %get-tuple-element.101.mem_ref, bf16[2,384,576]{2,1,0:T(8,128)(2,1)} %slice.4.w_ref, ...), custom_call_target="tpu_custom_call" | custom-call | flops 20000000000 | tf_op jit(solution)/shard_map/attend/pallas_call | solution.py:635
  84.0 13.2 %first_mlp.1 = (f32[2,784,384]{2,1,0:T(8,128)}, f32[2,784,384]{2,1,0:T(8,128)}, bf16[2,208,384]{2,1,0:T(8,128)(2,1)}, bf16[2,112,384]{2,1,0:T(8,128)(2,1)}) custom-call(bf16[2,784,384]{2,1,0:T(8,128)(2,1)} %reshape.171.x_ref, bf16[2,784,384]{2,1,0:T(8,128)(2,1)} %get-tuple-element.104.comb_ref, bf16[2,384,1792]{2,1,0:T(8,128)(2,1)} %bitcast.93, ...), custom_call_target="tpu_custom_call" | custom-call | flops 12999999488 | tf_op jit(solution)/shard_map/first_mlp/pallas_call | solution.py:635
  97.2 28.9 %share_pooled.3 = (bf16[4,2,208,384]{3,2,1,0:T(8,128)(2,1)}, bf16[4,2,112,384]{3,2,1,0:T(8,128)(2,1)}) custom-call(bf16[2,208,384]{2,1,0:T(8,128)(2,1)} %get-tuple-element.108.refs_0_.x_ref, bf16[2,112,384]{2,1,0:T(8,128)(2,1)} %get-tuple-element.109.refs_1_, f32[2,4]{1,0:T(2,128)} %compare_convert_fusion.refs_2_.refs_1_), custom_call_target="tpu_custom_call" | custom-call | flops 20000000000 | tf_op jit(solution)/shard_map/share_pooled/pallas_call | solution.py:863
  126.1 16.2 %attend.3 = (bf16[2,208,768]{2,1,0:T(8,128)(2,1)}, f32[2,208,128]{2,1,0:T(8,128)}) custom-call(bf16[2,208,384]{2,1,0:T(8,128)(2,1)} %get-tuple-element.108.refs_0_.x_ref, bf16[4,2,208,384]{3,2,1,0:T(8,128)(2,1)} %get-tuple-element.110.own_ref, bf16[4,2,112,384]{3,2,1,0:T(8,128)(2,1)} %get-tuple-element.111.mem_ref, bf16[2,384,1728]{2,1,0:T(8,128)(2,1)} %bitcast.85, ...), custom_call_target="tpu_custom_call" | custom-call | flops 20000000000 | tf_op jit(solution)/shard_map/attend/pallas_call | solution.py:635
  142.3 26.6 %second_mlp.1 = (bf16[2,196,768]{2,1,0:T(8,128)(2,1)}, bf16[416,768]{1,0:T(8,128)(2,1)}, f32[416,384]{1,0:T(8,128)}, bf16[2,4,2,192,1536]{4,3,2,1,0:T(8,128)(2,1...) custom-call(bf16[416,768]{1,0:T(8,128)(2,1)} %bitcast.104, ...), custom_call_target="tpu_custom_call" | custom-call | flops 25999998976 | tf_op jit(solution)/shard_map/second_mlp/pallas_call | solution.py:635
  169.0 33.5 %attend_back.2 = (f32[2,208,384]{2,1,0:T(8,128)}, bf16[4,2,320,384]{3,2,1,0:T(8,128)(2,1)}, bf16[2,384,1152]{2,1,0:T(8,128)(2,1)}, f32[8,768]{1,0:T(8,128)}) custom-call(bf16[2,208,384]{2,1,0:T(8,128)(2,1)} %get-tuple-element.108.refs_0_.x_ref, bf16[2,208,768]{2,1,0:T(8,128)(2,1)} %bitcast.103, bf16[4,2,208,384]{3,2,1,0:T(8,128)(2,1)} %get-tuple-element.110.own_ref, ...), custom_call_target="tpu_custom_call" | custom-call | flops 35999997952 | tf_op jit(solution)/shard_map/attend_back/pallas_call | solution.py:635
  202.5 3.1 pad_maximum_fusion
  205.7 27.5 %give_back.2 = (f32[2,208,384]{2,1,0:T(8,128)}, f32[2,112,384]{2,1,0:T(8,128)}) custom-call(bf16[4,2,320,384]{3,2,1,0:T(8,128)(2,1)} %get-tuple-element.121.refs_0_, f32[2,4]{1,0:T(2,128)} %compare_convert_fusion.refs_2_.refs_1_), custom_call_target="tpu_custom_call" | custom-call | flops 1000000000 | tf_op jit(solution)/shard_map/give_back/pallas_call | solution.py:1037
  233.2 26.7 %first_back.1 = (f32[2,784,384]{2,1,0:T(8,128)}, bf16[2,784,384]{2,1,0:T(8,128)(2,1)}, bf16[2,384,1792]{2,1,0:T(8,128)(2,1)}, f32[2,1,768]{2,1,0:T(1,128)}, f32[8,384]{1,0:T(8,128)}) custom-call(f32[2,784,384]{2,1,0:T(8,128)} %get-tuple-element.106.middle_ref, f32[2,784,384]{2,1,0:T(8,128)} %get-tuple-element.107.after_ref, ...), custom_call_target="tpu_custom_call" | custom-call | flops 25999998976 | tf_op jit(solution)/shard_map/first_back/pallas_call | solution.py:635
  261.1 3.4 collective-permute-start.2
  265.6 37.4 %attend_back.3 = (f32[2,784,384]{2,1,0:T(8,128)}, bf16[4,2,320,384]{3,2,1,0:T(8,128)(2,1)}, bf16[2,384,576]{2,1,0:T(8,128)(2,1)}, f32[8,384]{1,0:T(8,128)}) custom-call(bf16[2,784,384]{2,1,0:T(8,128)(2,1)} %get-tuple-element.96.x_ref, bf16[2,784,384]{2,1,0:T(8,128)(2,1)} %get-tuple-element.127.g_ref, bf16[4,2,208,384]{3,2,1,0:T(8,128)(2,1)} %get-tuple-element.100.own_ref, ...), custom_call_target="tpu_custom_call" | custom-call | flops 35999997952 | tf_op jit(solution)/shard_map/attend_back/pallas_call | solution.py:635
  304.3 2.4 collective-permute-start.3
  309.1 33.4 %give_back.3 = (f32[2,208,384]{2,1,0:T(8,128)}, f32[2,112,384]{2,1,0:T(8,128)}, bf16[2,2,196,768]{3,2,1,0:T(8,128)(2,1)}, bf16[96,640]{1,0:T(8,128)(2,1)}) custom-call(bf16[4,2,320,384]{3,2,1,0:T(8,128)(2,1)} %get-tuple-element.131.refs_0_, f32[2,4]{1,0:T(2,128)} %compare_convert_fusion.refs_2_.refs_1_, bf16[2,196,768]{2,1,0:T(8,128)(2,1)} %get-tuple-element.132.refs_2_, ...), custom_call_target="tpu_custom_call" | custom-call | flops 1000000000 | tf_op jit(solution)/shard_map/give_back/pallas_call | solution.py:1037
  342.5 2.4 reshape_reshape.3
  345.0 6.0 %last_back.1 = (bf16[2,784,384]{2,1,0:T(8,128)(2,1)}, f32[8,384]{1,0:T(8,128)}) custom-call(bf16[2,784,384]{2,1,0:T(8,128)(2,1)} %reshape.171.x_ref, f32[2,784,384]{2,1,0:T(8,128)} %get-tuple-element.135.res_ref, f32[2,784,384]{2,1,0:T(8,128)} %get-tuple-element.136.dx_ref, f32[2,208,384]{2,1,0:T(8,128)} %get-tuple-element.137.own_ref, ...), custom_call_target="tpu_custom_call" | custom-call | flops 1000000000 | tf_op jit(solution)/shard_map/last_back/pallas_call | solution.py:635
  353.2 3.3 reduce-scatter.6.cloned.1.call-done
  356.5 41.6 %finish.1 = (bf16[2,2,784,384]{3,2,1,0:T(8,128)(2,1)}, f32[40,384]{1,0:T(8,128)}, bf16[96,4736]{1,0:T(8,128)(2,1)}) custom-call(bf16[2,784,384]{2,1,0:T(8,128)(2,1)} %get-tuple-element.139.half_ref, f32[8,384]{1,0:T(8,128)} %get-tuple-element.140.last_ref, f32[8,384]{1,0:T(8,128)} %get-tuple-element.141.qv_a_rows, f32[8,384]{1,0:T(8,128)} %get-tuple-element.142.a_ref, ...), custom_call_target="tpu_custom_call" | custom-call | flops 40000000000 | tf_op jit(solution)/shard_map/finish/pallas_call | solution.py:1158
  398.1 5.6 %reshape.192 = f32[1,4,196,4,384]{4,3,2,1,0:T(4,128)} reshape(bf16[2,2,784,384]{3,2,1,0:T(8,128)(2,1)} %get-tuple-element.152) | data formatting | bytes 7225344 | tf_op jit(solution)/shard_map/transpose | solution.py:1270
  403.7 3.8 write.1
  (78 shorter events, 16.9 us)
Async XLA Ops:
  7.2 5.6 %copy-start = (bf16[1,4,4,49,768]{4,2,3,1,0:T(4,128)(2,1)S(1)}, bf16[1,4,4,49,768]{4,2,3,1,0:T(4,128)(2,1)}, u32[]{:S(2)}) copy-start(bf16[1,4,4,49,768]{4,2,3,1,0:T(4,128)(2,1)} %param.45) | copy-start | bytes 3612676
  7.2 76.7 %all-gather.5.cloned.1.call-start = ((), (), s32[]{:S(2)}) async-start(), calls=%async_computation.6 | async-start | bytes 3096576 | tf_op jit(solution)/shard_map/all_gather | solution.py:1286
  9.2 133.1 %all-gather.7.cloned.1.call-start = ((), (), s32[]{:S(2)}) async-start(), calls=%async_computation.7 | async-start | bytes 13271040 | tf_op jit(solution)/shard_map/all_gather | solution.py:1303
  10.9 1.2 copy-start.10
  10.9 1.2 copy-start.12
  12.1 1.3 copy-start.9
  13.0 1.6 copy-start.13
  19.6 35.7 %copy-start.5 = (bf16[192,1536]{1,0:T(8,128)(2,1)S(1)}, bf16[192,1536]{1,0:T(8,128)(2,1)}, u32[]{:S(2)}) copy-start(bf16[192,1536]{1,0:T(8,128)(2,1)} %param.35) | copy-start | bytes 1769476
  19.6 35.7 %copy-start.6 = (bf16[192,1536]{1,0:T(8,128)(2,1)S(1)}, bf16[192,1536]{1,0:T(8,128)(2,1)}, u32[]{:S(2)}) copy-start(bf16[192,1536]{1,0:T(8,128)(2,1)} %param.36) | copy-start | bytes 1769476
  19.6 35.7 %copy-start.8 = (bf16[192,384]{1,0:T(8,128)(2,1)S(1)}, bf16[192,384]{1,0:T(8,128)(2,1)}, u32[]{:S(2)}) copy-start(bf16[192,384]{1,0:T(8,128)(2,1)} %param.33) | copy-start | bytes 442372
  57.9 202.0 %reduce-scatter.4.cloned.1.call-start = ((), (), s32[]{:S(2)}) async-start(), calls=%async_computation.3 | async-start | bytes 10616832 | tf_op jit(solution)/shard_map/reduce_scatter | solution.py:1348
  60.4 1.6 copy-start.14
  168.9 184.3 %reduce-scatter.8.cloned.1.call-start = ((), (), s32[]{:S(2)}) async-start(), calls=%async_computation.5 | async-start | bytes 3981312 | tf_op jit(solution)/shard_map/reduce_scatter | solution.py:1348
  169.0 33.5 %copy-start.2 = (bf16[2,4,96,768]{3,2,1,0:T(8,128)(2,1)S(1)}, bf16[2,4,96,768]{3,2,1,0:T(8,128)(2,1)}, u32[]{:S(2)}) copy-start(bf16[2,4,96,768]{3,2,1,0:T(8,128)(2,1)} %get-tuple-element.150) | copy-start | bytes 3538948
  169.0 33.5 %copy-start.4 = (bf16[2,4,96,384]{3,2,1,0:T(8,128)(2,1)S(1)}, bf16[2,4,96,384]{3,2,1,0:T(8,128)(2,1)}, u32[]{:S(2)}) copy-start(bf16[2,4,96,384]{3,2,1,0:T(8,128)(2,1)} %get-tuple-element.151) | copy-start | bytes 1769476
  205.6 150.9 %reduce-scatter.6.cloned.1.call-start = ((), (), s32[]{:S(2)}) async-start(), calls=%async_computation.4 | async-start | bytes 3096576 | tf_op jit(solution)/shard_map/reduce_scatter | solution.py:1348
  261.1 41.9 %collective-permute-start.2 = (bf16[96,1536]{1,0:T(8,128)(2,1)S(1)}, bf16[96,1536]{1,0:T(8,128)(2,1)S(1)}, u32[]{:S(2)}, u32[]{:S(2)}) collective-permute-start(bf16[96,1536]{1,0:T(8,128)(2,1)S(1)} %get-tuple-element.174), channel_id=1, source_target_pairs={{0,24},{8,0},{16,8},{24,16},{1,25},{9,1},{17,9},{25,17},{2,26},{10... | collective-permute-start | bytes 884744 | tf_op jit(solution)/shard_map/ppermute | solution.py:1234
  264.5 38.6 %collective-permute-start.1 = (bf16[96,1536]{1,0:T(8,128)(2,1)S(1)}, bf16[96,1536]{1,0:T(8,128)(2,1)S(1)}, u32[]{:S(2)}, u32[]{:S(2)}) collective-permute-start(bf16[96,1536]{1,0:T(8,128)(2,1)S(1)} %get-tuple-element.175), channel_id=1, source_target_pairs={{0,16},{8,24},{16,0},{24,8},{1,17},{9,25},{17,1},{25,9},{2,18},{10... | collective-permute-start | bytes 884744 | tf_op jit(solution)/shard_map/ppermute | solution.py:1234
  264.5 38.6 %collective-permute-start = (bf16[96,1536]{1,0:T(8,128)(2,1)S(1)}, bf16[96,1536]{1,0:T(8,128)(2,1)}, u32[]{:S(2)}, u32[]{:S(2)}) collective-permute-start(bf16[96,1536]{1,0:T(8,128)(2,1)S(1)} %get-tuple-element.173), channel_id=1, source_target_pairs={{0,8},{8,16},{16,24},{24,0},{1,9},{9,17},{17,25},{25,1},{2,10},{10... | collective-permute-start | bytes 884744 | tf_op jit(solution)/shard_map/ppermute | solution.py:1234
  304.3 46.8 %collective-permute-start.3 = (bf16[96,1536]{1,0:T(8,128)(2,1)S(1)}, bf16[96,1536]{1,0:T(8,128)(2,1)}, u32[]{:S(2)}, u32[]{:S(2)}) collective-permute-start(bf16[96,1536]{1,0:T(8,128)(2,1)S(1)} %fusion.2), channel_id=1, source_target_pairs={{0,8},{8,16},{16,24},{24,0},{1,9},{9,17},{17,25},{25,1},{2,10},{10... | collective-permute-start | bytes 884744 | tf_op jit(solution)/shard_map/ppermute | solution.py:1243
  306.7 45.4 %collective-permute-start.4 = (bf16[96,1536]{1,0:T(8,128)(2,1)S(1)}, bf16[96,1536]{1,0:T(8,128)(2,1)}, u32[]{:S(2)}, u32[]{:S(2)}) collective-permute-start(bf16[96,1536]{1,0:T(8,128)(2,1)S(1)} %fusion.2), channel_id=1, source_target_pairs={{0,16},{8,24},{16,0},{24,8},{1,17},{9,25},{17,1},{25,9},{2,18},{10... | collective-permute-start | bytes 884744 | tf_op jit(solution)/shard_map/ppermute | solution.py:1243
  307.5 45.6 %collective-permute-start.5 = (bf16[96,1536]{1,0:T(8,128)(2,1)S(1)}, bf16[96,1536]{1,0:T(8,128)(2,1)S(1)}, u32[]{:S(2)}, u32[]{:S(2)}) collective-permute-start(bf16[96,1536]{1,0:T(8,128)(2,1)S(1)} %fusion.2), channel_id=1, source_target_pairs={{0,24},{8,0},{16,8},{24,16},{1,25},{9,1},{17,9},{25,17},{2,26},{10... | collective-permute-start | bytes 884744 | tf_op jit(solution)/shard_map/ppermute | solution.py:1243
  353.2 45.0 %copy-start.3 = (bf16[4,96,1536]{2,1,0:T(8,128)(2,1)}, bf16[4,96,1536]{2,1,0:T(8,128)(2,1)S(1)}, u32[]{:S(2)}) copy-start(bf16[4,96,1536]{2,1,0:T(8,128)(2,1)S(1)} %bitcast_dynamic-update-slice_fusion) | copy-start | bytes 3538948
  403.7 3.8 copy-start.1
  (2 other events, 1.9 us)
Sparse Core Ops, SparseCore 0:
  10.5 42.4 all-gather.4
  58.0 79.8 all-gather.6
  169.0 86.0 reduce-scatter.3
  259.1 48.0 reduce-scatter.7
  310.4 46.0 reduce-scatter.5

commit v12 on v11

--- a/solution.py
+++ b/solution.py
@@ -515,9 +515,7 @@
 
     @pl.when(step == pl.num_programs(0) - 1)
     def _():
-        padded = sum_s.shape[0] // mixed_ref.shape[0]
-        for m in range(mixed_ref.shape[0]):
-            mixed_ref[m] = sum_s[padded * m:padded * m + mixed_ref.shape[1], :].astype(bf16)
+        mixed_ref[...] = sum_s[...].astype(bf16)
         unit, inverse = norm(after_s[...])
         dlow = dlow_s[...]
         cot = cot_ref[...].astype(f32)
@@ -1332,7 +1330,7 @@
          (all_b, pl.BlockSpec((1, d2, chunk), lambda j: (j // per_head, 0, per_head + j % per_head))),
          (ub_b, pl.BlockSpec((1, chunk), lambda j: (0, j))),
          (gains_b[None], None), (shifts_b, None)],
-        [(shape((share, pooled_tokens, d2), bf16), None), (shape((rows2, d2), bf16), None), (shape((rows2, d1), f32), None),
+        [(shape((rows2, d2), bf16), None), (shape((rows2, d2), bf16), None), (shape((rows2, d1), f32), None),
          (shape((heads, toks, 2, d2 // toks, fb), bf16),
           pl.BlockSpec((1, toks, 2, d2 // toks, chunk), lambda j: (j // per_head, 0, 0, 0, j % per_head))),
          (shape((heads, toks, d2 // toks // 2, 2 * hb), bf16), None), (shape((heads, toks, d2 // toks // 2, 2 * hs), bf16), None),
@@ -1375,7 +1373,7 @@
     dpool1, sum_mlp_b = lax.optimization_barrier((dpool1, sum_mlp_b))
     sum_mlp_b = spread_clips(sum_mlp_b)
     own_back1, mem_back1, mixed_all, sum_qkv_a = give_back(
-        dpool1, pick, own_rows, 3, mixed, by_owner(g_qkv_a))
+        dpool1, pick, own_rows, 3, mixed.reshape(share, own_rows, d2), by_owner(g_qkv_a))
     stream_grad, rows_last = call(
         last_back_kernel, share,
         [(stream, 0), (res1, 0), (dx1, 0), (own_back1, 0), (mem_back1, 0), (gains_a, None),
@@ -1396,7 +1394,7 @@
         [(shape(dims, f32), None) for dims in outs],
         name="write", us=4,
     )
-    mixed_all = mixed_all.reshape(micro, pooled_tokens, d2)
+    mixed_all = mixed_all.reshape(micro, own_rows, d2)[:, :pooled_tokens]
     return (
         by_frame(mixed_all, cotangent.shape),
         by_frame(stream_all.astype(f32), clips_in.shape),

time: 419 us -> 417 us (level)
  no operation moved by 1% of the time
where the time goes in v12:
time: 417 us; the launch traced here: 414 us
  Pallas kernels  357 us (86%)
  local copies, waits for them, and re-layouts  25 us (6%)
  between operations  14.5 us (3%)
  starting transfers between devices  9.69 us (2%)
  other arithmetic  5.63 us (1%)
    pallas_call x10, Pallas kernels, call(): pl.pallas_call(kernel, grid=(steps,), in_specs=[spec(a, how) for a, how i...  189 us
    pallas_call x2, Pallas kernels, share_pooled(): pl.pallas_call(functools.partial(share_kernel, block is not None, len(bia...  64.5 us
    pallas_call x2, Pallas kernels, give_back(): pl.pallas_call(functools.partial(give_back_kernel, half is not None), in_...  62 us
    pallas_call x1, Pallas kernels, finish(): pl.pallas_call(finish_kernel, in_specs=[INVMEM] * (len(rows) + 4), out_sp...  41.7 us
  transfers between devices with their start and end apart: 11, of which 1 were waited for; matrix products, arithmetic and copies ran while one was open for 6% of the time, Pallas kernels for 69%

profile of v12, /device:TPU:0, one launch (start us, length us, event | category | flops | bytes accessed | tf_op | source)
XLA Modules:
  0.0 413.5 jit_solution(11121004836373417357)
XLA Ops:
  7.3 1.9 concatenate.17
  9.2 1.7 dynamic-slice_bitcast_fusion
  15.3 4.3 %norm_pool.1 = (bf16[2,784,384]{2,1,0:T(8,128)(2,1)}, bf16[2,208,384]{2,1,0:T(8,128)(2,1)}, bf16[2,112,384]{2,1,0:T(8,128)(2,1)}) custom-call(bf16[2,784,384]{2,1,0:T(8,128)(2,1)} %reshape.180.x_ref, f32[3,384]{1,0:T(4,128)} %gains_ref.7, f32[5,384]{1,0:T(8,128)} %shifts_ref.7, bf16[208,784]{1,0:T(8,128)(2,1)} %constant.120.clone.pool_ref, ...), custom_call_target="tpu_custom_call" | custom-call | flops 5000000000 | tf_op jit(solution)/shard_map/norm_pool/pallas_call | solution.py:633
  19.7 35.6 %share_pooled.2 = (bf16[4,2,208,384]{3,2,1,0:T(8,128)(2,1)}, bf16[4,2,112,384]{3,2,1,0:T(8,128)(2,1)}, bf16[2,4,96,1728]{3,2,1,0:T(8,128)(2,1)}, f32[2,384]{1,0:...) custom-call(bf16[2,208,384]{2,1,0:T(8,128)(2,1)} %get-tuple-element.97.refs_0_, ...), custom_call_target="tpu_custom_call" | custom-call | flops 30000001024 | tf_op jit(solution)/shard_map/share_pooled/pallas_call | solution.py:861
  55.3 1.8 concatenate.18
  57.4 2.2 slice.8.w_ref
  61.7 21.4 %attend.2 = (bf16[2,784,384]{2,1,0:T(8,128)(2,1)}, f32[2,784,128]{2,1,0:T(8,128)}) custom-call(bf16[2,784,384]{2,1,0:T(8,128)(2,1)} %get-tuple-element.96.x_ref, bf16[4,2,208,384]{3,2,1,0:T(8,128)(2,1)} %get-tuple-element.100.own_ref, bf16[4,2,112,384]{3,2,1,0:T(8,128)(2,1)} %get-tuple-element.101.mem_ref, bf16[2,384,576]{2,1,0:T(8,128)(2,1)} %slice.8.w_ref, ...), custom_call_target="tpu_custom_call" | custom-call | flops 20000000000 | tf_op jit(solution)/shard_map/attend/pallas_call | solution.py:633
  83.1 13.2 %first_mlp.1 = (f32[2,784,384]{2,1,0:T(8,128)}, f32[2,784,384]{2,1,0:T(8,128)}, bf16[2,208,384]{2,1,0:T(8,128)(2,1)}, bf16[2,112,384]{2,1,0:T(8,128)(2,1)}) custom-call(bf16[2,784,384]{2,1,0:T(8,128)(2,1)} %reshape.180.x_ref, bf16[2,784,384]{2,1,0:T(8,128)(2,1)} %get-tuple-element.104.comb_ref, bf16[2,384,1792]{2,1,0:T(8,128)(2,1)} %bitcast.98, ...), custom_call_target="tpu_custom_call" | custom-call | flops 12999999488 | tf_op jit(solution)/shard_map/first_mlp/pallas_call | solution.py:633
  96.3 28.9 %share_pooled.3 = (bf16[4,2,208,384]{3,2,1,0:T(8,128)(2,1)}, bf16[4,2,112,384]{3,2,1,0:T(8,128)(2,1)}) custom-call(bf16[2,208,384]{2,1,0:T(8,128)(2,1)} %get-tuple-element.108.refs_0_.x_ref, bf16[2,112,384]{2,1,0:T(8,128)(2,1)} %get-tuple-element.109.refs_1_, f32[2,4]{1,0:T(2,128)} %compare_convert_fusion.refs_2_.refs_1_), custom_call_target="tpu_custom_call" | custom-call | flops 20000000000 | tf_op jit(solution)/shard_map/share_pooled/pallas_call | solution.py:861
  125.2 16.2 %attend.3 = (bf16[2,208,768]{2,1,0:T(8,128)(2,1)}, f32[2,208,128]{2,1,0:T(8,128)}) custom-call(bf16[2,208,384]{2,1,0:T(8,128)(2,1)} %get-tuple-element.108.refs_0_.x_ref, bf16[4,2,208,384]{3,2,1,0:T(8,128)(2,1)} %get-tuple-element.110.own_ref, bf16[4,2,112,384]{3,2,1,0:T(8,128)(2,1)} %get-tuple-element.111.mem_ref, bf16[2,384,1728]{2,1,0:T(8,128)(2,1)} %bitcast.90, ...), custom_call_target="tpu_custom_call" | custom-call | flops 20000000000 | tf_op jit(solution)/shard_map/attend/pallas_call | solution.py:633
  141.4 26.5 %second_mlp.1 = (bf16[416,768]{1,0:T(8,128)(2,1)}, bf16[416,768]{1,0:T(8,128)(2,1)}, f32[416,384]{1,0:T(8,128)}, bf16[2,4,2,192,1536]{4,3,2,1,0:T(8,128)(2,1)}, ...) custom-call(bf16[416,768]{1,0:T(8,128)(2,1)} %bitcast.110, ...), custom_call_target="tpu_custom_call" | custom-call | flops 25999998976 | tf_op jit(solution)/shard_map/second_mlp/pallas_call | solution.py:633
  168.1 33.5 %attend_back.2 = (f32[2,208,384]{2,1,0:T(8,128)}, bf16[4,2,320,384]{3,2,1,0:T(8,128)(2,1)}, bf16[2,384,1152]{2,1,0:T(8,128)(2,1)}, f32[8,768]{1,0:T(8,128)}) custom-call(bf16[2,208,384]{2,1,0:T(8,128)(2,1)} %get-tuple-element.108.refs_0_.x_ref, bf16[2,208,768]{2,1,0:T(8,128)(2,1)} %bitcast.109, bf16[4,2,208,384]{3,2,1,0:T(8,128)(2,1)} %get-tuple-element.110.own_ref, ...), custom_call_target="tpu_custom_call" | custom-call | flops 35999997952 | tf_op jit(solution)/shard_map/attend_back/pallas_call | solution.py:633
  201.6 3.1 pad_maximum_fusion
  204.8 27.5 %give_back.2 = (f32[2,208,384]{2,1,0:T(8,128)}, f32[2,112,384]{2,1,0:T(8,128)}) custom-call(bf16[4,2,320,384]{3,2,1,0:T(8,128)(2,1)} %get-tuple-element.121.refs_0_, f32[2,4]{1,0:T(2,128)} %compare_convert_fusion.refs_2_.refs_1_), custom_call_target="tpu_custom_call" | custom-call | flops 1000000000 | tf_op jit(solution)/shard_map/give_back/pallas_call | solution.py:1035
  232.3 26.7 %first_back.1 = (f32[2,784,384]{2,1,0:T(8,128)}, bf16[2,784,384]{2,1,0:T(8,128)(2,1)}, bf16[2,384,1792]{2,1,0:T(8,128)(2,1)}, f32[2,1,768]{2,1,0:T(1,128)}, f32[8,384]{1,0:T(8,128)}) custom-call(f32[2,784,384]{2,1,0:T(8,128)} %get-tuple-element.106.middle_ref, f32[2,784,384]{2,1,0:T(8,128)} %get-tuple-element.107.after_ref, ...), custom_call_target="tpu_custom_call" | custom-call | flops 25999998976 | tf_op jit(solution)/shard_map/first_back/pallas_call | solution.py:633
  260.2 3.4 collective-permute-start.2
  264.8 37.4 %attend_back.3 = (f32[2,784,384]{2,1,0:T(8,128)}, bf16[4,2,320,384]{3,2,1,0:T(8,128)(2,1)}, bf16[2,384,576]{2,1,0:T(8,128)(2,1)}, f32[8,384]{1,0:T(8,128)}) custom-call(bf16[2,784,384]{2,1,0:T(8,128)(2,1)} %get-tuple-element.96.x_ref, bf16[2,784,384]{2,1,0:T(8,128)(2,1)} %get-tuple-element.127.g_ref, bf16[4,2,208,384]{3,2,1,0:T(8,128)(2,1)} %get-tuple-element.100.own_ref, ...), custom_call_target="tpu_custom_call" | custom-call | flops 35999997952 | tf_op jit(solution)/shard_map/attend_back/pallas_call | solution.py:633
  303.4 2.4 collective-permute-start.3
  306.6 1.6 collective-permute-start.5
  308.2 34.4 %give_back.3 = (f32[2,208,384]{2,1,0:T(8,128)}, f32[2,112,384]{2,1,0:T(8,128)}, bf16[2,2,208,768]{3,2,1,0:T(8,128)(2,1)}, bf16[96,640]{1,0:T(8,128)(2,1)}) custom-call(bf16[4,2,320,384]{3,2,1,0:T(8,128)(2,1)} %get-tuple-element.131.refs_0_, f32[2,4]{1,0:T(2,128)} %compare_convert_fusion.refs_2_.refs_1_, bf16[2,208,768]{2,1,0:T(8,128)(2,1)} %bitcast.107, ...), custom_call_target="tpu_custom_call" | custom-call | flops 1000000000 | tf_op jit(solution)/shard_map/give_back/pallas_call | solution.py:1035
  346.0 6.1 %last_back.1 = (bf16[2,784,384]{2,1,0:T(8,128)(2,1)}, f32[8,384]{1,0:T(8,128)}) custom-call(bf16[2,784,384]{2,1,0:T(8,128)(2,1)} %reshape.180.x_ref, f32[2,784,384]{2,1,0:T(8,128)} %get-tuple-element.135.res_ref, f32[2,784,384]{2,1,0:T(8,128)} %get-tuple-element.136.dx_ref, f32[2,208,384]{2,1,0:T(8,128)} %get-tuple-element.137.own_ref, ...), custom_call_target="tpu_custom_call" | custom-call | flops 1000000000 | tf_op jit(solution)/shard_map/last_back/pallas_call | solution.py:633
  355.6 41.7 %finish.1 = (bf16[2,2,784,384]{3,2,1,0:T(8,128)(2,1)}, f32[40,384]{1,0:T(8,128)}, bf16[96,4736]{1,0:T(8,128)(2,1)}) custom-call(bf16[2,784,384]{2,1,0:T(8,128)(2,1)} %get-tuple-element.139.half_ref, f32[8,384]{1,0:T(8,128)} %get-tuple-element.140.last_ref, f32[8,384]{1,0:T(8,128)} %get-tuple-element.141.qv_a_rows, f32[8,384]{1,0:T(8,128)} %get-tuple-element.142.a_ref, ...), custom_call_target="tpu_custom_call" | custom-call | flops 40000000000 | tf_op jit(solution)/shard_map/finish/pallas_call | solution.py:1156
  397.3 5.6 %reshape.204 = f32[1,4,196,4,384]{4,3,2,1,0:T(4,128)} reshape(bf16[2,2,784,384]{3,2,1,0:T(8,128)(2,1)} %get-tuple-element.152) | data formatting | bytes 7225344 | tf_op jit(solution)/shard_map/transpose | solution.py:1268
  402.9 3.8 write.1
  (82 shorter events, 18.1 us)
Async XLA Ops:
  7.2 5.6 %copy-start = (bf16[1,4,4,49,768]{4,2,3,1,0:T(4,128)(2,1)S(1)}, bf16[1,4,4,49,768]{4,2,3,1,0:T(4,128)(2,1)}, u32[]{:S(2)}) copy-start(bf16[1,4,4,49,768]{4,2,3,1,0:T(4,128)(2,1)} %param.45) | copy-start | bytes 3612676
  7.2 75.9 %all-gather.5.cloned.1.call-start = ((), (), s32[]{:S(2)}) async-start(), calls=%async_computation.6 | async-start | bytes 3096576 | tf_op jit(solution)/shard_map/all_gather | solution.py:1284
  9.2 132.3 %all-gather.7.cloned.1.call-start = ((), (), s32[]{:S(2)}) async-start(), calls=%async_computation.7 | async-start | bytes 13271040 | tf_op jit(solution)/shard_map/all_gather | solution.py:1301
  10.9 1.2 copy-start.11
  12.1 1.3 copy-start.9
  13.0 1.6 copy-start.14
  19.6 35.7 %copy-start.5 = (bf16[192,1536]{1,0:T(8,128)(2,1)S(1)}, bf16[192,1536]{1,0:T(8,128)(2,1)}, u32[]{:S(2)}) copy-start(bf16[192,1536]{1,0:T(8,128)(2,1)} %param.35) | copy-start | bytes 1769476
  19.6 35.7 %copy-start.6 = (bf16[192,1536]{1,0:T(8,128)(2,1)S(1)}, bf16[192,1536]{1,0:T(8,128)(2,1)}, u32[]{:S(2)}) copy-start(bf16[192,1536]{1,0:T(8,128)(2,1)} %param.36) | copy-start | bytes 1769476
  19.6 35.7 %copy-start.8 = (bf16[192,384]{1,0:T(8,128)(2,1)S(1)}, bf16[192,384]{1,0:T(8,128)(2,1)}, u32[]{:S(2)}) copy-start(bf16[192,384]{1,0:T(8,128)(2,1)} %param.33) | copy-start | bytes 442372
  19.6 35.7 %copy-start.10 = (bf16[192,192]{1,0:T(8,128)(2,1)S(1)}, bf16[192,192]{1,0:T(8,128)(2,1)}, u32[]{:S(2)}) copy-start(bf16[192,192]{1,0:T(8,128)(2,1)} %param.34) | copy-start | bytes 221188
  57.2 201.8 %reduce-scatter.4.cloned.1.call-start = ((), (), s32[]{:S(2)}) async-start(), calls=%async_computation.3 | async-start | bytes 10616832 | tf_op jit(solution)/shard_map/reduce_scatter | solution.py:1346
  59.6 1.5 copy-start.15
  168.0 186.3 %reduce-scatter.8.cloned.1.call-start = ((), (), s32[]{:S(2)}) async-start(), calls=%async_computation.5 | async-start | bytes 3981312 | tf_op jit(solution)/shard_map/reduce_scatter | solution.py:1346
  168.1 33.5 %copy-start.2 = (bf16[2,4,96,768]{3,2,1,0:T(8,128)(2,1)S(1)}, bf16[2,4,96,768]{3,2,1,0:T(8,128)(2,1)}, u32[]{:S(2)}) copy-start(bf16[2,4,96,768]{3,2,1,0:T(8,128)(2,1)} %get-tuple-element.150) | copy-start | bytes 3538948
  168.1 33.5 %copy-start.4 = (bf16[2,4,96,384]{3,2,1,0:T(8,128)(2,1)S(1)}, bf16[2,4,96,384]{3,2,1,0:T(8,128)(2,1)}, u32[]{:S(2)}) copy-start(bf16[2,4,96,384]{3,2,1,0:T(8,128)(2,1)} %get-tuple-element.151) | copy-start | bytes 1769476
  204.7 150.9 %reduce-scatter.6.cloned.1.call-start = ((), (), s32[]{:S(2)}) async-start(), calls=%async_computation.4 | async-start | bytes 3096576 | tf_op jit(solution)/shard_map/reduce_scatter | solution.py:1346
  260.2 41.9 %collective-permute-start.2 = (bf16[96,1536]{1,0:T(8,128)(2,1)S(1)}, bf16[96,1536]{1,0:T(8,128)(2,1)S(1)}, u32[]{:S(2)}, u32[]{:S(2)}) collective-permute-start(bf16[96,1536]{1,0:T(8,128)(2,1)S(1)} %get-tuple-element.212), channel_id=1, source_target_pairs={{0,24},{8,0},{16,8},{24,16},{1,25},{9,1},{17,9},{25,17},{2,26},{10... | collective-permute-start | bytes 884744 | tf_op jit(solution)/shard_map/ppermute | solution.py:1232
  263.6 38.6 %collective-permute-start.1 = (bf16[96,1536]{1,0:T(8,128)(2,1)S(1)}, bf16[96,1536]{1,0:T(8,128)(2,1)S(1)}, u32[]{:S(2)}, u32[]{:S(2)}) collective-permute-start(bf16[96,1536]{1,0:T(8,128)(2,1)S(1)} %get-tuple-element.213), channel_id=1, source_target_pairs={{0,16},{8,24},{16,0},{24,8},{1,17},{9,25},{17,1},{25,9},{2,18},{10... | collective-permute-start | bytes 884744 | tf_op jit(solution)/shard_map/ppermute | solution.py:1232
  263.6 38.6 %collective-permute-start = (bf16[96,1536]{1,0:T(8,128)(2,1)S(1)}, bf16[96,1536]{1,0:T(8,128)(2,1)}, u32[]{:S(2)}, u32[]{:S(2)}) collective-permute-start(bf16[96,1536]{1,0:T(8,128)(2,1)S(1)} %get-tuple-element.211), channel_id=1, source_target_pairs={{0,8},{8,16},{16,24},{24,0},{1,9},{9,17},{17,25},{25,1},{2,10},{10... | collective-permute-start | bytes 884744 | tf_op jit(solution)/shard_map/ppermute | solution.py:1232
  303.4 48.8 %collective-permute-start.3 = (bf16[96,1536]{1,0:T(8,128)(2,1)S(1)}, bf16[96,1536]{1,0:T(8,128)(2,1)}, u32[]{:S(2)}, u32[]{:S(2)}) collective-permute-start(bf16[96,1536]{1,0:T(8,128)(2,1)S(1)} %fusion.2), channel_id=1, source_target_pairs={{0,8},{8,16},{16,24},{24,0},{1,9},{9,17},{17,25},{25,1},{2,10},{10... | collective-permute-start | bytes 884744 | tf_op jit(solution)/shard_map/ppermute | solution.py:1241
  305.8 47.5 %collective-permute-start.4 = (bf16[96,1536]{1,0:T(8,128)(2,1)S(1)}, bf16[96,1536]{1,0:T(8,128)(2,1)}, u32[]{:S(2)}, u32[]{:S(2)}) collective-permute-start(bf16[96,1536]{1,0:T(8,128)(2,1)S(1)} %fusion.2), channel_id=1, source_target_pairs={{0,16},{8,24},{16,0},{24,8},{1,17},{9,25},{17,1},{25,9},{2,18},{10... | collective-permute-start | bytes 884744 | tf_op jit(solution)/shard_map/ppermute | solution.py:1241
  306.6 47.6 %collective-permute-start.5 = (bf16[96,1536]{1,0:T(8,128)(2,1)S(1)}, bf16[96,1536]{1,0:T(8,128)(2,1)S(1)}, u32[]{:S(2)}, u32[]{:S(2)}) collective-permute-start(bf16[96,1536]{1,0:T(8,128)(2,1)S(1)} %fusion.2), channel_id=1, source_target_pairs={{0,24},{8,0},{16,8},{24,16},{1,25},{9,1},{17,9},{25,17},{2,26},{10... | collective-permute-start | bytes 884744 | tf_op jit(solution)/shard_map/ppermute | solution.py:1241
  354.3 43.0 %copy-start.3 = (bf16[4,96,1536]{2,1,0:T(8,128)(2,1)}, bf16[4,96,1536]{2,1,0:T(8,128)(2,1)S(1)}, u32[]{:S(2)}) copy-start(bf16[4,96,1536]{2,1,0:T(8,128)(2,1)S(1)} %bitcast_dynamic-update-slice_fusion) | copy-start | bytes 3538948
  402.9 3.8 copy-start.1
  (3 other events, 3.1 us)
Sparse Core Ops, SparseCore 0:
  10.5 42.4 all-gather.4
  57.3 79.8 all-gather.6
  168.1 86.0 reduce-scatter.3
  258.2 48.0 reduce-scatter.7
  309.5 46.0 reduce-scatter.5
